TPU v7x, 32 devices: a whole 2x2x4 slice. The times are simulated.
32 devices in a mesh: seq: 8 (over z, y), tp: 4 (over x, core).
Axes of the slice: x: 2, y: 2, z: 4, core: 2. Of those that a mesh axis runs over, the one named last changes fastest.
Arguments:
- tokens: bfloat16 [4, 2048, 2048], P(None, 'seq'), may hold values from -6 to 6
- norm1_gain: bfloat16 [2048], P('seq'), may hold values from 0.5 to 1.5
- in_weight: bfloat16 [2048, 2, 2816], P('seq', None, 'tp'), may hold values from -0.125 to 0.125
- conv_weight: bfloat16 [4, 2816], P(None, 'tp'), may hold values from -3 to 3
- conv_bias: bfloat16 [2816], P('tp'), may hold values from -1.5 to 1.5
- gate_matrix: bfloat16 [2, 16, 176, 176], P(None, 'tp'), may hold values from -0.4375 to 0.4375
- gate_bias: bfloat16 [2, 2816], P(None, 'tp'), may hold values from -4 to 4
- decay_rate: bfloat16 [2816], P('tp'), may hold values from 0.00012207031 to 0.019897461
- out_weight: bfloat16 [2816, 2048], P('tp', 'seq'), may hold values from -0.3125 to 0.3125
- norm2_gain: bfloat16 [2048], P('seq'), may hold values from 0.5 to 1.5
- mlp_weight: bfloat16 [2048, 2, 6144], P('seq', None, 'tp'), may hold values from -0.125 to 0.125
- down_weight: bfloat16 [6144, 2048], P('tp', 'seq'), may hold values from -0.15625 to 0.15625
- cotangent: bfloat16 [4, 2048, 2048], P(None, 'seq'), may hold values from -6 to 6
Outputs:
- output: bfloat16 [4, 2048, 2048], P(None, 'seq')
- grad_tokens: float32 [4, 2048, 2048], P(None, 'seq')
- grad_norm1_gain: float32 [2048], P('seq')
- grad_in_weight: float32 [2048, 2, 2816], P('seq', None, 'tp')
- grad_conv_weight: float32 [4, 2816], P(None, 'tp')
- grad_conv_bias: float32 [2816], P('tp')
- grad_gate_weight: float32 [2, 16, 176, 176], P(None, 'tp')
- grad_gate_bias: float32 [2, 2816], P(None, 'tp')
- grad_decay_rate: float32 [2816], P('tp')
- grad_out_weight: float32 [2816, 2048], P('tp', 'seq')
- grad_norm2_gain: float32 [2048], P('seq')
- grad_mlp_weight: float32 [2048, 2, 6144], P('seq', None, 'tp')
- grad_down_weight: float32 [6144, 2048], P('tp', 'seq')
All inputs are finite; a program needn't handle non-finite values.
Results may differ from a plain program's by a relative error of at most 0.018.
Values may be sent and summed in bfloat16 or wider, within the bound.
No kernel may reach another device: no remote copies, remote signals or barrier semaphores. Data moves between devices by JAX's collectives and lax.ppermute only.
A program may use at most 320 MiB of HBM per device.

v0:
```python
import jax
import jax.numpy as jnp
from jax import lax
from jax.sharding import PartitionSpec as P

eps = 1e-06


def shifted(shard, axis, by):
    length = lax.axis_size(axis)
    pairs = [(i, i + by) for i in range(length) if 0 <= i + by < length]
    return lax.ppermute(shard, axis, pairs)


def chain(earlier, later):
    return (earlier[0] * later[0], later[0] * earlier[1] + later[1])


def root_norm(values):
    inverse = lax.rsqrt(jnp.mean(values * values, axis=-1, keepdims=True) + eps)
    return (values * inverse, inverse)


def norm_back(grad_normed, scaled_in, inverse, gain):
    weighted = grad_normed * gain
    grad_gain = jnp.sum(grad_normed * scaled_in, axis=0)
    grad_in = inverse * (
        weighted - scaled_in * jnp.mean(weighted * scaled_in, axis=-1, keepdims=True)
    )
    return (grad_in, grad_gain)


def linear_unit_gates(gates, rate, mixed):
    recur = jax.nn.sigmoid(gates[0])
    admit = jax.nn.sigmoid(gates[1])
    log_decay = -8.0 * recur * rate
    decay = jnp.exp(log_decay)
    drive = jnp.sqrt(-jnp.expm1(2.0 * log_decay)) * admit * mixed
    return (decay, drive)


def mlp_gate(values):
    return jax.nn.gelu(values[:, 0]) * values[:, 1]


def shards(
    tokens,
    norm1_gain,
    in_weight,
    conv_weight,
    conv_bias,
    gate_matrix,
    gate_bias,
    decay_rate,
    out_weight,
    norm2_gain,
    mlp_weight,
    down_weight,
    cotangent,
):
    seqs, piece, width = tokens.shape
    rows = seqs * piece
    lanes = in_weight.shape[2]
    heads = gate_matrix.shape[1]
    head_width = gate_matrix.shape[2]
    taps = conv_weight.shape[0]
    gain1, w_in, w_out = (
        lax.all_gather(norm1_gain, "seq", axis=0, tiled=True),
        lax.all_gather(in_weight, "seq", axis=0, tiled=True),
        lax.all_gather(out_weight, "seq", axis=1, tiled=True),
    )
    gain1 = gain1.astype(jnp.float32)
    start = tokens.reshape(rows, width).astype(jnp.float32)
    scaled1, inverse1 = root_norm(start)
    normed1 = (scaled1 * gain1).astype(jnp.bfloat16)
    branches = jnp.einsum("td,dkr->tkr", normed1, w_in, preferred_element_type=jnp.float32).astype(
        jnp.bfloat16
    )
    inner = branches[:, 0].reshape(seqs, piece, lanes)
    gate_in = branches[:, 1].astype(jnp.float32)
    before = shifted(inner[:, piece - taps + 1 :], "seq", 1)
    extended = jnp.concatenate([before, inner], axis=1).astype(jnp.float32)
    conv_w = conv_weight.astype(jnp.float32)
    conv_total = jnp.zeros((seqs, piece, lanes), jnp.float32)
    for lag in range(taps):
        conv_total = conv_total + conv_w[lag] * extended[:, taps - 1 - lag : taps - 1 - lag + piece]
    mixed = conv_bias.astype(jnp.float32) + conv_total
    blended_reduced = mixed.astype(jnp.bfloat16).reshape(seqs, piece, heads, head_width)
    gates = jnp.einsum(
        "nvcb,zcbr->znvcr", blended_reduced, gate_matrix, preferred_element_type=jnp.float32
    )
    gates = gates.reshape(2, seqs, piece, lanes) + gate_bias.astype(jnp.float32)[:, None, None, :]
    (decay, drive), pull_gates = jax.vjp(
        linear_unit_gates, gates, decay_rate.astype(jnp.float32), mixed
    )
    cum_decay, local_state = lax.associative_scan(chain, (decay, drive), axis=1)
    ends = (cum_decay[:, -1], local_state[:, -1])

    def forward_step(turn, state):
        return shifted(ends[0] * state + ends[1], "seq", 1)

    entry = lax.fori_loop(0, lax.axis_size("seq") - 1, forward_step, jnp.zeros_like(ends[1]))
    states = local_state + cum_decay * entry[:, None]
    gate_act, pull_gelu = jax.vjp(jax.nn.gelu, gate_in)
    gate_act = gate_act.reshape(seqs, piece, lanes)
    product = (states * gate_act).astype(jnp.bfloat16).reshape(rows, lanes)
    recurrent = lax.psum(jnp.dot(product, w_out, preferred_element_type=jnp.float32), "tp")
    middle = start + recurrent
    gain2, w_mlp, w_down = (
        lax.all_gather(norm2_gain, "seq", axis=0, tiled=True),
        lax.all_gather(mlp_weight, "seq", axis=0, tiled=True),
        lax.all_gather(down_weight, "seq", axis=1, tiled=True),
    )
    gain2 = gain2.astype(jnp.float32)
    scaled2, inverse2 = root_norm(middle)
    normed2 = (scaled2 * gain2).astype(jnp.bfloat16)
    both = jnp.einsum("td,dkf->tkf", normed2, w_mlp, preferred_element_type=jnp.float32).astype(
        jnp.bfloat16
    )
    hidden_full, pull_mlp = jax.vjp(mlp_gate, both.astype(jnp.float32))
    hidden = hidden_full.astype(jnp.bfloat16)
    mlp_out = lax.psum(
        jnp.dot(hidden, w_down, preferred_element_type=jnp.float32).astype(jnp.bfloat16), "tp"
    ).astype(jnp.float32)
    output = (middle + mlp_out).astype(jnp.bfloat16).reshape(seqs, piece, width)
    grad_low = cotangent.reshape(rows, width)
    grad_out = grad_low.astype(jnp.float32)
    grad_down = jnp.einsum("tf,td->fd", hidden, grad_low, preferred_element_type=jnp.float32)
    grad_hidden = jnp.einsum("td,fd->tf", grad_low, w_down, preferred_element_type=jnp.float32)
    grad_both = pull_mlp(grad_hidden)[0].astype(jnp.bfloat16)
    grad_mlpw = jnp.einsum("td,tkf->dkf", normed2, grad_both, preferred_element_type=jnp.float32)
    grad_normed2 = lax.psum(
        jnp.einsum("tkf,dkf->td", grad_both, w_mlp, preferred_element_type=jnp.float32), "tp"
    )
    grad_mid, grad_gain2 = norm_back(grad_normed2, scaled2, inverse2, gain2)
    grad_middle = grad_out + grad_mid
    grad_rec = grad_middle.astype(jnp.bfloat16)
    grad_outw = jnp.einsum("tr,td->rd", product, grad_rec, preferred_element_type=jnp.float32)
    grad_product = jnp.einsum(
        "td,rd->tr", grad_rec, w_out, preferred_element_type=jnp.float32
    ).reshape(seqs, piece, lanes)
    grad_direct = grad_product * gate_act
    grad_gate_in = pull_gelu((grad_product * states).reshape(rows, lanes))[0]
    next_decay = jnp.concatenate([decay[:, 1:], jnp.ones_like(decay[:, :1])], axis=1)
    tail_decay, local_grad = lax.associative_scan(
        chain, (next_decay, grad_direct), axis=1, reverse=True
    )
    first = (decay[:, 0] * tail_decay[:, 0], decay[:, 0] * local_grad[:, 0])

    def reverse_pass_step(turn, state):
        return shifted(first[0] * state + first[1], "seq", -1)

    incoming = lax.fori_loop(
        0, lax.axis_size("seq") - 1, reverse_pass_step, jnp.zeros_like(first[1])
    )
    grad_total = local_grad + tail_decay * incoming[:, None]
    previous = jnp.concatenate([entry[:, None], states[:, :-1]], axis=1)
    grad_gates, grad_rate, grad_drive_mixed = pull_gates((grad_total * previous, grad_total))
    grad_gates_low = grad_gates.astype(jnp.bfloat16)
    grad_gate_b = jnp.sum(grad_gates_low.astype(jnp.float32), axis=(1, 2))
    split_gate_pair = grad_gates_low.reshape(2, seqs, piece, heads, head_width)
    gate_matrix_gradient = jnp.einsum(
        "vglz,tvglm->tlzm", blended_reduced, split_gate_pair, preferred_element_type=jnp.float32
    )
    grad_from_gates = jnp.einsum(
        "ynfte,ytme->nftm", split_gate_pair, gate_matrix, preferred_element_type=jnp.float32
    )
    blended_gradient = (grad_drive_mixed + grad_from_gates.reshape(seqs, piece, lanes)).astype(
        jnp.bfloat16
    )
    grad_mixed_full = blended_gradient.astype(jnp.float32)
    grad_conv_b = jnp.sum(grad_mixed_full, axis=(0, 1))
    after = shifted(blended_gradient[:, : taps - 1], "seq", -1)
    grad_ext = jnp.concatenate([blended_gradient, after], axis=1).astype(jnp.float32)
    grad_inner = jnp.zeros((seqs, piece, lanes), jnp.float32)
    lag_terms = []
    for lag in range(taps):
        grad_inner = grad_inner + conv_w[lag] * grad_ext[:, lag : lag + piece]
        lag_terms.append(
            jnp.sum(
                grad_mixed_full * extended[:, taps - 1 - lag : taps - 1 - lag + piece], axis=(0, 1)
            )
        )
    grad_conv_w = jnp.stack(lag_terms, axis=0)
    grad_branches = jnp.stack([grad_inner.reshape(rows, lanes), grad_gate_in], axis=1).astype(
        jnp.bfloat16
    )
    grad_inw = jnp.einsum("td,tkr->dkr", normed1, grad_branches, preferred_element_type=jnp.float32)
    grad_normed1 = lax.psum(
        jnp.einsum("tkr,dkr->td", grad_branches, w_in, preferred_element_type=jnp.float32).astype(
            jnp.bfloat16
        ),
        "tp",
    ).astype(jnp.float32)
    grad_start, grad_gain1 = norm_back(grad_normed1, scaled1, inverse1, gain1)
    grad_tokens = (grad_middle + grad_start).reshape(seqs, piece, width)
    shard_g1, shard_in, shard_out, shard_g2, shard_mlp, shard_down = (
        lax.psum_scatter(
            grad_gain1.astype(jnp.bfloat16), "seq", scatter_dimension=0, tiled=True
        ).astype(jnp.float32),
        lax.psum_scatter(
            grad_inw.astype(jnp.bfloat16), "seq", scatter_dimension=0, tiled=True
        ).astype(jnp.float32),
        lax.psum_scatter(
            grad_outw.astype(jnp.bfloat16), "seq", scatter_dimension=1, tiled=True
        ).astype(jnp.float32),
        lax.psum_scatter(
            grad_gain2.astype(jnp.bfloat16), "seq", scatter_dimension=0, tiled=True
        ).astype(jnp.float32),
        lax.psum_scatter(
            grad_mlpw.astype(jnp.bfloat16), "seq", scatter_dimension=0, tiled=True
        ).astype(jnp.float32),
        lax.psum_scatter(
            grad_down.astype(jnp.bfloat16), "seq", scatter_dimension=1, tiled=True
        ).astype(jnp.float32),
    )
    summed = (
        lax.psum(grad_conv_w.astype(jnp.bfloat16), "seq").astype(jnp.float32),
        lax.psum(grad_conv_b.astype(jnp.bfloat16), "seq").astype(jnp.float32),
        lax.psum(gate_matrix_gradient.astype(jnp.bfloat16), "seq").astype(jnp.float32),
        lax.psum(grad_gate_b.astype(jnp.bfloat16), "seq").astype(jnp.float32),
        lax.psum(grad_rate.astype(jnp.bfloat16), "seq").astype(jnp.float32),
    )
    return (
        output,
        grad_tokens,
        shard_g1,
        shard_in,
        summed[0],
        summed[1],
        summed[2],
        summed[3],
        summed[4],
        shard_out,
        shard_g2,
        shard_mlp,
        shard_down,
    )


def solution(mesh):
    in_specs = (
        P(None, "seq", None),
        P("seq"),
        P("seq", None, "tp"),
        P(None, "tp"),
        P("tp"),
        P(None, "tp", None, None),
        P(None, "tp"),
        P("tp"),
        P("tp", "seq"),
        P("seq"),
        P("seq", None, "tp"),
        P("tp", "seq"),
        P(None, "seq", None),
    )
    out_specs = (
        P(None, "seq", None),
        P(None, "seq", None),
        P("seq"),
        P("seq", None, "tp"),
        P(None, "tp"),
        P("tp"),
        P(None, "tp", None, None),
        P(None, "tp"),
        P("tp"),
        P("tp", "seq"),
        P("seq"),
        P("seq", None, "tp"),
        P("tp", "seq"),
    )
    return jax.shard_map(shards, mesh=mesh, in_specs=in_specs, out_specs=out_specs, check_vma=False)
```

profile of v0, /device:TPU:0, one launch (start us, length us, event | category | flops | bytes accessed | tf_op | source)
XLA Modules:
  0.0 4746.2 jit_solution(14613940173560139811)
XLA Ops:
  13.3 22.4 all-gather
  39.4 67.1 %all-gather.7.cloned.1.call-done = bf16[2048,2,704]{0,2,1:T(8,128)(2,1)} async-done(((bf16[256,2,704]{0,2,1:T(8,128)(2,1)}), bf16[2048,2,704]{0,2,1:T(8,128)(2,1)}) %all-gather.7.cloned.1.call-update) | async-done | bytes 5767184 | tf_op jit(solution)/shard_map/all_gather | solution.py:69
  145.9 62.3 %slice.638 = f32[4,127,704]{1,2,0:T(8,128)} slice(f32[4,256,704]{1,2,0:T(8,128)} %get-tuple-element.177), slice={[0:4:1], [2:256:2], [0:704:1]} | slice | bytes 2861056 | tf_op jit(solution)/shard_map/slice | solution.py:96
  208.2 63.0 %slice.584 = f32[4,128,704]{1,2,0:T(8,128)} slice(f32[4,256,704]{1,2,0:T(8,128)} %get-tuple-element.177), slice={[0:4:1], [1:256:2], [0:704:1]} | slice | bytes 2883584 | tf_op jit(solution)/shard_map/slice | solution.py:96
  271.2 62.7 %slice.583 = f32[4,128,704]{1,2,0:T(8,128)} slice(f32[4,256,704]{1,2,0:T(8,128)} %get-tuple-element.177), slice={[0:4:1], [0:255:2], [0:704:1]} | slice | bytes 2883584 | tf_op jit(solution)/shard_map/slice | solution.py:96
  337.9 62.7 %slice.586 = f32[4,128,704]{1,2,0:T(8,128)} slice(f32[4,256,704]{1,2,0:T(8,128)} %get-tuple-element.178), slice={[0:4:1], [0:255:2], [0:704:1]} | slice | bytes 2883584 | tf_op jit(solution)/shard_map/slice | solution.py:96
  400.6 62.8 %slice.582 = f32[4,128,704]{1,2,0:T(8,128)} slice(f32[4,256,704]{1,2,0:T(8,128)} %get-tuple-element.178), slice={[0:4:1], [1:256:2], [0:704:1]} | slice | bytes 2883584 | tf_op jit(solution)/shard_map/slice | solution.py:96
  467.5 32.9 slice.636
  500.4 33.0 slice.590
  533.4 32.5 slice.589
  566.0 32.1 slice.592
  598.1 34.4 slice.588
  636.6 17.6 slice.634
  654.1 18.0 slice.596
  706.6 17.9 slice.594
  974.5 32.6 slice.587
  1007.0 62.5 %slice.581 = f32[4,127,704]{1,2,0:T(8,128)} slice(f32[4,256,704]{1,2,0:T(8,128)} %get-tuple-element.178), slice={[0:4:1], [2:256:2], [0:704:1]} | slice | bytes 2861056 | tf_op jit(solution)/shard_map/slice | solution.py:96
  1313.1 26.9 pad.223
  1340.0 27.1 pad.239
  1373.3 26.5 pad.222
  1402.7 27.0 pad.238
  1438.4 50.7 %pad.240 = f32[4,256,704]{1,2,0:T(8,128)} pad(f32[4,128,704]{1,2,0:T(8,128)} %pad_maximum_fusion.13, f32[]{:T(128)} %constant.22.clone.1), padding=0_0_0x0_1_1x0_0_0 | pad | bytes 4325380 | tf_op jit(solution)/shard_map/pad | solution.py:96
  1492.0 50.9 %pad.224 = f32[4,256,704]{1,2,0:T(8,128)} pad(f32[4,128,704]{1,2,0:T(8,128)} %pad_maximum_fusion.6, f32[]{:T(128)} %constant.22.clone.1), padding=0_0_0x0_1_1x0_0_0 | pad | bytes 4325380 | tf_op jit(solution)/shard_map/pad | solution.py:96
  1543.0 51.2 %pad.225 = f32[4,256,704]{1,2,0:T(8,128)} pad(f32[4,128,704]{1,2,0:T(8,128)} %add.506, f32[]{:T(128)} %constant.22.clone.1), padding=0_0_0x1_0_1x0_0_0 | pad | bytes 4325380 | tf_op jit(solution)/shard_map/pad | solution.py:96
  1594.2 50.3 %pad.241 = f32[4,256,704]{1,2,0:T(8,128)} pad(f32[4,128,704]{1,2,0:T(8,128)S(1)} %copy-done.87, f32[]{:T(128)} %constant.22.clone.1), padding=0_0_0x1_0_1x0_0_0 | pad | bytes 4325380 | tf_op jit(solution)/shard_map/pad | solution.py:96
  1650.3 39.4 while.20
  1709.2 21.4 all-gather.1
  1730.5 131.7 %all-reduce.79.cloned.1.call-done = f32[1024,2048]{1,0:T(8,128)} async-done(((f32[1024,2048]{1,0:T(8,128)}), f32[1024,2048]{1,0:T(8,128)}) %all-reduce.79.cloned.1.call-update) | async-done | bytes 8388624 | tf_op jit(solution)/shard_map/psum | solution.py:107
  1871.3 170.1 %all-gather.11.cloned.1.call-done = bf16[2048,2,1536]{2,0,1:T(8,128)(2,1)} async-done(((bf16[256,2,1536]{2,0,1:T(8,128)(2,1)}), bf16[2048,2,1536]{2,0,1:T(8,128)(2,1)}) %all-gather.11.cloned.1.call-update) | async-done | bytes 12582928 | tf_op jit(solution)/shard_map/all_gather | solution.py:111
  2041.4 20.3 convert_convert_fusion
  2061.8 79.7 %all-gather.13.cloned.1.call-done = bf16[1536,2048]{1,0:T(8,128)(2,1)} async-done(((bf16[1536,256]{1,0:T(8,128)(2,1)}), bf16[1536,2048]{1,0:T(8,128)(2,1)}) %all-gather.13.cloned.1.call-update) | async-done | bytes 6291472 | tf_op jit(solution)/shard_map/all_gather | solution.py:112
  2141.5 19.0 multiply_bitcast_fusion
  2160.4 21.1 convolution_bitcast_fusion
  2187.2 63.2 %slice.670 = f32[4,128,704]{1,2,0:T(8,128)} slice(f32[4,256,704]{1,2,0:T(8,128)} %concatenate.111), slice={[0:4:1], [1:256:2], [0:704:1]} | slice | bytes 2883584 | tf_op jit(solution)/shard_map/slice | solution.py:145
  2250.4 62.5 %slice.663 = f32[4,128,704]{1,2,0:T(8,128)S(1)} slice(f32[4,256,704]{1,2,0:T(8,128)} %concatenate.111), slice={[0:4:1], [0:255:2], [0:704:1]} | slice | bytes 2883584 | tf_op jit(solution)/shard_map/slice | solution.py:145
  2312.9 62.8 %slice.661 = f32[4,127,704]{1,2,0:T(8,128)} slice(f32[4,256,704]{1,2,0:T(8,128)} %concatenate.111), slice={[0:4:1], [1:254:2], [0:704:1]} | slice | bytes 2861056 | tf_op jit(solution)/shard_map/slice | solution.py:145
  2449.7 62.8 %slice.723 = f32[4,127,704]{1,2,0:T(8,128)} slice(f32[4,256,704]{1,2,0:T(8,128)} %get-tuple-element.181), slice={[0:4:1], [1:254:2], [0:704:1]} | slice | bytes 2861056 | tf_op jit(solution)/shard_map/slice | solution.py:145
  2512.5 62.7 %slice.667 = f32[4,128,704]{1,2,0:T(8,128)} slice(f32[4,256,704]{1,2,0:T(8,128)} %get-tuple-element.181), slice={[0:4:1], [0:255:2], [0:704:1]} | slice | bytes 2883584 | tf_op jit(solution)/shard_map/slice | solution.py:145
  2575.2 62.7 %slice.665 = f32[4,128,704]{1,2,0:T(8,128)S(1)} slice(f32[4,256,704]{1,2,0:T(8,128)} %get-tuple-element.181), slice={[0:4:1], [1:256:2], [0:704:1]} | slice | bytes 2883584 | tf_op jit(solution)/shard_map/slice | solution.py:145
  2666.9 32.5 slice.677
  2699.4 33.0 slice.673
  2732.4 32.6 slice.672
  2765.0 33.9 slice.721
  2798.9 34.4 slice.675
  2833.3 32.5 slice.674
  2887.8 17.9 slice.679
  2940.7 17.9 slice.681
  3508.3 27.0 pad.273
  3535.3 26.8 pad.257
  3565.5 26.7 pad.272
  3595.2 26.6 pad.256
  3630.8 51.1 %pad.258 = f32[4,256,704]{1,2,0:T(8,128)} pad(f32[4,128,704]{1,2,0:T(8,128)} %pad_maximum_fusion.17, f32[]{:T(128)} %constant.22.clone.1), padding=0_0_0x0_1_1x0_0_0 | pad | bytes 4325380 | tf_op jit(solution)/shard_map/pad | solution.py:145
  3681.9 50.2 %pad.274 = f32[4,256,704]{1,2,0:T(8,128)} pad(f32[4,128,704]{1,2,0:T(8,128)S(1)} %concatenate.125, f32[]{:T(128)} %constant.22.clone.1), padding=0_0_0x0_1_1x0_0_0 | pad | bytes 4325380 | tf_op jit(solution)/shard_map/pad | solution.py:145
  3732.1 51.1 %pad.275 = f32[4,256,704]{1,2,0:T(8,128)} pad(f32[4,128,704]{1,2,0:T(8,128)} %add.555, f32[]{:T(128)} %constant.22.clone.1), padding=0_0_0x1_0_1x0_0_0 | pad | bytes 4325380 | tf_op jit(solution)/shard_map/pad | solution.py:145
  3783.1 50.5 %pad.259 = f32[4,256,704]{1,2,0:T(8,128)} pad(f32[4,128,704]{1,2,0:T(8,128)S(1)} %copy-done.88, f32[]{:T(128)} %constant.22.clone.1), padding=0_0_0x1_0_1x0_0_0 | pad | bytes 4325380 | tf_op jit(solution)/shard_map/pad | solution.py:145
  3859.8 25.8 rev.8
  3885.6 25.9 rev.9
  3911.5 43.9 while.21
  4036.9 22.8 convolution_convert_fusion
  4072.4 138.5 %all-reduce.85.cloned.1.call-done = (bf16[1024,2048]{1,0:T(8,128)(2,1)}, bf16[1024,2048]{1,0:T(8,128)(2,1)}) async-done(((bf16[1024,2048]{1,0:T(8,128)(2,1)}, bf16[1024,2048]{1,0:T(8,128)(2,1)}), (bf16[1024,2048]{1,0:T(8,128)(2,1)}, bf16[1024,2048]{1,0:T(8,128)(2,1)})) %all-reduce.85.cloned.1.call-update) | async-done | bytes 8388624 | tf_op jit(solution)/shard_map/psum | solution.py:122
  4215.9 38.0 all-reduce.72
  4290.3 119.5 %reduce-scatter.11.cloned.1.call-done = bf16[1536,256]{1,0:T(8,128)(2,1)} async-done(((bf16[1536,2048]{1,0:T(8,128)(2,1)}), bf16[1536,256]{1,0:T(8,128)(2,1)}) %reduce-scatter.11.cloned.1.call-update) | async-done | bytes 786448 | tf_op jit(solution)/shard_map/reduce_scatter | solution.py:213
  4412.2 111.3 %reduce-scatter.5.cloned.1.call-done = bf16[256,2,704]{0,2,1:T(8,128)(2,1)} async-done(((bf16[2048,2,704]{0,2,1:T(8,128)(2,1)}), bf16[256,2,704]{0,2,1:T(8,128)(2,1)}) %reduce-scatter.5.cloned.1.call-update) | async-done | bytes 720912 | tf_op jit(solution)/shard_map/reduce_scatter | solution.py:201
  4525.9 208.6 %reduce-scatter.9.cloned.1.call-done = bf16[256,2,1536]{2,0,1:T(8,128)(2,1)} async-done(((bf16[2048,2,1536]{2,0,1:T(8,128)(2,1)}), bf16[256,2,1536]{2,0,1:T(8,128)(2,1)}) %reduce-scatter.9.cloned.1.call-update) | async-done | bytes 1572880 | tf_op jit(solution)/shard_map/reduce_scatter | solution.py:210
  (672 shorter events, 1627.2 us)
Async XLA Ops:
  7.2 131.3 %copy-start = (bf16[2,4,176,176]{3,2,1,0:T(8,128)(2,1)S(1)}, bf16[2,4,176,176]{3,2,1,0:T(8,128)(2,1)}, u32[]{:S(2)}) copy-start(bf16[2,4,176,176]{3,2,1,0:T(8,128)(2,1)} %param.22) | copy-start | bytes 1486852
  7.2 99.3 %all-gather.7.cloned.1.call-start = ((), (), s32[]{:S(2)}) async-start(), calls=%async_computation.4 | async-start | bytes 6488064 | tf_op jit(solution)/shard_map/all_gather | solution.py:69
  7.9 1689.8 %all-gather.9.cloned.1.call-start = ((), (), s32[]{:S(2)}) async-start(), calls=%async_computation.5 | async-start | bytes 3244032 | tf_op jit(solution)/shard_map/all_gather | solution.py:70
  8.7 1853.5 %all-reduce.79.cloned.1.call-start = ((), (), s32[]{:S(2)}) async-start(), calls=%async_computation.6 | async-start | bytes 16777216 | tf_op jit(solution)/shard_map/psum | solution.py:107
  10.1 130.7 %copy-start.117 = (f32[704]{0:T(1024)}, f32[704]{0:T(1024)S(1)}, u32[]{:S(2)}) copy-start(f32[704]{0:T(1024)S(1)} %broadcast_multiply_fusion.2) | copy-start | bytes 8452
  10.1 25.7 copy-start.136
  10.1 26.3 copy-start.3
  13.3 22.5 copy-start.121
  122.8 10.1 collective-permute-start.2
  126.8 7.5 copy-start.123
  126.8 7.5 copy-start.125
  467.5 130.6 %copy-start.10 = (f32[4,128,704]{1,2,0:T(8,128)}, f32[4,128,704]{1,2,0:T(8,128)S(1)}, u32[]{:S(2)}) copy-start(f32[4,128,704]{1,2,0:T(8,128)S(1)} %get-tuple-element.254) | copy-start | bytes 4325380
  636.6 70.0 %copy-start.13 = (f32[4,64,704]{1,2,0:T(8,128)}, f32[4,64,704]{1,2,0:T(8,128)S(1)}, u32[]{:S(2)}) copy-start(f32[4,64,704]{1,2,0:T(8,128)S(1)} %get-tuple-element.252) | copy-start | bytes 2162692
  728.5 48.6 %copy-start.16 = (f32[4,32,704]{1,2,0:T(8,128)}, f32[4,32,704]{1,2,0:T(8,128)S(1)}, u32[]{:S(2)}) copy-start(f32[4,32,704]{1,2,0:T(8,128)S(1)} %get-tuple-element.250) | copy-start | bytes 1081348
  791.3 40.5 copy-start.19
  843.8 36.8 copy-start.21
  1202.2 9.1 copy-start.18
  1214.2 8.8 copy-start.17
  1276.0 14.7 copy-start.14
  1373.3 26.5 copy-start.11
  1402.7 27.0 copy-start.52
  1438.4 50.8 %copy-start.83 = (f32[4,1,704]{1,2,0:T(8,128)S(1)}, f32[4,1,704]{1,2,0:T(8,128)}, u32[]{:S(2)}) copy-start(f32[4,1,704]{1,2,0:T(8,128)} %slice.759) | copy-start | bytes 33796
  1543.0 51.2 %copy-start.87 = (f32[4,128,704]{1,2,0:T(8,128)S(1)}, f32[4,128,704]{1,2,0:T(8,128)}, u32[]{:S(2)}) copy-start(f32[4,128,704]{1,2,0:T(8,128)} %add.515) | copy-start | bytes 4325380
  1650.4 3.3 collective-permute-start
  1653.7 5.6 collective-permute-start
  1659.2 5.6 collective-permute-start
  1664.8 5.6 collective-permute-start
  1670.4 6.3 collective-permute-start
  1676.8 6.5 collective-permute-start
  1683.2 6.5 collective-permute-start
  1697.7 8.1 copy-start.114
  1705.8 335.7 %all-gather.11.cloned.1.call-start = ((), (), s32[]{:S(2)}) async-start(), calls=%async_computation.7 | async-start | bytes 14155776 | tf_op jit(solution)/shard_map/all_gather | solution.py:111
  1708.5 433.0 %all-gather.13.cloned.1.call-start = ((), (), s32[]{:S(2)}) async-start(), calls=%async_computation.8 | async-start | bytes 7077888 | tf_op jit(solution)/shard_map/all_gather | solution.py:112
  1709.1 717.1 %all-reduce.81.cloned.1.call-start = ((), (), s32[]{:S(2)}) async-start(), calls=%async_computation.9 | async-start | bytes 16777216 | tf_op jit(solution)/shard_map/psum | solution.py:132
  1730.5 703.5 %copy-start.119 = (f32[8,1,256]{2,1,0:T(1,128)}, f32[8,1,256]{2,1,0:T(1,128)S(1)}, u32[]{:S(2)}) copy-start(f32[8,1,256]{2,1,0:T(1,128)S(1)} %convert_element_type.228) | copy-start | bytes 24580
  1871.3 562.7 %copy-start.131 = (f32[1024]{0:T(1024)}, f32[1024]{0:T(1024)S(1)}, u32[]{:S(2)}) copy-start(f32[1024]{0:T(1024)S(1)} %add_rsqrt_fusion) | copy-start | bytes 12292
  2181.5 1888.3 %all-reduce.83.cloned.1.call-start = ((), (), s32[]{:S(2)}) async-start(), calls=%async_computation.11 | async-start | bytes 1441792 | tf_op jit(solution)/shard_map/psum | solution.py:220
  2426.2 8.2 copy-start.25
  2426.2 9.4 copy-start.112
  3595.2 26.6 copy-start.61
  3732.1 51.1 %copy-start.88 = (f32[4,128,704]{1,2,0:T(8,128)S(1)}, f32[4,128,704]{1,2,0:T(8,128)}, u32[]{:S(2)}) copy-start(f32[4,128,704]{1,2,0:T(8,128)} %add.546) | copy-start | bytes 4325380
  3885.6 69.9 %copy-start.90 = (f32[4,1,704]{1,2,0:T(8,128)S(1)}, f32[4,1,704]{1,2,0:T(8,128)}, u32[]{:S(2)}) copy-start(f32[4,1,704]{1,2,0:T(8,128)} %copy.224) | copy-start | bytes 33796
  3885.6 69.9 %copy-start.118 = (f32[704]{0:T(1024)S(1)}, f32[704]{0:T(1024)}, u32[]{:S(2)}) copy-start(f32[704]{0:T(1024)} %copy-done.117) | copy-start | bytes 8452
  3911.6 5.6 collective-permute-start.1
  3917.1 5.9 collective-permute-start.1
  3923.1 6.5 collective-permute-start.1
  3929.5 6.5 collective-permute-start.1
  3936.0 6.5 collective-permute-start.1
  3942.5 6.5 collective-permute-start.1
  3949.0 6.5 collective-permute-start.1
  3955.5 8.8 slice-start
  3955.5 8.8 slice-start.1
  3955.5 8.8 copy-start.8
  3955.5 8.8 copy-start.133
  3974.5 6.6 collective-permute-start.3
  3979.8 231.1 %all-reduce.85.cloned.1.call-start = ((), (), s32[]{:S(2)}) async-start(), calls=%async_computation.15 | async-start | bytes 16777216 | tf_op jit(solution)/shard_map/psum | solution.py:122
  4002.8 285.6 %reduce-scatter.7.cloned.1.call-start = ((), (), s32[]{:S(2)}) async-start(), calls=%async_computation.12 | async-start | bytes 3244032 | tf_op jit(solution)/shard_map/reduce_scatter | solution.py:204
  4011.5 398.3 %reduce-scatter.11.cloned.1.call-start = ((), (), s32[]{:S(2)}) async-start(), calls=%async_computation.14 | async-start | bytes 7077888 | tf_op jit(solution)/shard_map/reduce_scatter | solution.py:213
  4025.5 498.0 %reduce-scatter.5.cloned.1.call-start = ((), (), s32[]{:S(2)}) async-start(), calls=%async_computation.10 | async-start | bytes 6488064 | tf_op jit(solution)/shard_map/reduce_scatter | solution.py:201
  4036.2 698.3 %reduce-scatter.9.cloned.1.call-start = ((), (), s32[]{:S(2)}) async-start(), calls=%async_computation.13 | async-start | bytes 14155776 | tf_op jit(solution)/shard_map/reduce_scatter | solution.py:210
  4069.7 141.2 %copy-start.116 = (f32[8,1,256]{2,1,0:T(1,128)S(1)}, f32[8,1,256]{2,1,0:T(1,128)}, u32[]{:S(2)}) copy-start(f32[8,1,256]{2,1,0:T(1,128)} %copy-done.115) | copy-start | bytes 24580
  4069.7 141.2 %copy-start.122 = (f32[1,2,4,128]{3,1,2,0:T(2,128)S(1)}, f32[1,2,4,128]{3,1,2,0:T(2,128)}, u32[]{:S(2)}) copy-start(f32[1,2,4,128]{3,1,2,0:T(2,128)} %copy-done.121) | copy-start | bytes 12292
  4257.6 8.6 copy-start.4
  4257.6 8.6 copy-start.34
  (108 other events, 334.8 us)
Sparse Core Ops, SparseCore 0:
  10.1 96.3 all-gather.6
  108.5 58.1 all-gather.8
  1705.9 156.2 all-reduce.78
  1864.8 176.5 all-gather.10
  2043.3 98.1 all-gather.12
  2181.7 151.0 all-reduce.80
  3980.0 75.7 all-reduce.82
  4058.5 152.3 all-reduce.84
  4215.5 72.8 reduce-scatter.6
  4292.3 117.4 reduce-scatter.10
  4413.9 109.5 reduce-scatter.4
  4527.4 207.0 reduce-scatter.8
where the time goes:
time: 4780 us; the launch traced here: 4750 us
  local copies, waits for them, and re-layouts  3000 us (63%)
  waiting for transfers between devices  1090 us (23%)
  other arithmetic  344 us (7%)
  matrix products  168 us (4%)
  blocking collectives  81.8 us (2%)
    slice x48, local copies, waits for them, and re-layouts, shards(): lax.associative_scan(chain, (next_decay, grad_direct), axis=1, reverse=True)  1000 us
    slice x42, local copies, waits for them, and re-layouts, shards(): cum_decay, local_state = lax.associative_scan(chain, (decay, drive), axis=1)  899 us
    pad x28, local copies, waits for them, and re-layouts, shards(): lax.associative_scan(chain, (next_decay, grad_direct), axis=1, reverse=True)  473 us
    pad x28, local copies, waits for them, and re-layouts, shards(): cum_decay, local_state = lax.associative_scan(chain, (decay, drive), axis=1)  468 us
    reduce_scatter x1, waiting for transfers between devices, shards(): lax.psum_scatter(grad_mlpw.astype(jnp.bfloat16), 'seq', scatter_dimension...  209 us
    all_gather x1, waiting for transfers between devices, shards(): lax.all_gather(mlp_weight, 'seq', axis=0, tiled=True)  170 us
    psum x1, waiting for transfers between devices, shards(): lax.psum(jnp.dot(hidden, w_down, preferred_element_type=jnp.float32).asty...  139 us
    psum x1, waiting for transfers between devices, shards(): lax.psum(jnp.dot(product, w_out, preferred_element_type=jnp.float32), 'tp')  132 us
  transfers between devices with their start and end apart: 28, of which 24 were waited for; matrix products, arithmetic and copies ran while one was open for 41% of the time, Pallas kernels for 0%

commit v1 on v0

v1 whole, which is shorter than its diff:
```python
import functools
import math

import jax
import jax.numpy as jnp
from jax import lax
from jax.experimental import pallas as pl
from jax.experimental.pallas import tpu as pltpu
from jax.sharding import PartitionSpec as P

f32 = jnp.float32
bf16 = jnp.bfloat16
eps = 1e-06
gelu_scale = math.sqrt(2.0 / math.pi)
step_rows = 16
pad_rows = 8
vmem_bytes = 48 * 2**20
ring_most = 8
lane_depth = 2
norm_rows = 128


def ring_order(n):
    return [*range(0, n, 2), *range(n - 1 - n % 2, 0, -2)]


class Lane:
    def __init__(self, order, by, depth):
        n = len(order)
        self.pairs = [(order[i], order[(i + by) % n]) for i in range(n)]
        self.depth = depth
        self.sent = []

    def send(self, message):
        if len(self.sent) >= self.depth:
            message = lax.optimization_barrier((message, self.sent[-self.depth]))[0]
        arrived = lax.ppermute(message, "seq", self.pairs)
        self.sent.append(arrived)
        return arrived


def gather(first, second, right, left, n, chunk):
    half = n // 2
    if n > ring_most:
        both = [lax.all_gather(p, "seq")[chunk] for p in (first, second)]
        return [[p[k] for k in range(n)] for p in both]
    ra, la, rb, lb = [first], [first], [second], [second]
    for _ in range(half - 1):
        ra.append(right.send(ra[-1]))
        la.append(left.send(la[-1]))
        rb.append(right.send(rb[-1]))
        lb.append(left.send(lb[-1]))
    far_a = right.send(ra[-1])
    far_b = left.send(lb[-1])
    return ra + [far_a] + la[:0:-1], rb + [far_b] + lb[:0:-1]


def scatter(first, second, right, left, n, chunk):
    half = n // 2
    if n > ring_most:
        slot = jnp.argsort(chunk)
        both = [jnp.stack([p(k).astype(bf16) for k in range(n)])[slot] for p in (first, second)]
        return [lax.psum_scatter(p, "seq", scatter_dimension=0).astype(f32) for p in both]
    chains = [
        (first, right, list(range(half, n))),
        (second, left, list(range(half, 0, -1))),
        (second, right, list(range(half + 1, n))),
        (first, left, list(range(half - 1, 0, -1))),
    ]
    arrived = [None] * 4
    for step in range(half):
        for i, (part, lane, slots) in enumerate(chains):
            if step < len(slots):
                total = part(slots[step])
                if arrived[i] is not None:
                    total = total + arrived[i].astype(f32)
                arrived[i] = lane.send(total.astype(bf16))
    total_a, total_b = first(0), second(0)
    for i in (0, 3):
        if arrived[i] is not None:
            total_a = total_a + arrived[i].astype(f32)
    for i in (1, 2):
        if arrived[i] is not None:
            total_b = total_b + arrived[i].astype(f32)
    return total_a, total_b


def core_swap(values):
    size = lax.axis_size("tp")
    return lax.ppermute(values, "tp", [(i, i ^ 1) for i in range(size)])


def chip_swap(values):
    size = lax.axis_size("tp")
    return lax.ppermute(values, "tp", [(i, i ^ 2) for i in range(size)])


def tp_sum(part, cuts):
    got = [core_swap(part(1, q).astype(bf16)) for q in range(cuts)]
    chip = [(part(0, q) + got[q].astype(f32)).astype(bf16) for q in range(cuts)]
    total = [(c.astype(f32) + chip_swap(c).astype(f32)).astype(bf16) for c in chip]
    other = [core_swap(t) for t in total]
    return jnp.concatenate(total + other, axis=0)


def gelu_parts(x):
    t = jnp.tanh(gelu_scale * (x + 0.044715 * x * x * x))
    value = 0.5 * x * (1.0 + t)
    slope = 0.5 * (1.0 + t) + 0.5 * x * (1.0 - t * t) * gelu_scale * (1.0 + 3 * 0.044715 * x * x)
    return value, slope


def drive_square(log_decay, decay):
    y = -2.0 * log_decay
    series = 1.0 - y * (1.0 / 9.0)
    for k in range(8, 1, -1):
        series = 1.0 - y * (1.0 / k) * series
    return jnp.where(y < 0.5, y * series, 1.0 - decay * decay)


def scan_block(a, b, rows, reverse):
    count = a.shape[0]
    by = 1
    while by < count:
        turn = count - by if reverse else by
        pa = pltpu.roll(a, turn, 0)
        pb = pltpu.roll(b, turn, 0)
        inside = rows < count - by if reverse else rows >= by
        b = jnp.where(inside, a * pb + b, b)
        a = jnp.where(inside, a * pa, a)
        by *= 2
    return a, b


def forward_kernel(
    inner, before, conv_w, conv_b, gate_m, gate_b, rate,
    mixed, recur, admit, decay, cum, local, ends, ext, gates,
):
    length, lanes = inner.shape
    ext[:pad_rows] = before[...]
    ext[pad_rows:] = inner[...].astype(f32)
    taps = conv_w.shape[0]
    total = jnp.broadcast_to(conv_b[...], (length, lanes))
    for lag in range(taps):
        total = total + conv_w[lag : lag + 1] * ext[pad_rows - lag : pad_rows - lag + length]
    mixed[...] = total
    low = total.astype(bf16)
    for k in range(2):
        gates[k] = jnp.dot(low, gate_m[k], preferred_element_type=f32) + gate_b[k : k + 1]
    rows = lax.broadcasted_iota(jnp.int32, (step_rows, lanes), 0)

    def step(i, carry):
        at = pl.ds(pl.multiple_of(i * step_rows, step_rows), step_rows)
        r = jax.nn.sigmoid(gates[0, at])
        g = jax.nn.sigmoid(gates[1, at])
        log_decay = -8.0 * r * rate[...]
        d = jnp.exp(log_decay)
        drive = jnp.sqrt(drive_square(log_decay, d)) * g * mixed[at]
        recur[at] = r
        admit[at] = g
        decay[at] = d
        a, b = scan_block(d, drive, rows, False)
        b = b + a * carry[1]
        a = a * carry[0]
        cum[at] = a
        local[at] = b
        return a[step_rows - 1 :], b[step_rows - 1 :]

    a, b = lax.fori_loop(
        0, length // step_rows, step, (jnp.ones((1, lanes), f32), jnp.zeros((1, lanes), f32))
    )
    ends[0:1] = a
    ends[1:2] = b
    ends[2:] = jnp.zeros((pad_rows - 2, lanes), f32)


def reverse_kernel(grad_product, gate_in, decay, tail, grad, first, nexts):
    length, lanes = gate_in.shape
    nexts[...] = pltpu.roll(decay[...], length - 1, 0)
    nexts[length - 1 :] = jnp.ones((1, lanes), f32)
    rows = lax.broadcasted_iota(jnp.int32, (step_rows, lanes), 0)
    steps = length // step_rows

    def step(i, carry):
        at = pl.ds(pl.multiple_of((steps - 1 - i) * step_rows, step_rows), step_rows)
        x = gate_in[at].astype(f32)
        direct = grad_product[at] * gelu_parts(x)[0]
        a, b = scan_block(nexts[at], direct, rows, True)
        b = b + a * carry[1]
        a = a * carry[0]
        tail[at] = a
        grad[at] = b
        return a[:1], b[:1]

    a, b = lax.fori_loop(0, steps, step, (jnp.ones((1, lanes), f32), jnp.zeros((1, lanes), f32)))
    first[0:1] = decay[0:1] * a
    first[1:2] = decay[0:1] * b
    first[2:] = jnp.zeros((pad_rows - 2, lanes), f32)


def gates_back_kernel(
    grad_product, gate_in, tail, grad, incoming, cum, local, entry, recur, admit, decay, mixed, gate_m, rate,
    grad_gates, grad_mixed, grad_gate_in, sums, previous, grad_mix,
):
    length, lanes = gate_in.shape
    enter = entry[0:1]
    later = incoming[0:1]
    previous[0:pad_rows] = jnp.broadcast_to(enter, (pad_rows, lanes))
    previous[pad_rows:] = local[...] + cum[...] * enter

    def step(i, carry):
        row = pl.multiple_of(i * step_rows, step_rows)
        at = pl.ds(row, step_rows)
        x = gate_in[at].astype(f32)
        slope = gelu_parts(x)[1]
        states = previous[pl.ds(row + pad_rows, step_rows)]
        head = previous[pl.ds(row, pad_rows)]
        rows = lax.broadcasted_iota(jnp.int32, (step_rows, lanes), 0)
        before = jnp.where(rows == 0, head[pad_rows - 1 :], pltpu.roll(states, 1, 0))
        grad_gate_in[at] = (slope * (grad_product[at] * states)).astype(bf16)
        total = grad[at] + tail[at] * later
        r, g, d, mix = recur[at], admit[at], decay[at], mixed[at]
        root = jnp.sqrt(drive_square(-8.0 * r * rate[...], d))
        grad_mix[at] = total * root * g
        both = total * mix
        gate1 = both * root * g * (1.0 - g)
        grad_log = total * before * d - both * g * d * d / root
        gate0 = -8.0 * rate[...] * grad_log * r * (1.0 - r)
        low0 = gate0.astype(bf16)
        low1 = gate1.astype(bf16)
        grad_gates[0, at] = low0
        grad_gates[1, at] = low1
        return (
            carry[0] - 8.0 * (grad_log * r),
            carry[1] + low0.astype(f32),
            carry[2] + low1.astype(f32),
        )

    zero = jnp.zeros((step_rows, lanes), f32)
    totals = lax.fori_loop(0, length // step_rows, step, (zero, zero, zero))
    back = grad_mix[...]
    for k in range(2):
        back = back + lax.dot_general(
            grad_gates[k], gate_m[k], (((1,), (1,)), ((), ())), preferred_element_type=f32
        )
    low = back.astype(bf16)
    grad_mixed[...] = low

    @pl.when(pl.program_id(0) == 0)
    def _():
        sums[...] = jnp.zeros_like(sums)

    for k in range(3):
        sums[k : k + 1] += jnp.sum(totals[k], axis=0, keepdims=True)
    sums[3:4] += jnp.sum(low.astype(f32), axis=0, keepdims=True)


def conv_back_kernel(grad_mixed, after, inner, before, conv_w, grad_inner, sums, grad_ext, ext):
    length, lanes = inner.shape
    taps = conv_w.shape[0]
    ext[:pad_rows] = before[...]
    ext[pad_rows:] = inner[...].astype(f32)
    grad_ext[length:] = after[...]
    grad = grad_mixed[...].astype(f32)
    grad_ext[:length] = grad

    @pl.when(pl.program_id(0) == 0)
    def _():
        sums[...] = jnp.zeros_like(sums)

    total = jnp.zeros((length, lanes), f32)
    for lag in range(taps):
        total = total + conv_w[lag : lag + 1] * grad_ext[lag : lag + length]
        term = grad * ext[pad_rows - lag : pad_rows - lag + length]
        sums[lag : lag + 1] += jnp.sum(term, axis=0, keepdims=True)
    grad_inner[...] = total.astype(bf16)


def per_sequence(kernel, seqs, inputs, outputs, scratch, flops):
    def spec(shape, kind):
        if kind == "whole":
            return pl.BlockSpec(shape, lambda s: (0,) * len(shape))
        if kind == "pair":
            return pl.BlockSpec((shape[0], None) + shape[2:], lambda s: (0, s, 0, 0))
        return pl.BlockSpec((None,) + shape[1:], lambda s: (s,) + (0,) * (len(shape) - 1))

    moved = sum(a.size * a.dtype.itemsize for a, _ in inputs)
    moved += sum(math.prod(shape) * jnp.dtype(t).itemsize for shape, t, _ in outputs)
    return pl.pallas_call(
        kernel,
        grid=(seqs,),
        in_specs=[spec(a.shape, kind) for a, kind in inputs],
        out_specs=[spec(shape, kind) for shape, _, kind in outputs],
        out_shape=[jax.ShapeDtypeStruct(shape, t) for shape, t, _ in outputs],
        scratch_shapes=scratch,
        compiler_params=pltpu.CompilerParams(vmem_limit_bytes=vmem_bytes),
        cost_estimate=pl.CostEstimate(flops=flops, bytes_accessed=moved, transcendentals=0),
    )(*[a for a, _ in inputs])


def moved_bytes(*arrays):
    return sum(math.prod(a.shape) * jnp.dtype(a.dtype).itemsize for a in arrays)


def by_rows(kernel, arrays, whole, outputs, sums, order=None, back=False):
    seqs, length, width = arrays[0].shape
    block = min(norm_rows, length)
    near = pl.BlockSpec((None, block, width), lambda s, r, *_: (s, r, 0))
    far = pl.BlockSpec((None, block, width), lambda s, r, sequence, chunk: (sequence[s], r, 0))
    moves = order is not None
    total = pl.BlockSpec((pad_rows, width), lambda s, r, *_: (0, 0))
    out_shape = [jax.ShapeDtypeStruct((seqs, length, width), t) for t in outputs]
    out_shape += [jax.ShapeDtypeStruct((pad_rows, width), f32)] * sums
    return pl.pallas_call(
        kernel,
        grid_spec=pltpu.PrefetchScalarGridSpec(
            num_scalar_prefetch=2 if moves else 0,
            grid=(seqs, length // block),
            in_specs=[far if moves and not back else near] * len(arrays)
            + [pl.BlockSpec(w.shape, lambda s, r, *_: (0, 0)) for w in whole],
            out_specs=[far if moves and back else near] * len(outputs) + [total] * sums,
        ),
        out_shape=out_shape,
        compiler_params=pltpu.CompilerParams(vmem_limit_bytes=vmem_bytes),
        cost_estimate=pl.CostEstimate(
            flops=8 * seqs * length * width,
            bytes_accessed=moved_bytes(*arrays, *out_shape),
            transcendentals=0,
        ),
    )(*(order if moves else ()), *arrays, *whole)


def enter_kernel(sequence, chunk, *refs):
    count = len(refs) // 2
    part = refs[0].shape[1] // chunk.shape[0]
    for k in range(chunk.shape[0]):
        at = pl.ds(pl.multiple_of(chunk[k] * part, part), part)
        for i in range(count):
            refs[count + i][:, k * part : (k + 1) * part] = refs[i][:, at]


def norm_kernel(x, added, gain, middle, normed):
    total = x[...].astype(f32) + added[...].astype(f32)
    middle[...] = total
    inverse = lax.rsqrt(jnp.mean(total * total, axis=-1, keepdims=True) + eps)
    normed[...] = (total * inverse * gain[...]).astype(bf16)


def norm_back(values, grad, gain):
    inverse = lax.rsqrt(jnp.mean(values * values, axis=-1, keepdims=True) + eps)
    scaled = values * inverse
    weighted = grad * gain
    inner = jnp.mean(weighted * scaled, axis=-1, keepdims=True)
    return inverse * (weighted - scaled * inner), grad * scaled


def add_rows(total, values):
    @pl.when((pl.program_id(0) == 0) & (pl.program_id(1) == 0))
    def _():
        total[...] = jnp.zeros_like(total)

    rows, width = values.shape
    total[...] += jnp.sum(values.reshape(rows // pad_rows, pad_rows, width), axis=0)


def middle_back_kernel(middle, grad_normed, cot, gain, grad_middle, grad_low, total):
    grad, terms = norm_back(middle[...], grad_normed[...].astype(f32), gain[...])
    grad = grad + cot[...].astype(f32)
    grad_middle[...] = grad
    grad_low[...] = grad.astype(bf16)
    add_rows(total, terms)


def put_chunks(chunk, target, values):
    part = values.shape[1] // chunk.shape[0]
    for k in range(chunk.shape[0]):
        at = pl.ds(pl.multiple_of(chunk[k] * part, part), part)
        target[:, at] = values[:, k * part : (k + 1) * part]


def start_back_kernel(sequence, chunk, x, grad_normed, grad_middle, gain, grad_tokens, total):
    grad, terms = norm_back(x[...].astype(f32), grad_normed[...].astype(f32), gain[...])
    put_chunks(chunk, grad_tokens, grad + grad_middle[...])
    add_rows(total, terms)


def output_kernel(sequence, chunk, middle, added, output):
    put_chunks(chunk, output, (middle[...] + added[...].astype(f32)).astype(bf16))


def own_order(array, order, back=False):
    sequence, chunk = order
    if back:
        sequence, chunk = jnp.argsort(sequence), jnp.argsort(chunk)
    seqs, length, width = array.shape
    chunks = chunk.shape[0]
    split = array[sequence].reshape(seqs, length, chunks, width // chunks)
    return split[:, :, chunk].reshape(array.shape)


def carried(ends, way, n):
    def shifted(values, by):
        pairs = [(i, i + way * by) for i in range(n) if 0 <= i + way * by < n]
        return lax.ppermute(values, "seq", pairs)

    ends = ends[:, :2]
    by = 1
    while 2 * by < n:
        earlier = shifted(ends, by)
        ends = ends[:, :1] * earlier + jnp.concatenate(
            [jnp.zeros_like(ends[:, 1:]), ends[:, 1:]], axis=1
        )
        by *= 2
    near, far = shifted(ends, 1), shifted(ends, 1 + by)
    state = near[:, :1] * far[:, 1:] + near[:, 1:]
    return jnp.pad(state, ((0, 0), (0, pad_rows - 1), (0, 0)))


def seq_sum(values, n):
    by = 1
    while by < n:
        values = values + lax.ppermute(values, "seq", [(i, i ^ by) for i in range(n)])
        by *= 2
    return values


def dense_heads(matrix):
    kinds, heads, width, _ = matrix.shape
    rows = [
        jnp.pad(matrix[:, h], ((0, 0), (0, 0), (h * width, (heads - 1 - h) * width)))
        for h in range(heads)
    ]
    return jnp.concatenate(rows, axis=1)


def across(a, b):
    return lax.dot_general(a, b, (((1,), (1,)), ((), ())), preferred_element_type=f32)


def down(a, b):
    return lax.dot_general(a, b, (((0,), (0,)), ((), ())), preferred_element_type=f32)


def dot(a, b):
    return jnp.dot(a, b, preferred_element_type=f32)


def shards(
    tokens,
    norm1_gain,
    in_weight,
    conv_weight,
    conv_bias,
    gate_matrix,
    gate_bias,
    decay_rate,
    out_weight,
    norm2_gain,
    mlp_weight,
    down_weight,
    cotangent,
):
    seqs, piece, width = tokens.shape
    rows = seqs * piece
    lanes = in_weight.shape[2]
    units = mlp_weight.shape[2]
    heads, head_width = gate_matrix.shape[1:3]
    taps = conv_weight.shape[0]
    n = lax.axis_size("seq")
    part = width // n
    order = ring_order(n)
    place = [order.index(i) for i in range(n)]
    me = jnp.asarray(place, jnp.int32)[lax.axis_index("seq")]
    chunk = jnp.asarray(order, jnp.int32)[(me - jnp.arange(n, dtype=jnp.int32)) % n]
    odd = lax.axis_index("tp") % 2
    sequence = (jnp.arange(seqs, dtype=jnp.int32) + odd * (seqs // 2)) % seqs
    move = (sequence, chunk)
    right, left = Lane(order, 1, lane_depth), Lane(order, -1, lane_depth)
    tiled = part % 128 == 0

    def sl(a, k):
        return a[:, k * part : (k + 1) * part]

    w_in = jnp.transpose(in_weight, (1, 2, 0))
    half_lanes = lanes // 2
    half_units = units // 2
    own_gain = jnp.pad(jnp.stack([norm1_gain, norm2_gain]), ((0, 14), (0, 0)))
    first, second = gather(
        jnp.concatenate([w_in[0], out_weight[:half_lanes]], axis=0),
        jnp.concatenate([w_in[1], out_weight[half_lanes:], own_gain], axis=0),
        right,
        left,
        n,
        chunk,
    )
    mlp0, mlp1 = gather(mlp_weight[:, 0], mlp_weight[:, 1], right, left, n, chunk)
    down0, down1 = gather(
        down_weight[:half_units], down_weight[half_units:], right, left, n, chunk
    )
    in0 = [p[:lanes] for p in first]
    in1 = [p[:lanes] for p in second]
    gains = [p[lanes + half_lanes : lanes + half_lanes + 2] for p in second]
    gain1, gain2 = (
        jnp.concatenate([g[i : i + 1] for g in gains], axis=1).astype(f32) for i in range(2)
    )

    if tiled:
        x, cot = by_rows(enter_kernel, [tokens, cotangent], [], [bf16, bf16], 0, move)
    else:
        x, cot = own_order(tokens, move), own_order(cotangent, move)
    full = x.shape
    grad_low = cot.reshape(rows, width)
    start = x.reshape(rows, width).astype(f32)
    inverse1 = lax.rsqrt(jnp.mean(start * start, axis=-1, keepdims=True) + eps)
    normed1 = [
        (sl(start, k) * inverse1 * gains[k][:1].astype(f32)).astype(bf16) for k in range(n)
    ]
    inner = sum(across(normed1[k], in0[k]) for k in range(n)).astype(bf16)
    gate_in = sum(across(normed1[k], in1[k]) for k in range(n)).astype(bf16)
    inner = inner.reshape(seqs, piece, lanes)
    gate_in = gate_in.reshape(seqs, piece, lanes)
    before = lax.ppermute(
        inner[:, piece - taps + 1 :], "seq", [(i, i + 1) for i in range(n - 1)]
    ).astype(f32)
    before = jnp.pad(before, ((0, 0), (pad_rows - taps + 1, 0), (0, 0)))
    conv_w = conv_weight.astype(f32)
    rate = decay_rate.astype(f32)[None]
    gate_m = dense_heads(gate_matrix)
    wide = (seqs, piece, lanes)
    edge = (seqs, pad_rows, lanes)
    gate_flops = 4 * rows * lanes * lanes
    mixed, recur, admit, decay, cum, local, ends = per_sequence(
        forward_kernel,
        seqs,
        [
            (inner, "seq"),
            (before, "seq"),
            (conv_w, "whole"),
            (conv_bias.astype(f32)[None], "whole"),
            (gate_m, "whole"),
            (gate_bias.astype(f32), "whole"),
            (rate, "whole"),
        ],
        [(wide, f32, "seq")] * 6 + [(edge, f32, "seq")],
        [pltpu.VMEM((piece + pad_rows, lanes), f32), pltpu.VMEM((2, piece, lanes), f32)],
        gate_flops,
    )
    entry = carried(ends, 1, n)
    product = (
        ((local + cum * entry[:, :1]) * jax.nn.gelu(gate_in.astype(f32)))
        .astype(bf16)
        .reshape(rows, lanes)
    )
    w_out = jnp.concatenate(
        [
            jnp.concatenate([p[lanes : lanes + half_lanes] for p in pieces], axis=1)
            for pieces in (first, second)
        ],
        axis=0,
    )
    cuts = 1
    block = rows // (2 * cuts)

    def rows_of(a, h, q):
        begin = (h * cuts + q) * block
        return a[begin : begin + block]

    recurrent = tp_sum(lambda h, q: dot(rows_of(product, h, q), w_out), cuts)

    middle, normed2 = by_rows(norm_kernel, [x, recurrent.reshape(full)], [gain2], [f32, bf16], 0)
    normed2 = normed2.reshape(rows, width)
    w_mlp = jnp.concatenate(
        [jnp.concatenate(mlp0, axis=0), jnp.concatenate(mlp1, axis=0)], axis=1
    )
    both = dot(normed2, w_mlp).astype(bf16).astype(f32)
    both0, both1 = both[:, :units], both[:, units:]
    act, slope = gelu_parts(both0)
    hidden = (act * both1).astype(bf16)
    grad_down = scatter(
        lambda k: down(hidden[:, :half_units], sl(grad_low, k)),
        lambda k: down(hidden[:, half_units:], sl(grad_low, k)),
        right,
        left,
        n,
        chunk,
    )
    w_down = jnp.concatenate(
        [jnp.concatenate(down0, axis=1), jnp.concatenate(down1, axis=1)], axis=0
    )
    grad_hidden = across(grad_low, w_down)
    grad_both = jnp.concatenate(
        [(grad_hidden * both1 * slope).astype(bf16), (grad_hidden * act).astype(bf16)], axis=1
    )
    grad_normed2 = tp_sum(lambda h, q: across(rows_of(grad_both, h, q), w_mlp), cuts)
    grad_mlp = scatter(
        lambda k: down(sl(normed2, k), grad_both[:, :units]),
        lambda k: down(sl(normed2, k), grad_both[:, units:]),
        right,
        left,
        n,
        chunk,
    )
    mlp_out = tp_sum(lambda h, q: dot(rows_of(hidden, h, q), w_down), cuts)

    grad_middle, grad_rec, sum_gain2 = by_rows(
        middle_back_kernel,
        [middle, grad_normed2.reshape(full), cot],
        [gain2],
        [f32, bf16],
        1,
    )
    grad_rec = grad_rec.reshape(rows, width)

    grad_product = across(grad_rec, w_out).reshape(wide)
    tail, local_grad, first = per_sequence(
        reverse_kernel,
        seqs,
        [(grad_product, "seq"), (gate_in, "seq"), (decay, "seq")],
        [(wide, f32, "seq")] * 2 + [(edge, f32, "seq")],
        [pltpu.VMEM((piece, lanes), f32)],
        rows * lanes * 50,
    )
    incoming = carried(first, -1, n)
    grad_gates, grad_mixed, grad_gate_in, sums = per_sequence(
        gates_back_kernel,
        seqs,
        [
            (grad_product, "seq"),
            (gate_in, "seq"),
            (tail, "seq"),
            (local_grad, "seq"),
            (incoming, "seq"),
            (cum, "seq"),
            (local, "seq"),
            (entry, "seq"),
            (recur, "seq"),
            (admit, "seq"),
            (decay, "seq"),
            (mixed, "seq"),
            (gate_m, "whole"),
            (rate, "whole"),
        ],
        [
            ((2,) + wide, bf16, "pair"),
            (wide, bf16, "seq"),
            (wide, bf16, "seq"),
            ((pad_rows, lanes), f32, "whole"),
        ],
        [pltpu.VMEM((piece + pad_rows, lanes), f32), pltpu.VMEM((piece, lanes), f32)],
        gate_flops,
    )
    after = lax.ppermute(
        grad_mixed[:, : taps - 1], "seq", [(i + 1, i) for i in range(n - 1)]
    ).astype(f32)
    after = jnp.pad(after, ((0, 0), (0, pad_rows - taps + 1), (0, 0)))
    grad_inner, conv_sums = per_sequence(
        conv_back_kernel,
        seqs,
        [
            (grad_mixed, "seq"),
            (after, "seq"),
            (inner, "seq"),
            (before, "seq"),
            (conv_w, "whole"),
        ],
        [(wide, bf16, "seq"), ((pad_rows, lanes), f32, "whole")],
        [pltpu.VMEM((piece + pad_rows, lanes), f32)] * 2,
        rows * lanes * 16,
    )
    back0 = grad_inner.reshape(rows, lanes)
    back1 = grad_gate_in.reshape(rows, lanes)
    back = jnp.concatenate([back0, back1], axis=1)
    w_both = jnp.concatenate(
        [jnp.concatenate(in0, axis=1), jnp.concatenate(in1, axis=1)], axis=0
    )
    grad_normed1 = tp_sum(lambda h, q: dot(rows_of(back, h, q), w_both), cuts)
    low_mixed = mixed.astype(bf16).reshape(rows, lanes)
    grad_matrix = []
    for k in range(2):
        dense = down(low_mixed, grad_gates[k].reshape(rows, lanes)).astype(bf16)
        for h in range(heads):
            at = slice(h * head_width, (h + 1) * head_width)
            grad_matrix.append(dense[at, at])
    small = jnp.concatenate([sums[:4], conv_sums[:taps]], axis=0).astype(bf16)
    packed = jnp.concatenate(grad_matrix + [small.reshape(-1, head_width)], axis=0)
    packed = lax.psum(packed, "seq")
    grads = scatter(
        lambda k: jnp.concatenate(
            [down(back0, normed1[k]), down(product[:, :half_lanes], sl(grad_rec, k))], axis=0
        ),
        lambda k: jnp.concatenate(
            [down(back1, normed1[k]), down(product[:, half_lanes:], sl(grad_rec, k))], axis=0
        ),
        right,
        left,
        n,
        chunk,
    )

    if tiled:
        output = by_rows(
            output_kernel, [middle, mlp_out.reshape(full)], [], [bf16], 0, move, back=True
        )[0]
        grad_tokens, sum_gain1 = by_rows(
            start_back_kernel,
            [x, grad_normed1.reshape(full), grad_middle],
            [gain1],
            [f32],
            1,
            move,
            back=True,
        )
    else:
        output = own_order((middle + mlp_out.reshape(full).astype(f32)).astype(bf16), move, True)
        grad_start, terms = norm_back(
            x.astype(f32), grad_normed1.reshape(full).astype(f32), gain1
        )
        grad_tokens = own_order(grad_middle + grad_start, move, True)
        sum_gain1 = jnp.sum(terms, axis=(0, 1))[None]
    mine = lax.axis_index("seq")
    slots = (me - jnp.asarray(place, jnp.int32)) % n
    grad_gains = jnp.stack([jnp.sum(sum_gain1, axis=0), jnp.sum(sum_gain2, axis=0)])
    grad_gains = 0.5 * (grad_gains + core_swap(grad_gains))
    grad_gains = seq_sum(grad_gains.reshape(2, n, part)[:, slots], n)
    grad_gains = lax.dynamic_index_in_dim(grad_gains, mine, 1, keepdims=False)

    packed, grad_gains = lax.optimization_barrier((packed, grad_gains))
    packed = packed.astype(f32)
    matrix_rows = 2 * heads * head_width
    grad_matrix = packed[:matrix_rows].reshape(gate_matrix.shape)
    small = packed[matrix_rows:].reshape(4 + taps, lanes)
    return (
        output,
        grad_tokens,
        grad_gains[0],
        jnp.transpose(jnp.stack([g[:lanes] for g in grads]), (2, 0, 1)),
        small[4:],
        small[3],
        grad_matrix,
        small[1:3],
        small[0],
        jnp.concatenate([g[lanes:] for g in grads], axis=0),
        grad_gains[1],
        jnp.stack(grad_mlp, axis=1),
        jnp.concatenate(grad_down, axis=0),
    )


def solution(mesh):
    in_specs = (
        P(None, "seq", None),
        P("seq"),
        P("seq", None, "tp"),
        P(None, "tp"),
        P("tp"),
        P(None, "tp", None, None),
        P(None, "tp"),
        P("tp"),
        P("tp", "seq"),
        P("seq"),
        P("seq", None, "tp"),
        P("tp", "seq"),
        P(None, "seq", None),
    )
    out_specs = (
        P(None, "seq", None),
        P(None, "seq", None),
        P("seq"),
        P("seq", None, "tp"),
        P(None, "tp"),
        P("tp"),
        P(None, "tp", None, None),
        P(None, "tp"),
        P("tp"),
        P("tp", "seq"),
        P("seq"),
        P("seq", None, "tp"),
        P("tp", "seq"),
    )
    return jax.shard_map(shards, mesh=mesh, in_specs=in_specs, out_specs=out_specs, check_vma=False)
```

time: 4780 us -> 932 us (0.19)
  local copies, waits for them, and re-layouts: 3000 us -> 85 us
  waiting for transfers between devices: 1090 us -> 333 us
  other arithmetic: 344 us -> 48.9 us
  Pallas kernels: 0 us -> 102 us
  starting transfers between devices: 44.2 us -> 141 us
  blocking collectives: 81.8 us -> 0 us
    slice x95 -> x29, local copies, waits for them, and re-layouts: 1900 us -> 10.6 us  [the longest x1 2.24 us: shards(): mlp_weight[:, 1]]
    pad x56 -> x2, local copies, waits for them, and re-layouts: 942 us -> 0.02 us  [carried(): return jnp.pad(state, ((0, 0), (0, pad_rows - 1), (0, 0)))]
    reduce_scatter x4 -> x0, waiting for transfers between devices: 455 us -> none  [the longest x1 209 us: shards(): lax.psum_scatter(grad_mlpw.astype(jnp.bfloat16), 'seq', scatter_dimension...]
    all_gather x4 -> x0, waiting for transfers between devices: 317 us -> none  [the longest x1 170 us: shards(): lax.all_gather(mlp_weight, 'seq', axis=0, tiled=True)]
    ppermute x16 -> x110, waiting for transfers between devices: 45.7 us -> 333 us  [the longest x84 275 us: send(): arrived = lax.ppermute(message, 'seq', self.pairs)]
    psum x4 -> x1, waiting for transfers between devices: 270 us -> 0.01 us  [shards(): packed = lax.psum(packed, 'seq')]
    add x68 -> x10, other arithmetic: 138 us -> 1.6 us  [the longest x1 1.26 us: scatter(): total_a = total_a + arrived[i].astype(f32)]
    pallas_call x0 -> x9, Pallas kernels: none -> 102 us  [the longest x5 52.5 us: by_rows(): pl.pallas_call(kernel, grid_spec=pltpu.PrefetchScalarGridSpec(num_scalar_...]
  transfers between devices with their start and end apart: 28 -> 111, of which waited for: 24 -> 48; matrix products, arithmetic and copies ran while one was open for 41% -> 26% of each run, Pallas kernels for 0% -> 8%
where the time goes in v1:
time: 932 us; the launch traced here: 924 us
  waiting for transfers between devices  333 us (36%)
  matrix products  198 us (21%)
  starting transfers between devices  141 us (15%)
  Pallas kernels  102 us (11%)
  local copies, waits for them, and re-layouts  85 us (9%)
  other arithmetic  48.9 us (5%)
  between operations  16.8 us (2%)
    ppermute x84, waiting for transfers between devices, send(): arrived = lax.ppermute(message, 'seq', self.pairs)  275 us
    ppermute x84, starting transfers between devices, send(): arrived = lax.ppermute(message, 'seq', self.pairs)  100 us
    dot_general x66, matrix products, down(): lax.dot_general(a, b, (((0,), (0,)), ((), ())), preferred_element_type=f32)  82.8 us
    dot_general x20, matrix products, across(): lax.dot_general(a, b, (((1,), (1,)), ((), ())), preferred_element_type=f32)  67.1 us
    unnamed x324, local copies, waits for them, and re-layouts  53.9 us
    pallas_call x5, Pallas kernels, by_rows(): pl.pallas_call(kernel, grid_spec=pltpu.PrefetchScalarGridSpec(num_scalar_...  52.5 us
    pallas_call x4, Pallas kernels, per_sequence(): pl.pallas_call(kernel, grid=(seqs,), in_specs=[spec(a.shape, kind) for a,...  49.6 us
    dot_general x7, matrix products, dot(): return jnp.dot(a, b, preferred_element_type=f32)  48 us
  transfers between devices with their start and end apart: 111, of which 48 were waited for; matrix products, arithmetic and copies ran while one was open for 26% of the time, Pallas kernels for 8%

profile of v1, /device:TPU:0, one launch (start us, length us, event | category | flops | bytes accessed | tf_op | source)
XLA Modules:
  0.0 924.4 jit_solution(1920152105567561210)
XLA Ops:
  20.0 8.5 shard_map.255
  48.4 6.3 collective-permute-done.10
  57.6 8.8 collective-permute-done.7
  70.1 9.7 %collective-permute-done.5 = bf16[1056,256]{1,0:T(8,128)(2,1)S(1)} collective-permute-done((bf16[1056,256]{1,0:T(8,128)(2,1)S(1)}, bf16[1056,256]{1,0:T(8,128)(2,1)S(1)}, u32[]{:S(2)}, u32[]{:S(2)}) %collective-permute-start.5) | collective-permute-done | bytes 540704 | tf_op jit(solution)/shard_map/ppermute | solution.py:37
  80.8 7.0 collective-permute-done.8
  95.1 8.1 collective-permute-done.13
  122.2 3.9 collective-permute-start.14
  133.3 4.0 add_convert_fusion.8
  138.0 16.1 %shard_map.256 = (f32[4,256,704]{2,1,0:T(8,128)}, f32[4,256,704]{2,1,0:T(8,128)}, f32[4,256,704]{2,1,0:T(8,128)}, f32[4,256,704]{2,1,0:T(8,128)}, f32[4,256,704]...) custom-call(bf16[4,256,704]{2,1,0:T(8,128)(2,1)S(1)} %bitcast.182, ...), custom_call_target="tpu_custom_call" | custom-call | flops 2030043136 | bytes 20928512 | tf_op jit(solution)/shard_map/pallas_call | solution.py:289
  154.1 3.4 collective-permute-start.15
  159.1 5.2 collective-permute-start.16
  165.8 5.3 collective-permute-start.18
  171.1 4.4 collective-permute-start.17
  179.0 4.3 fusion.23
  185.2 3.3 convolution_convert_fusion.1
  197.7 12.3 %collective-permute-done.32 = bf16[256,1536]{1,0:T(8,128)(2,1)S(1)} collective-permute-done((bf16[256,1536]{1,0:T(8,128)(2,1)}, bf16[256,1536]{1,0:T(8,128)(2,1)S(1)}, u32[]{:S(2)}, u32[]{:S(2)}) %collective-permute-start.32) | collective-permute-done | bytes 786464 | tf_op jit(solution)/shard_map/ppermute | solution.py:37
  218.6 8.3 collective-permute-done.27
  229.8 13.9 %collective-permute-done.33 = bf16[256,1536]{1,0:T(8,128)(2,1)S(1)} collective-permute-done((bf16[256,1536]{1,0:T(8,128)(2,1)S(1)}, bf16[256,1536]{1,0:T(8,128)(2,1)S(1)}, u32[]{:S(2)}, u32[]{:S(2)}) %collective-permute-start.33) | collective-permute-done | bytes 786464 | tf_op jit(solution)/shard_map/ppermute | solution.py:37
  251.6 9.3 %collective-permute-done.31 = bf16[256,1536]{1,0:T(8,128)(2,1)S(1)} collective-permute-done((bf16[256,1536]{1,0:T(8,128)(2,1)S(1)}, bf16[256,1536]{1,0:T(8,128)(2,1)S(1)}, u32[]{:S(2)}, u32[]{:S(2)}) %collective-permute-start.31) | collective-permute-done | bytes 786464 | tf_op jit(solution)/shard_map/ppermute | solution.py:37
  262.7 14.3 %collective-permute-done.34 = bf16[256,1536]{1,0:T(8,128)(2,1)S(1)} collective-permute-done((bf16[256,1536]{1,0:T(8,128)(2,1)S(1)}, bf16[256,1536]{1,0:T(8,128)(2,1)S(1)}, u32[]{:S(2)}, u32[]{:S(2)}) %collective-permute-start.34) | collective-permute-done | bytes 786464 | tf_op jit(solution)/shard_map/ppermute | solution.py:37
  282.4 3.8 collective-permute-done.36
  290.4 4.2 collective-permute-done.43
  296.4 6.7 collective-permute-done.37
  307.2 14.2 %collective-permute-done.46 = bf16[768,256]{1,0:T(8,128)(2,1)S(1)} collective-permute-done((bf16[768,256]{1,0:T(8,128)(2,1)S(1)}, bf16[768,256]{1,0:T(8,128)(2,1)S(1)}, u32[]{:S(2)}, u32[]{:S(2)}) %collective-permute-start.46) | collective-permute-done | bytes 393248 | tf_op jit(solution)/shard_map/ppermute | solution.py:37
  325.7 7.8 collective-permute-done.47
  334.5 7.4 collective-permute-done.42
  341.9 6.2 collective-permute-done.48
  348.9 8.4 collective-permute-done.49
  361.7 9.5 %shard_map.257 = (f32[4,256,2048]{2,1,0:T(8,128)}, bf16[4,256,2048]{2,1,0:T(8,128)(2,1)S(1)}) custom-call(bf16[4,256,2048]{2,1,0:T(8,128)(2,1)} %copy-done, bf16[4,256,2048]{2,1,0:T(8,128)(2,1)} %bitcast.237, f32[1,2048]{1,0:T(1,128)S(1)} %convert_element_type.461.gain), custom_call_target="tpu_custom_call" | custom-call | flops 16777216 | bytes 20971520 | tf_op jit(solution)/shard_map/pallas_call | solution.py:314
  373.3 20.1 %convert_convert_fusion = f32[1024,3072]{1,0:T(8,128)} fusion(bf16[1024,2048]{1,0:T(8,128)(2,1)} %bitcast.184, bf16[2048,1536]{1,0:T(8,128)(2,1)} %copy-done.100, bf16[2048,1536]{1,0:T(8,128)(2,1)} %constant_dynamic-update-slice_fusion.10), kind=kOutput, calls=%fused_computation.22 | convolution fusion | flops 12916359168 | bytes 29360128 | tf_op jit(solution)/shard_map/dot_general | solution.py:445
  393.4 18.5 %fusion.6 = (bf16[1024,1536]{1,0:T(8,128)(2,1)}, bf16[1024,1536]{1,0:T(8,128)(2,1)S(1)}, bf16[1024,1536]{1,0:T(8,128)(2,1)}) fusion(f32[1024,3072]{1,0:T(8,128)} %convert_convert_fusion, bf16[1024,2048]{1,0:T(8,128)(2,1)} %bitcast.260, bf16[768,2048]{1,0:T(8,128)(2,1)} %copy-done.102, bf16[768,2048]{1,0:T(8,128)(2,1)} %copy-done.106), kind=kOutput, calls=%fused_computation.16 | convolution fusion | flops 6494355456 | bytes 32505856 | tf_op jit(solution)/shard_map/dot_general | solution.py:437
  422.1 4.6 convolution_convert_fusion
  426.7 11.2 %fusion.27 = bf16[512,2048]{1,0:T(8,128)(2,1)} fusion(bf16[2048,1536]{1,0:T(8,128)(2,1)} %copy-done.100, bf16[2048,1536]{1,0:T(8,128)(2,1)} %constant_dynamic-update-slice_fusion.10, bf16[1024,1536]{1,0:T(8,128)(2,1)S(1)} %get-tuple-element.258, bf16[1024,1536]{1,0:T(8,128)(2,1)} %get-tuple-element.257), kind=kOutput, calls=%fused_computation.64 | convolution fusion | flops 6474956800 | bytes 20971520 | tf_op jit(solution)/shard_map/dot_general | solution.py:437
  448.6 3.8 collective-permute-done.89
  455.1 5.7 collective-permute-done.79
  465.9 3.4 collective-permute-done.90
  472.1 4.1 collective-permute-done.69
  480.4 5.7 collective-permute-done.91
  496.4 6.0 collective-permute-done.92
  508.2 8.4 collective-permute-done.82
  527.2 6.1 add_convert_fusion.5
  536.1 11.5 %add_convert_fusion.3 = bf16[512,2048]{1,0:T(8,128)(2,1)} fusion(bf16[512,2048]{1,0:T(8,128)(2,1)} %copy-done.124, bf16[2048,1536]{1,0:T(8,128)(2,1)} %copy-done.100, bf16[2048,1536]{1,0:T(8,128)(2,1)} %constant_dynamic-update-slice_fusion.10, bf16[1024,1536]{1,0:T(8,128)(2,1)} %get-tuple-element.257, bf16[1024,1536]{1,0:T(8,128)(2,1)S(1)} %get-tuple-element.258), kind=kOutput, calls=%fused_computation.44 | convolution fusion | flops 6477053952 | bytes 23068672 | tf_op jit(solution)/shard_map/dot_general | solution.py:437
  561.0 10.3 %collective-permute-done.73 = bf16[256,1536]{1,0:T(8,128)(2,1)S(1)} collective-permute-done((bf16[256,1536]{1,0:T(8,128)(2,1)S(1)}, bf16[256,1536]{1,0:T(8,128)(2,1)S(1)}, u32[]{:S(2)}, u32[]{:S(2)}) %collective-permute-start.73) | collective-permute-done | bytes 786464 | tf_op jit(solution)/shard_map/ppermute | solution.py:37
  575.4 12.7 %collective-permute-done.105 = bf16[256,1536]{1,0:T(8,128)(2,1)S(1)} collective-permute-done((bf16[256,1536]{1,0:T(8,128)(2,1)S(1)}, bf16[256,1536]{1,0:T(8,128)(2,1)S(1)}, u32[]{:S(2)}, u32[]{:S(2)}) %collective-permute-start.105) | collective-permute-done | bytes 786464 | tf_op jit(solution)/shard_map/ppermute | solution.py:37
  590.7 29.3 %collective-permute-done.54 = bf16[512,2048]{1,0:T(8,128)(2,1)S(1)} collective-permute-done((bf16[512,2048]{1,0:T(8,128)(2,1)}, bf16[512,2048]{1,0:T(8,128)(2,1)S(1)}, u32[]{:S(2)}, u32[]{:S(2)}) %collective-permute-start.54) | collective-permute-done | bytes 2097184 | tf_op jit(solution)/shard_map/ppermute | solution.py:95
  627.7 4.4 collective-permute-done.106
  633.1 9.2 collective-permute-done.85
  643.7 4.1 copy.57
  650.3 13.4 %shard_map.259 = (f32[4,256,2048]{2,1,0:T(8,128)}, bf16[4,256,2048]{2,1,0:T(8,128)(2,1)S(1)}, f32[8,2048]{1,0:T(8,128)S(1)}) custom-call(f32[4,256,2048]{2,1,0:T(8,128)} %get-tuple-element.134.middle, bf16[4,256,2048]{2,1,0:T(8,128)(2,1)} %bitcast.239, bf16[4,256,2048]{2,1,0:T(8,128)(2,1)} %get-tuple-element.164.cot, f32[1,2048]{1,0:T(1,128)S(1)} %copy-done.12), custom_call_target="tpu_custom_call" | custom-call | flops 16777216 | bytes 29425664 | tf_op jit(solution)/shard_map/pallas_call | solution.py:314
  665.2 6.4 fusion.29.grad_product
  679.2 8.1 shard_map.260
  697.5 4.4 pad_maximum_fusion.4
  703.3 6.4 collective-permute-done.57
  715.4 8.5 shard_map.258
  724.0 20.8 %shard_map.261 = (bf16[2,4,256,704]{3,2,1,0:T(8,128)(2,1)}, bf16[4,256,704]{2,1,0:T(8,128)(2,1)S(1)}, bf16[4,256,704]{2,1,0:T(8,128)(2,1)S(1)}, f32[8,704]{1,0:T(8,128)S(1)}) custom-call(f32[4,256,704]{2,1,0:T(8,128)} %fusion.29.grad_product, bf16[4,256,704]{2,1,0:T(8,128)(2,1)S(1)} %bitcast.179, f32[4,256,704]{2,1,0:T(8,128)} %copy-done.6, ...), custom_call_target="tpu_custom_call" | custom-call | flops 2030043136 | bytes 35349248 | tf_op jit(solution)/shard_map/pallas_call | solution.py:289
  758.7 4.7 collective-permute-start.107
  768.6 4.6 shard_map.262
  781.2 4.7 fusion.28
  801.2 5.9 add_convert_fusion.1
  813.4 12.7 %collective-permute-done.97 = bf16[1056,256]{1,0:T(8,128)(2,1)S(1)} collective-permute-done((bf16[1056,256]{1,0:T(8,128)(2,1)S(1)}, bf16[1056,256]{1,0:T(8,128)(2,1)S(1)}, u32[]{:S(2)}, u32[]{:S(2)}) %collective-permute-start.97) | collective-permute-done | bytes 540704 | tf_op jit(solution)/shard_map/ppermute | solution.py:37
  828.9 7.8 collective-permute-done.76
  839.5 15.3 %collective-permute-done.62 = bf16[512,2048]{1,0:T(8,128)(2,1)S(1)} collective-permute-done((bf16[512,2048]{1,0:T(8,128)(2,1)S(1)}, bf16[512,2048]{1,0:T(8,128)(2,1)S(1)}, u32[]{:S(2)}, u32[]{:S(2)}) %collective-permute-start.62) | collective-permute-done | bytes 2097184 | tf_op jit(solution)/shard_map/ppermute | solution.py:95
  863.7 13.1 %collective-permute-done.99 = bf16[1056,256]{1,0:T(8,128)(2,1)S(1)} collective-permute-done((bf16[1056,256]{1,0:T(8,128)(2,1)S(1)}, bf16[1056,256]{1,0:T(8,128)(2,1)S(1)}, u32[]{:S(2)}, u32[]{:S(2)}) %collective-permute-start.99) | collective-permute-done | bytes 540704 | tf_op jit(solution)/shard_map/ppermute | solution.py:37
  881.1 12.6 %shard_map.263 = (f32[4,256,2048]{2,1,0:T(8,128)}, f32[8,2048]{1,0:T(8,128)S(1)}) custom-call(s32[4]{0:T(128)S(1)} %copy-done.16, s32[8]{0:T(128)S(1)} %copy-done.14, bf16[4,256,2048]{2,1,0:T(8,128)(2,1)S(1)} %copy-done.1, bf16[4,256,2048]{2,1,0:T(8,128)(2,1)} %bitcast.238, f32[4,256,2048]{2,1,0:T(8,128)} %get-tuple-element.176.grad_middle, ...), custom_call_target="tpu_custom_call" | custom-call | flops 16777216 | bytes 25231360 | tf_op jit(solution)/shard_map/pallas_call | solution.py:314
  (714 shorter events, 354.1 us)
Async XLA Ops:
  7.2 901.2 %all-reduce.15.cloned.1.call-start = ((), (), s32[]{:S(2)}) async-start(), calls=%async_computation | async-start | bytes 1081344 | tf_op jit(solution)/shard_map/psum | solution.py:686
  11.1 28.1 %collective-permute-start.9 = (bf16[1056,256]{1,0:T(8,128)(2,1)}, bf16[1056,256]{1,0:T(8,128)(2,1)}, u32[]{:S(2)}, u32[]{:S(2)}) collective-permute-start(bf16[1056,256]{1,0:T(8,128)(2,1)} %pad_maximum_fusion.37), channel_id=1, source_target_pairs={{0,4},{8,0},{16,8},{24,16},{28,24},{20,28},{12,20},{4,12},{1,5},{9... | collective-permute-start | bytes 1622024 | tf_op jit(solution)/shard_map/ppermute | solution.py:37
  14.1 27.1 %collective-permute-start.1 = (bf16[1056,256]{1,0:T(8,128)(2,1)}, bf16[1056,256]{1,0:T(8,128)(2,1)S(1)}, u32[]{:S(2)}, u32[]{:S(2)}) collective-permute-start(bf16[1056,256]{1,0:T(8,128)(2,1)} %pad_maximum_fusion.37), channel_id=1, source_target_pairs={{0,8},{8,16},{16,24},{24,28},{28,20},{20,12},{12,4},{4,0},{1,9},{9... | collective-permute-start | bytes 1622024 | tf_op jit(solution)/shard_map/ppermute | solution.py:37
  15.0 27.1 %collective-permute-start.6 = (bf16[1072,256]{1,0:T(8,128)(2,1)}, bf16[1072,256]{1,0:T(8,128)(2,1)}, u32[]{:S(2)}, u32[]{:S(2)}) collective-permute-start(bf16[1072,256]{1,0:T(8,128)(2,1)} %pad_maximum_fusion.36), channel_id=1, source_target_pairs={{0,4},{8,0},{16,8},{24,16},{28,24},{20,28},{12,20},{4,12},{1,5},{9... | collective-permute-start | bytes 1646600 | tf_op jit(solution)/shard_map/ppermute | solution.py:37
  17.0 27.0 %collective-permute-start = (bf16[1072,256]{1,0:T(8,128)(2,1)}, bf16[1072,256]{1,0:T(8,128)(2,1)}, u32[]{:S(2)}, u32[]{:S(2)}) collective-permute-start(bf16[1072,256]{1,0:T(8,128)(2,1)} %pad_maximum_fusion.36), channel_id=1, source_target_pairs={{0,8},{8,16},{16,24},{24,28},{28,20},{20,12},{12,4},{4,0},{1,9},{9... | collective-permute-start | bytes 1646600 | tf_op jit(solution)/shard_map/ppermute | solution.py:37
  42.2 24.3 %collective-permute-start.7 = (bf16[1072,256]{1,0:T(8,128)(2,1)}, bf16[1072,256]{1,0:T(8,128)(2,1)S(1)}, u32[]{:S(2)}, u32[]{:S(2)}) collective-permute-start(bf16[1072,256]{1,0:T(8,128)(2,1)} %collective-permute-done.6), channel_id=1, source_target_pairs={{0,4},{8,0},{16,8},{24,16},{28,24},{20,28},{12,20},{4,12},{1,5},{9... | collective-permute-start | bytes 1646600 | tf_op jit(solution)/shard_map/ppermute | solution.py:37
  44.0 24.4 %collective-permute-start.2 = (bf16[1072,256]{1,0:T(8,128)(2,1)}, bf16[1072,256]{1,0:T(8,128)(2,1)S(1)}, u32[]{:S(2)}, u32[]{:S(2)}) collective-permute-start(bf16[1072,256]{1,0:T(8,128)(2,1)} %collective-permute-done), channel_id=1, source_target_pairs={{0,8},{8,16},{16,24},{24,28},{28,20},{20,12},{12,4},{4,0},{1,9},{9... | collective-permute-start | bytes 1646600 | tf_op jit(solution)/shard_map/ppermute | solution.py:37
  54.7 26.1 %collective-permute-start.11 = (bf16[1056,256]{1,0:T(8,128)(2,1)S(1)}, bf16[1056,256]{1,0:T(8,128)(2,1)S(1)}, u32[]{:S(2)}, u32[]{:S(2)}) collective-permute-start(bf16[1056,256]{1,0:T(8,128)(2,1)S(1)} %collective-permute-done.10), channel_id=1, source_target_pairs={{0,4},{8,0},{16,8},{24,16},{28,24},{20,28},{12,20},{4,12},{1,5},{9... | collective-permute-start | bytes 1622024 | tf_op jit(solution)/shard_map/ppermute | solution.py:37
  56.6 23.1 %collective-permute-start.5 = (bf16[1056,256]{1,0:T(8,128)(2,1)S(1)}, bf16[1056,256]{1,0:T(8,128)(2,1)S(1)}, u32[]{:S(2)}, u32[]{:S(2)}) collective-permute-start(bf16[1056,256]{1,0:T(8,128)(2,1)S(1)} %collective-permute-done.3), channel_id=1, source_target_pairs={{0,8},{8,16},{16,24},{24,28},{28,20},{20,12},{12,4},{4,0},{1,9},{9... | collective-permute-start | bytes 1622024 | tf_op jit(solution)/shard_map/ppermute | solution.py:37
  66.5 21.3 %collective-permute-start.8 = (bf16[1072,256]{1,0:T(8,128)(2,1)S(1)}, bf16[1072,256]{1,0:T(8,128)(2,1)S(1)}, u32[]{:S(2)}, u32[]{:S(2)}) collective-permute-start(bf16[1072,256]{1,0:T(8,128)(2,1)S(1)} %collective-permute-done.7), channel_id=1, source_target_pairs={{0,4},{8,0},{16,8},{24,16},{28,24},{20,28},{12,20},{4,12},{1,5},{9... | collective-permute-start | bytes 1646600 | tf_op jit(solution)/shard_map/ppermute | solution.py:37
  68.4 23.1 %collective-permute-start.4 = (bf16[1072,256]{1,0:T(8,128)(2,1)S(1)}, bf16[1072,256]{1,0:T(8,128)(2,1)S(1)}, u32[]{:S(2)}, u32[]{:S(2)}) collective-permute-start(bf16[1072,256]{1,0:T(8,128)(2,1)S(1)} %collective-permute-done.2), channel_id=1, source_target_pairs={{0,8},{8,16},{16,24},{24,28},{28,20},{20,12},{12,4},{4,0},{1,9},{9... | collective-permute-start | bytes 1646600 | tf_op jit(solution)/shard_map/ppermute | solution.py:37
  79.8 23.3 %collective-permute-start.13 = (bf16[1056,256]{1,0:T(8,128)(2,1)S(1)}, bf16[1056,256]{1,0:T(8,128)(2,1)S(1)}, u32[]{:S(2)}, u32[]{:S(2)}) collective-permute-start(bf16[1056,256]{1,0:T(8,128)(2,1)S(1)} %collective-permute-done.5), channel_id=1, source_target_pairs={{0,8},{8,16},{16,24},{24,28},{28,20},{20,12},{12,4},{4,0},{1,9},{9... | collective-permute-start | bytes 1622024 | tf_op jit(solution)/shard_map/ppermute | solution.py:37
  91.5 98.2 %collective-permute-start.22 = (bf16[256,1536]{1,0:T(8,128)(2,1)}, bf16[256,1536]{1,0:T(8,128)(2,1)}, u32[]{:S(2)}, u32[]{:S(2)}) collective-permute-start(bf16[256,1536]{1,0:T(8,128)(2,1)} %get-tuple-element.140), channel_id=1, source_target_pairs={{0,8},{8,16},{16,24},{24,28},{28,20},{20,12},{12,4},{4,0},{1,9},{9... | collective-permute-start | bytes 2359304 | tf_op jit(solution)/shard_map/ppermute | solution.py:37
  91.7 103.2 %collective-permute-start.26 = (bf16[256,1536]{1,0:T(8,128)(2,1)}, bf16[256,1536]{1,0:T(8,128)(2,1)}, u32[]{:S(2)}, u32[]{:S(2)}) collective-permute-start(bf16[256,1536]{1,0:T(8,128)(2,1)} %get-tuple-element.140), channel_id=1, source_target_pairs={{0,4},{8,0},{16,8},{24,16},{28,24},{20,28},{12,20},{4,12},{1,5},{9... | collective-permute-start | bytes 2359304 | tf_op jit(solution)/shard_map/ppermute | solution.py:37
  103.1 92.9 %collective-permute-start.29 = (bf16[256,1536]{1,0:T(8,128)(2,1)}, bf16[256,1536]{1,0:T(8,128)(2,1)}, u32[]{:S(2)}, u32[]{:S(2)}) collective-permute-start(bf16[256,1536]{1,0:T(8,128)(2,1)} %get-tuple-element.143), channel_id=1, source_target_pairs={{0,8},{8,16},{16,24},{24,28},{28,20},{20,12},{12,4},{4,0},{1,9},{9... | collective-permute-start | bytes 2359304 | tf_op jit(solution)/shard_map/ppermute | solution.py:37
  188.6 57.2 %collective-permute-start.19 = (bf16[512,2048]{1,0:T(8,128)(2,1)S(1)}, bf16[512,2048]{1,0:T(8,128)(2,1)S(1)}, u32[]{:S(2)}, u32[]{:S(2)}) collective-permute-start(bf16[512,2048]{1,0:T(8,128)(2,1)S(1)} %convolution_convert_fusion.1), channel_id=1, source_target_pairs={{0,1},{1,0},{2,3},{3,2},{4,5},{5,4},{6,7},{7,6},{8,9},{9,8},{10,11... | collective-permute-start | bytes 6291464 | tf_op jit(solution)/shard_map/ppermute | solution.py:90
  189.8 20.6 %collective-permute-start.23 = (bf16[256,1536]{1,0:T(8,128)(2,1)}, bf16[256,1536]{1,0:T(8,128)(2,1)S(1)}, u32[]{:S(2)}, u32[]{:S(2)}) collective-permute-start(bf16[256,1536]{1,0:T(8,128)(2,1)} %collective-permute-done.22), channel_id=1, source_target_pairs={{0,8},{8,16},{16,24},{24,28},{28,20},{20,12},{12,4},{4,0},{1,9},{9... | collective-permute-start | bytes 2359304 | tf_op jit(solution)/shard_map/ppermute | solution.py:37
  194.9 32.0 %collective-permute-start.27 = (bf16[256,1536]{1,0:T(8,128)(2,1)}, bf16[256,1536]{1,0:T(8,128)(2,1)S(1)}, u32[]{:S(2)}, u32[]{:S(2)}) collective-permute-start(bf16[256,1536]{1,0:T(8,128)(2,1)} %collective-permute-done.26), channel_id=1, source_target_pairs={{0,4},{8,0},{16,8},{24,16},{28,24},{20,28},{12,20},{4,12},{1,5},{9... | collective-permute-start | bytes 2359304 | tf_op jit(solution)/shard_map/ppermute | solution.py:37
  196.0 32.1 %collective-permute-start.30 = (bf16[256,1536]{1,0:T(8,128)(2,1)}, bf16[256,1536]{1,0:T(8,128)(2,1)S(1)}, u32[]{:S(2)}, u32[]{:S(2)}) collective-permute-start(bf16[256,1536]{1,0:T(8,128)(2,1)} %collective-permute-done.29), channel_id=1, source_target_pairs={{0,8},{8,16},{16,24},{24,28},{28,20},{20,12},{12,4},{4,0},{1,9},{9... | collective-permute-start | bytes 2359304 | tf_op jit(solution)/shard_map/ppermute | solution.py:37
  210.0 33.7 %collective-permute-start.33 = (bf16[256,1536]{1,0:T(8,128)(2,1)S(1)}, bf16[256,1536]{1,0:T(8,128)(2,1)S(1)}, u32[]{:S(2)}, u32[]{:S(2)}) collective-permute-start(bf16[256,1536]{1,0:T(8,128)(2,1)S(1)} %collective-permute-done.32), channel_id=1, source_target_pairs={{0,4},{8,0},{16,8},{24,16},{28,24},{20,28},{12,20},{4,12},{1,5},{9... | collective-permute-start | bytes 2359304 | tf_op jit(solution)/shard_map/ppermute | solution.py:37
  210.4 33.7 %collective-permute-start.24 = (bf16[256,1536]{1,0:T(8,128)(2,1)S(1)}, bf16[256,1536]{1,0:T(8,128)(2,1)S(1)}, u32[]{:S(2)}, u32[]{:S(2)}) collective-permute-start(bf16[256,1536]{1,0:T(8,128)(2,1)S(1)} %collective-permute-done.23), channel_id=1, source_target_pairs={{0,8},{8,16},{16,24},{24,28},{28,20},{20,12},{12,4},{4,0},{1,9},{9... | collective-permute-start | bytes 2359304 | tf_op jit(solution)/shard_map/ppermute | solution.py:37
  226.9 50.5 %collective-permute-start.28 = (bf16[256,1536]{1,0:T(8,128)(2,1)S(1)}, bf16[256,1536]{1,0:T(8,128)(2,1)S(1)}, u32[]{:S(2)}, u32[]{:S(2)}) collective-permute-start(bf16[256,1536]{1,0:T(8,128)(2,1)S(1)} %collective-permute-done.27), channel_id=1, source_target_pairs={{0,4},{8,0},{16,8},{24,16},{28,24},{20,28},{12,20},{4,12},{1,5},{9... | collective-permute-start | bytes 2359304 | tf_op jit(solution)/shard_map/ppermute | solution.py:37
  228.1 32.8 %collective-permute-start.31 = (bf16[256,1536]{1,0:T(8,128)(2,1)S(1)}, bf16[256,1536]{1,0:T(8,128)(2,1)S(1)}, u32[]{:S(2)}, u32[]{:S(2)}) collective-permute-start(bf16[256,1536]{1,0:T(8,128)(2,1)S(1)} %collective-permute-done.30), channel_id=1, source_target_pairs={{0,8},{8,16},{16,24},{24,28},{28,20},{20,12},{12,4},{4,0},{1,9},{9... | collective-permute-start | bytes 2359304 | tf_op jit(solution)/shard_map/ppermute | solution.py:37
  243.7 33.3 %collective-permute-start.34 = (bf16[256,1536]{1,0:T(8,128)(2,1)S(1)}, bf16[256,1536]{1,0:T(8,128)(2,1)S(1)}, u32[]{:S(2)}, u32[]{:S(2)}) collective-permute-start(bf16[256,1536]{1,0:T(8,128)(2,1)S(1)} %collective-permute-done.33), channel_id=1, source_target_pairs={{0,4},{8,0},{16,8},{24,16},{28,24},{20,28},{12,20},{4,12},{1,5},{9... | collective-permute-start | bytes 2359304 | tf_op jit(solution)/shard_map/ppermute | solution.py:37
  244.1 33.7 %collective-permute-start.25 = (bf16[256,1536]{1,0:T(8,128)(2,1)S(1)}, bf16[256,1536]{1,0:T(8,128)(2,1)S(1)}, u32[]{:S(2)}, u32[]{:S(2)}) collective-permute-start(bf16[256,1536]{1,0:T(8,128)(2,1)S(1)} %collective-permute-done.24), channel_id=1, source_target_pairs={{0,8},{8,16},{16,24},{24,28},{28,20},{20,12},{12,4},{4,0},{1,9},{9... | collective-permute-start | bytes 2359304 | tf_op jit(solution)/shard_map/ppermute | solution.py:37
  249.0 57.2 %collective-permute-start.20 = (bf16[512,2048]{1,0:T(8,128)(2,1)S(1)}, bf16[512,2048]{1,0:T(8,128)(2,1)S(1)}, u32[]{:S(2)}, u32[]{:S(2)}) collective-permute-start(bf16[512,2048]{1,0:T(8,128)(2,1)S(1)} %add_convert_fusion.7), channel_id=1, source_target_pairs={{0,2},{1,3},{2,0},{3,1},{4,6},{5,7},{6,4},{7,5},{8,10},{9,11},{10,... | collective-permute-start | bytes 6291464 | tf_op jit(solution)/shard_map/ppermute | solution.py:95
  260.9 25.3 %collective-permute-start.36 = (bf16[768,256]{1,0:T(8,128)(2,1)S(1)}, bf16[768,256]{1,0:T(8,128)(2,1)S(1)}, u32[]{:S(2)}, u32[]{:S(2)}) collective-permute-start(bf16[768,256]{1,0:T(8,128)(2,1)S(1)} %copy-done.89), channel_id=1, source_target_pairs={{0,8},{8,16},{16,24},{24,28},{28,20},{20,12},{12,4},{4,0},{1,9},{9... | collective-permute-start | bytes 1179656 | tf_op jit(solution)/shard_map/ppermute | solution.py:37
  277.3 28.6 %collective-permute-start.35 = (bf16[256,1536]{1,0:T(8,128)(2,1)S(1)}, bf16[256,1536]{1,0:T(8,128)(2,1)S(1)}, u32[]{:S(2)}, u32[]{:S(2)}) collective-permute-start(bf16[256,1536]{1,0:T(8,128)(2,1)S(1)} %collective-permute-done.34), channel_id=1, source_target_pairs={{0,4},{8,0},{16,8},{24,16},{28,24},{20,28},{12,20},{4,12},{1,5},{9... | collective-permute-start | bytes 2359304 | tf_op jit(solution)/shard_map/ppermute | solution.py:37
  290.1 31.8 %collective-permute-start.41 = (bf16[768,256]{1,0:T(8,128)(2,1)S(1)}, bf16[768,256]{1,0:T(8,128)(2,1)S(1)}, u32[]{:S(2)}, u32[]{:S(2)}) collective-permute-start(bf16[768,256]{1,0:T(8,128)(2,1)S(1)} %collective-permute-done.40), channel_id=1, source_target_pairs={{0,4},{8,0},{16,8},{24,16},{28,24},{20,28},{12,20},{4,12},{1,5},{9... | collective-permute-start | bytes 1179656 | tf_op jit(solution)/shard_map/ppermute | solution.py:37
  294.6 27.8 %collective-permute-start.44 = (bf16[768,256]{1,0:T(8,128)(2,1)S(1)}, bf16[768,256]{1,0:T(8,128)(2,1)S(1)}, u32[]{:S(2)}, u32[]{:S(2)}) collective-permute-start(bf16[768,256]{1,0:T(8,128)(2,1)S(1)} %collective-permute-done.43), channel_id=1, source_target_pairs={{0,8},{8,16},{16,24},{24,28},{28,20},{20,12},{12,4},{4,0},{1,9},{9... | collective-permute-start | bytes 1179656 | tf_op jit(solution)/shard_map/ppermute | solution.py:37
  303.1 20.9 %collective-permute-start.38 = (bf16[768,256]{1,0:T(8,128)(2,1)S(1)}, bf16[768,256]{1,0:T(8,128)(2,1)S(1)}, u32[]{:S(2)}, u32[]{:S(2)}) collective-permute-start(bf16[768,256]{1,0:T(8,128)(2,1)S(1)} %collective-permute-done.37), channel_id=1, source_target_pairs={{0,8},{8,16},{16,24},{24,28},{28,20},{20,12},{12,4},{4,0},{1,9},{9... | collective-permute-start | bytes 1179656 | tf_op jit(solution)/shard_map/ppermute | solution.py:37
  307.1 52.1 %collective-permute-start.21 = (bf16[512,2048]{1,0:T(8,128)(2,1)S(1)}, bf16[512,2048]{1,0:T(8,128)(2,1)S(1)}, u32[]{:S(2)}, u32[]{:S(2)}) collective-permute-start(bf16[512,2048]{1,0:T(8,128)(2,1)S(1)} %add_convert_fusion.6), channel_id=1, source_target_pairs={{0,1},{1,0},{2,3},{3,2},{4,5},{5,4},{6,7},{7,6},{8,9},{9,8},{10,11... | collective-permute-start | bytes 6291464 | tf_op jit(solution)/shard_map/ppermute | solution.py:90
  324.0 24.7 %collective-permute-start.39 = (bf16[768,256]{1,0:T(8,128)(2,1)S(1)}, bf16[768,256]{1,0:T(8,128)(2,1)S(1)}, u32[]{:S(2)}, u32[]{:S(2)}) collective-permute-start(bf16[768,256]{1,0:T(8,128)(2,1)S(1)} %collective-permute-done.38), channel_id=1, source_target_pairs={{0,8},{8,16},{16,24},{24,28},{28,20},{20,12},{12,4},{4,0},{1,9},{9... | collective-permute-start | bytes 1179656 | tf_op jit(solution)/shard_map/ppermute | solution.py:37
  426.7 36.8 %collective-permute-start.68 = (bf16[768,256]{1,0:T(8,128)(2,1)S(1)}, bf16[768,256]{1,0:T(8,128)(2,1)S(1)}, u32[]{:S(2)}, u32[]{:S(2)}) collective-permute-start(bf16[768,256]{1,0:T(8,128)(2,1)S(1)} %convolution_convert_fusion.11), channel_id=1, source_target_pairs={{0,8},{8,16},{16,24},{24,28},{28,20},{20,12},{12,4},{4,0},{1,9},{9... | collective-permute-start | bytes 1179656 | tf_op jit(solution)/shard_map/ppermute | solution.py:37
  446.4 79.9 %collective-permute-start.50 = (bf16[512,2048]{1,0:T(8,128)(2,1)S(1)}, bf16[512,2048]{1,0:T(8,128)(2,1)S(1)}, u32[]{:S(2)}, u32[]{:S(2)}) collective-permute-start(bf16[512,2048]{1,0:T(8,128)(2,1)S(1)} %copy-done.123), channel_id=1, source_target_pairs={{0,1},{1,0},{2,3},{3,2},{4,5},{5,4},{6,7},{7,6},{8,9},{9,8},{10,11... | collective-permute-start | bytes 6291464 | tf_op jit(solution)/shard_map/ppermute | solution.py:90
  464.8 26.7 %collective-permute-start.102 = (bf16[768,256]{1,0:T(8,128)(2,1)S(1)}, bf16[768,256]{1,0:T(8,128)(2,1)S(1)}, u32[]{:S(2)}, u32[]{:S(2)}) collective-permute-start(bf16[768,256]{1,0:T(8,128)(2,1)S(1)} %add_convert_fusion.20), channel_id=1, source_target_pairs={{0,8},{8,16},{16,24},{24,28},{28,20},{20,12},{12,4},{4,0},{1,9},{9... | collective-permute-start | bytes 1179656 | tf_op jit(solution)/shard_map/ppermute | solution.py:37
  492.1 41.2 %collective-permute-start.53 = (bf16[512,2048]{1,0:T(8,128)(2,1)S(1)}, bf16[512,2048]{1,0:T(8,128)(2,1)S(1)}, u32[]{:S(2)}, u32[]{:S(2)}) collective-permute-start(bf16[512,2048]{1,0:T(8,128)(2,1)S(1)} %copy-done.122), channel_id=1, source_target_pairs={{0,1},{1,0},{2,3},{3,2},{4,5},{5,4},{6,7},{7,6},{8,9},{9,8},{10,11... | collective-permute-start | bytes 6291464 | tf_op jit(solution)/shard_map/ppermute | solution.py:90
  494.5 22.1 %collective-permute-start.82 = (bf16[256,1536]{1,0:T(8,128)(2,1)S(1)}, bf16[256,1536]{1,0:T(8,128)(2,1)S(1)}, u32[]{:S(2)}, u32[]{:S(2)}) collective-permute-start(bf16[256,1536]{1,0:T(8,128)(2,1)S(1)} %convolution_convert_fusion.4), channel_id=1, source_target_pairs={{0,4},{8,0},{16,8},{24,16},{28,24},{20,28},{12,20},{4,12},{1,5},{9... | collective-permute-start | bytes 2359304 | tf_op jit(solution)/shard_map/ppermute | solution.py:37
  503.9 43.7 %collective-permute-start.72 = (bf16[256,1536]{1,0:T(8,128)(2,1)S(1)}, bf16[256,1536]{1,0:T(8,128)(2,1)}, u32[]{:S(2)}, u32[]{:S(2)}) collective-permute-start(bf16[256,1536]{1,0:T(8,128)(2,1)S(1)} %convolution_convert_fusion.5), channel_id=1, source_target_pairs={{0,8},{8,16},{16,24},{24,28},{28,20},{20,12},{12,4},{4,0},{1,9},{9... | collective-permute-start | bytes 2359304 | tf_op jit(solution)/shard_map/ppermute | solution.py:37
  516.5 34.2 %collective-permute-start.93 = (bf16[256,1536]{1,0:T(8,128)(2,1)S(1)}, bf16[256,1536]{1,0:T(8,128)(2,1)}, u32[]{:S(2)}, u32[]{:S(2)}) collective-permute-start(bf16[256,1536]{1,0:T(8,128)(2,1)S(1)} %convolution_convert_fusion.3), channel_id=1, source_target_pairs={{0,4},{8,0},{16,8},{24,16},{28,24},{20,28},{12,20},{4,12},{1,5},{9... | collective-permute-start | bytes 2359304 | tf_op jit(solution)/shard_map/ppermute | solution.py:37
  522.9 34.4 %collective-permute-start.83 = (bf16[256,1536]{1,0:T(8,128)(2,1)}, bf16[256,1536]{1,0:T(8,128)(2,1)}, u32[]{:S(2)}, u32[]{:S(2)}) collective-permute-start(bf16[256,1536]{1,0:T(8,128)(2,1)} %add_convert_fusion.17), channel_id=1, source_target_pairs={{0,4},{8,0},{16,8},{24,16},{28,24},{20,28},{12,20},{4,12},{1,5},{9... | collective-permute-start | bytes 2359304 | tf_op jit(solution)/shard_map/ppermute | solution.py:37
  526.4 28.1 %collective-permute-start.104 = (bf16[256,1536]{1,0:T(8,128)(2,1)}, bf16[256,1536]{1,0:T(8,128)(2,1)}, u32[]{:S(2)}, u32[]{:S(2)}) collective-permute-start(bf16[256,1536]{1,0:T(8,128)(2,1)} %add_convert_fusion.12), channel_id=1, source_target_pairs={{0,8},{8,16},{16,24},{24,28},{28,20},{20,12},{12,4},{4,0},{1,9},{9... | collective-permute-start | bytes 2359304 | tf_op jit(solution)/shard_map/ppermute | solution.py:37
  534.7 87.5 %collective-permute-start.51 = (bf16[512,2048]{1,0:T(8,128)(2,1)}, bf16[512,2048]{1,0:T(8,128)(2,1)}, u32[]{:S(2)}, u32[]{:S(2)}) collective-permute-start(bf16[512,2048]{1,0:T(8,128)(2,1)} %add_convert_fusion.5), channel_id=1, source_target_pairs={{0,2},{1,3},{2,0},{3,1},{4,6},{5,7},{6,4},{7,5},{8,10},{9,11},{10,... | collective-permute-start | bytes 6291464 | tf_op jit(solution)/shard_map/ppermute | solution.py:95
  547.7 72.4 %collective-permute-start.54 = (bf16[512,2048]{1,0:T(8,128)(2,1)}, bf16[512,2048]{1,0:T(8,128)(2,1)S(1)}, u32[]{:S(2)}, u32[]{:S(2)}) collective-permute-start(bf16[512,2048]{1,0:T(8,128)(2,1)} %add_convert_fusion.3), channel_id=1, source_target_pairs={{0,2},{1,3},{2,0},{3,1},{4,6},{5,7},{6,4},{7,5},{8,10},{9,11},{10,... | collective-permute-start | bytes 6291464 | tf_op jit(solution)/shard_map/ppermute | solution.py:95
  557.2 30.9 %collective-permute-start.105 = (bf16[256,1536]{1,0:T(8,128)(2,1)S(1)}, bf16[256,1536]{1,0:T(8,128)(2,1)S(1)}, u32[]{:S(2)}, u32[]{:S(2)}) collective-permute-start(bf16[256,1536]{1,0:T(8,128)(2,1)S(1)} %add_convert_fusion.11), channel_id=1, source_target_pairs={{0,8},{8,16},{16,24},{24,28},{28,20},{20,12},{12,4},{4,0},{1,9},{9... | collective-permute-start | bytes 2359304 | tf_op jit(solution)/shard_map/ppermute | solution.py:37
  571.3 49.7 %collective-permute-start.84 = (bf16[256,1536]{1,0:T(8,128)(2,1)S(1)}, bf16[256,1536]{1,0:T(8,128)(2,1)S(1)}, u32[]{:S(2)}, u32[]{:S(2)}) collective-permute-start(bf16[256,1536]{1,0:T(8,128)(2,1)S(1)} %add_convert_fusion.16), channel_id=1, source_target_pairs={{0,4},{8,0},{16,8},{24,16},{28,24},{20,28},{12,20},{4,12},{1,5},{9... | collective-permute-start | bytes 2359304 | tf_op jit(solution)/shard_map/ppermute | solution.py:37
  573.9 59.2 %collective-permute-start.74 = (bf16[256,1536]{1,0:T(8,128)(2,1)S(1)}, bf16[256,1536]{1,0:T(8,128)(2,1)S(1)}, u32[]{:S(2)}, u32[]{:S(2)}) collective-permute-start(bf16[256,1536]{1,0:T(8,128)(2,1)S(1)} %add_convert_fusion.18), channel_id=1, source_target_pairs={{0,8},{8,16},{16,24},{24,28},{28,20},{20,12},{12,4},{4,0},{1,9},{9... | collective-permute-start | bytes 2359304 | tf_op jit(solution)/shard_map/ppermute | solution.py:37
  588.1 39.3 %collective-permute-start.95 = (bf16[256,1536]{1,0:T(8,128)(2,1)S(1)}, bf16[256,1536]{1,0:T(8,128)(2,1)S(1)}, u32[]{:S(2)}, u32[]{:S(2)}) collective-permute-start(bf16[256,1536]{1,0:T(8,128)(2,1)S(1)} %add_convert_fusion.13), channel_id=1, source_target_pairs={{0,4},{8,0},{16,8},{24,16},{28,24},{20,28},{12,20},{4,12},{1,5},{9... | collective-permute-start | bytes 2359304 | tf_op jit(solution)/shard_map/ppermute | solution.py:37
  621.0 26.7 %collective-permute-start.55 = (bf16[512,2048]{1,0:T(8,128)(2,1)S(1)}, bf16[512,2048]{1,0:T(8,128)(2,1)S(1)}, u32[]{:S(2)}, u32[]{:S(2)}) collective-permute-start(bf16[512,2048]{1,0:T(8,128)(2,1)S(1)} %add_convert_fusion.2), channel_id=1, source_target_pairs={{0,1},{1,0},{2,3},{3,2},{4,5},{5,4},{6,7},{7,6},{8,9},{9,8},{10,11... | collective-permute-start | bytes 6291464 | tf_op jit(solution)/shard_map/ppermute | solution.py:90
  627.4 70.1 %collective-permute-start.52 = (bf16[512,2048]{1,0:T(8,128)(2,1)S(1)}, bf16[512,2048]{1,0:T(8,128)(2,1)}, u32[]{:S(2)}, u32[]{:S(2)}) collective-permute-start(bf16[512,2048]{1,0:T(8,128)(2,1)S(1)} %add_convert_fusion.4), channel_id=1, source_target_pairs={{0,1},{1,0},{2,3},{3,2},{4,5},{5,4},{6,7},{7,6},{8,9},{9,8},{10,11... | collective-permute-start | bytes 6291464 | tf_op jit(solution)/shard_map/ppermute | solution.py:90
  758.7 39.3 %collective-permute-start.107 = (bf16[1056,256]{1,0:T(8,128)(2,1)}, bf16[1056,256]{1,0:T(8,128)(2,1)}, u32[]{:S(2)}, u32[]{:S(2)}) collective-permute-start(bf16[1056,256]{1,0:T(8,128)(2,1)} %pad_maximum_fusion.41), channel_id=1, source_target_pairs={{0,8},{8,16},{16,24},{24,28},{28,20},{20,12},{12,4},{4,0},{1,9},{9... | collective-permute-start | bytes 1622024 | tf_op jit(solution)/shard_map/ppermute | solution.py:37
  763.4 32.2 %collective-permute-start.96 = (bf16[1056,256]{1,0:T(8,128)(2,1)}, bf16[1056,256]{1,0:T(8,128)(2,1)}, u32[]{:S(2)}, u32[]{:S(2)}) collective-permute-start(bf16[1056,256]{1,0:T(8,128)(2,1)} %pad_maximum_fusion.40), channel_id=1, source_target_pairs={{0,4},{8,0},{16,8},{24,16},{28,24},{20,28},{12,20},{4,12},{1,5},{9... | collective-permute-start | bytes 1622024 | tf_op jit(solution)/shard_map/ppermute | solution.py:37
  797.3 28.8 %collective-permute-start.97 = (bf16[1056,256]{1,0:T(8,128)(2,1)S(1)}, bf16[1056,256]{1,0:T(8,128)(2,1)S(1)}, u32[]{:S(2)}, u32[]{:S(2)}) collective-permute-start(bf16[1056,256]{1,0:T(8,128)(2,1)S(1)} %fusion.51), channel_id=1, source_target_pairs={{0,4},{8,0},{16,8},{24,16},{28,24},{20,28},{12,20},{4,12},{1,5},{9... | collective-permute-start | bytes 1622024 | tf_op jit(solution)/shard_map/ppermute | solution.py:37
  799.5 26.9 %collective-permute-start.108 = (bf16[1056,256]{1,0:T(8,128)(2,1)S(1)}, bf16[1056,256]{1,0:T(8,128)(2,1)S(1)}, u32[]{:S(2)}, u32[]{:S(2)}) collective-permute-start(bf16[1056,256]{1,0:T(8,128)(2,1)S(1)} %fusion.53), channel_id=1, source_target_pairs={{0,8},{8,16},{16,24},{24,28},{28,20},{20,12},{12,4},{4,0},{1,9},{9... | collective-permute-start | bytes 1622024 | tf_op jit(solution)/shard_map/ppermute | solution.py:37
  807.2 47.5 %collective-permute-start.62 = (bf16[512,2048]{1,0:T(8,128)(2,1)S(1)}, bf16[512,2048]{1,0:T(8,128)(2,1)S(1)}, u32[]{:S(2)}, u32[]{:S(2)}) collective-permute-start(bf16[512,2048]{1,0:T(8,128)(2,1)S(1)} %add_convert_fusion.1), channel_id=1, source_target_pairs={{0,2},{1,3},{2,0},{3,1},{4,6},{5,7},{6,4},{7,5},{8,10},{9,11},{10,... | collective-permute-start | bytes 6291464 | tf_op jit(solution)/shard_map/ppermute | solution.py:95
  810.0 26.7 %collective-permute-start.76 = (bf16[1056,256]{1,0:T(8,128)(2,1)S(1)}, bf16[1056,256]{1,0:T(8,128)(2,1)S(1)}, u32[]{:S(2)}, u32[]{:S(2)}) collective-permute-start(bf16[1056,256]{1,0:T(8,128)(2,1)S(1)} %fusion.45), channel_id=1, source_target_pairs={{0,8},{8,16},{16,24},{24,28},{28,20},{20,12},{12,4},{4,0},{1,9},{9... | collective-permute-start | bytes 1622024 | tf_op jit(solution)/shard_map/ppermute | solution.py:37
  813.4 44.3 %collective-permute-start.87 = (bf16[1056,256]{1,0:T(8,128)(2,1)S(1)}, bf16[1056,256]{1,0:T(8,128)(2,1)S(1)}, u32[]{:S(2)}, u32[]{:S(2)}) collective-permute-start(bf16[1056,256]{1,0:T(8,128)(2,1)S(1)} %fusion.47), channel_id=1, source_target_pairs={{0,4},{8,0},{16,8},{24,16},{28,24},{20,28},{12,20},{4,12},{1,5},{9... | collective-permute-start | bytes 1622024 | tf_op jit(solution)/shard_map/ppermute | solution.py:37
  826.3 29.5 %collective-permute-start.98 = (bf16[1056,256]{1,0:T(8,128)(2,1)S(1)}, bf16[1056,256]{1,0:T(8,128)(2,1)S(1)}, u32[]{:S(2)}, u32[]{:S(2)}) collective-permute-start(bf16[1056,256]{1,0:T(8,128)(2,1)S(1)} %fusion.50), channel_id=1, source_target_pairs={{0,4},{8,0},{16,8},{24,16},{28,24},{20,28},{12,20},{4,12},{1,5},{9... | collective-permute-start | bytes 1622024 | tf_op jit(solution)/shard_map/ppermute | solution.py:37
  826.6 37.2 %collective-permute-start.109 = (bf16[1056,256]{1,0:T(8,128)(2,1)S(1)}, bf16[1056,256]{1,0:T(8,128)(2,1)S(1)}, u32[]{:S(2)}, u32[]{:S(2)}) collective-permute-start(bf16[1056,256]{1,0:T(8,128)(2,1)S(1)} %fusion.52), channel_id=1, source_target_pairs={{0,8},{8,16},{16,24},{24,28},{28,20},{20,12},{12,4},{4,0},{1,9},{9... | collective-permute-start | bytes 1622024 | tf_op jit(solution)/shard_map/ppermute | solution.py:37
  836.9 24.1 %collective-permute-start.77 = (bf16[1056,256]{1,0:T(8,128)(2,1)S(1)}, bf16[1056,256]{1,0:T(8,128)(2,1)S(1)}, u32[]{:S(2)}, u32[]{:S(2)}) collective-permute-start(bf16[1056,256]{1,0:T(8,128)(2,1)S(1)} %fusion.44), channel_id=1, source_target_pairs={{0,8},{8,16},{16,24},{24,28},{28,20},{20,12},{12,4},{4,0},{1,9},{9... | collective-permute-start | bytes 1622024 | tf_op jit(solution)/shard_map/ppermute | solution.py:37
  855.7 21.4 %collective-permute-start.63 = (bf16[512,2048]{1,0:T(8,128)(2,1)S(1)}, bf16[512,2048]{1,0:T(8,128)(2,1)S(1)}, u32[]{:S(2)}, u32[]{:S(2)}) collective-permute-start(bf16[512,2048]{1,0:T(8,128)(2,1)S(1)} %add_convert_fusion), channel_id=1, source_target_pairs={{0,1},{1,0},{2,3},{3,2},{4,5},{5,4},{6,7},{7,6},{8,9},{9,8},{10,11... | collective-permute-start | bytes 6291464 | tf_op jit(solution)/shard_map/ppermute | solution.py:90
  855.9 20.9 %collective-permute-start.99 = (bf16[1056,256]{1,0:T(8,128)(2,1)S(1)}, bf16[1056,256]{1,0:T(8,128)(2,1)S(1)}, u32[]{:S(2)}, u32[]{:S(2)}) collective-permute-start(bf16[1056,256]{1,0:T(8,128)(2,1)S(1)} %fusion.49), channel_id=1, source_target_pairs={{0,4},{8,0},{16,8},{24,16},{28,24},{20,28},{12,20},{4,12},{1,5},{9... | collective-permute-start | bytes 1622024 | tf_op jit(solution)/shard_map/ppermute | solution.py:37
  858.6 35.2 %collective-permute-start.88 = (bf16[1056,256]{1,0:T(8,128)(2,1)}, bf16[1056,256]{1,0:T(8,128)(2,1)S(1)}, u32[]{:S(2)}, u32[]{:S(2)}) collective-permute-start(bf16[1056,256]{1,0:T(8,128)(2,1)} %fusion.46), channel_id=1, source_target_pairs={{0,4},{8,0},{16,8},{24,16},{28,24},{20,28},{12,20},{4,12},{1,5},{9... | collective-permute-start | bytes 1622024 | tf_op jit(solution)/shard_map/ppermute | solution.py:37
  861.2 32.6 %collective-permute-start.78 = (bf16[1056,256]{1,0:T(8,128)(2,1)S(1)}, bf16[1056,256]{1,0:T(8,128)(2,1)}, u32[]{:S(2)}, u32[]{:S(2)}) collective-permute-start(bf16[1056,256]{1,0:T(8,128)(2,1)S(1)} %fusion.43), channel_id=1, source_target_pairs={{0,8},{8,16},{16,24},{24,28},{28,20},{20,12},{12,4},{4,0},{1,9},{9... | collective-permute-start | bytes 1622024 | tf_op jit(solution)/shard_map/ppermute | solution.py:37
  (179 other events, 2434.2 us)
Sparse Core Ops, SparseCore 0:
  795.8 81.3 all-reduce.14

commit v2 on v1

--- a/solution.py
+++ b/solution.py
@@ -24,65 +24,134 @@
     return [*range(0, n, 2), *range(n - 1 - n % 2, 0, -2)]
 
 
-class Lane:
-    def __init__(self, order, by, depth):
+def after(values, *earlier):
+    return lax.optimization_barrier((values, *earlier))[0]
+
+
+class Ring:
+    def __init__(self, order, depth):
         n = len(order)
-        self.pairs = [(order[i], order[(i + by) % n]) for i in range(n)]
+        self.n = n
         self.depth = depth
-        self.sent = []
-
-    def send(self, message):
-        if len(self.sent) >= self.depth:
-            message = lax.optimization_barrier((message, self.sent[-self.depth]))[0]
-        arrived = lax.ppermute(message, "seq", self.pairs)
-        self.sent.append(arrived)
-        return arrived
-
-
-def gather(first, second, right, left, n, chunk):
-    half = n // 2
-    if n > ring_most:
-        both = [lax.all_gather(p, "seq")[chunk] for p in (first, second)]
-        return [[p[k] for k in range(n)] for p in both]
-    ra, la, rb, lb = [first], [first], [second], [second]
-    for _ in range(half - 1):
-        ra.append(right.send(ra[-1]))
-        la.append(left.send(la[-1]))
-        rb.append(right.send(rb[-1]))
-        lb.append(left.send(lb[-1]))
-    far_a = right.send(ra[-1])
-    far_b = left.send(lb[-1])
-    return ra + [far_a] + la[:0:-1], rb + [far_b] + lb[:0:-1]
-
-
-def scatter(first, second, right, left, n, chunk):
-    half = n // 2
-    if n > ring_most:
-        slot = jnp.argsort(chunk)
-        both = [jnp.stack([p(k).astype(bf16) for k in range(n)])[slot] for p in (first, second)]
-        return [lax.psum_scatter(p, "seq", scatter_dimension=0).astype(f32) for p in both]
-    chains = [
-        (first, right, list(range(half, n))),
-        (second, left, list(range(half, 0, -1))),
-        (second, right, list(range(half + 1, n))),
-        (first, left, list(range(half - 1, 0, -1))),
-    ]
-    arrived = [None] * 4
-    for step in range(half):
-        for i, (part, lane, slots) in enumerate(chains):
-            if step < len(slots):
-                total = part(slots[step])
-                if arrived[i] is not None:
-                    total = total + arrived[i].astype(f32)
-                arrived[i] = lane.send(total.astype(bf16))
-    total_a, total_b = first(0), second(0)
-    for i in (0, 3):
-        if arrived[i] is not None:
-            total_a = total_a + arrived[i].astype(f32)
-    for i in (1, 2):
-        if arrived[i] is not None:
-            total_b = total_b + arrived[i].astype(f32)
-    return total_a, total_b
+        self.pairs = {w: [(order[i], order[(i + w) % n]) for i in range(n)] for w in (1, -1)}
+        self.queue = {1: [], -1: []}
+        self.flying = {1: [], -1: []}
+        self.landed = {1: [], -1: []}
+        self.sent = {1: 0, -1: 0}
+        self.last = {1: None, -1: None}
+
+    def add(self, weights, delays=None):
+        half = self.n // 2
+        delays = delays or [0] * len(weights)
+        left = {id(flow): flow.count for w in weights for flow in w.flows.values()}
+        for turn in range(half + max(delays)):
+            for late in (True, False):
+                for weight, delay in zip(weights, delays):
+                    if (delay > 0) != late or turn < delay:
+                        continue
+                    for way, flow in weight.flows.items():
+                        if left[id(flow)]:
+                            left[id(flow)] -= 1
+                            self.queue[way].append(flow)
+
+    def issue(self, most=None):
+        for way in (1, -1):
+            queue, flying, landed = self.queue[way], self.flying[way], self.landed[way]
+            while queue and len(flying) < (most or self.depth) and not queue[0].busy:
+                flow = queue.pop(0)
+                message = flow.message()
+                gate = self.sent[way] - self.depth
+                if gate >= 0:
+                    message = after(message, landed[gate])
+                flow.busy = True
+                self.sent[way] += 1
+                self.last[way] = message
+                flying.append((flow, lax.ppermute(message, "seq", self.pairs[way])))
+
+    def hold(self, values):
+        last = [message for message in self.last.values() if message is not None]
+        return after(values, *last) if last else values
+
+    def land(self, values=None, count=1):
+        for turn in range(count):
+            taken = [(w, *self.flying[w].pop(0)) for w in (1, -1) if self.flying[w]]
+            arrived = [message for _, _, message in taken]
+            if values is not None and taken and turn == count - 1:
+                values, *arrived = lax.optimization_barrier((values, *arrived))
+            for (way, flow, _), message in zip(taken, arrived):
+                flow.arrive(message)
+                flow.busy = False
+                self.landed[way].append(message)
+            self.issue()
+        return values
+
+    def drain(self):
+        while self.queue[1] or self.queue[-1] or self.flying[1] or self.flying[-1]:
+            self.land()
+
+
+class Pieces:
+    def __init__(self, own, count):
+        self.value, self.count, self.busy, self.got = own, count, False, []
+
+    def message(self):
+        return self.value
+
+    def arrive(self, message):
+        self.value = message
+        self.got.append(message)
+
+
+class Totals:
+    def __init__(self, part, slots):
+        self.part, self.slots, self.count, self.busy = part, slots, len(slots), False
+        self.got, self.at = None, 0
+
+    def message(self):
+        total = self.part(self.slots[self.at])
+        if self.got is not None:
+            total = total + self.got.astype(f32)
+        self.at += 1
+        return total.astype(bf16)
+
+    def arrive(self, message):
+        self.got = message
+
+
+class Gather:
+    def __init__(self, piece, far, n, chunk):
+        half = n // 2
+        self.piece, self.n, self.chunk, self.flows = piece, n, chunk, {}
+        if n <= ring_most:
+            self.flows = {w: Pieces(piece, half if w == far else half - 1) for w in (1, -1)}
+
+    def slots(self):
+        if not self.flows:
+            pieces = lax.all_gather(self.piece, "seq")[self.chunk]
+            return [pieces[k] for k in range(self.n)]
+        return [self.piece, *self.flows[1].got, *self.flows[-1].got[::-1]]
+
+
+class Scatter:
+    def __init__(self, part, far, n, chunk):
+        half = n // 2
+        self.part, self.n, self.chunk, self.flows = part, n, chunk, {}
+        if n <= ring_most:
+            self.flows = {
+                1: Totals(part, list(range(half if far == 1 else half + 1, n))),
+                -1: Totals(part, list(range(half if far == -1 else half - 1, 0, -1))),
+            }
+
+    def total(self):
+        if not self.flows:
+            parts = jnp.stack([self.part(k).astype(bf16) for k in range(self.n)])
+            parts = parts[jnp.argsort(self.chunk)]
+            return lax.psum_scatter(parts, "seq", scatter_dimension=0).astype(f32)
+        total = self.part(0)
+        for flow in self.flows.values():
+            if flow.got is not None:
+                total = total + flow.got.astype(f32)
+        return total
 
 
 def core_swap(values):
@@ -95,12 +164,12 @@
     return lax.ppermute(values, "tp", [(i, i ^ 2) for i in range(size)])
 
 
-def tp_sum(part, cuts):
-    got = [core_swap(part(1, q).astype(bf16)) for q in range(cuts)]
-    chip = [(part(0, q) + got[q].astype(f32)).astype(bf16) for q in range(cuts)]
-    total = [(c.astype(f32) + chip_swap(c).astype(f32)).astype(bf16) for c in chip]
-    other = [core_swap(t) for t in total]
-    return jnp.concatenate(total + other, axis=0)
+def tp_sum(part, others=lambda v: v, chips=lambda v: v, totals=lambda v: v):
+    got = core_swap(others(part(1).astype(bf16)))
+    chip = chips((part(0) + got.astype(f32)).astype(bf16))
+    far = chip_swap(chip)
+    total = totals((chip.astype(f32) + far.astype(f32)).astype(bf16))
+    return jnp.concatenate([total, core_swap(total)], axis=0), total
 
 
 def gelu_parts(x):
@@ -255,12 +324,12 @@
     sums[3:4] += jnp.sum(low.astype(f32), axis=0, keepdims=True)
 
 
-def conv_back_kernel(grad_mixed, after, inner, before, conv_w, grad_inner, sums, grad_ext, ext):
+def conv_back_kernel(grad_mixed, behind, inner, before, conv_w, grad_inner, sums, grad_ext, ext):
     length, lanes = inner.shape
     taps = conv_w.shape[0]
     ext[:pad_rows] = before[...]
     ext[pad_rows:] = inner[...].astype(f32)
-    grad_ext[length:] = after[...]
+    grad_ext[length:] = behind[...]
     grad = grad_mixed[...].astype(f32)
     grad_ext[:length] = grad
 
@@ -302,7 +371,7 @@
     return sum(math.prod(a.shape) * jnp.dtype(a.dtype).itemsize for a in arrays)
 
 
-def by_rows(kernel, arrays, whole, outputs, sums, order=None, back=False):
+def by_rows(kernel, arrays, whole, outputs, sums, order=None, back=False, moved=()):
     seqs, length, width = arrays[0].shape
     block = min(norm_rows, length)
     near = pl.BlockSpec((None, block, width), lambda s, r, *_: (s, r, 0))
@@ -316,7 +385,9 @@
         grid_spec=pltpu.PrefetchScalarGridSpec(
             num_scalar_prefetch=2 if moves else 0,
             grid=(seqs, length // block),
-            in_specs=[far if moves and not back else near] * len(arrays)
+            in_specs=[
+                far if moves and (not back or i in moved) else near for i in range(len(arrays))
+            ]
             + [pl.BlockSpec(w.shape, lambda s, r, *_: (0, 0)) for w in whole],
             out_specs=[far if moves and back else near] * len(outputs) + [total] * sums,
         ),
@@ -378,10 +449,9 @@
         target[:, at] = values[:, k * part : (k + 1) * part]
 
 
-def start_back_kernel(sequence, chunk, x, grad_normed, grad_middle, gain, grad_tokens, total):
-    grad, terms = norm_back(x[...].astype(f32), grad_normed[...].astype(f32), gain[...])
+def start_back_kernel(sequence, chunk, x, grad_normed, grad_middle, gain, grad_tokens):
+    grad = norm_back(x[...].astype(f32), grad_normed[...].astype(f32), gain[...])[0]
     put_chunks(chunk, grad_tokens, grad + grad_middle[...])
-    add_rows(total, terms)
 
 
 def output_kernel(sequence, chunk, middle, added, output):
@@ -398,7 +468,7 @@
     return split[:, :, chunk].reshape(array.shape)
 
 
-def carried(ends, way, n):
+def carried(ends, way, n, between=lambda v: v):
     def shifted(values, by):
         pairs = [(i, i + way * by) for i in range(n) if 0 <= i + way * by < n]
         return lax.ppermute(values, "seq", pairs)
@@ -411,6 +481,8 @@
             [jnp.zeros_like(ends[:, 1:]), ends[:, 1:]], axis=1
         )
         by *= 2
+        if by == 2:
+            ends = between(ends)
     near, far = shifted(ends, 1), shifted(ends, 1 + by)
     state = near[:, :1] * far[:, 1:] + near[:, 1:]
     return jnp.pad(state, ((0, 0), (0, pad_rows - 1), (0, 0)))
@@ -475,7 +547,7 @@
     odd = lax.axis_index("tp") % 2
     sequence = (jnp.arange(seqs, dtype=jnp.int32) + odd * (seqs // 2)) % seqs
     move = (sequence, chunk)
-    right, left = Lane(order, 1, lane_depth), Lane(order, -1, lane_depth)
+    ring = Ring(order, lane_depth)
     tiled = part % 128 == 0
 
     def sl(a, k):
@@ -483,40 +555,43 @@
 
     w_in = jnp.transpose(in_weight, (1, 2, 0))
     half_lanes = lanes // 2
-    half_units = units // 2
     own_gain = jnp.pad(jnp.stack([norm1_gain, norm2_gain]), ((0, 14), (0, 0)))
-    first, second = gather(
-        jnp.concatenate([w_in[0], out_weight[:half_lanes]], axis=0),
-        jnp.concatenate([w_in[1], out_weight[half_lanes:], own_gain], axis=0),
-        right,
-        left,
-        n,
-        chunk,
-    )
-    mlp0, mlp1 = gather(mlp_weight[:, 0], mlp_weight[:, 1], right, left, n, chunk)
-    down0, down1 = gather(
-        down_weight[:half_units], down_weight[half_units:], right, left, n, chunk
-    )
+    first = Gather(jnp.concatenate([w_in[0], out_weight[:half_lanes]], axis=0), 1, n, chunk)
+    second = Gather(
+        jnp.concatenate([w_in[1], out_weight[half_lanes:], own_gain], axis=0), -1, n, chunk
+    )
+    mlp = [Gather(mlp_weight[:, 0], 1, n, chunk), Gather(mlp_weight[:, 1], -1, n, chunk)]
+    downs = Gather(down_weight, 1, n, chunk)
+    ring.add([first, second])
+    ring.add([*mlp, downs], [0, 0, 2])
+    ring.issue()
+
+    tokens, cotangent = ring.land((tokens, cotangent))
+    move = (sequence, chunk)
+    if tiled:
+        x, cot = by_rows(enter_kernel, [tokens, cotangent], [], [bf16, bf16], 0, move)
+    else:
+        x, cot = own_order(tokens, move), own_order(cotangent, move)
+    full = x.shape
+    x, cot = ring.land((x, cot))
+    grad_low = cot.reshape(rows, width)
+    start = x.reshape(rows, width).astype(f32)
+    inverse1 = lax.rsqrt(jnp.mean(start * start, axis=-1, keepdims=True) + eps)
+    for _ in range(n - 3):
+        ring.land()
+    first, second = first.slots(), second.slots()
     in0 = [p[:lanes] for p in first]
     in1 = [p[:lanes] for p in second]
     gains = [p[lanes + half_lanes : lanes + half_lanes + 2] for p in second]
     gain1, gain2 = (
         jnp.concatenate([g[i : i + 1] for g in gains], axis=1).astype(f32) for i in range(2)
     )
-
-    if tiled:
-        x, cot = by_rows(enter_kernel, [tokens, cotangent], [], [bf16, bf16], 0, move)
-    else:
-        x, cot = own_order(tokens, move), own_order(cotangent, move)
-    full = x.shape
-    grad_low = cot.reshape(rows, width)
-    start = x.reshape(rows, width).astype(f32)
-    inverse1 = lax.rsqrt(jnp.mean(start * start, axis=-1, keepdims=True) + eps)
     normed1 = [
         (sl(start, k) * inverse1 * gains[k][:1].astype(f32)).astype(bf16) for k in range(n)
     ]
     inner = sum(across(normed1[k], in0[k]) for k in range(n)).astype(bf16)
     gate_in = sum(across(normed1[k], in1[k]) for k in range(n)).astype(bf16)
+    inner = ring.land(inner)
     inner = inner.reshape(seqs, piece, lanes)
     gate_in = gate_in.reshape(seqs, piece, lanes)
     before = lax.ppermute(
@@ -545,7 +620,8 @@
         [pltpu.VMEM((piece + pad_rows, lanes), f32), pltpu.VMEM((2, piece, lanes), f32)],
         gate_flops,
     )
-    entry = carried(ends, 1, n)
+    ends = ring.land(ends)
+    entry = ring.land(carried(ends, 1, n, ring.land))
     product = (
         ((local + cum * entry[:, :1]) * jax.nn.gelu(gate_in.astype(f32)))
         .astype(bf16)
@@ -558,49 +634,61 @@
         ],
         axis=0,
     )
-    cuts = 1
-    block = rows // (2 * cuts)
-
-    def rows_of(a, h, q):
-        begin = (h * cuts + q) * block
-        return a[begin : begin + block]
-
-    recurrent = tp_sum(lambda h, q: dot(rows_of(product, h, q), w_out), cuts)
+    block = rows // 2
+
+    def half_of(a, h):
+        return a[h * block : (h + 1) * block]
+
+    def wait_land(values, count):
+        for _ in range(count):
+            ring.land()
+        return ring.land(values)
+
+    recurrent, _ = tp_sum(
+        lambda h: dot(half_of(product, h), w_out),
+        chips=ring.land,
+        totals=lambda v: wait_land(v, 3),
+    )
 
     middle, normed2 = by_rows(norm_kernel, [x, recurrent.reshape(full)], [gain2], [f32, bf16], 0)
-    normed2 = normed2.reshape(rows, width)
+    normed2 = ring.land(normed2.reshape(rows, width))
     w_mlp = jnp.concatenate(
-        [jnp.concatenate(mlp0, axis=0), jnp.concatenate(mlp1, axis=0)], axis=1
-    )
-    both = dot(normed2, w_mlp).astype(bf16).astype(f32)
-    both0, both1 = both[:, :units], both[:, units:]
+        [jnp.concatenate(w.slots(), axis=0) for w in mlp], axis=1
+    )
+    both = dot(normed2, w_mlp).astype(bf16)
+    both0, both1 = both[:, :units].astype(f32), both[:, units:].astype(f32)
+    hidden = (gelu_parts(both0)[0] * both1).astype(bf16)
+    hidden, both = ring.land((hidden, both))
+    ring.drain()
+    w_down = jnp.concatenate(downs.slots(), axis=1)
+    grad_down = Scatter(lambda k: down(hidden, sl(grad_low, k)), 1, n, chunk)
+    grad_both = []
+    grad_mlp = [
+        Scatter(lambda k: down(sl(normed2, k), grad_both[0][:, :units]), -1, n, chunk),
+        Scatter(lambda k: down(sl(normed2, k), grad_both[0][:, units:]), 1, n, chunk),
+    ]
+    ring.add([grad_down, *grad_mlp])
+    ring.issue(1)
+    both, w_down = ring.hold((both, w_down))
+    both0, both1 = both[:, :units].astype(f32), both[:, units:].astype(f32)
     act, slope = gelu_parts(both0)
-    hidden = (act * both1).astype(bf16)
-    grad_down = scatter(
-        lambda k: down(hidden[:, :half_units], sl(grad_low, k)),
-        lambda k: down(hidden[:, half_units:], sl(grad_low, k)),
-        right,
-        left,
-        n,
-        chunk,
-    )
-    w_down = jnp.concatenate(
-        [jnp.concatenate(down0, axis=1), jnp.concatenate(down1, axis=1)], axis=0
-    )
     grad_hidden = across(grad_low, w_down)
-    grad_both = jnp.concatenate(
-        [(grad_hidden * both1 * slope).astype(bf16), (grad_hidden * act).astype(bf16)], axis=1
-    )
-    grad_normed2 = tp_sum(lambda h, q: across(rows_of(grad_both, h, q), w_mlp), cuts)
-    grad_mlp = scatter(
-        lambda k: down(sl(normed2, k), grad_both[:, :units]),
-        lambda k: down(sl(normed2, k), grad_both[:, units:]),
-        right,
-        left,
-        n,
-        chunk,
-    )
-    mlp_out = tp_sum(lambda h, q: dot(rows_of(hidden, h, q), w_down), cuts)
+    grad_both.append(
+        jnp.concatenate(
+            [(grad_hidden * both1 * slope).astype(bf16), (grad_hidden * act).astype(bf16)],
+            axis=1,
+        )
+    )
+    grad_both[0] = ring.land(grad_both[0])
+    grad_normed2, total2 = tp_sum(
+        lambda h: across(half_of(grad_both[0], h), w_mlp),
+        others=ring.land,
+        chips=ring.land,
+        totals=lambda v: wait_land(v, 2),
+    )
+    turned = jnp.concatenate([half_of(hidden, 1), half_of(hidden, 0)], axis=0)
+    turned = jnp.where(odd == 1, turned, hidden)
+    mlp_out = lax.psum(dot(after(turned, total2), w_down).astype(bf16), "tp")
 
     grad_middle, grad_rec, sum_gain2 = by_rows(
         middle_back_kernel,
@@ -611,6 +699,7 @@
     )
     grad_rec = grad_rec.reshape(rows, width)
 
+    grad_rec = ring.land(grad_rec)
     grad_product = across(grad_rec, w_out).reshape(wide)
     tail, local_grad, first = per_sequence(
         reverse_kernel,
@@ -620,7 +709,7 @@
         [pltpu.VMEM((piece, lanes), f32)],
         rows * lanes * 50,
     )
-    incoming = carried(first, -1, n)
+    incoming = carried(ring.land(first), -1, n, ring.land)
     grad_gates, grad_mixed, grad_gate_in, sums = per_sequence(
         gates_back_kernel,
         seqs,
@@ -649,16 +738,18 @@
         [pltpu.VMEM((piece + pad_rows, lanes), f32), pltpu.VMEM((piece, lanes), f32)],
         gate_flops,
     )
-    after = lax.ppermute(
+    grad_mixed = ring.land(grad_mixed)
+    behind = lax.ppermute(
         grad_mixed[:, : taps - 1], "seq", [(i + 1, i) for i in range(n - 1)]
     ).astype(f32)
-    after = jnp.pad(after, ((0, 0), (0, pad_rows - taps + 1), (0, 0)))
+    behind = jnp.pad(behind, ((0, 0), (0, pad_rows - taps + 1), (0, 0)))
+    behind = ring.land(behind)
     grad_inner, conv_sums = per_sequence(
         conv_back_kernel,
         seqs,
         [
             (grad_mixed, "seq"),
-            (after, "seq"),
+            (behind, "seq"),
             (inner, "seq"),
             (before, "seq"),
             (conv_w, "whole"),
@@ -673,7 +764,41 @@
     w_both = jnp.concatenate(
         [jnp.concatenate(in0, axis=1), jnp.concatenate(in1, axis=1)], axis=0
     )
-    grad_normed1 = tp_sum(lambda h, q: dot(rows_of(back, h, q), w_both), cuts)
+    ring.drain()
+    grads = [
+        Scatter(
+            lambda k: jnp.concatenate(
+                [down(back0, normed1[k]), down(product[:, :half_lanes], sl(grad_rec, k))], axis=0
+            ),
+            1,
+            n,
+            chunk,
+        ),
+        Scatter(
+            lambda k: jnp.concatenate(
+                [down(back1, normed1[k]), down(product[:, half_lanes:], sl(grad_rec, k))], axis=0
+            ),
+            -1,
+            n,
+            chunk,
+        ),
+    ]
+    ring.add(grads)
+    ring.issue()
+    late = []
+
+    def hold_output(chip):
+        late.append(after(mlp_out, chip))
+        return chip
+
+    grad_normed1, total1 = tp_sum(
+        lambda h: dot(half_of(back, h), w_both),
+        chips=hold_output,
+        totals=lambda v: wait_land(v, 2),
+    )
+    mlp_out = late[0]
+    ring.drain()
+    grads = [g.total() for g in grads]
     low_mixed = mixed.astype(bf16).reshape(rows, lanes)
     grad_matrix = []
     for k in range(2):
@@ -684,43 +809,37 @@
     small = jnp.concatenate([sums[:4], conv_sums[:taps]], axis=0).astype(bf16)
     packed = jnp.concatenate(grad_matrix + [small.reshape(-1, head_width)], axis=0)
     packed = lax.psum(packed, "seq")
-    grads = scatter(
-        lambda k: jnp.concatenate(
-            [down(back0, normed1[k]), down(product[:, :half_lanes], sl(grad_rec, k))], axis=0
-        ),
-        lambda k: jnp.concatenate(
-            [down(back1, normed1[k]), down(product[:, half_lanes:], sl(grad_rec, k))], axis=0
-        ),
-        right,
-        left,
-        n,
-        chunk,
-    )
-
     if tiled:
         output = by_rows(
-            output_kernel, [middle, mlp_out.reshape(full)], [], [bf16], 0, move, back=True
+            output_kernel,
+            [middle, mlp_out.reshape(full)],
+            [],
+            [bf16],
+            0,
+            move,
+            back=True,
+            moved=(1,),
         )[0]
-        grad_tokens, sum_gain1 = by_rows(
+        grad_normed1, output = after((grad_normed1, output), output)
+        grad_tokens = by_rows(
             start_back_kernel,
             [x, grad_normed1.reshape(full), grad_middle],
             [gain1],
             [f32],
-            1,
+            0,
             move,
             back=True,
-        )
+        )[0]
     else:
-        output = own_order((middle + mlp_out.reshape(full).astype(f32)).astype(bf16), move, True)
-        grad_start, terms = norm_back(
-            x.astype(f32), grad_normed1.reshape(full).astype(f32), gain1
-        )
+        mlp_out = mlp_out.reshape(full)[sequence].astype(f32)
+        output = own_order((middle + mlp_out).astype(bf16), move, True)
+        grad_start = norm_back(x.astype(f32), grad_normed1.reshape(full).astype(f32), gain1)[0]
         grad_tokens = own_order(grad_middle + grad_start, move, True)
-        sum_gain1 = jnp.sum(terms, axis=(0, 1))[None]
     mine = lax.axis_index("seq")
     slots = (me - jnp.asarray(place, jnp.int32)) % n
-    grad_gains = jnp.stack([jnp.sum(sum_gain1, axis=0), jnp.sum(sum_gain2, axis=0)])
-    grad_gains = 0.5 * (grad_gains + core_swap(grad_gains))
+    sum_gain1 = jnp.sum(total1.astype(f32) * (start[:block] * inverse1[:block]), axis=0)
+    grad_gains = jnp.stack([sum_gain1, 0.5 * jnp.sum(sum_gain2, axis=0)])
+    grad_gains = grad_gains + core_swap(grad_gains)
     grad_gains = seq_sum(grad_gains.reshape(2, n, part)[:, slots], n)
     grad_gains = lax.dynamic_index_in_dim(grad_gains, mine, 1, keepdims=False)
 
@@ -741,8 +860,8 @@
         small[0],
         jnp.concatenate([g[lanes:] for g in grads], axis=0),
         grad_gains[1],
-        jnp.stack(grad_mlp, axis=1),
-        jnp.concatenate(grad_down, axis=0),
+        jnp.stack([g.total() for g in grad_mlp], axis=1),
+        grad_down.total(),
     )
 
 

time: 932 us -> 874 us (0.938)
  waiting for transfers between devices: 333 us -> 226 us
  matrix products: 198 us -> 224 us
  local copies, waits for them, and re-layouts: 85 us -> 105 us
  other arithmetic: 48.9 us -> 68.3 us
  starting transfers between devices: 141 us -> 122 us
    ppermute x84 -> x70, waiting for transfers between devices: 275 us -> 157 us  [issue(): flying.append((flow, lax.ppermute(message, 'seq', self.pairs[way])))]
    dot_general x66 -> x58, matrix products: 82.8 us -> 110 us  [down(): lax.dot_general(a, b, (((0,), (0,)), ((), ())), preferred_element_type=f32)]
    ppermute x84 -> x70, starting transfers between devices: 100 us -> 82.6 us  [issue(): flying.append((flow, lax.ppermute(message, 'seq', self.pairs[way])))]
    ppermute x4 -> x3, waiting for transfers between devices: 44.6 us -> 31.1 us  [chip_swap(): return lax.ppermute(values, 'tp', [(i, i ^ 2) for i in range(size)])]
    ppermute x8, waiting for transfers between devices: 9.36 us -> 21.4 us  [shifted(): return lax.ppermute(values, 'seq', pairs)]
    ppermute x3, waiting for transfers between devices: 4.05 us -> 15.6 us  [seq_sum(): lax.ppermute(values, 'seq', [(i, i ^ by) for i in range(n)])]
    convert_element_type x14, other arithmetic: 13 us -> 23.7 us  [the longest x10 13.3 us: message(): return total.astype(bf16)]
    unnamed x324 -> x378, local copies, waits for them, and re-layouts: 53.9 us -> 61.8 us
  transfers between devices with their start and end apart: 111 -> 95, of which waited for: 48 -> 27; matrix products, arithmetic and copies ran while one was open for 26% -> 41% of each run, Pallas kernels for 8% -> 10%
where the time goes in v2:
time: 874 us; the launch traced here: 864 us
  waiting for transfers between devices  226 us (26%)
  matrix products  224 us (26%)
  starting transfers between devices  122 us (14%)
  local copies, waits for them, and re-layouts  105 us (12%)
  Pallas kernels  103 us (12%)
  other arithmetic  68.3 us (8%)
  between operations  16.4 us (2%)
    ppermute x70, waiting for transfers between devices, issue(): flying.append((flow, lax.ppermute(message, 'seq', self.pairs[way])))  157 us
    dot_general x58, matrix products, down(): lax.dot_general(a, b, (((0,), (0,)), ((), ())), preferred_element_type=f32)  110 us
    ppermute x70, starting transfers between devices, issue(): flying.append((flow, lax.ppermute(message, 'seq', self.pairs[way])))  82.6 us
    dot_general x20, matrix products, across(): lax.dot_general(a, b, (((1,), (1,)), ((), ())), preferred_element_type=f32)  63.1 us
    unnamed x378, local copies, waits for them, and re-layouts  61.8 us
    pallas_call x5, Pallas kernels, by_rows(): pl.pallas_call(kernel, grid_spec=pltpu.PrefetchScalarGridSpec(num_scalar_...  52.7 us
    pallas_call x4, Pallas kernels, per_sequence(): pl.pallas_call(kernel, grid=(seqs,), in_specs=[spec(a.shape, kind) for a,...  50.1 us
    dot_general x6, matrix products, dot(): return jnp.dot(a, b, preferred_element_type=f32)  49.9 us
  transfers between devices with their start and end apart: 95, of which 27 were waited for; matrix products, arithmetic and copies ran while one was open for 41% of the time, Pallas kernels for 10%

profile of v2, /device:TPU:0, one launch (start us, length us, event | category | flops | bytes accessed | tf_op | source)
XLA Modules:
  0.0 864.2 jit_solution(12906292406203733915)
XLA Ops:
  29.3 3.4 constant_dynamic-update-slice_fusion.25
  34.9 8.5 shard_map.255
  58.5 4.1 collective-permute-done.4
  65.5 8.7 %collective-permute-done.7 = bf16[1056,256]{1,0:T(8,128)(2,1)S(1)} collective-permute-done((bf16[1056,256]{1,0:T(8,128)(2,1)S(1)}, bf16[1056,256]{1,0:T(8,128)(2,1)S(1)}, u32[]{:S(2)}, u32[]{:S(2)}) %collective-permute-start.7) | collective-permute-done | bytes 540704 | tf_op jit(solution)/shard_map/ppermute | solution.py:69
  76.3 10.3 %collective-permute-done.9 = bf16[1072,256]{1,0:T(8,128)(2,1)S(1)} collective-permute-done((bf16[1072,256]{1,0:T(8,128)(2,1)S(1)}, bf16[1072,256]{1,0:T(8,128)(2,1)S(1)}, u32[]{:S(2)}, u32[]{:S(2)}) %collective-permute-start.9) | collective-permute-done | bytes 548896 | tf_op jit(solution)/shard_map/ppermute | solution.py:69
  89.7 7.8 collective-permute-done.13
  111.3 3.2 add_convert_fusion.6
  128.7 3.6 collective-permute-start.16
  136.5 16.1 %shard_map.256 = (f32[4,256,704]{2,1,0:T(8,128)}, f32[4,256,704]{2,1,0:T(8,128)}, f32[4,256,704]{2,1,0:T(8,128)}, f32[4,256,704]{2,1,0:T(8,128)}, f32[4,256,704]...) custom-call(bf16[4,256,704]{2,1,0:T(8,128)(2,1)S(1)} %bitcast.185, ...), custom_call_target="tpu_custom_call" | custom-call | flops 2030043136 | bytes 20928512 | tf_op jit(solution)/shard_map/pallas_call | solution.py:358
  152.6 3.4 collective-permute-start.19
  158.6 5.3 collective-permute-start.22
  163.9 6.3 collective-permute-done.22
  170.3 5.1 collective-permute-start.23
  175.4 5.4 collective-permute-start.24
  184.9 4.3 fusion.36
  191.1 3.3 convolution_convert_fusion.2
  208.4 3.3 add_convert_fusion.5
  211.8 11.4 %collective-permute-done.28 = bf16[1536,256]{1,0:T(8,128)(2,1)S(1)} collective-permute-done((bf16[1536,256]{1,0:T(8,128)(2,1)S(1)}, bf16[1536,256]{1,0:T(8,128)(2,1)S(1)}, u32[]{:S(2)}, u32[]{:S(2)}) %collective-permute-start.28) | collective-permute-done | bytes 786464 | tf_op jit(solution)/shard_map/ppermute | solution.py:69
  233.4 6.7 collective-permute-done.31
  244.4 12.5 %collective-permute-done.32 = bf16[256,1536]{1,0:T(8,128)(2,1)S(1)} collective-permute-done((bf16[256,1536]{1,0:T(8,128)(2,1)}, bf16[256,1536]{1,0:T(8,128)(2,1)S(1)}, u32[]{:S(2)}, u32[]{:S(2)}) %collective-permute-start.32) | collective-permute-done | bytes 786464 | tf_op jit(solution)/shard_map/ppermute | solution.py:69
  258.9 14.8 %collective-permute-done.37 = bf16[1536,256]{1,0:T(8,128)(2,1)S(1)} collective-permute-done((bf16[1536,256]{1,0:T(8,128)(2,1)S(1)}, bf16[1536,256]{1,0:T(8,128)(2,1)S(1)}, u32[]{:S(2)}, u32[]{:S(2)}) %collective-permute-start.37) | collective-permute-done | bytes 786464 | tf_op jit(solution)/shard_map/ppermute | solution.py:69
  276.7 13.9 %collective-permute-done.33 = bf16[256,1536]{1,0:T(8,128)(2,1)S(1)} collective-permute-done((bf16[256,1536]{1,0:T(8,128)(2,1)S(1)}, bf16[256,1536]{1,0:T(8,128)(2,1)S(1)}, u32[]{:S(2)}, u32[]{:S(2)}) %collective-permute-start.33) | collective-permute-done | bytes 786464 | tf_op jit(solution)/shard_map/ppermute | solution.py:69
  300.3 9.5 %shard_map.257 = (f32[4,256,2048]{2,1,0:T(8,128)}, bf16[4,256,2048]{2,1,0:T(8,128)(2,1)S(1)}) custom-call(bf16[4,256,2048]{2,1,0:T(8,128)(2,1)} %copy-done, bf16[4,256,2048]{2,1,0:T(8,128)(2,1)} %bitcast.253, f32[1,2048]{1,0:T(1,128)S(1)} %convert_element_type.413.gain), custom_call_target="tpu_custom_call" | custom-call | flops 16777216 | bytes 20971520 | tf_op jit(solution)/shard_map/pallas_call | solution.py:383
  315.4 18.0 %convolution_convert_fusion = bf16[1024,3072]{1,0:T(8,128)(2,1)} fusion(bf16[1024,2048]{1,0:T(8,128)(2,1)S(1)} %bitcast.188, bf16[2048,1536]{1,0:T(8,128)(2,1)} %copy-done.123, bf16[2048,1536]{1,0:T(8,128)(2,1)} %copy-done.122), kind=kOutput, calls=%fused_computation.40 | convolution fusion | flops 12913213440 | bytes 23068672 | tf_op jit(solution)/shard_map/dot_general | solution.py:517
  333.4 4.5 fusion.11
  337.9 3.4 convolution_convert_fusion.8
  352.0 15.1 %fusion.6 = (bf16[1024,1536]{1,0:T(8,128)(2,1)S(1)}, bf16[1024,1536]{1,0:T(8,128)(2,1)}) fusion(bf16[1024,3072]{1,0:T(8,128)(2,1)S(1)} %bitcast.263, bf16[1024,2048]{1,0:T(8,128)(2,1)} %bitcast.282, bf16[1536,2048]{1,0:T(8,128)(2,1)} %constant_dynamic-update-slice_fusion.26), kind=kOutput, calls=%fused_computation.26 | convolution fusion | flops 6481772544 | bytes 23068672 | tf_op jit(solution)/shard_map/dot_general | solution.py:509
  370.7 6.2 pad_maximum_fusion.1
  376.9 3.8 convolution_convert_fusion.5
  385.4 11.8 %fusion.40 = bf16[512,2048]{1,0:T(8,128)(2,1)} fusion(bf16[2048,1536]{1,0:T(8,128)(2,1)} %copy-done.123, bf16[2048,1536]{1,0:T(8,128)(2,1)} %copy-done.122, bf16[1024,3072]{1,0:T(8,128)(2,1)} %pad_maximum_fusion.1), kind=kOutput, calls=%fused_computation.83 | convolution fusion | flops 6468665344 | bytes 17825792 | tf_op jit(solution)/shard_map/dot_general | solution.py:509
  401.8 3.8 convolution_convert_fusion.4
  409.6 3.4 fusion.51
  413.8 3.3 fusion.53
  420.3 12.0 %add_convert_fusion.3 = bf16[512,2048]{1,0:T(8,128)(2,1)} fusion(bf16[512,2048]{1,0:T(8,128)(2,1)} %collective-permute-done.47, bf16[2048,1536]{1,0:T(8,128)(2,1)} %copy-done.123, bf16[2048,1536]{1,0:T(8,128)(2,1)} %copy-done.122, bf16[1024,3072]{1,0:T(8,128)(2,1)} %pad_maximum_fusion.1), kind=kOutput, calls=%fused_computation.62 | convolution fusion | flops 6470762496 | bytes 19922944 | tf_op jit(solution)/shard_map/dot_general | solution.py:509
  433.9 10.7 %collective-permute-done.51 = bf16[1536,256]{1,0:T(8,128)(2,1)} collective-permute-done((bf16[1536,256]{1,0:T(8,128)(2,1)}, bf16[1536,256]{1,0:T(8,128)(2,1)}, u32[]{:S(2)}, u32[]{:S(2)}) %collective-permute-start.51) | collective-permute-done | bytes 786464 | tf_op jit(solution)/shard_map/ppermute | solution.py:69
  444.6 3.4 fusion.54
  448.0 3.4 fusion.56
  457.6 14.2 %collective-permute-done.56 = bf16[256,1536]{1,0:T(8,128)(2,1)S(1)} collective-permute-done((bf16[256,1536]{1,0:T(8,128)(2,1)S(1)}, bf16[256,1536]{1,0:T(8,128)(2,1)S(1)}, u32[]{:S(2)}, u32[]{:S(2)}) %collective-permute-start.56) | collective-permute-done | bytes 786464 | tf_op jit(solution)/shard_map/ppermute | solution.py:69
  481.7 7.0 collective-permute-done.52
  493.5 11.2 %convolution_convert_fusion.1 = bf16[1024,2048]{1,0:T(8,128)(2,1)} fusion(bf16[1024,1536]{1,0:T(8,128)(2,1)S(1)} %copy-done.52, bf16[1536,2048]{1,0:T(8,128)(2,1)} %constant_dynamic-update-slice_fusion.26), kind=kOutput, calls=%fused_computation.65 | convolution fusion | flops 6444548096 | bytes 13631488 | tf_op jit(solution)/shard_map/dot_general | solution.py:517
  504.8 4.1 fusion.61
  508.9 5.1 pad_maximum_fusion.4
  514.0 13.9 %shard_map.258 = (f32[4,256,2048]{2,1,0:T(8,128)}, bf16[4,256,2048]{2,1,0:T(8,128)(2,1)S(1)}, f32[8,2048]{1,0:T(8,128)S(1)}) custom-call(f32[4,256,2048]{2,1,0:T(8,128)} %get-tuple-element.224.middle, bf16[4,256,2048]{2,1,0:T(8,128)(2,1)} %bitcast.255, bf16[4,256,2048]{2,1,0:T(8,128)(2,1)} %get-tuple-element.225.cot, f32[1,2048]{1,0:T(1,128)S(1)} %convert_element_type.413.gain), custom_call_target="tpu_custom_call" | custom-call | flops 16777216 | bytes 29425664 | tf_op jit(solution)/shard_map/pallas_call | solution.py:383
  527.9 7.5 fusion.111
  535.4 8.3 shard_map.259
  568.1 3.6 collective-permute-start.63
  579.3 10.8 %collective-permute-done.63 = bf16[256,1536]{1,0:T(8,128)(2,1)} collective-permute-done((bf16[256,1536]{1,0:T(8,128)(2,1)}, bf16[256,1536]{1,0:T(8,128)(2,1)}, u32[]{:S(2)}, u32[]{:S(2)}) %collective-permute-start.63) | collective-permute-done | bytes 786464 | tf_op jit(solution)/shard_map/ppermute | solution.py:69
  593.9 14.4 %collective-permute-done.65 = f32[4,2,704]{2,1,0:T(2,128)S(1)} collective-permute-done((f32[4,2,704]{2,1,0:T(2,128)S(1)}, f32[4,2,704]{2,1,0:T(2,128)S(1)}, u32[]{:S(2)}, u32[]{:S(2)}) %collective-permute-start.65) | collective-permute-done | bytes 22560 | tf_op jit(solution)/shard_map/ppermute | solution.py:474
  611.1 4.1 fusion.64
  617.4 21.0 %shard_map.260 = (bf16[2,4,256,704]{3,2,1,0:T(8,128)(2,1)}, bf16[4,256,704]{2,1,0:T(8,128)(2,1)S(1)}, bf16[4,256,704]{2,1,0:T(8,128)(2,1)S(1)}, f32[8,704]{1,0:T(8,128)S(1)}) custom-call(f32[4,256,704]{2,1,0:T(8,128)} %bitcast.257, bf16[4,256,704]{2,1,0:T(8,128)(2,1)S(1)} %bitcast.183, f32[4,256,704]{2,1,0:T(8,128)} %copy-done.6, ...), custom_call_target="tpu_custom_call" | custom-call | flops 2030043136 | bytes 35349248 | tf_op jit(solution)/shard_map/pallas_call | solution.py:358
  655.0 3.8 fusion.46
  658.9 4.2 collective-permute-start.89
  663.1 3.5 fusion.49
  669.2 4.8 collective-permute-done.89
  675.5 4.7 shard_map.261
  682.7 6.7 fusion.39
  708.4 7.4 add_convert_fusion.1
  717.5 4.1 copy.55
  734.0 29.3 %collective-permute-done.73 = bf16[512,2048]{1,0:T(8,128)(2,1)} collective-permute-done((bf16[512,2048]{1,0:T(8,128)(2,1)}, bf16[512,2048]{1,0:T(8,128)(2,1)}, u32[]{:S(2)}, u32[]{:S(2)}) %collective-permute-start.73) | collective-permute-done | bytes 2097184 | tf_op jit(solution)/shard_map/ppermute | solution.py:164
  777.7 8.8 %shard_map.262 = bf16[4,256,2048]{2,1,0:T(8,128)(2,1)} custom-call(s32[4]{0:T(128)S(1)} %copy-done.13, s32[8]{0:T(128)S(1)} %gather_fusion, f32[4,256,2048]{2,1,0:T(8,128)} %get-tuple-element.224.middle, bf16[4,256,2048]{2,1,0:T(8,128)(2,1)S(1)} %bitcast.187), custom_call_target="tpu_custom_call" | custom-call | flops 16777216 | bytes 16777216 | tf_op jit(solution)/shard_map/pallas_call | solution.py:383
  794.0 14.3 %collective-permute-done.82 = f32[2,8,256]{2,0,1:T(2,128)S(1)} collective-permute-done((f32[2,8,256]{2,0,1:T(2,128)S(1)}, f32[2,8,256]{2,0,1:T(2,128)S(1)}, u32[]{:S(2)}, u32[]{:S(2)}) %collective-permute-start.82) | collective-permute-done | bytes 16416 | tf_op jit(solution)/shard_map/ppermute | solution.py:494
  828.1 10.0 %collective-permute-done.84 = bf16[1056,256]{1,0:T(8,128)(2,1)S(1)} collective-permute-done((bf16[1056,256]{1,0:T(8,128)(2,1)S(1)}, bf16[1056,256]{1,0:T(8,128)(2,1)S(1)}, u32[]{:S(2)}, u32[]{:S(2)}) %collective-permute-start.84) | collective-permute-done | bytes 540704 | tf_op jit(solution)/shard_map/ppermute | solution.py:69
  840.5 4.5 pad_maximum_fusion.5
  845.0 12.1 %shard_map.263 = f32[4,256,2048]{2,1,0:T(8,128)} custom-call(s32[4]{0:T(128)S(1)} %copy-done.13, s32[8]{0:T(128)S(1)} %gather_fusion, bf16[4,256,2048]{2,1,0:T(8,128)(2,1)S(1)} %copy-done.1, bf16[4,256,2048]{2,1,0:T(8,128)(2,1)} %bitcast.254, f32[4,256,2048]{2,1,0:T(8,128)} %get-tuple-element.308.grad_middle, f32[1,2048]{1,0:T(1,128)S(1)} %convert_element_type.475.gain), custom_call_target="tpu_custom_call" | custom-call | flops 16777216 | bytes 25165824 | tf_op jit(solution)/shard_map/pallas_call | solution.py:383
  (737 shorter events, 330.5 us)
Async XLA Ops:
  7.2 768.2 %all-reduce.16.cloned.1.call-start = ((), (), s32[]{:S(2)}) async-start(), calls=%async_computation | async-start | bytes 8388608 | tf_op jit(solution)/shard_map/psum | solution.py:691
  11.2 21.6 %collective-permute-start = (bf16[1056,256]{1,0:T(8,128)(2,1)}, bf16[1056,256]{1,0:T(8,128)(2,1)S(1)}, u32[]{:S(2)}, u32[]{:S(2)}) collective-permute-start(bf16[1056,256]{1,0:T(8,128)(2,1)} %pad_maximum_fusion.30), channel_id=1, source_target_pairs={{0,8},{8,16},{16,24},{24,28},{28,20},{20,12},{12,4},{4,0},{1,9},{9... | collective-permute-start | bytes 1622024 | tf_op jit(solution)/shard_map/ppermute | solution.py:69
  15.1 29.2 %collective-permute-start.2 = (bf16[1072,256]{1,0:T(8,128)(2,1)}, bf16[1072,256]{1,0:T(8,128)(2,1)}, u32[]{:S(2)}, u32[]{:S(2)}) collective-permute-start(bf16[1072,256]{1,0:T(8,128)(2,1)} %pad_maximum_fusion.29), channel_id=1, source_target_pairs={{0,8},{8,16},{16,24},{24,28},{28,20},{20,12},{12,4},{4,0},{1,9},{9... | collective-permute-start | bytes 1646600 | tf_op jit(solution)/shard_map/ppermute | solution.py:69
  17.1 27.2 %collective-permute-start.3 = (bf16[1072,256]{1,0:T(8,128)(2,1)}, bf16[1072,256]{1,0:T(8,128)(2,1)}, u32[]{:S(2)}, u32[]{:S(2)}) collective-permute-start(bf16[1072,256]{1,0:T(8,128)(2,1)} %pad_maximum_fusion.29), channel_id=1, source_target_pairs={{0,4},{8,0},{16,8},{24,16},{28,24},{20,28},{12,20},{4,12},{1,5},{9... | collective-permute-start | bytes 1646600 | tf_op jit(solution)/shard_map/ppermute | solution.py:69
  32.8 22.8 %collective-permute-start.10 = (bf16[1056,256]{1,0:T(8,128)(2,1)}, bf16[1056,256]{1,0:T(8,128)(2,1)S(1)}, u32[]{:S(2)}, u32[]{:S(2)}) collective-permute-start(bf16[1056,256]{1,0:T(8,128)(2,1)} %collective-permute-done.1), channel_id=1, source_target_pairs={{0,4},{8,0},{16,8},{24,16},{28,24},{20,28},{12,20},{4,12},{1,5},{9... | collective-permute-start | bytes 1622024 | tf_op jit(solution)/shard_map/ppermute | solution.py:69
  34.8 22.7 %collective-permute-start.5 = (bf16[1056,256]{1,0:T(8,128)(2,1)S(1)}, bf16[1056,256]{1,0:T(8,128)(2,1)S(1)}, u32[]{:S(2)}, u32[]{:S(2)}) collective-permute-start(bf16[1056,256]{1,0:T(8,128)(2,1)S(1)} %collective-permute-done), channel_id=1, source_target_pairs={{0,8},{8,16},{16,24},{24,28},{28,20},{20,12},{12,4},{4,0},{1,9},{9... | collective-permute-start | bytes 1622024 | tf_op jit(solution)/shard_map/ppermute | solution.py:69
  55.6 20.7 %collective-permute-start.11 = (bf16[1056,256]{1,0:T(8,128)(2,1)S(1)}, bf16[1056,256]{1,0:T(8,128)(2,1)S(1)}, u32[]{:S(2)}, u32[]{:S(2)}) collective-permute-start(bf16[1056,256]{1,0:T(8,128)(2,1)S(1)} %collective-permute-done.10), channel_id=1, source_target_pairs={{0,4},{8,0},{16,8},{24,16},{28,24},{20,28},{12,20},{4,12},{1,5},{9... | collective-permute-start | bytes 1622024 | tf_op jit(solution)/shard_map/ppermute | solution.py:69
  62.6 24.4 %collective-permute-start.6 = (bf16[1072,256]{1,0:T(8,128)(2,1)S(1)}, bf16[1072,256]{1,0:T(8,128)(2,1)S(1)}, u32[]{:S(2)}, u32[]{:S(2)}) collective-permute-start(bf16[1072,256]{1,0:T(8,128)(2,1)S(1)} %collective-permute-done.4), channel_id=1, source_target_pairs={{0,8},{8,16},{16,24},{24,28},{28,20},{20,12},{12,4},{4,0},{1,9},{9... | collective-permute-start | bytes 1646600 | tf_op jit(solution)/shard_map/ppermute | solution.py:69
  64.7 21.9 %collective-permute-start.9 = (bf16[1072,256]{1,0:T(8,128)(2,1)S(1)}, bf16[1072,256]{1,0:T(8,128)(2,1)S(1)}, u32[]{:S(2)}, u32[]{:S(2)}) collective-permute-start(bf16[1072,256]{1,0:T(8,128)(2,1)S(1)} %collective-permute-done.8), channel_id=1, source_target_pairs={{0,4},{8,0},{16,8},{24,16},{28,24},{20,28},{12,20},{4,12},{1,5},{9... | collective-permute-start | bytes 1646600 | tf_op jit(solution)/shard_map/ppermute | solution.py:69
  74.2 23.3 %collective-permute-start.13 = (bf16[1056,256]{1,0:T(8,128)(2,1)S(1)}, bf16[1056,256]{1,0:T(8,128)(2,1)S(1)}, u32[]{:S(2)}, u32[]{:S(2)}) collective-permute-start(bf16[1056,256]{1,0:T(8,128)(2,1)S(1)} %collective-permute-done.7), channel_id=1, source_target_pairs={{0,8},{8,16},{16,24},{24,28},{28,20},{20,12},{12,4},{4,0},{1,9},{9... | collective-permute-start | bytes 1622024 | tf_op jit(solution)/shard_map/ppermute | solution.py:69
  86.9 38.3 %collective-permute-start.14 = (bf16[256,1536]{1,0:T(8,128)(2,1)}, bf16[256,1536]{1,0:T(8,128)(2,1)}, u32[]{:S(2)}, u32[]{:S(2)}) collective-permute-start(bf16[256,1536]{1,0:T(8,128)(2,1)} %get-tuple-element.191), channel_id=1, source_target_pairs={{0,8},{8,16},{16,24},{24,28},{28,20},{20,12},{12,4},{4,0},{1,9},{9... | collective-permute-start | bytes 2359304 | tf_op jit(solution)/shard_map/ppermute | solution.py:69
  88.7 36.6 %collective-permute-start.15 = (bf16[256,1536]{1,0:T(8,128)(2,1)}, bf16[256,1536]{1,0:T(8,128)(2,1)}, u32[]{:S(2)}, u32[]{:S(2)}) collective-permute-start(bf16[256,1536]{1,0:T(8,128)(2,1)} %get-tuple-element.191), channel_id=1, source_target_pairs={{0,4},{8,0},{16,8},{24,16},{28,24},{20,28},{12,20},{4,12},{1,5},{9... | collective-permute-start | bytes 2359304 | tf_op jit(solution)/shard_map/ppermute | solution.py:69
  97.5 55.1 %collective-permute-start.17 = (bf16[256,1536]{1,0:T(8,128)(2,1)}, bf16[256,1536]{1,0:T(8,128)(2,1)}, u32[]{:S(2)}, u32[]{:S(2)}) collective-permute-start(bf16[256,1536]{1,0:T(8,128)(2,1)} %get-tuple-element.197), channel_id=1, source_target_pairs={{0,8},{8,16},{16,24},{24,28},{28,20},{20,12},{12,4},{4,0},{1,9},{9... | collective-permute-start | bytes 2359304 | tf_op jit(solution)/shard_map/ppermute | solution.py:69
  107.7 44.9 %collective-permute-start.18 = (bf16[256,1536]{1,0:T(8,128)(2,1)}, bf16[256,1536]{1,0:T(8,128)(2,1)}, u32[]{:S(2)}, u32[]{:S(2)}) collective-permute-start(bf16[256,1536]{1,0:T(8,128)(2,1)} %get-tuple-element.197), channel_id=1, source_target_pairs={{0,4},{8,0},{16,8},{24,16},{28,24},{20,28},{12,20},{4,12},{1,5},{9... | collective-permute-start | bytes 2359304 | tf_op jit(solution)/shard_map/ppermute | solution.py:69
  132.3 26.3 %collective-permute-start.20 = (bf16[256,1536]{1,0:T(8,128)(2,1)}, bf16[256,1536]{1,0:T(8,128)(2,1)S(1)}, u32[]{:S(2)}, u32[]{:S(2)}) collective-permute-start(bf16[256,1536]{1,0:T(8,128)(2,1)} %collective-permute-done.14), channel_id=1, source_target_pairs={{0,8},{8,16},{16,24},{24,28},{28,20},{20,12},{12,4},{4,0},{1,9},{9... | collective-permute-start | bytes 2359304 | tf_op jit(solution)/shard_map/ppermute | solution.py:69
  133.9 24.7 %collective-permute-start.21 = (bf16[256,1536]{1,0:T(8,128)(2,1)}, bf16[256,1536]{1,0:T(8,128)(2,1)S(1)}, u32[]{:S(2)}, u32[]{:S(2)}) collective-permute-start(bf16[256,1536]{1,0:T(8,128)(2,1)} %collective-permute-done.15), channel_id=1, source_target_pairs={{0,4},{8,0},{16,8},{24,16},{28,24},{20,28},{12,20},{4,12},{1,5},{9... | collective-permute-start | bytes 2359304 | tf_op jit(solution)/shard_map/ppermute | solution.py:69
  156.1 28.1 %collective-permute-start.25 = (bf16[256,1536]{1,0:T(8,128)(2,1)}, bf16[256,1536]{1,0:T(8,128)(2,1)}, u32[]{:S(2)}, u32[]{:S(2)}) collective-permute-start(bf16[256,1536]{1,0:T(8,128)(2,1)} %collective-permute-done.17), channel_id=1, source_target_pairs={{0,8},{8,16},{16,24},{24,28},{28,20},{20,12},{12,4},{4,0},{1,9},{9... | collective-permute-start | bytes 2359304 | tf_op jit(solution)/shard_map/ppermute | solution.py:69
  157.7 26.4 %collective-permute-start.26 = (bf16[256,1536]{1,0:T(8,128)(2,1)}, bf16[256,1536]{1,0:T(8,128)(2,1)}, u32[]{:S(2)}, u32[]{:S(2)}) collective-permute-start(bf16[256,1536]{1,0:T(8,128)(2,1)} %collective-permute-done.18), channel_id=1, source_target_pairs={{0,4},{8,0},{16,8},{24,16},{28,24},{20,28},{12,20},{4,12},{1,5},{9... | collective-permute-start | bytes 2359304 | tf_op jit(solution)/shard_map/ppermute | solution.py:69
  201.8 21.4 %collective-permute-start.28 = (bf16[1536,256]{1,0:T(8,128)(2,1)S(1)}, bf16[1536,256]{1,0:T(8,128)(2,1)S(1)}, u32[]{:S(2)}, u32[]{:S(2)}) collective-permute-start(bf16[1536,256]{1,0:T(8,128)(2,1)S(1)} %copy-done.84), channel_id=1, source_target_pairs={{0,8},{8,16},{16,24},{24,28},{28,20},{20,12},{12,4},{4,0},{1,9},{9... | collective-permute-start | bytes 2359304 | tf_op jit(solution)/shard_map/ppermute | solution.py:69
  206.4 33.6 %collective-permute-start.31 = (bf16[256,1536]{1,0:T(8,128)(2,1)S(1)}, bf16[256,1536]{1,0:T(8,128)(2,1)S(1)}, u32[]{:S(2)}, u32[]{:S(2)}) collective-permute-start(bf16[256,1536]{1,0:T(8,128)(2,1)S(1)} %copy-done.86), channel_id=1, source_target_pairs={{0,8},{8,16},{16,24},{24,28},{28,20},{20,12},{12,4},{4,0},{1,9},{9... | collective-permute-start | bytes 2359304 | tf_op jit(solution)/shard_map/ppermute | solution.py:69
  206.4 33.7 %collective-permute-start.39 = (bf16[256,1536]{1,0:T(8,128)(2,1)S(1)}, bf16[256,1536]{1,0:T(8,128)(2,1)S(1)}, u32[]{:S(2)}, u32[]{:S(2)}) collective-permute-start(bf16[256,1536]{1,0:T(8,128)(2,1)S(1)} %collective-permute-done.21), channel_id=1, source_target_pairs={{0,4},{8,0},{16,8},{24,16},{28,24},{20,28},{12,20},{4,12},{1,5},{9... | collective-permute-start | bytes 2359304 | tf_op jit(solution)/shard_map/ppermute | solution.py:69
  223.2 52.6 %collective-permute-start.30 = (bf16[512,2048]{1,0:T(8,128)(2,1)S(1)}, bf16[512,2048]{1,0:T(8,128)(2,1)S(1)}, u32[]{:S(2)}, u32[]{:S(2)}) collective-permute-start(bf16[512,2048]{1,0:T(8,128)(2,1)S(1)} %add_convert_fusion.5), channel_id=1, source_target_pairs={{0,2},{1,3},{2,0},{3,1},{4,6},{5,7},{6,4},{7,5},{8,10},{9,11},{10,... | collective-permute-start | bytes 6291464 | tf_op jit(solution)/shard_map/ppermute | solution.py:164
  231.1 25.8 %collective-permute-start.32 = (bf16[256,1536]{1,0:T(8,128)(2,1)}, bf16[256,1536]{1,0:T(8,128)(2,1)S(1)}, u32[]{:S(2)}, u32[]{:S(2)}) collective-permute-start(bf16[256,1536]{1,0:T(8,128)(2,1)} %collective-permute-done.25), channel_id=1, source_target_pairs={{0,8},{8,16},{16,24},{24,28},{28,20},{20,12},{12,4},{4,0},{1,9},{9... | collective-permute-start | bytes 2359304 | tf_op jit(solution)/shard_map/ppermute | solution.py:69
  233.4 23.6 %collective-permute-start.34 = (bf16[256,1536]{1,0:T(8,128)(2,1)}, bf16[256,1536]{1,0:T(8,128)(2,1)S(1)}, u32[]{:S(2)}, u32[]{:S(2)}) collective-permute-start(bf16[256,1536]{1,0:T(8,128)(2,1)} %collective-permute-done.26), channel_id=1, source_target_pairs={{0,4},{8,0},{16,8},{24,16},{28,24},{20,28},{12,20},{4,12},{1,5},{9... | collective-permute-start | bytes 2359304 | tf_op jit(solution)/shard_map/ppermute | solution.py:69
  240.1 33.7 %collective-permute-start.37 = (bf16[1536,256]{1,0:T(8,128)(2,1)S(1)}, bf16[1536,256]{1,0:T(8,128)(2,1)S(1)}, u32[]{:S(2)}, u32[]{:S(2)}) collective-permute-start(bf16[1536,256]{1,0:T(8,128)(2,1)S(1)} %collective-permute-done.28), channel_id=1, source_target_pairs={{0,8},{8,16},{16,24},{24,28},{28,20},{20,12},{12,4},{4,0},{1,9},{9... | collective-permute-start | bytes 2359304 | tf_op jit(solution)/shard_map/ppermute | solution.py:69
  240.1 33.7 %collective-permute-start.40 = (bf16[1536,256]{1,0:T(8,128)(2,1)S(1)}, bf16[1536,256]{1,0:T(8,128)(2,1)S(1)}, u32[]{:S(2)}, u32[]{:S(2)}) collective-permute-start(bf16[1536,256]{1,0:T(8,128)(2,1)S(1)} %collective-permute-done.29), channel_id=1, source_target_pairs={{0,4},{8,0},{16,8},{24,16},{28,24},{20,28},{12,20},{4,12},{1,5},{9... | collective-permute-start | bytes 2359304 | tf_op jit(solution)/shard_map/ppermute | solution.py:69
  256.9 33.7 %collective-permute-start.33 = (bf16[256,1536]{1,0:T(8,128)(2,1)S(1)}, bf16[256,1536]{1,0:T(8,128)(2,1)S(1)}, u32[]{:S(2)}, u32[]{:S(2)}) collective-permute-start(bf16[256,1536]{1,0:T(8,128)(2,1)S(1)} %collective-permute-done.31), channel_id=1, source_target_pairs={{0,8},{8,16},{16,24},{24,28},{28,20},{20,12},{12,4},{4,0},{1,9},{9... | collective-permute-start | bytes 2359304 | tf_op jit(solution)/shard_map/ppermute | solution.py:69
  256.9 33.7 %collective-permute-start.35 = (bf16[256,1536]{1,0:T(8,128)(2,1)S(1)}, bf16[256,1536]{1,0:T(8,128)(2,1)S(1)}, u32[]{:S(2)}, u32[]{:S(2)}) collective-permute-start(bf16[256,1536]{1,0:T(8,128)(2,1)S(1)} %collective-permute-done.34), channel_id=1, source_target_pairs={{0,4},{8,0},{16,8},{24,16},{28,24},{20,28},{12,20},{4,12},{1,5},{9... | collective-permute-start | bytes 2359304 | tf_op jit(solution)/shard_map/ppermute | solution.py:69
  273.8 36.0 %collective-permute-start.38 = (bf16[1536,256]{1,0:T(8,128)(2,1)S(1)}, bf16[1536,256]{1,0:T(8,128)(2,1)}, u32[]{:S(2)}, u32[]{:S(2)}) collective-permute-start(bf16[1536,256]{1,0:T(8,128)(2,1)S(1)} %collective-permute-done.37), channel_id=1, source_target_pairs={{0,8},{8,16},{16,24},{24,28},{28,20},{20,12},{12,4},{4,0},{1,9},{9... | collective-permute-start | bytes 2359304 | tf_op jit(solution)/shard_map/ppermute | solution.py:69
  273.8 36.0 %collective-permute-start.41 = (bf16[1536,256]{1,0:T(8,128)(2,1)S(1)}, bf16[1536,256]{1,0:T(8,128)(2,1)S(1)}, u32[]{:S(2)}, u32[]{:S(2)}) collective-permute-start(bf16[1536,256]{1,0:T(8,128)(2,1)S(1)} %collective-permute-done.40), channel_id=1, source_target_pairs={{0,4},{8,0},{16,8},{24,16},{28,24},{20,28},{12,20},{4,12},{1,5},{9... | collective-permute-start | bytes 2359304 | tf_op jit(solution)/shard_map/ppermute | solution.py:69
  310.8 27.1 %collective-permute-start.42 = (bf16[1536,256]{1,0:T(8,128)(2,1)}, bf16[1536,256]{1,0:T(8,128)(2,1)S(1)}, u32[]{:S(2)}, u32[]{:S(2)}) collective-permute-start(bf16[1536,256]{1,0:T(8,128)(2,1)} %collective-permute-done.38), channel_id=1, source_target_pairs={{0,8},{8,16},{16,24},{24,28},{28,20},{20,12},{12,4},{4,0},{1,9},{9... | collective-permute-start | bytes 2359304 | tf_op jit(solution)/shard_map/ppermute | solution.py:69
  349.5 35.9 %collective-permute-start.43 = (bf16[1536,256]{1,0:T(8,128)(2,1)}, bf16[1536,256]{1,0:T(8,128)(2,1)}, u32[]{:S(2)}, u32[]{:S(2)}) collective-permute-start(bf16[1536,256]{1,0:T(8,128)(2,1)} %convolution_convert_fusion.8), channel_id=1, source_target_pairs={{0,8},{8,16},{16,24},{24,28},{28,20},{20,12},{12,4},{4,0},{1,9},{9... | collective-permute-start | bytes 2359304 | tf_op jit(solution)/shard_map/ppermute | solution.py:69
  351.6 33.8 %collective-permute-start.44 = (bf16[1536,256]{1,0:T(8,128)(2,1)}, bf16[1536,256]{1,0:T(8,128)(2,1)}, u32[]{:S(2)}, u32[]{:S(2)}) collective-permute-start(bf16[1536,256]{1,0:T(8,128)(2,1)} %convolution_convert_fusion.7), channel_id=1, source_target_pairs={{0,4},{8,0},{16,8},{24,16},{28,24},{20,28},{12,20},{4,12},{1,5},{9... | collective-permute-start | bytes 2359304 | tf_op jit(solution)/shard_map/ppermute | solution.py:69
  407.5 24.9 %collective-permute-start.48 = (bf16[256,1536]{1,0:T(8,128)(2,1)}, bf16[256,1536]{1,0:T(8,128)(2,1)S(1)}, u32[]{:S(2)}, u32[]{:S(2)}) collective-permute-start(bf16[256,1536]{1,0:T(8,128)(2,1)} %convolution_convert_fusion.4), channel_id=1, source_target_pairs={{0,8},{8,16},{16,24},{24,28},{28,20},{20,12},{12,4},{4,0},{1,9},{9... | collective-permute-start | bytes 2359304 | tf_op jit(solution)/shard_map/ppermute | solution.py:69
  408.3 24.1 %collective-permute-start.49 = (bf16[256,1536]{1,0:T(8,128)(2,1)}, bf16[256,1536]{1,0:T(8,128)(2,1)S(1)}, u32[]{:S(2)}, u32[]{:S(2)}) collective-permute-start(bf16[256,1536]{1,0:T(8,128)(2,1)} %convolution_convert_fusion.3), channel_id=1, source_target_pairs={{0,4},{8,0},{16,8},{24,16},{28,24},{20,28},{12,20},{4,12},{1,5},{9... | collective-permute-start | bytes 2359304 | tf_op jit(solution)/shard_map/ppermute | solution.py:69
  413.0 31.5 %collective-permute-start.51 = (bf16[1536,256]{1,0:T(8,128)(2,1)}, bf16[1536,256]{1,0:T(8,128)(2,1)}, u32[]{:S(2)}, u32[]{:S(2)}) collective-permute-start(bf16[1536,256]{1,0:T(8,128)(2,1)} %fusion.51), channel_id=1, source_target_pairs={{0,8},{8,16},{16,24},{24,28},{28,20},{20,12},{12,4},{4,0},{1,9},{9... | collective-permute-start | bytes 2359304 | tf_op jit(solution)/shard_map/ppermute | solution.py:69
  417.1 30.9 %collective-permute-start.53 = (bf16[1536,256]{1,0:T(8,128)(2,1)}, bf16[1536,256]{1,0:T(8,128)(2,1)}, u32[]{:S(2)}, u32[]{:S(2)}) collective-permute-start(bf16[1536,256]{1,0:T(8,128)(2,1)} %fusion.53), channel_id=1, source_target_pairs={{0,4},{8,0},{16,8},{24,16},{28,24},{20,28},{12,20},{4,12},{1,5},{9... | collective-permute-start | bytes 2359304 | tf_op jit(solution)/shard_map/ppermute | solution.py:69
  432.3 47.2 %collective-permute-start.50 = (bf16[512,2048]{1,0:T(8,128)(2,1)}, bf16[512,2048]{1,0:T(8,128)(2,1)S(1)}, u32[]{:S(2)}, u32[]{:S(2)}) collective-permute-start(bf16[512,2048]{1,0:T(8,128)(2,1)} %add_convert_fusion.3), channel_id=1, source_target_pairs={{0,2},{1,3},{2,0},{3,1},{4,6},{5,7},{6,4},{7,5},{8,10},{9,11},{10,... | collective-permute-start | bytes 6291464 | tf_op jit(solution)/shard_map/ppermute | solution.py:164
  452.2 20.5 %collective-permute-start.58 = (bf16[256,1536]{1,0:T(8,128)(2,1)S(1)}, bf16[256,1536]{1,0:T(8,128)(2,1)S(1)}, u32[]{:S(2)}, u32[]{:S(2)}) collective-permute-start(bf16[256,1536]{1,0:T(8,128)(2,1)S(1)} %fusion.57), channel_id=1, source_target_pairs={{0,4},{8,0},{16,8},{24,16},{28,24},{20,28},{12,20},{4,12},{1,5},{9... | collective-permute-start | bytes 2359304 | tf_op jit(solution)/shard_map/ppermute | solution.py:69
  454.5 34.2 %collective-permute-start.52 = (bf16[256,1536]{1,0:T(8,128)(2,1)S(1)}, bf16[256,1536]{1,0:T(8,128)(2,1)S(1)}, u32[]{:S(2)}, u32[]{:S(2)}) collective-permute-start(bf16[256,1536]{1,0:T(8,128)(2,1)S(1)} %fusion.50), channel_id=1, source_target_pairs={{0,8},{8,16},{16,24},{24,28},{28,20},{20,12},{12,4},{4,0},{1,9},{9... | collective-permute-start | bytes 2359304 | tf_op jit(solution)/shard_map/ppermute | solution.py:69
  456.3 33.2 %collective-permute-start.54 = (bf16[256,1536]{1,0:T(8,128)(2,1)S(1)}, bf16[256,1536]{1,0:T(8,128)(2,1)S(1)}, u32[]{:S(2)}, u32[]{:S(2)}) collective-permute-start(bf16[256,1536]{1,0:T(8,128)(2,1)S(1)} %fusion.52), channel_id=1, source_target_pairs={{0,4},{8,0},{16,8},{24,16},{28,24},{20,28},{12,20},{4,12},{1,5},{9... | collective-permute-start | bytes 2359304 | tf_op jit(solution)/shard_map/ppermute | solution.py:69
  471.8 56.0 %collective-permute-start.57 = (bf16[1536,256]{1,0:T(8,128)(2,1)}, bf16[1536,256]{1,0:T(8,128)(2,1)S(1)}, u32[]{:S(2)}, u32[]{:S(2)}) collective-permute-start(bf16[1536,256]{1,0:T(8,128)(2,1)} %fusion.54), channel_id=1, source_target_pairs={{0,8},{8,16},{16,24},{24,28},{28,20},{20,12},{12,4},{4,0},{1,9},{9... | collective-permute-start | bytes 2359304 | tf_op jit(solution)/shard_map/ppermute | solution.py:69
  472.7 55.2 %collective-permute-start.59 = (bf16[1536,256]{1,0:T(8,128)(2,1)}, bf16[1536,256]{1,0:T(8,128)(2,1)S(1)}, u32[]{:S(2)}, u32[]{:S(2)}) collective-permute-start(bf16[1536,256]{1,0:T(8,128)(2,1)} %fusion.56), channel_id=1, source_target_pairs={{0,4},{8,0},{16,8},{24,16},{28,24},{20,28},{12,20},{4,12},{1,5},{9... | collective-permute-start | bytes 2359304 | tf_op jit(solution)/shard_map/ppermute | solution.py:69
  491.5 52.3 %collective-permute-start.60 = (bf16[256,1536]{1,0:T(8,128)(2,1)}, bf16[256,1536]{1,0:T(8,128)(2,1)}, u32[]{:S(2)}, u32[]{:S(2)}) collective-permute-start(bf16[256,1536]{1,0:T(8,128)(2,1)} %fusion.58), channel_id=1, source_target_pairs={{0,8},{8,16},{16,24},{24,28},{28,20},{20,12},{12,4},{4,0},{1,9},{9... | collective-permute-start | bytes 2359304 | tf_op jit(solution)/shard_map/ppermute | solution.py:69
  491.7 52.0 %collective-permute-start.61 = (bf16[256,1536]{1,0:T(8,128)(2,1)}, bf16[256,1536]{1,0:T(8,128)(2,1)}, u32[]{:S(2)}, u32[]{:S(2)}) collective-permute-start(bf16[256,1536]{1,0:T(8,128)(2,1)} %fusion.59), channel_id=1, source_target_pairs={{0,4},{8,0},{16,8},{24,16},{28,24},{20,28},{12,20},{4,12},{1,5},{9... | collective-permute-start | bytes 2359304 | tf_op jit(solution)/shard_map/ppermute | solution.py:69
  504.7 303.5 %all-reduce.18.cloned.1.call-start = ((), (), s32[]{:S(2)}) async-start(), calls=%async_computation.1 | async-start | bytes 1081344 | tf_op jit(solution)/shard_map/psum | solution.py:811
  568.1 21.9 %collective-permute-start.63 = (bf16[256,1536]{1,0:T(8,128)(2,1)}, bf16[256,1536]{1,0:T(8,128)(2,1)}, u32[]{:S(2)}, u32[]{:S(2)}) collective-permute-start(bf16[256,1536]{1,0:T(8,128)(2,1)} %fusion.60), channel_id=1, source_target_pairs={{0,8},{8,16},{16,24},{24,28},{28,20},{20,12},{12,4},{4,0},{1,9},{9... | collective-permute-start | bytes 2359304 | tf_op jit(solution)/shard_map/ppermute | solution.py:69
  571.8 20.8 %collective-permute-start.64 = (bf16[256,1536]{1,0:T(8,128)(2,1)}, bf16[256,1536]{1,0:T(8,128)(2,1)}, u32[]{:S(2)}, u32[]{:S(2)}) collective-permute-start(bf16[256,1536]{1,0:T(8,128)(2,1)} %fusion.61), channel_id=1, source_target_pairs={{0,4},{8,0},{16,8},{24,16},{28,24},{20,28},{12,20},{4,12},{1,5},{9... | collective-permute-start | bytes 2359304 | tf_op jit(solution)/shard_map/ppermute | solution.py:69
  571.8 77.1 %collective-permute-start.68 = (bf16[1536,256]{1,0:T(8,128)(2,1)}, bf16[1536,256]{1,0:T(8,128)(2,1)}, u32[]{:S(2)}, u32[]{:S(2)}) collective-permute-start(bf16[1536,256]{1,0:T(8,128)(2,1)} %fusion.62), channel_id=1, source_target_pairs={{0,8},{8,16},{16,24},{24,28},{28,20},{20,12},{12,4},{4,0},{1,9},{9... | collective-permute-start | bytes 2359304 | tf_op jit(solution)/shard_map/ppermute | solution.py:69
  577.0 71.9 %collective-permute-start.69 = (bf16[256,1536]{1,0:T(8,128)(2,1)}, bf16[256,1536]{1,0:T(8,128)(2,1)}, u32[]{:S(2)}, u32[]{:S(2)}) collective-permute-start(bf16[256,1536]{1,0:T(8,128)(2,1)} %fusion.63), channel_id=1, source_target_pairs={{0,4},{8,0},{16,8},{24,16},{28,24},{20,28},{12,20},{4,12},{1,5},{9... | collective-permute-start | bytes 2359304 | tf_op jit(solution)/shard_map/ppermute | solution.py:69
  615.2 60.3 %collective-permute-start.71 = (bf16[256,1536]{1,0:T(8,128)(2,1)}, bf16[256,1536]{1,0:T(8,128)(2,1)}, u32[]{:S(2)}, u32[]{:S(2)}) collective-permute-start(bf16[256,1536]{1,0:T(8,128)(2,1)} %fusion.64), channel_id=1, source_target_pairs={{0,8},{8,16},{16,24},{24,28},{28,20},{20,12},{12,4},{4,0},{1,9},{9... | collective-permute-start | bytes 2359304 | tf_op jit(solution)/shard_map/ppermute | solution.py:69
  675.0 48.9 %collective-permute-start.90 = (bf16[1056,256]{1,0:T(8,128)(2,1)}, bf16[1056,256]{1,0:T(8,128)(2,1)}, u32[]{:S(2)}, u32[]{:S(2)}) collective-permute-start(bf16[1056,256]{1,0:T(8,128)(2,1)} %fusion.94), channel_id=1, source_target_pairs={{0,4},{8,0},{16,8},{24,16},{28,24},{20,28},{12,20},{4,12},{1,5},{9... | collective-permute-start | bytes 1622024 | tf_op jit(solution)/shard_map/ppermute | solution.py:69
  690.2 35.9 %collective-permute-start.74 = (bf16[1056,256]{1,0:T(8,128)(2,1)}, bf16[1056,256]{1,0:T(8,128)(2,1)}, u32[]{:S(2)}, u32[]{:S(2)}) collective-permute-start(bf16[1056,256]{1,0:T(8,128)(2,1)} %pad_maximum_fusion.31), channel_id=1, source_target_pairs={{0,8},{8,16},{16,24},{24,28},{28,20},{20,12},{12,4},{4,0},{1,9},{9... | collective-permute-start | bytes 1622024 | tf_op jit(solution)/shard_map/ppermute | solution.py:69
  692.5 36.0 %collective-permute-start.76 = (bf16[1056,256]{1,0:T(8,128)(2,1)}, bf16[1056,256]{1,0:T(8,128)(2,1)}, u32[]{:S(2)}, u32[]{:S(2)}) collective-permute-start(bf16[1056,256]{1,0:T(8,128)(2,1)} %pad_maximum_fusion.32), channel_id=1, source_target_pairs={{0,4},{8,0},{16,8},{24,16},{28,24},{20,28},{12,20},{4,12},{1,5},{9... | collective-permute-start | bytes 1622024 | tf_op jit(solution)/shard_map/ppermute | solution.py:69
  693.9 36.8 %collective-permute-start.86 = (bf16[1056,256]{1,0:T(8,128)(2,1)}, bf16[1056,256]{1,0:T(8,128)(2,1)}, u32[]{:S(2)}, u32[]{:S(2)}) collective-permute-start(bf16[1056,256]{1,0:T(8,128)(2,1)} %pad_maximum_fusion.33), channel_id=1, source_target_pairs={{0,8},{8,16},{16,24},{24,28},{28,20},{20,12},{12,4},{4,0},{1,9},{9... | collective-permute-start | bytes 1622024 | tf_op jit(solution)/shard_map/ppermute | solution.py:69
  715.8 47.5 %collective-permute-start.73 = (bf16[512,2048]{1,0:T(8,128)(2,1)}, bf16[512,2048]{1,0:T(8,128)(2,1)}, u32[]{:S(2)}, u32[]{:S(2)}) collective-permute-start(bf16[512,2048]{1,0:T(8,128)(2,1)} %add_convert_fusion.1), channel_id=1, source_target_pairs={{0,2},{1,3},{2,0},{3,1},{4,6},{5,7},{6,4},{7,5},{8,10},{9,11},{10,... | collective-permute-start | bytes 6291464 | tf_op jit(solution)/shard_map/ppermute | solution.py:164
  725.2 42.8 %collective-permute-start.91 = (bf16[1056,256]{1,0:T(8,128)(2,1)S(1)}, bf16[1056,256]{1,0:T(8,128)(2,1)S(1)}, u32[]{:S(2)}, u32[]{:S(2)}) collective-permute-start(bf16[1056,256]{1,0:T(8,128)(2,1)S(1)} %fusion.93), channel_id=1, source_target_pairs={{0,4},{8,0},{16,8},{24,16},{28,24},{20,28},{12,20},{4,12},{1,5},{9... | collective-permute-start | bytes 1622024 | tf_op jit(solution)/shard_map/ppermute | solution.py:69
  727.3 39.0 %collective-permute-start.75 = (bf16[1056,256]{1,0:T(8,128)(2,1)S(1)}, bf16[1056,256]{1,0:T(8,128)(2,1)S(1)}, u32[]{:S(2)}, u32[]{:S(2)}) collective-permute-start(bf16[1056,256]{1,0:T(8,128)(2,1)S(1)} %fusion.83), channel_id=1, source_target_pairs={{0,8},{8,16},{16,24},{24,28},{28,20},{20,12},{12,4},{4,0},{1,9},{9... | collective-permute-start | bytes 1622024 | tf_op jit(solution)/shard_map/ppermute | solution.py:69
  729.7 36.6 %collective-permute-start.77 = (bf16[1056,256]{1,0:T(8,128)(2,1)S(1)}, bf16[1056,256]{1,0:T(8,128)(2,1)S(1)}, u32[]{:S(2)}, u32[]{:S(2)}) collective-permute-start(bf16[1056,256]{1,0:T(8,128)(2,1)S(1)} %fusion.84), channel_id=1, source_target_pairs={{0,4},{8,0},{16,8},{24,16},{28,24},{20,28},{12,20},{4,12},{1,5},{9... | collective-permute-start | bytes 1622024 | tf_op jit(solution)/shard_map/ppermute | solution.py:69
  732.7 38.9 %collective-permute-start.87 = (bf16[1056,256]{1,0:T(8,128)(2,1)}, bf16[1056,256]{1,0:T(8,128)(2,1)}, u32[]{:S(2)}, u32[]{:S(2)}) collective-permute-start(bf16[1056,256]{1,0:T(8,128)(2,1)} %fusion.91), channel_id=1, source_target_pairs={{0,8},{8,16},{16,24},{24,28},{28,20},{20,12},{12,4},{4,0},{1,9},{9... | collective-permute-start | bytes 1622024 | tf_op jit(solution)/shard_map/ppermute | solution.py:69
  773.7 52.7 %collective-permute-start.88 = (bf16[1056,256]{1,0:T(8,128)(2,1)}, bf16[1056,256]{1,0:T(8,128)(2,1)}, u32[]{:S(2)}, u32[]{:S(2)}) collective-permute-start(bf16[1056,256]{1,0:T(8,128)(2,1)} %fusion.90), channel_id=1, source_target_pairs={{0,8},{8,16},{16,24},{24,28},{28,20},{20,12},{12,4},{4,0},{1,9},{9... | collective-permute-start | bytes 1622024 | tf_op jit(solution)/shard_map/ppermute | solution.py:69
  786.4 54.1 %collective-permute-start.78 = (bf16[512,2048]{1,0:T(8,128)(2,1)S(1)}, bf16[512,2048]{1,0:T(8,128)(2,1)}, u32[]{:S(2)}, u32[]{:S(2)}) collective-permute-start(bf16[512,2048]{1,0:T(8,128)(2,1)S(1)} %add_convert_fusion), channel_id=1, source_target_pairs={{0,1},{1,0},{2,3},{3,2},{4,5},{5,4},{6,7},{7,6},{8,9},{9,8},{10,11... | collective-permute-start | bytes 6291464 | tf_op jit(solution)/shard_map/ppermute | solution.py:159
  789.2 20.6 %collective-permute-start.85 = (bf16[1056,256]{1,0:T(8,128)(2,1)}, bf16[1056,256]{1,0:T(8,128)(2,1)S(1)}, u32[]{:S(2)}, u32[]{:S(2)}) collective-permute-start(bf16[1056,256]{1,0:T(8,128)(2,1)} %fusion.88), channel_id=1, source_target_pairs={{0,4},{8,0},{16,8},{24,16},{28,24},{20,28},{12,20},{4,12},{1,5},{9... | collective-permute-start | bytes 1622024 | tf_op jit(solution)/shard_map/ppermute | solution.py:69
  792.8 30.2 %collective-permute-start.83 = (bf16[1056,256]{1,0:T(8,128)(2,1)}, bf16[1056,256]{1,0:T(8,128)(2,1)}, u32[]{:S(2)}, u32[]{:S(2)}) collective-permute-start(bf16[1056,256]{1,0:T(8,128)(2,1)} %fusion.87), channel_id=1, source_target_pairs={{0,8},{8,16},{16,24},{24,28},{28,20},{20,12},{12,4},{4,0},{1,9},{9... | collective-permute-start | bytes 1622024 | tf_op jit(solution)/shard_map/ppermute | solution.py:69
  (191 other events, 2161.9 us)
Sparse Core Ops, SparseCore 0:
  504.8 84.2 all-reduce.15
  723.9 76.6 all-reduce.17

commit v3 on v2

--- a/solution.py
+++ b/solution.py
@@ -39,6 +39,7 @@
         self.landed = {1: [], -1: []}
         self.sent = {1: 0, -1: 0}
         self.last = {1: None, -1: None}
+        self.token = None
 
     def add(self, weights, delays=None):
         half = self.n // 2
@@ -63,6 +64,8 @@
                 gate = self.sent[way] - self.depth
                 if gate >= 0:
                     message = after(message, landed[gate])
+                if self.token is not None:
+                    message = after(message, self.token)
                 flow.busy = True
                 self.sent[way] += 1
                 self.last[way] = message
@@ -71,6 +74,19 @@
     def hold(self, values):
         last = [message for message in self.last.values() if message is not None]
         return after(values, *last) if last else values
+
+    def resume(self, token):
+        self.token = token
+        self.issue()
+        return token
+
+    def quiet(self, values):
+        waiting = {w: self.queue[w] for w in (1, -1)}
+        self.queue = {1: [], -1: []}
+        for _ in range(self.depth):
+            values = self.land(values)
+        self.queue = waiting
+        return values
 
     def land(self, values=None, count=1):
         for turn in range(count):
@@ -169,7 +185,7 @@
     chip = chips((part(0) + got.astype(f32)).astype(bf16))
     far = chip_swap(chip)
     total = totals((chip.astype(f32) + far.astype(f32)).astype(bf16))
-    return jnp.concatenate([total, core_swap(total)], axis=0), total
+    return total, core_swap(total)
 
 
 def gelu_parts(x):
@@ -203,7 +219,7 @@
 
 def forward_kernel(
     inner, before, conv_w, conv_b, gate_m, gate_b, rate,
-    mixed, recur, admit, decay, cum, local, ends, ext, gates,
+    mixed, recur, admit, decay, root, cum, local, ends, ext, gates,
 ):
     length, lanes = inner.shape
     ext[:pad_rows] = before[...]
@@ -224,7 +240,9 @@
         g = jax.nn.sigmoid(gates[1, at])
         log_decay = -8.0 * r * rate[...]
         d = jnp.exp(log_decay)
-        drive = jnp.sqrt(drive_square(log_decay, d)) * g * mixed[at]
+        m = jnp.sqrt(drive_square(log_decay, d))
+        drive = m * g * mixed[at]
+        root[at] = m
         recur[at] = r
         admit[at] = g
         decay[at] = d
@@ -243,8 +261,8 @@
     ends[2:] = jnp.zeros((pad_rows - 2, lanes), f32)
 
 
-def reverse_kernel(grad_product, gate_in, decay, tail, grad, first, nexts):
-    length, lanes = gate_in.shape
+def reverse_kernel(grad_product, act, decay, tail, grad, first, nexts):
+    length, lanes = act.shape
     nexts[...] = pltpu.roll(decay[...], length - 1, 0)
     nexts[length - 1 :] = jnp.ones((1, lanes), f32)
     rows = lax.broadcasted_iota(jnp.int32, (step_rows, lanes), 0)
@@ -252,8 +270,7 @@
 
     def step(i, carry):
         at = pl.ds(pl.multiple_of((steps - 1 - i) * step_rows, step_rows), step_rows)
-        x = gate_in[at].astype(f32)
-        direct = grad_product[at] * gelu_parts(x)[0]
+        direct = grad_product[at] * act[at]
         a, b = scan_block(nexts[at], direct, rows, True)
         b = b + a * carry[1]
         a = a * carry[0]
@@ -268,32 +285,26 @@
 
 
 def gates_back_kernel(
-    grad_product, gate_in, tail, grad, incoming, cum, local, entry, recur, admit, decay, mixed, gate_m, rate,
-    grad_gates, grad_mixed, grad_gate_in, sums, previous, grad_mix,
+    grad_product, slope, tail, grad, incoming, states, entry, recur, admit, decay, root, mixed, inner, before,
+    gate_m, rate, conv_w, grad_gates, grad_inner, grad_gate_in, head, last, sums, grad_mix, grad_ext, ext,
 ):
-    length, lanes = gate_in.shape
+    length, lanes = inner.shape
     enter = entry[0:1]
     later = incoming[0:1]
-    previous[0:pad_rows] = jnp.broadcast_to(enter, (pad_rows, lanes))
-    previous[pad_rows:] = local[...] + cum[...] * enter
+    taps = conv_w.shape[0]
 
     def step(i, carry):
-        row = pl.multiple_of(i * step_rows, step_rows)
-        at = pl.ds(row, step_rows)
-        x = gate_in[at].astype(f32)
-        slope = gelu_parts(x)[1]
-        states = previous[pl.ds(row + pad_rows, step_rows)]
-        head = previous[pl.ds(row, pad_rows)]
+        at = pl.ds(pl.multiple_of(i * step_rows, step_rows), step_rows)
+        state = states[at]
         rows = lax.broadcasted_iota(jnp.int32, (step_rows, lanes), 0)
-        before = jnp.where(rows == 0, head[pad_rows - 1 :], pltpu.roll(states, 1, 0))
-        grad_gate_in[at] = (slope * (grad_product[at] * states)).astype(bf16)
+        earlier = jnp.where(rows == 0, carry[3], pltpu.roll(state, 1, 0))
+        grad_gate_in[at] = (slope[at] * (grad_product[at] * state)).astype(bf16)
         total = grad[at] + tail[at] * later
-        r, g, d, mix = recur[at], admit[at], decay[at], mixed[at]
-        root = jnp.sqrt(drive_square(-8.0 * r * rate[...], d))
-        grad_mix[at] = total * root * g
+        r, g, d, m, mix = recur[at], admit[at], decay[at], root[at], mixed[at]
+        grad_mix[at] = total * m * g
         both = total * mix
-        gate1 = both * root * g * (1.0 - g)
-        grad_log = total * before * d - both * g * d * d / root
+        gate1 = both * m * g * (1.0 - g)
+        grad_log = total * earlier * d - both * g * d * d / m
         gate0 = -8.0 * rate[...] * grad_log * r * (1.0 - r)
         low0 = gate0.astype(bf16)
         low1 = gate1.astype(bf16)
@@ -303,17 +314,22 @@
             carry[0] - 8.0 * (grad_log * r),
             carry[1] + low0.astype(f32),
             carry[2] + low1.astype(f32),
+            state[step_rows - 1 :],
         )
 
     zero = jnp.zeros((step_rows, lanes), f32)
-    totals = lax.fori_loop(0, length // step_rows, step, (zero, zero, zero))
+    totals = lax.fori_loop(0, length // step_rows, step, (zero, zero, zero, enter))
     back = grad_mix[...]
     for k in range(2):
         back = back + lax.dot_general(
             grad_gates[k], gate_m[k], (((1,), (1,)), ((), ())), preferred_element_type=f32
         )
-    low = back.astype(bf16)
-    grad_mixed[...] = low
+    back = back.astype(bf16).astype(f32)
+    head[...] = back[:pad_rows]
+    grad_ext[:length] = back
+    grad_ext[length:] = jnp.zeros((pad_rows, lanes), f32)
+    ext[:pad_rows] = before[...]
+    ext[pad_rows:] = inner[...].astype(f32)
 
     @pl.when(pl.program_id(0) == 0)
     def _():
@@ -321,28 +337,27 @@
 
     for k in range(3):
         sums[k : k + 1] += jnp.sum(totals[k], axis=0, keepdims=True)
-    sums[3:4] += jnp.sum(low.astype(f32), axis=0, keepdims=True)
-
-
-def conv_back_kernel(grad_mixed, behind, inner, before, conv_w, grad_inner, sums, grad_ext, ext):
-    length, lanes = inner.shape
-    taps = conv_w.shape[0]
-    ext[:pad_rows] = before[...]
-    ext[pad_rows:] = inner[...].astype(f32)
-    grad_ext[length:] = behind[...]
-    grad = grad_mixed[...].astype(f32)
-    grad_ext[:length] = grad
-
-    @pl.when(pl.program_id(0) == 0)
-    def _():
-        sums[...] = jnp.zeros_like(sums)
-
+    sums[3:4] += jnp.sum(back, axis=0, keepdims=True)
     total = jnp.zeros((length, lanes), f32)
     for lag in range(taps):
         total = total + conv_w[lag : lag + 1] * grad_ext[lag : lag + length]
-        term = grad * ext[pad_rows - lag : pad_rows - lag + length]
-        sums[lag : lag + 1] += jnp.sum(term, axis=0, keepdims=True)
+        term = back * ext[pad_rows - lag : pad_rows - lag + length]
+        sums[4 + lag : 5 + lag] += jnp.sum(term, axis=0, keepdims=True)
     grad_inner[...] = total.astype(bf16)
+    last[...] = total[length - pad_rows :]
+
+
+def hidden_back_kernel(cot, w_down, act, slope, grad_both):
+    units = w_down.shape[0]
+    cut = math.gcd(units, 512)
+    for j in range(0, units, cut):
+        grad = lax.dot_general(
+            cot[...], w_down[j : j + cut], (((1,), (1,)), ((), ())), preferred_element_type=f32
+        )
+        grad_both[:, j : j + cut] = (grad * slope[:, j : j + cut].astype(f32)).astype(bf16)
+        grad_both[:, units + j : units + j + cut] = (
+            grad * act[:, j : j + cut].astype(f32)
+        ).astype(bf16)
 
 
 def per_sequence(kernel, seqs, inputs, outputs, scratch, flops):
@@ -371,34 +386,73 @@
     return sum(math.prod(a.shape) * jnp.dtype(a.dtype).itemsize for a in arrays)
 
 
-def by_rows(kernel, arrays, whole, outputs, sums, order=None, back=False, moved=()):
+def by_rows(
+    kernel, arrays, whole, outputs, sums, order=None, back=False, moved=(), half=None, earlier=()
+):
     seqs, length, width = arrays[0].shape
     block = min(norm_rows, length)
-    near = pl.BlockSpec((None, block, width), lambda s, r, *_: (s, r, 0))
-    far = pl.BlockSpec((None, block, width), lambda s, r, sequence, chunk: (sequence[s], r, 0))
+    count = seqs if half is None else seqs // 2
+    skip = count * (half or 0)
     moves = order is not None
+    tile = (None, block, width)
+    near = pl.BlockSpec(tile, lambda s, r, *_: (s + skip, r, 0))
+    own = pl.BlockSpec(tile, lambda s, r, *_: (s, r, 0))
+    far = pl.BlockSpec(tile, lambda s, r, sequence, chunk: (sequence[s + skip], r, 0))
     total = pl.BlockSpec((pad_rows, width), lambda s, r, *_: (0, 0))
     out_shape = [jax.ShapeDtypeStruct((seqs, length, width), t) for t in outputs]
     out_shape += [jax.ShapeDtypeStruct((pad_rows, width), f32)] * sums
+    scalars = 2 if moves else 0
+    given = scalars + len(arrays) + len(whole)
+
+    def body(*refs):
+        kernel(*refs[:given], *refs[given + len(earlier) :])
+
     return pl.pallas_call(
-        kernel,
+        body,
         grid_spec=pltpu.PrefetchScalarGridSpec(
-            num_scalar_prefetch=2 if moves else 0,
-            grid=(seqs, length // block),
+            num_scalar_prefetch=scalars,
+            grid=(count, length // block),
             in_specs=[
-                far if moves and (not back or i in moved) else near for i in range(len(arrays))
+                own
+                if a.shape[0] != seqs
+                else far
+                if moves and (not back or i in moved)
+                else near
+                for i, a in enumerate(arrays)
             ]
-            + [pl.BlockSpec(w.shape, lambda s, r, *_: (0, 0)) for w in whole],
+            + [pl.BlockSpec(w.shape, lambda s, r, *_: (0, 0)) for w in whole]
+            + [pl.BlockSpec(memory_space=pl.ANY)] * len(earlier),
             out_specs=[far if moves and back else near] * len(outputs) + [total] * sums,
         ),
         out_shape=out_shape,
+        input_output_aliases={given + i: i for i in range(len(earlier))},
         compiler_params=pltpu.CompilerParams(vmem_limit_bytes=vmem_bytes),
         cost_estimate=pl.CostEstimate(
-            flops=8 * seqs * length * width,
-            bytes_accessed=moved_bytes(*arrays, *out_shape),
+            flops=8 * count * length * width,
+            bytes_accessed=moved_bytes(*arrays, *out_shape) * count // seqs,
             transcendentals=0,
         ),
-    )(*(order if moves else ()), *arrays, *whole)
+    )(*(order if moves else ()), *arrays, *whole, *earlier)
+
+
+def in_halves(kernel, arrays, summed, whole, outputs, sums, order=None, back=False):
+    ready = by_rows(
+        kernel, [arrays[0], summed[0], *arrays[1:]], whole, outputs, sums, order, back, (), 0
+    )
+    count = len(outputs)
+    done = by_rows(
+        kernel,
+        [arrays[0], summed[1], *arrays[1:]],
+        whole,
+        outputs,
+        sums,
+        order,
+        back,
+        (),
+        1,
+        tuple(ready[:count]),
+    )
+    return [*done[:count], *(a + b for a, b in zip(ready[count:], done[count:]))]
 
 
 def enter_kernel(sequence, chunk, *refs):
@@ -553,6 +607,7 @@
     def sl(a, k):
         return a[:, k * part : (k + 1) * part]
 
+    move = (sequence, chunk)
     w_in = jnp.transpose(in_weight, (1, 2, 0))
     half_lanes = lanes // 2
     own_gain = jnp.pad(jnp.stack([norm1_gain, norm2_gain]), ((0, 14), (0, 0)))
@@ -567,12 +622,12 @@
     ring.issue()
 
     tokens, cotangent = ring.land((tokens, cotangent))
-    move = (sequence, chunk)
     if tiled:
         x, cot = by_rows(enter_kernel, [tokens, cotangent], [], [bf16, bf16], 0, move)
     else:
         x, cot = own_order(tokens, move), own_order(cotangent, move)
     full = x.shape
+    part_full = (seqs // 2, piece, width)
     x, cot = ring.land((x, cot))
     grad_low = cot.reshape(rows, width)
     start = x.reshape(rows, width).astype(f32)
@@ -597,14 +652,14 @@
     before = lax.ppermute(
         inner[:, piece - taps + 1 :], "seq", [(i, i + 1) for i in range(n - 1)]
     ).astype(f32)
-    before = jnp.pad(before, ((0, 0), (pad_rows - taps + 1, 0), (0, 0)))
+    before = ring.land(jnp.pad(before, ((0, 0), (pad_rows - taps + 1, 0), (0, 0))))
     conv_w = conv_weight.astype(f32)
     rate = decay_rate.astype(f32)[None]
     gate_m = dense_heads(gate_matrix)
     wide = (seqs, piece, lanes)
     edge = (seqs, pad_rows, lanes)
     gate_flops = 4 * rows * lanes * lanes
-    mixed, recur, admit, decay, cum, local, ends = per_sequence(
+    mixed, recur, admit, decay, root, cum, local, ends = per_sequence(
         forward_kernel,
         seqs,
         [
@@ -616,17 +671,13 @@
             (gate_bias.astype(f32), "whole"),
             (rate, "whole"),
         ],
-        [(wide, f32, "seq")] * 6 + [(edge, f32, "seq")],
+        [(wide, f32, "seq")] * 7 + [(edge, f32, "seq")],
         [pltpu.VMEM((piece + pad_rows, lanes), f32), pltpu.VMEM((2, piece, lanes), f32)],
         gate_flops,
     )
-    ends = ring.land(ends)
-    entry = ring.land(carried(ends, 1, n, ring.land))
-    product = (
-        ((local + cum * entry[:, :1]) * jax.nn.gelu(gate_in.astype(f32)))
-        .astype(bf16)
-        .reshape(rows, lanes)
-    )
+    entry = ring.land(carried(ring.land(ends), 1, n, ring.land))
+    states = local + cum * entry[:, :1]
+    product = (states * gelu_parts(gate_in.astype(f32))[0]).astype(bf16).reshape(rows, lanes)
     w_out = jnp.concatenate(
         [
             jnp.concatenate([p[lanes : lanes + half_lanes] for p in pieces], axis=1)
@@ -639,149 +690,149 @@
     def half_of(a, h):
         return a[h * block : (h + 1) * block]
 
-    def wait_land(values, count):
+    def lands(values, count):
         for _ in range(count):
             ring.land()
-        return ring.land(values)
-
-    recurrent, _ = tp_sum(
+        return ring.resume(values)
+
+    chips = []
+
+    def keep(chip):
+        chips.append(ring.land(chip))
+        return chips[0]
+
+    recurrent = tp_sum(
         lambda h: dot(half_of(product, h), w_out),
-        chips=ring.land,
-        totals=lambda v: wait_land(v, 3),
-    )
-
-    middle, normed2 = by_rows(norm_kernel, [x, recurrent.reshape(full)], [gain2], [f32, bf16], 0)
+        chips=keep,
+        totals=lambda v: lands(v, 3),
+    )
+    gate_act, gate_slope = gelu_parts(after(gate_in, chips[0]).astype(f32))
+
+    middle, normed2 = in_halves(
+        norm_kernel, [x], [r.reshape(part_full) for r in recurrent], [gain2], [f32, bf16], 0
+    )
     normed2 = ring.land(normed2.reshape(rows, width))
-    w_mlp = jnp.concatenate(
-        [jnp.concatenate(w.slots(), axis=0) for w in mlp], axis=1
-    )
+    w_mlp = jnp.concatenate([jnp.concatenate(w.slots(), axis=0) for w in mlp], axis=1)
     both = dot(normed2, w_mlp).astype(bf16)
     both0, both1 = both[:, :units].astype(f32), both[:, units:].astype(f32)
-    hidden = (gelu_parts(both0)[0] * both1).astype(bf16)
-    hidden, both = ring.land((hidden, both))
+    act, slope = gelu_parts(both0)
+    hidden = (act * both1).astype(bf16)
+    hidden, act, slope = ring.land((hidden, act.astype(bf16), (slope * both1).astype(bf16)))
     ring.drain()
     w_down = jnp.concatenate(downs.slots(), axis=1)
+    ring.token = None
+    grad_both = []
     grad_down = Scatter(lambda k: down(hidden, sl(grad_low, k)), 1, n, chunk)
-    grad_both = []
     grad_mlp = [
         Scatter(lambda k: down(sl(normed2, k), grad_both[0][:, :units]), -1, n, chunk),
         Scatter(lambda k: down(sl(normed2, k), grad_both[0][:, units:]), 1, n, chunk),
     ]
     ring.add([grad_down, *grad_mlp])
     ring.issue(1)
-    both, w_down = ring.hold((both, w_down))
-    both0, both1 = both[:, :units].astype(f32), both[:, units:].astype(f32)
-    act, slope = gelu_parts(both0)
-    grad_hidden = across(grad_low, w_down)
+    act, slope, w_down = ring.hold((act, slope, w_down))
     grad_both.append(
-        jnp.concatenate(
-            [(grad_hidden * both1 * slope).astype(bf16), (grad_hidden * act).astype(bf16)],
-            axis=1,
-        )
-    )
-    grad_both[0] = ring.land(grad_both[0])
-    grad_normed2, total2 = tp_sum(
+        pl.pallas_call(
+            hidden_back_kernel,
+            grid=(seqs,),
+            in_specs=[
+                pl.BlockSpec((piece, width), lambda s: (s, 0)),
+                pl.BlockSpec((units, width), lambda s: (0, 0)),
+                pl.BlockSpec((piece, units), lambda s: (s, 0)),
+                pl.BlockSpec((piece, units), lambda s: (s, 0)),
+            ],
+            out_specs=pl.BlockSpec((piece, 2 * units), lambda s: (s, 0)),
+            out_shape=jax.ShapeDtypeStruct((rows, 2 * units), bf16),
+            compiler_params=pltpu.CompilerParams(vmem_limit_bytes=vmem_bytes),
+            cost_estimate=pl.CostEstimate(
+                flops=2 * rows * width * units,
+                bytes_accessed=moved_bytes(grad_low, w_down, act, slope, both),
+                transcendentals=0,
+            ),
+        )(grad_low, w_down, act, slope)
+    )
+    ring.issue()
+    grad_normed2 = tp_sum(
         lambda h: across(half_of(grad_both[0], h), w_mlp),
         others=ring.land,
         chips=ring.land,
-        totals=lambda v: wait_land(v, 2),
+        totals=lambda v: lands(v, 3),
     )
     turned = jnp.concatenate([half_of(hidden, 1), half_of(hidden, 0)], axis=0)
     turned = jnp.where(odd == 1, turned, hidden)
-    mlp_out = lax.psum(dot(after(turned, total2), w_down).astype(bf16), "tp")
-
-    grad_middle, grad_rec, sum_gain2 = by_rows(
+    mlp_out = lax.psum(dot(after(turned, grad_normed2[0]), w_down).astype(bf16), "tp")
+
+    grad_middle, grad_rec, sum_gain2 = in_halves(
         middle_back_kernel,
-        [middle, grad_normed2.reshape(full), cot],
+        [middle, cot],
+        [g.reshape(part_full) for g in grad_normed2],
         [gain2],
         [f32, bf16],
         1,
     )
-    grad_rec = grad_rec.reshape(rows, width)
-
-    grad_rec = ring.land(grad_rec)
+    grad_rec = ring.land(grad_rec.reshape(rows, width))
+
     grad_product = across(grad_rec, w_out).reshape(wide)
-    tail, local_grad, first = per_sequence(
+    tail, local_grad, early = per_sequence(
         reverse_kernel,
         seqs,
-        [(grad_product, "seq"), (gate_in, "seq"), (decay, "seq")],
+        [(grad_product, "seq"), (gate_act, "seq"), (decay, "seq")],
         [(wide, f32, "seq")] * 2 + [(edge, f32, "seq")],
         [pltpu.VMEM((piece, lanes), f32)],
         rows * lanes * 50,
     )
-    incoming = carried(ring.land(first), -1, n, ring.land)
-    grad_gates, grad_mixed, grad_gate_in, sums = per_sequence(
+    incoming = ring.land(carried(ring.land(early), -1, n, ring.land))
+    grad_gates, grad_inner, grad_gate_in, head, last, sums = per_sequence(
         gates_back_kernel,
         seqs,
         [
             (grad_product, "seq"),
-            (gate_in, "seq"),
+            (gate_slope, "seq"),
             (tail, "seq"),
             (local_grad, "seq"),
             (incoming, "seq"),
-            (cum, "seq"),
-            (local, "seq"),
+            (states, "seq"),
             (entry, "seq"),
             (recur, "seq"),
             (admit, "seq"),
             (decay, "seq"),
+            (root, "seq"),
             (mixed, "seq"),
+            (inner, "seq"),
+            (before, "seq"),
             (gate_m, "whole"),
             (rate, "whole"),
+            (conv_w, "whole"),
         ],
         [
             ((2,) + wide, bf16, "pair"),
             (wide, bf16, "seq"),
             (wide, bf16, "seq"),
+            (edge, f32, "seq"),
+            (edge, f32, "seq"),
             ((pad_rows, lanes), f32, "whole"),
         ],
-        [pltpu.VMEM((piece + pad_rows, lanes), f32), pltpu.VMEM((piece, lanes), f32)],
+        [pltpu.VMEM((piece, lanes), f32)] + [pltpu.VMEM((piece + pad_rows, lanes), f32)] * 2,
         gate_flops,
     )
-    grad_mixed = ring.land(grad_mixed)
+    head = ring.land(head)
     behind = lax.ppermute(
-        grad_mixed[:, : taps - 1], "seq", [(i + 1, i) for i in range(n - 1)]
+        head[:, : taps - 1].astype(bf16), "seq", [(i + 1, i) for i in range(n - 1)]
     ).astype(f32)
-    behind = jnp.pad(behind, ((0, 0), (0, pad_rows - taps + 1), (0, 0)))
-    behind = ring.land(behind)
-    grad_inner, conv_sums = per_sequence(
-        conv_back_kernel,
-        seqs,
-        [
-            (grad_mixed, "seq"),
-            (behind, "seq"),
-            (inner, "seq"),
-            (before, "seq"),
-            (conv_w, "whole"),
-        ],
-        [(wide, bf16, "seq"), ((pad_rows, lanes), f32, "whole")],
-        [pltpu.VMEM((piece + pad_rows, lanes), f32)] * 2,
-        rows * lanes * 16,
+    beyond = jnp.concatenate([jnp.zeros_like(last), behind], axis=1)
+    beyond = jnp.pad(beyond, ((0, 0), (0, 1), (0, 0)))
+    for lag in range(1, taps):
+        last = last + conv_w[lag] * beyond[:, lag : lag + pad_rows]
+    grad_inner = lax.dynamic_update_slice(
+        grad_inner, last.astype(bf16), (0, piece - pad_rows, 0)
     )
     back0 = grad_inner.reshape(rows, lanes)
     back1 = grad_gate_in.reshape(rows, lanes)
-    back = jnp.concatenate([back0, back1], axis=1)
-    w_both = jnp.concatenate(
-        [jnp.concatenate(in0, axis=1), jnp.concatenate(in1, axis=1)], axis=0
-    )
-    ring.drain()
+    back = ring.land(jnp.concatenate([back0, back1], axis=1))
+    w_both = jnp.concatenate([jnp.concatenate(in0, axis=1), jnp.concatenate(in1, axis=1)], axis=0)
     grads = [
-        Scatter(
-            lambda k: jnp.concatenate(
-                [down(back0, normed1[k]), down(product[:, :half_lanes], sl(grad_rec, k))], axis=0
-            ),
-            1,
-            n,
-            chunk,
-        ),
-        Scatter(
-            lambda k: jnp.concatenate(
-                [down(back1, normed1[k]), down(product[:, half_lanes:], sl(grad_rec, k))], axis=0
-            ),
-            -1,
-            n,
-            chunk,
-        ),
+        Scatter(lambda k: down(back0, normed1[k]), 1, n, chunk),
+        Scatter(lambda k: down(back1, normed1[k]), -1, n, chunk),
+        Scatter(lambda k: down(product, sl(grad_rec, k)), -1, n, chunk),
     ]
     ring.add(grads)
     ring.issue()
@@ -789,12 +840,12 @@
 
     def hold_output(chip):
         late.append(after(mlp_out, chip))
-        return chip
-
-    grad_normed1, total1 = tp_sum(
+        return ring.land(chip)
+
+    grad_normed1 = tp_sum(
         lambda h: dot(half_of(back, h), w_both),
         chips=hold_output,
-        totals=lambda v: wait_land(v, 2),
+        totals=lambda v: lands(v, 4),
     )
     mlp_out = late[0]
     ring.drain()
@@ -806,9 +857,11 @@
         for h in range(heads):
             at = slice(h * head_width, (h + 1) * head_width)
             grad_matrix.append(dense[at, at])
-    small = jnp.concatenate([sums[:4], conv_sums[:taps]], axis=0).astype(bf16)
-    packed = jnp.concatenate(grad_matrix + [small.reshape(-1, head_width)], axis=0)
+    packed = jnp.concatenate(
+        grad_matrix + [sums.astype(bf16).reshape(-1, head_width)], axis=0
+    )
     packed = lax.psum(packed, "seq")
+
     if tiled:
         output = by_rows(
             output_kernel,
@@ -820,10 +873,10 @@
             back=True,
             moved=(1,),
         )[0]
-        grad_normed1, output = after((grad_normed1, output), output)
-        grad_tokens = by_rows(
+        grad_tokens = in_halves(
             start_back_kernel,
-            [x, grad_normed1.reshape(full), grad_middle],
+            [x, grad_middle],
+            [g.reshape(part_full) for g in grad_normed1],
             [gain1],
             [f32],
             0,
@@ -833,11 +886,13 @@
     else:
         mlp_out = mlp_out.reshape(full)[sequence].astype(f32)
         output = own_order((middle + mlp_out).astype(bf16), move, True)
-        grad_start = norm_back(x.astype(f32), grad_normed1.reshape(full).astype(f32), gain1)[0]
+        grad_normed1_all = jnp.concatenate(grad_normed1, axis=0).reshape(full).astype(f32)
+        grad_start = norm_back(x.astype(f32), grad_normed1_all, gain1)[0]
         grad_tokens = own_order(grad_middle + grad_start, move, True)
     mine = lax.axis_index("seq")
     slots = (me - jnp.asarray(place, jnp.int32)) % n
-    sum_gain1 = jnp.sum(total1.astype(f32) * (start[:block] * inverse1[:block]), axis=0)
+    scaled1 = start[:block] * inverse1[:block]
+    sum_gain1 = jnp.sum(grad_normed1[0].astype(f32) * scaled1, axis=0)
     grad_gains = jnp.stack([sum_gain1, 0.5 * jnp.sum(sum_gain2, axis=0)])
     grad_gains = grad_gains + core_swap(grad_gains)
     grad_gains = seq_sum(grad_gains.reshape(2, n, part)[:, slots], n)
@@ -852,13 +907,13 @@
         output,
         grad_tokens,
         grad_gains[0],
-        jnp.transpose(jnp.stack([g[:lanes] for g in grads]), (2, 0, 1)),
+        jnp.transpose(jnp.stack(grads[:2]), (2, 0, 1)),
         small[4:],
         small[3],
         grad_matrix,
         small[1:3],
         small[0],
-        jnp.concatenate([g[lanes:] for g in grads], axis=0),
+        grads[2],
         grad_gains[1],
         jnp.stack([g.total() for g in grad_mlp], axis=1),
         grad_down.total(),

time: 874 us -> 818 us (0.936)
  other arithmetic: 68.3 us -> 39.3 us
  matrix products: 224 us -> 203 us
  waiting for transfers between devices: 226 us -> 205 us
  Pallas kernels: 103 us -> 112 us
    concatenate x10 -> x2, other arithmetic: 22.5 us -> 0.88 us  [the longest x1 0.86 us: shards(): back = ring.land(jnp.concatenate([back0, back1], axis=1))]
    ppermute x3, waiting for transfers between devices: 31.1 us -> 12.6 us  [chip_swap(): return lax.ppermute(values, 'tp', [(i, i ^ 2) for i in range(size)])]
    pallas_call x5 -> x9, Pallas kernels: 52.7 us -> 68.8 us  [the longest x8 56.4 us: by_rows(): pl.pallas_call(body, grid_spec=pltpu.PrefetchScalarGridSpec(num_scalar_pr...]
    ppermute x3, waiting for transfers between devices: 15.6 us -> 0.33 us  [seq_sum(): lax.ppermute(values, 'seq', [(i, i ^ by) for i in range(n)])]
    dot_general x20 -> x19, matrix products: 63.1 us -> 48.6 us  [across(): lax.dot_general(a, b, (((1,), (1,)), ((), ())), preferred_element_type=f32)]
    ppermute x1, waiting for transfers between devices: 0.01 us -> 12.2 us  [shards(): lax.ppermute(inner[:, piece - taps + 1:], 'seq', [(i, i + 1) for i in ran...]
    convert_element_type x12 -> x3, other arithmetic: 22 us -> 12.3 us  [the longest x1 6.4 us: shards(): (slope * both1).astype(bf16)]
    ppermute x8, waiting for transfers between devices: 21.4 us -> 30.3 us  [shifted(): return lax.ppermute(values, 'seq', pairs)]
  transfers between devices with their start and end apart: 95 -> 102, of which waited for: 27 -> 26; matrix products, arithmetic and copies ran while one was open for 41% -> 38% of each run, Pallas kernels for 10% -> 13%
where the time goes in v3:
time: 818 us; the launch traced here: 808 us
  waiting for transfers between devices  205 us (25%)
  matrix products  203 us (25%)
  starting transfers between devices  127 us (16%)
  Pallas kernels  112 us (14%)
  local copies, waits for them, and re-layouts  106 us (13%)
  other arithmetic  39.3 us (5%)
  between operations  16.7 us (2%)
    ppermute x77, waiting for transfers between devices, issue(): flying.append((flow, lax.ppermute(message, 'seq', self.pairs[way])))  150 us
    dot_general x50, matrix products, down(): lax.dot_general(a, b, (((0,), (0,)), ((), ())), preferred_element_type=f32)  109 us
    ppermute x77, starting transfers between devices, issue(): flying.append((flow, lax.ppermute(message, 'seq', self.pairs[way])))  91.2 us
    unnamed x352, local copies, waits for them, and re-layouts  67 us
    pallas_call x8, Pallas kernels, by_rows(): pl.pallas_call(body, grid_spec=pltpu.PrefetchScalarGridSpec(num_scalar_pr...  56.4 us
    dot_general x19, matrix products, across(): lax.dot_general(a, b, (((1,), (1,)), ((), ())), preferred_element_type=f32)  48.6 us
    dot_general x6, matrix products, dot(): return jnp.dot(a, b, preferred_element_type=f32)  44.9 us
    pallas_call x3, Pallas kernels, per_sequence(): pl.pallas_call(kernel, grid=(seqs,), in_specs=[spec(a.shape, kind) for a,...  42.7 us
  transfers between devices with their start and end apart: 102, of which 26 were waited for; matrix products, arithmetic and copies ran while one was open for 38% of the time, Pallas kernels for 13%

profile of v3, /device:TPU:0, one launch (start us, length us, event | category | flops | bytes accessed | tf_op | source)
XLA Modules:
  0.0 808.4 jit_solution(2958305468122332540)
XLA Ops:
  31.1 3.4 constant_dynamic-update-slice_fusion.25
  36.7 8.5 %shard_map.255 = (bf16[4,256,2048]{2,1,0:T(8,128)(2,1)S(1)}, bf16[4,256,2048]{2,1,0:T(8,128)(2,1)}) custom-call(s32[4]{0:T(128)S(1)} %and_select_fusion.2.refs_0_, s32[8]{0:T(128)S(1)} %gather_fusion, bf16[4,256,2048]{2,1,0:T(8,128)(2,1)} %refs_2_, bf16[4,256,2048]{2,1,0:T(8,128)(2,1)} %refs_3_), custom_call_target="tpu_custom_call" | custom-call | flops 16777216 | bytes 16777216 | tf_op jit(solution)/shard_map/pallas_call | solution.py:410
  67.5 8.2 %collective-permute-done.7 = bf16[1056,256]{1,0:T(8,128)(2,1)S(1)} collective-permute-done((bf16[1056,256]{1,0:T(8,128)(2,1)}, bf16[1056,256]{1,0:T(8,128)(2,1)S(1)}, u32[]{:S(2)}, u32[]{:S(2)}) %collective-permute-start.7) | collective-permute-done | bytes 540704 | tf_op jit(solution)/shard_map/ppermute | solution.py:72
  77.8 8.8 %collective-permute-done.9 = bf16[1072,256]{1,0:T(8,128)(2,1)S(1)} collective-permute-done((bf16[1072,256]{1,0:T(8,128)(2,1)S(1)}, bf16[1072,256]{1,0:T(8,128)(2,1)S(1)}, u32[]{:S(2)}, u32[]{:S(2)}) %collective-permute-start.9) | collective-permute-done | bytes 548896 | tf_op jit(solution)/shard_map/ppermute | solution.py:72
  91.0 8.1 collective-permute-done.13
  114.0 3.4 add_convert_fusion.6
  122.1 3.3 add_convert_fusion.7
  132.4 3.5 collective-permute-start.16
  136.6 12.2 %collective-permute-done.16 = bf16[4,3,704]{2,1,0:T(4,128)(2,1)S(1)} collective-permute-done((bf16[4,3,704]{2,1,0:T(4,128)(2,1)S(1)}, bf16[4,3,704]{2,1,0:T(4,128)(2,1)S(1)}, u32[]{:S(2)}, u32[]{:S(2)}) %collective-permute-start.16) | collective-permute-done | bytes 16928 | tf_op jit(solution)/shard_map/ppermute | solution.py:652
  148.9 3.3 collective-permute-start.22
  154.3 16.0 %shard_map.256 = (f32[4,256,704]{2,1,0:T(8,128)}, f32[4,256,704]{2,1,0:T(8,128)}, f32[4,256,704]{2,1,0:T(8,128)}, f32[4,256,704]{2,1,0:T(8,128)}, f32[4,256,704]...) custom-call(bf16[4,256,704]{2,1,0:T(8,128)(2,1)S(1)} %bitcast.190, ...), custom_call_target="tpu_custom_call" | custom-call | flops 2030043136 | bytes 23812096 | tf_op jit(solution)/shard_map/pallas_call | solution.py:373
  170.4 3.2 collective-permute-start.21
  176.0 5.3 collective-permute-start.24
  181.4 7.6 collective-permute-done.24
  189.0 5.3 collective-permute-start.25
  194.4 5.0 collective-permute-start.26
  203.5 5.9 fusion.30
  211.3 3.6 convolution_convert_fusion.2
  229.7 3.4 add_convert_fusion.5
  233.1 10.0 %collective-permute-done.30 = bf16[256,1536]{1,0:T(8,128)(2,1)S(1)} collective-permute-done((bf16[256,1536]{1,0:T(8,128)(2,1)}, bf16[256,1536]{1,0:T(8,128)(2,1)S(1)}, u32[]{:S(2)}, u32[]{:S(2)}) %collective-permute-start.30) | collective-permute-done | bytes 786464 | tf_op jit(solution)/shard_map/ppermute | solution.py:72
  247.2 12.0 %collective-permute-done.40 = bf16[256,1536]{1,0:T(8,128)(2,1)S(1)} collective-permute-done((bf16[256,1536]{1,0:T(8,128)(2,1)S(1)}, bf16[256,1536]{1,0:T(8,128)(2,1)S(1)}, u32[]{:S(2)}, u32[]{:S(2)}) %collective-permute-start.40) | collective-permute-done | bytes 786464 | tf_op jit(solution)/shard_map/ppermute | solution.py:72
  265.0 14.6 %collective-permute-done.41 = bf16[256,1536]{1,0:T(8,128)(2,1)S(1)} collective-permute-done((bf16[256,1536]{1,0:T(8,128)(2,1)S(1)}, bf16[256,1536]{1,0:T(8,128)(2,1)S(1)}, u32[]{:S(2)}, u32[]{:S(2)}) %collective-permute-start.41) | collective-permute-done | bytes 786464 | tf_op jit(solution)/shard_map/ppermute | solution.py:72
  284.8 5.6 collective-permute-done.32
  291.5 4.7 fusion.19
  296.1 5.6 collective-permute-done.34
  303.7 14.8 %collective-permute-done.39 = bf16[256,1536]{1,0:T(8,128)(2,1)S(1)} collective-permute-done((bf16[256,1536]{1,0:T(8,128)(2,1)S(1)}, bf16[256,1536]{1,0:T(8,128)(2,1)S(1)}, u32[]{:S(2)}, u32[]{:S(2)}) %collective-permute-start.39) | collective-permute-done | bytes 786464 | tf_op jit(solution)/shard_map/ppermute | solution.py:72
  324.1 5.1 shard_map.257
  329.1 5.0 shard_map.258
  337.1 17.5 %convolution_convert_fusion = bf16[1024,3072]{1,0:T(8,128)(2,1)S(1)} fusion(bf16[1024,2048]{1,0:T(8,128)(2,1)} %bitcast.226, bf16[2048,1536]{1,0:T(8,128)(2,1)} %copy-done.105, bf16[2048,1536]{1,0:T(8,128)(2,1)} %copy-done.104), kind=kOutput, calls=%fused_computation.40 | convolution fusion | flops 12913213440 | bytes 23068672 | tf_op jit(solution)/shard_map/dot_general | solution.py:571
  354.6 6.4 fusion.6
  377.1 12.3 %shard_map.259 = bf16[1024,3072]{1,0:T(8,128)(2,1)} custom-call(bf16[1024,2048]{1,0:T(8,128)(2,1)} %bitcast.215, bf16[1536,2048]{1,0:T(8,128)(2,1)} %constant_dynamic-update-slice_fusion.26.w_down, bf16[1024,1536]{1,0:T(8,128)(2,1)S(1)} %get-tuple-element.288.act, bf16[1024,1536]{1,0:T(8,128)(2,1)} %get-tuple-element.289.slope), custom_call_target="tpu_custom_call" | custom-call | flops 6442450944 | bytes 23068672 | tf_op jit(solution)/shard_map/pallas_call | solution.py:734
  389.4 11.8 %fusion.40 = bf16[512,2048]{1,0:T(8,128)(2,1)} fusion(bf16[2048,1536]{1,0:T(8,128)(2,1)} %copy-done.105, bf16[2048,1536]{1,0:T(8,128)(2,1)} %copy-done.104, bf16[1024,3072]{1,0:T(8,128)(2,1)} %shard_map.259), kind=kOutput, calls=%fused_computation.85 | convolution fusion | flops 6468665344 | bytes 17825792 | tf_op jit(solution)/shard_map/dot_general | solution.py:563
  401.2 3.9 convolution_convert_fusion.6
  405.2 3.8 convolution_convert_fusion.5
  423.1 26.2 %collective-permute-done.50 = bf16[256,1536]{1,0:T(8,128)(2,1)S(1)} collective-permute-done((bf16[256,1536]{1,0:T(8,128)(2,1)S(1)}, bf16[256,1536]{1,0:T(8,128)(2,1)S(1)}, u32[]{:S(2)}, u32[]{:S(2)}) %collective-permute-start.50) | collective-permute-done | bytes 786464 | tf_op jit(solution)/shard_map/ppermute | solution.py:72
  451.2 12.0 %add_convert_fusion.3 = bf16[512,2048]{1,0:T(8,128)(2,1)} fusion(bf16[512,2048]{1,0:T(8,128)(2,1)} %collective-permute-done.45, bf16[2048,1536]{1,0:T(8,128)(2,1)} %copy-done.105, bf16[2048,1536]{1,0:T(8,128)(2,1)} %copy-done.104, bf16[1024,3072]{1,0:T(8,128)(2,1)} %shard_map.259), kind=kOutput, calls=%fused_computation.56 | convolution fusion | flops 6470762496 | bytes 19922944 | tf_op jit(solution)/shard_map/dot_general | solution.py:563
  464.8 4.0 fusion.52
  470.8 3.1 fusion.55
  479.0 10.3 %collective-permute-done.51 = bf16[1536,256]{1,0:T(8,128)(2,1)S(1)} collective-permute-done((bf16[1536,256]{1,0:T(8,128)(2,1)S(1)}, bf16[1536,256]{1,0:T(8,128)(2,1)S(1)}, u32[]{:S(2)}, u32[]{:S(2)}) %collective-permute-start.51) | collective-permute-done | bytes 786464 | tf_op jit(solution)/shard_map/ppermute | solution.py:72
  493.3 12.8 %collective-permute-done.56 = bf16[256,1536]{1,0:T(8,128)(2,1)S(1)} collective-permute-done((bf16[256,1536]{1,0:T(8,128)(2,1)S(1)}, bf16[256,1536]{1,0:T(8,128)(2,1)S(1)}, u32[]{:S(2)}, u32[]{:S(2)}) %collective-permute-start.56) | collective-permute-done | bytes 786464 | tf_op jit(solution)/shard_map/ppermute | solution.py:72
  516.4 8.2 %convolution_convert_fusion.1 = bf16[1024,2048]{1,0:T(8,128)(2,1)} fusion(bf16[1024,1536]{1,0:T(8,128)(2,1)S(1)} %copy-done.66, bf16[1536,2048]{1,0:T(8,128)(2,1)S(1)} %bitcast.278), kind=kOutput, calls=%fused_computation.59 | convolution fusion | flops 6444548096 | bytes 13631488 | tf_op jit(solution)/shard_map/dot_general | solution.py:571
  524.7 7.6 shard_map.260
  532.2 7.9 shard_map.261
  540.2 7.9 fusion.92
  548.0 7.9 shard_map.262
  558.2 3.2 fusion.60
  563.8 3.2 fusion.61
  567.7 3.4 fusion.62
  578.5 3.8 collective-permute-done.61
  582.3 5.6 collective-permute-done.62
  591.9 12.1 %collective-permute-done.63 = f32[4,2,704]{2,1,0:T(2,128)S(1)} collective-permute-done((f32[4,2,704]{2,1,0:T(2,128)S(1)}, f32[4,2,704]{2,1,0:T(2,128)S(1)}, u32[]{:S(2)}, u32[]{:S(2)}) %collective-permute-start.63) | collective-permute-done | bytes 22560 | tf_op jit(solution)/shard_map/ppermute | solution.py:528
  608.7 7.4 collective-permute-done.64
  621.3 18.8 %shard_map.263 = (bf16[2,4,256,704]{3,2,1,0:T(8,128)(2,1)}, bf16[4,256,704]{2,1,0:T(8,128)(2,1)S(1)}, bf16[4,256,704]{2,1,0:T(8,128)(2,1)S(1)}, f32[4,8,704]{2,1...) custom-call(f32[4,256,704]{2,1,0:T(8,128)} %bitcast.225, f32[4,256,704]{2,1,0:T(8,128)} %get-tuple-element.462.slope, ...), custom_call_target="tpu_custom_call" | custom-call | flops 2030043136 | bytes 38514432 | tf_op jit(solution)/shard_map/pallas_call | solution.py:373
  654.1 3.3 fusion.46
  662.6 5.5 fusion.39
  668.2 3.6 fusion.49
  679.4 4.1 copy.60
  684.9 6.7 add_convert_fusion.1
  702.6 8.5 %shard_map.264 = bf16[4,256,2048]{2,1,0:T(8,128)(2,1)} custom-call(s32[4]{0:T(128)S(1)} %copy-done.23, s32[8]{0:T(128)S(1)} %copy-done.19, f32[4,256,2048]{2,1,0:T(8,128)} %get-tuple-element.261.refs_0_.refs_2_, bf16[4,256,2048]{2,1,0:T(8,128)(2,1)S(1)} %bitcast.192), custom_call_target="tpu_custom_call" | custom-call | flops 16777216 | bytes 16777216 | tf_op jit(solution)/shard_map/pallas_call | solution.py:410
  732.5 7.0 collective-permute-done.75
  739.5 4.1 fusion.18
  760.3 6.7 shard_map.265.refs_6_
  784.6 3.7 collective-permute-done.88
  793.9 7.2 shard_map.266
  (693 shorter events, 314.7 us)
Async XLA Ops:
  7.2 692.4 %all-reduce.16.cloned.1.call-start = ((), (), s32[]{:S(2)}) async-start(), calls=%async_computation | async-start | bytes 8388608 | tf_op jit(solution)/shard_map/psum | solution.py:762
  11.2 23.3 %collective-permute-start = (bf16[1056,256]{1,0:T(8,128)(2,1)}, bf16[1056,256]{1,0:T(8,128)(2,1)S(1)}, u32[]{:S(2)}, u32[]{:S(2)}) collective-permute-start(bf16[1056,256]{1,0:T(8,128)(2,1)} %pad_maximum_fusion.24), channel_id=1, source_target_pairs={{0,8},{8,16},{16,24},{24,28},{28,20},{20,12},{12,4},{4,0},{1,9},{9... | collective-permute-start | bytes 1622024 | tf_op jit(solution)/shard_map/ppermute | solution.py:72
  15.1 32.0 %collective-permute-start.2 = (bf16[1072,256]{1,0:T(8,128)(2,1)}, bf16[1072,256]{1,0:T(8,128)(2,1)}, u32[]{:S(2)}, u32[]{:S(2)}) collective-permute-start(bf16[1072,256]{1,0:T(8,128)(2,1)} %pad_maximum_fusion.23), channel_id=1, source_target_pairs={{0,8},{8,16},{16,24},{24,28},{28,20},{20,12},{12,4},{4,0},{1,9},{9... | collective-permute-start | bytes 1646600 | tf_op jit(solution)/shard_map/ppermute | solution.py:72
  17.1 30.0 %collective-permute-start.3 = (bf16[1072,256]{1,0:T(8,128)(2,1)}, bf16[1072,256]{1,0:T(8,128)(2,1)}, u32[]{:S(2)}, u32[]{:S(2)}) collective-permute-start(bf16[1072,256]{1,0:T(8,128)(2,1)} %pad_maximum_fusion.23), channel_id=1, source_target_pairs={{0,4},{8,0},{16,8},{24,16},{28,24},{20,28},{12,20},{4,12},{1,5},{9... | collective-permute-start | bytes 1646600 | tf_op jit(solution)/shard_map/ppermute | solution.py:72
  34.6 23.9 %collective-permute-start.10 = (bf16[1056,256]{1,0:T(8,128)(2,1)}, bf16[1056,256]{1,0:T(8,128)(2,1)S(1)}, u32[]{:S(2)}, u32[]{:S(2)}) collective-permute-start(bf16[1056,256]{1,0:T(8,128)(2,1)} %collective-permute-done.1), channel_id=1, source_target_pairs={{0,4},{8,0},{16,8},{24,16},{28,24},{20,28},{12,20},{4,12},{1,5},{9... | collective-permute-start | bytes 1622024 | tf_op jit(solution)/shard_map/ppermute | solution.py:72
  36.5 23.8 %collective-permute-start.5 = (bf16[1056,256]{1,0:T(8,128)(2,1)S(1)}, bf16[1056,256]{1,0:T(8,128)(2,1)}, u32[]{:S(2)}, u32[]{:S(2)}) collective-permute-start(bf16[1056,256]{1,0:T(8,128)(2,1)S(1)} %collective-permute-done), channel_id=1, source_target_pairs={{0,8},{8,16},{16,24},{24,28},{28,20},{20,12},{12,4},{4,0},{1,9},{9... | collective-permute-start | bytes 1622024 | tf_op jit(solution)/shard_map/ppermute | solution.py:72
  63.9 23.6 %collective-permute-start.6 = (bf16[1072,256]{1,0:T(8,128)(2,1)S(1)}, bf16[1072,256]{1,0:T(8,128)(2,1)S(1)}, u32[]{:S(2)}, u32[]{:S(2)}) collective-permute-start(bf16[1072,256]{1,0:T(8,128)(2,1)S(1)} %collective-permute-done.4), channel_id=1, source_target_pairs={{0,8},{8,16},{16,24},{24,28},{28,20},{20,12},{12,4},{4,0},{1,9},{9... | collective-permute-start | bytes 1646600 | tf_op jit(solution)/shard_map/ppermute | solution.py:72
  65.9 20.7 %collective-permute-start.9 = (bf16[1072,256]{1,0:T(8,128)(2,1)S(1)}, bf16[1072,256]{1,0:T(8,128)(2,1)S(1)}, u32[]{:S(2)}, u32[]{:S(2)}) collective-permute-start(bf16[1072,256]{1,0:T(8,128)(2,1)S(1)} %collective-permute-done.8), channel_id=1, source_target_pairs={{0,4},{8,0},{16,8},{24,16},{28,24},{20,28},{12,20},{4,12},{1,5},{9... | collective-permute-start | bytes 1646600 | tf_op jit(solution)/shard_map/ppermute | solution.py:72
  75.7 23.3 %collective-permute-start.13 = (bf16[1056,256]{1,0:T(8,128)(2,1)S(1)}, bf16[1056,256]{1,0:T(8,128)(2,1)S(1)}, u32[]{:S(2)}, u32[]{:S(2)}) collective-permute-start(bf16[1056,256]{1,0:T(8,128)(2,1)S(1)} %collective-permute-done.7), channel_id=1, source_target_pairs={{0,8},{8,16},{16,24},{24,28},{28,20},{20,12},{12,4},{4,0},{1,9},{9... | collective-permute-start | bytes 1622024 | tf_op jit(solution)/shard_map/ppermute | solution.py:72
  87.5 37.9 %collective-permute-start.14 = (bf16[256,1536]{1,0:T(8,128)(2,1)}, bf16[256,1536]{1,0:T(8,128)(2,1)}, u32[]{:S(2)}, u32[]{:S(2)}) collective-permute-start(bf16[256,1536]{1,0:T(8,128)(2,1)} %get-tuple-element.231), channel_id=1, source_target_pairs={{0,8},{8,16},{16,24},{24,28},{28,20},{20,12},{12,4},{4,0},{1,9},{9... | collective-permute-start | bytes 2359304 | tf_op jit(solution)/shard_map/ppermute | solution.py:72
  88.7 36.7 %collective-permute-start.15 = (bf16[256,1536]{1,0:T(8,128)(2,1)}, bf16[256,1536]{1,0:T(8,128)(2,1)}, u32[]{:S(2)}, u32[]{:S(2)}) collective-permute-start(bf16[256,1536]{1,0:T(8,128)(2,1)} %get-tuple-element.231), channel_id=1, source_target_pairs={{0,4},{8,0},{16,8},{24,16},{28,24},{20,28},{12,20},{4,12},{1,5},{9... | collective-permute-start | bytes 2359304 | tf_op jit(solution)/shard_map/ppermute | solution.py:72
  99.1 49.8 %collective-permute-start.17 = (bf16[256,1536]{1,0:T(8,128)(2,1)}, bf16[256,1536]{1,0:T(8,128)(2,1)}, u32[]{:S(2)}, u32[]{:S(2)}) collective-permute-start(bf16[256,1536]{1,0:T(8,128)(2,1)} %get-tuple-element.234), channel_id=1, source_target_pairs={{0,8},{8,16},{16,24},{24,28},{28,20},{20,12},{12,4},{4,0},{1,9},{9... | collective-permute-start | bytes 2359304 | tf_op jit(solution)/shard_map/ppermute | solution.py:72
  109.0 39.9 %collective-permute-start.18 = (bf16[256,1536]{1,0:T(8,128)(2,1)}, bf16[256,1536]{1,0:T(8,128)(2,1)}, u32[]{:S(2)}, u32[]{:S(2)}) collective-permute-start(bf16[256,1536]{1,0:T(8,128)(2,1)} %get-tuple-element.234), channel_id=1, source_target_pairs={{0,4},{8,0},{16,8},{24,16},{28,24},{20,28},{12,20},{4,12},{1,5},{9... | collective-permute-start | bytes 2359304 | tf_op jit(solution)/shard_map/ppermute | solution.py:72
  125.4 45.0 %collective-permute-start.19 = (bf16[256,1536]{1,0:T(8,128)(2,1)}, bf16[256,1536]{1,0:T(8,128)(2,1)}, u32[]{:S(2)}, u32[]{:S(2)}) collective-permute-start(bf16[256,1536]{1,0:T(8,128)(2,1)} %collective-permute-done.14), channel_id=1, source_target_pairs={{0,8},{8,16},{16,24},{24,28},{28,20},{20,12},{12,4},{4,0},{1,9},{9... | collective-permute-start | bytes 2359304 | tf_op jit(solution)/shard_map/ppermute | solution.py:72
  126.0 44.4 %collective-permute-start.20 = (bf16[256,1536]{1,0:T(8,128)(2,1)}, bf16[256,1536]{1,0:T(8,128)(2,1)}, u32[]{:S(2)}, u32[]{:S(2)}) collective-permute-start(bf16[256,1536]{1,0:T(8,128)(2,1)} %collective-permute-done.15), channel_id=1, source_target_pairs={{0,4},{8,0},{16,8},{24,16},{28,24},{20,28},{12,20},{4,12},{1,5},{9... | collective-permute-start | bytes 2359304 | tf_op jit(solution)/shard_map/ppermute | solution.py:72
  148.9 27.1 %collective-permute-start.22 = (bf16[256,1536]{1,0:T(8,128)(2,1)}, bf16[256,1536]{1,0:T(8,128)(2,1)S(1)}, u32[]{:S(2)}, u32[]{:S(2)}) collective-permute-start(bf16[256,1536]{1,0:T(8,128)(2,1)} %collective-permute-done.17), channel_id=1, source_target_pairs={{0,8},{8,16},{16,24},{24,28},{28,20},{20,12},{12,4},{4,0},{1,9},{9... | collective-permute-start | bytes 2359304 | tf_op jit(solution)/shard_map/ppermute | solution.py:72
  152.2 23.8 %collective-permute-start.23 = (bf16[256,1536]{1,0:T(8,128)(2,1)}, bf16[256,1536]{1,0:T(8,128)(2,1)S(1)}, u32[]{:S(2)}, u32[]{:S(2)}) collective-permute-start(bf16[256,1536]{1,0:T(8,128)(2,1)} %collective-permute-done.18), channel_id=1, source_target_pairs={{0,4},{8,0},{16,8},{24,16},{28,24},{20,28},{12,20},{4,12},{1,5},{9... | collective-permute-start | bytes 2359304 | tf_op jit(solution)/shard_map/ppermute | solution.py:72
  173.6 29.2 %collective-permute-start.27 = (bf16[1536,256]{1,0:T(8,128)(2,1)}, bf16[1536,256]{1,0:T(8,128)(2,1)}, u32[]{:S(2)}, u32[]{:S(2)}) collective-permute-start(bf16[1536,256]{1,0:T(8,128)(2,1)} %param.27), channel_id=1, source_target_pairs={{0,8},{8,16},{16,24},{24,28},{28,20},{20,12},{12,4},{4,0},{1,9},{9... | collective-permute-start | bytes 2359304 | tf_op jit(solution)/shard_map/ppermute | solution.py:72
  174.4 28.4 %collective-permute-start.28 = (bf16[1536,256]{1,0:T(8,128)(2,1)}, bf16[1536,256]{1,0:T(8,128)(2,1)}, u32[]{:S(2)}, u32[]{:S(2)}) collective-permute-start(bf16[1536,256]{1,0:T(8,128)(2,1)} %param.27), channel_id=1, source_target_pairs={{0,4},{8,0},{16,8},{24,16},{28,24},{20,28},{12,20},{4,12},{1,5},{9... | collective-permute-start | bytes 2359304 | tf_op jit(solution)/shard_map/ppermute | solution.py:72
  221.5 21.6 %collective-permute-start.30 = (bf16[256,1536]{1,0:T(8,128)(2,1)}, bf16[256,1536]{1,0:T(8,128)(2,1)S(1)}, u32[]{:S(2)}, u32[]{:S(2)}) collective-permute-start(bf16[256,1536]{1,0:T(8,128)(2,1)} %collective-permute-done.19), channel_id=1, source_target_pairs={{0,8},{8,16},{16,24},{24,28},{28,20},{20,12},{12,4},{4,0},{1,9},{9... | collective-permute-start | bytes 2359304 | tf_op jit(solution)/shard_map/ppermute | solution.py:72
  222.5 20.7 %collective-permute-start.31 = (bf16[256,1536]{1,0:T(8,128)(2,1)}, bf16[256,1536]{1,0:T(8,128)(2,1)S(1)}, u32[]{:S(2)}, u32[]{:S(2)}) collective-permute-start(bf16[256,1536]{1,0:T(8,128)(2,1)} %collective-permute-done.20), channel_id=1, source_target_pairs={{0,4},{8,0},{16,8},{24,16},{28,24},{20,28},{12,20},{4,12},{1,5},{9... | collective-permute-start | bytes 2359304 | tf_op jit(solution)/shard_map/ppermute | solution.py:72
  226.4 32.8 %collective-permute-start.40 = (bf16[256,1536]{1,0:T(8,128)(2,1)S(1)}, bf16[256,1536]{1,0:T(8,128)(2,1)S(1)}, u32[]{:S(2)}, u32[]{:S(2)}) collective-permute-start(bf16[256,1536]{1,0:T(8,128)(2,1)S(1)} %copy-done.91), channel_id=1, source_target_pairs={{0,4},{8,0},{16,8},{24,16},{28,24},{20,28},{12,20},{4,12},{1,5},{9... | collective-permute-start | bytes 2359304 | tf_op jit(solution)/shard_map/ppermute | solution.py:72
  229.6 35.3 %collective-permute-start.38 = (bf16[256,1536]{1,0:T(8,128)(2,1)S(1)}, bf16[256,1536]{1,0:T(8,128)(2,1)S(1)}, u32[]{:S(2)}, u32[]{:S(2)}) collective-permute-start(bf16[256,1536]{1,0:T(8,128)(2,1)S(1)} %copy-done.93), channel_id=1, source_target_pairs={{0,8},{8,16},{16,24},{24,28},{28,20},{20,12},{12,4},{4,0},{1,9},{9... | collective-permute-start | bytes 2359304 | tf_op jit(solution)/shard_map/ppermute | solution.py:72
  243.2 47.3 %collective-permute-start.32 = (bf16[512,2048]{1,0:T(8,128)(2,1)S(1)}, bf16[512,2048]{1,0:T(8,128)(2,1)S(1)}, u32[]{:S(2)}, u32[]{:S(2)}) collective-permute-start(bf16[512,2048]{1,0:T(8,128)(2,1)S(1)} %add_convert_fusion.5), channel_id=1, source_target_pairs={{0,2},{1,3},{2,0},{3,1},{4,6},{5,7},{6,4},{7,5},{8,10},{9,11},{10,... | collective-permute-start | bytes 6291464 | tf_op jit(solution)/shard_map/ppermute | solution.py:180
  281.0 20.7 %collective-permute-start.34 = (bf16[1536,256]{1,0:T(8,128)(2,1)}, bf16[1536,256]{1,0:T(8,128)(2,1)S(1)}, u32[]{:S(2)}, u32[]{:S(2)}) collective-permute-start(bf16[1536,256]{1,0:T(8,128)(2,1)} %collective-permute-done.27), channel_id=1, source_target_pairs={{0,8},{8,16},{16,24},{24,28},{28,20},{20,12},{12,4},{4,0},{1,9},{9... | collective-permute-start | bytes 2359304 | tf_op jit(solution)/shard_map/ppermute | solution.py:72
  282.8 20.7 %collective-permute-start.36 = (bf16[1536,256]{1,0:T(8,128)(2,1)}, bf16[1536,256]{1,0:T(8,128)(2,1)S(1)}, u32[]{:S(2)}, u32[]{:S(2)}) collective-permute-start(bf16[1536,256]{1,0:T(8,128)(2,1)} %collective-permute-done.28), channel_id=1, source_target_pairs={{0,4},{8,0},{16,8},{24,16},{28,24},{20,28},{12,20},{4,12},{1,5},{9... | collective-permute-start | bytes 2359304 | tf_op jit(solution)/shard_map/ppermute | solution.py:72
  283.0 35.5 %collective-permute-start.39 = (bf16[256,1536]{1,0:T(8,128)(2,1)S(1)}, bf16[256,1536]{1,0:T(8,128)(2,1)S(1)}, u32[]{:S(2)}, u32[]{:S(2)}) collective-permute-start(bf16[256,1536]{1,0:T(8,128)(2,1)S(1)} %collective-permute-done.30), channel_id=1, source_target_pairs={{0,8},{8,16},{16,24},{24,28},{28,20},{20,12},{12,4},{4,0},{1,9},{9... | collective-permute-start | bytes 2359304 | tf_op jit(solution)/shard_map/ppermute | solution.py:72
  291.3 37.8 %collective-permute-start.33 = (bf16[512,2048]{1,0:T(8,128)(2,1)S(1)}, bf16[512,2048]{1,0:T(8,128)(2,1)S(1)}, u32[]{:S(2)}, u32[]{:S(2)}) collective-permute-start(bf16[512,2048]{1,0:T(8,128)(2,1)S(1)} %add_convert_fusion.4), channel_id=1, source_target_pairs={{0,1},{1,0},{2,3},{3,2},{4,5},{5,4},{6,7},{7,6},{8,9},{9,8},{10,11... | collective-permute-start | bytes 6291464 | tf_op jit(solution)/shard_map/ppermute | solution.py:175
  301.7 32.5 %collective-permute-start.35 = (bf16[1536,256]{1,0:T(8,128)(2,1)S(1)}, bf16[1536,256]{1,0:T(8,128)(2,1)}, u32[]{:S(2)}, u32[]{:S(2)}) collective-permute-start(bf16[1536,256]{1,0:T(8,128)(2,1)S(1)} %collective-permute-done.34), channel_id=1, source_target_pairs={{0,8},{8,16},{16,24},{24,28},{28,20},{20,12},{12,4},{4,0},{1,9},{9... | collective-permute-start | bytes 2359304 | tf_op jit(solution)/shard_map/ppermute | solution.py:72
  303.5 30.7 %collective-permute-start.37 = (bf16[1536,256]{1,0:T(8,128)(2,1)S(1)}, bf16[1536,256]{1,0:T(8,128)(2,1)S(1)}, u32[]{:S(2)}, u32[]{:S(2)}) collective-permute-start(bf16[1536,256]{1,0:T(8,128)(2,1)S(1)} %collective-permute-done.36), channel_id=1, source_target_pairs={{0,4},{8,0},{16,8},{24,16},{28,24},{20,28},{12,20},{4,12},{1,5},{9... | collective-permute-start | bytes 2359304 | tf_op jit(solution)/shard_map/ppermute | solution.py:72
  335.1 28.5 %collective-permute-start.42 = (bf16[1536,256]{1,0:T(8,128)(2,1)}, bf16[1536,256]{1,0:T(8,128)(2,1)S(1)}, u32[]{:S(2)}, u32[]{:S(2)}) collective-permute-start(bf16[1536,256]{1,0:T(8,128)(2,1)} %collective-permute-done.35), channel_id=1, source_target_pairs={{0,8},{8,16},{16,24},{24,28},{28,20},{20,12},{12,4},{4,0},{1,9},{9... | collective-permute-start | bytes 2359304 | tf_op jit(solution)/shard_map/ppermute | solution.py:72
  374.6 35.6 %collective-permute-start.43 = (bf16[1536,256]{1,0:T(8,128)(2,1)S(1)}, bf16[1536,256]{1,0:T(8,128)(2,1)S(1)}, u32[]{:S(2)}, u32[]{:S(2)}) collective-permute-start(bf16[1536,256]{1,0:T(8,128)(2,1)S(1)} %convolution_convert_fusion.8), channel_id=1, source_target_pairs={{0,8},{8,16},{16,24},{24,28},{28,20},{20,12},{12,4},{4,0},{1,9},{9... | collective-permute-start | bytes 2359304 | tf_op jit(solution)/shard_map/ppermute | solution.py:72
  376.1 34.2 %collective-permute-start.44 = (bf16[1536,256]{1,0:T(8,128)(2,1)S(1)}, bf16[1536,256]{1,0:T(8,128)(2,1)S(1)}, u32[]{:S(2)}, u32[]{:S(2)}) collective-permute-start(bf16[1536,256]{1,0:T(8,128)(2,1)S(1)} %convolution_convert_fusion.7), channel_id=1, source_target_pairs={{0,4},{8,0},{16,8},{24,16},{28,24},{20,28},{12,20},{4,12},{1,5},{9... | collective-permute-start | bytes 2359304 | tf_op jit(solution)/shard_map/ppermute | solution.py:72
  410.3 41.0 %collective-permute-start.45 = (bf16[512,2048]{1,0:T(8,128)(2,1)}, bf16[512,2048]{1,0:T(8,128)(2,1)}, u32[]{:S(2)}, u32[]{:S(2)}) collective-permute-start(bf16[512,2048]{1,0:T(8,128)(2,1)} %fusion.40), channel_id=1, source_target_pairs={{0,1},{1,0},{2,3},{3,2},{4,5},{5,4},{6,7},{7,6},{8,9},{9,8},{10,11... | collective-permute-start | bytes 6291464 | tf_op jit(solution)/shard_map/ppermute | solution.py:175
  412.3 50.9 %collective-permute-start.46 = (bf16[256,1536]{1,0:T(8,128)(2,1)}, bf16[256,1536]{1,0:T(8,128)(2,1)}, u32[]{:S(2)}, u32[]{:S(2)}) collective-permute-start(bf16[256,1536]{1,0:T(8,128)(2,1)} %convolution_convert_fusion.6), channel_id=1, source_target_pairs={{0,8},{8,16},{16,24},{24,28},{28,20},{20,12},{12,4},{4,0},{1,9},{9... | collective-permute-start | bytes 2359304 | tf_op jit(solution)/shard_map/ppermute | solution.py:72
  413.7 49.5 %collective-permute-start.47 = (bf16[256,1536]{1,0:T(8,128)(2,1)}, bf16[256,1536]{1,0:T(8,128)(2,1)S(1)}, u32[]{:S(2)}, u32[]{:S(2)}) collective-permute-start(bf16[256,1536]{1,0:T(8,128)(2,1)} %convolution_convert_fusion.5), channel_id=1, source_target_pairs={{0,4},{8,0},{16,8},{24,16},{28,24},{20,28},{12,20},{4,12},{1,5},{9... | collective-permute-start | bytes 2359304 | tf_op jit(solution)/shard_map/ppermute | solution.py:72
  416.9 32.4 %collective-permute-start.50 = (bf16[256,1536]{1,0:T(8,128)(2,1)S(1)}, bf16[256,1536]{1,0:T(8,128)(2,1)S(1)}, u32[]{:S(2)}, u32[]{:S(2)}) collective-permute-start(bf16[256,1536]{1,0:T(8,128)(2,1)S(1)} %convolution_convert_fusion.4), channel_id=1, source_target_pairs={{0,8},{8,16},{16,24},{24,28},{28,20},{20,12},{12,4},{4,0},{1,9},{9... | collective-permute-start | bytes 2359304 | tf_op jit(solution)/shard_map/ppermute | solution.py:72
  418.3 46.5 %collective-permute-start.53 = (bf16[256,1536]{1,0:T(8,128)(2,1)}, bf16[256,1536]{1,0:T(8,128)(2,1)}, u32[]{:S(2)}, u32[]{:S(2)}) collective-permute-start(bf16[256,1536]{1,0:T(8,128)(2,1)} %convolution_convert_fusion.3), channel_id=1, source_target_pairs={{0,4},{8,0},{16,8},{24,16},{28,24},{20,28},{12,20},{4,12},{1,5},{9... | collective-permute-start | bytes 2359304 | tf_op jit(solution)/shard_map/ppermute | solution.py:72
  463.2 49.0 %collective-permute-start.48 = (bf16[512,2048]{1,0:T(8,128)(2,1)}, bf16[512,2048]{1,0:T(8,128)(2,1)S(1)}, u32[]{:S(2)}, u32[]{:S(2)}) collective-permute-start(bf16[512,2048]{1,0:T(8,128)(2,1)} %add_convert_fusion.3), channel_id=1, source_target_pairs={{0,2},{1,3},{2,0},{3,1},{4,6},{5,7},{6,4},{7,5},{8,10},{9,11},{10,... | collective-permute-start | bytes 6291464 | tf_op jit(solution)/shard_map/ppermute | solution.py:180
  468.8 20.5 %collective-permute-start.51 = (bf16[1536,256]{1,0:T(8,128)(2,1)S(1)}, bf16[1536,256]{1,0:T(8,128)(2,1)S(1)}, u32[]{:S(2)}, u32[]{:S(2)}) collective-permute-start(bf16[1536,256]{1,0:T(8,128)(2,1)S(1)} %copy-done.124), channel_id=1, source_target_pairs={{0,8},{8,16},{16,24},{24,28},{28,20},{20,12},{12,4},{4,0},{1,9},{9... | collective-permute-start | bytes 2359304 | tf_op jit(solution)/shard_map/ppermute | solution.py:72
  470.2 20.5 %collective-permute-start.54 = (bf16[1536,256]{1,0:T(8,128)(2,1)S(1)}, bf16[1536,256]{1,0:T(8,128)(2,1)S(1)}, u32[]{:S(2)}, u32[]{:S(2)}) collective-permute-start(bf16[1536,256]{1,0:T(8,128)(2,1)S(1)} %copy-done.123), channel_id=1, source_target_pairs={{0,4},{8,0},{16,8},{24,16},{28,24},{20,28},{12,20},{4,12},{1,5},{9... | collective-permute-start | bytes 2359304 | tf_op jit(solution)/shard_map/ppermute | solution.py:72
  473.9 32.2 %collective-permute-start.56 = (bf16[256,1536]{1,0:T(8,128)(2,1)S(1)}, bf16[256,1536]{1,0:T(8,128)(2,1)S(1)}, u32[]{:S(2)}, u32[]{:S(2)}) collective-permute-start(bf16[256,1536]{1,0:T(8,128)(2,1)S(1)} %fusion.55), channel_id=1, source_target_pairs={{0,8},{8,16},{16,24},{24,28},{28,20},{20,12},{12,4},{4,0},{1,9},{9... | collective-permute-start | bytes 2359304 | tf_op jit(solution)/shard_map/ppermute | solution.py:72
  478.3 31.2 %collective-permute-start.58 = (bf16[256,1536]{1,0:T(8,128)(2,1)S(1)}, bf16[256,1536]{1,0:T(8,128)(2,1)S(1)}, u32[]{:S(2)}, u32[]{:S(2)}) collective-permute-start(bf16[256,1536]{1,0:T(8,128)(2,1)S(1)} %fusion.57), channel_id=1, source_target_pairs={{0,4},{8,0},{16,8},{24,16},{28,24},{20,28},{12,20},{4,12},{1,5},{9... | collective-permute-start | bytes 2359304 | tf_op jit(solution)/shard_map/ppermute | solution.py:72
  489.2 50.9 %collective-permute-start.52 = (bf16[256,1536]{1,0:T(8,128)(2,1)}, bf16[256,1536]{1,0:T(8,128)(2,1)}, u32[]{:S(2)}, u32[]{:S(2)}) collective-permute-start(bf16[256,1536]{1,0:T(8,128)(2,1)} %fusion.50), channel_id=1, source_target_pairs={{0,8},{8,16},{16,24},{24,28},{28,20},{20,12},{12,4},{4,0},{1,9},{9... | collective-permute-start | bytes 2359304 | tf_op jit(solution)/shard_map/ppermute | solution.py:72
  490.7 49.5 %collective-permute-start.55 = (bf16[256,1536]{1,0:T(8,128)(2,1)}, bf16[256,1536]{1,0:T(8,128)(2,1)}, u32[]{:S(2)}, u32[]{:S(2)}) collective-permute-start(bf16[256,1536]{1,0:T(8,128)(2,1)} %fusion.52), channel_id=1, source_target_pairs={{0,4},{8,0},{16,8},{24,16},{28,24},{20,28},{12,20},{4,12},{1,5},{9... | collective-permute-start | bytes 2359304 | tf_op jit(solution)/shard_map/ppermute | solution.py:72
  506.1 49.8 %collective-permute-start.57 = (bf16[1536,256]{1,0:T(8,128)(2,1)}, bf16[1536,256]{1,0:T(8,128)(2,1)}, u32[]{:S(2)}, u32[]{:S(2)}) collective-permute-start(bf16[1536,256]{1,0:T(8,128)(2,1)} %fusion.54), channel_id=1, source_target_pairs={{0,8},{8,16},{16,24},{24,28},{28,20},{20,12},{12,4},{4,0},{1,9},{9... | collective-permute-start | bytes 2359304 | tf_op jit(solution)/shard_map/ppermute | solution.py:72
  509.5 46.4 %collective-permute-start.59 = (bf16[1536,256]{1,0:T(8,128)(2,1)}, bf16[1536,256]{1,0:T(8,128)(2,1)S(1)}, u32[]{:S(2)}, u32[]{:S(2)}) collective-permute-start(bf16[1536,256]{1,0:T(8,128)(2,1)} %fusion.56), channel_id=1, source_target_pairs={{0,4},{8,0},{16,8},{24,16},{28,24},{20,28},{12,20},{4,12},{1,5},{9... | collective-permute-start | bytes 2359304 | tf_op jit(solution)/shard_map/ppermute | solution.py:72
  524.6 243.4 %all-reduce.18.cloned.1.call-start = ((), (), s32[]{:S(2)}) async-start(), calls=%async_computation.1 | async-start | bytes 1081344 | tf_op jit(solution)/shard_map/psum | solution.py:863
  556.9 21.6 %collective-permute-start.60 = (f32[4,2,704]{2,1,0:T(2,128)S(1)}, f32[4,2,704]{2,1,0:T(2,128)S(1)}, u32[]{:S(2)}, u32[]{:S(2)}) collective-permute-start(f32[4,2,704]{2,1,0:T(2,128)S(1)} %slice.599), channel_id=1, source_target_pairs={{4,0},{8,4},{12,8},{16,12},{20,16},{24,20},{28,24},{5,1},{9,5},{13... | collective-permute-start | bytes 67592 | tf_op jit(solution)/shard_map/ppermute | solution.py:528
  561.4 20.9 %collective-permute-start.61 = (bf16[256,1536]{1,0:T(8,128)(2,1)S(1)}, bf16[256,1536]{1,0:T(8,128)(2,1)S(1)}, u32[]{:S(2)}, u32[]{:S(2)}) collective-permute-start(bf16[256,1536]{1,0:T(8,128)(2,1)S(1)} %copy-done.121), channel_id=1, source_target_pairs={{0,8},{8,16},{16,24},{24,28},{28,20},{20,12},{12,4},{4,0},{1,9},{9... | collective-permute-start | bytes 2359304 | tf_op jit(solution)/shard_map/ppermute | solution.py:72
  567.0 20.9 %collective-permute-start.62 = (bf16[256,1536]{1,0:T(8,128)(2,1)S(1)}, bf16[256,1536]{1,0:T(8,128)(2,1)S(1)}, u32[]{:S(2)}, u32[]{:S(2)}) collective-permute-start(bf16[256,1536]{1,0:T(8,128)(2,1)S(1)} %copy-done.122), channel_id=1, source_target_pairs={{0,4},{8,0},{16,8},{24,16},{28,24},{20,28},{12,20},{4,12},{1,5},{9... | collective-permute-start | bytes 2359304 | tf_op jit(solution)/shard_map/ppermute | solution.py:72
  571.2 48.0 %collective-permute-start.66 = (bf16[256,1536]{1,0:T(8,128)(2,1)S(1)}, bf16[256,1536]{1,0:T(8,128)(2,1)S(1)}, u32[]{:S(2)}, u32[]{:S(2)}) collective-permute-start(bf16[256,1536]{1,0:T(8,128)(2,1)S(1)} %fusion.60), channel_id=1, source_target_pairs={{0,8},{8,16},{16,24},{24,28},{28,20},{20,12},{12,4},{4,0},{1,9},{9... | collective-permute-start | bytes 2359304 | tf_op jit(solution)/shard_map/ppermute | solution.py:72
  573.0 46.3 %collective-permute-start.67 = (bf16[256,1536]{1,0:T(8,128)(2,1)S(1)}, bf16[256,1536]{1,0:T(8,128)(2,1)S(1)}, u32[]{:S(2)}, u32[]{:S(2)}) collective-permute-start(bf16[256,1536]{1,0:T(8,128)(2,1)S(1)} %fusion.61), channel_id=1, source_target_pairs={{0,4},{8,0},{16,8},{24,16},{28,24},{20,28},{12,20},{4,12},{1,5},{9... | collective-permute-start | bytes 2359304 | tf_op jit(solution)/shard_map/ppermute | solution.py:72
  589.3 63.2 %collective-permute-start.68 = (bf16[1536,256]{1,0:T(8,128)(2,1)}, bf16[1536,256]{1,0:T(8,128)(2,1)}, u32[]{:S(2)}, u32[]{:S(2)}) collective-permute-start(bf16[1536,256]{1,0:T(8,128)(2,1)} %fusion.62), channel_id=1, source_target_pairs={{0,8},{8,16},{16,24},{24,28},{28,20},{20,12},{12,4},{4,0},{1,9},{9... | collective-permute-start | bytes 2359304 | tf_op jit(solution)/shard_map/ppermute | solution.py:72
  616.1 36.4 %collective-permute-start.69 = (bf16[256,1536]{1,0:T(8,128)(2,1)}, bf16[256,1536]{1,0:T(8,128)(2,1)}, u32[]{:S(2)}, u32[]{:S(2)}) collective-permute-start(bf16[256,1536]{1,0:T(8,128)(2,1)} %fusion.63), channel_id=1, source_target_pairs={{0,4},{8,0},{16,8},{24,16},{28,24},{20,28},{12,20},{4,12},{1,5},{9... | collective-permute-start | bytes 2359304 | tf_op jit(solution)/shard_map/ppermute | solution.py:72
  621.2 40.0 %collective-permute-start.71 = (bf16[256,1536]{1,0:T(8,128)(2,1)}, bf16[256,1536]{1,0:T(8,128)(2,1)}, u32[]{:S(2)}, u32[]{:S(2)}) collective-permute-start(bf16[256,1536]{1,0:T(8,128)(2,1)} %fusion.64), channel_id=1, source_target_pairs={{0,8},{8,16},{16,24},{24,28},{28,20},{20,12},{12,4},{4,0},{1,9},{9... | collective-permute-start | bytes 2359304 | tf_op jit(solution)/shard_map/ppermute | solution.py:72
  657.5 26.1 %collective-permute-start.89 = (bf16[704,256]{1,0:T(8,128)(2,1)S(1)}, bf16[704,256]{1,0:T(8,128)(2,1)S(1)}, u32[]{:S(2)}, u32[]{:S(2)}) collective-permute-start(bf16[704,256]{1,0:T(8,128)(2,1)S(1)} %convolution_convert_fusion.12), channel_id=1, source_target_pairs={{0,4},{8,0},{16,8},{24,16},{28,24},{20,28},{12,20},{4,12},{1,5},{9... | collective-permute-start | bytes 1081352 | tf_op jit(solution)/shard_map/ppermute | solution.py:72
  691.6 47.8 %collective-permute-start.75 = (bf16[512,2048]{1,0:T(8,128)(2,1)}, bf16[512,2048]{1,0:T(8,128)(2,1)}, u32[]{:S(2)}, u32[]{:S(2)}) collective-permute-start(bf16[512,2048]{1,0:T(8,128)(2,1)} %add_convert_fusion.1), channel_id=1, source_target_pairs={{0,2},{1,3},{2,0},{3,1},{4,6},{5,7},{6,4},{7,5},{8,10},{9,11},{10,... | collective-permute-start | bytes 6291464 | tf_op jit(solution)/shard_map/ppermute | solution.py:180
  714.9 31.3 %collective-permute-start.94 = (bf16[704,256]{1,0:T(8,128)(2,1)}, bf16[704,256]{1,0:T(8,128)(2,1)}, u32[]{:S(2)}, u32[]{:S(2)}) collective-permute-start(bf16[704,256]{1,0:T(8,128)(2,1)} %fusion.72), channel_id=1, source_target_pairs={{0,4},{8,0},{16,8},{24,16},{28,24},{20,28},{12,20},{4,12},{1,5},{9... | collective-permute-start | bytes 1081352 | tf_op jit(solution)/shard_map/ppermute | solution.py:72
  719.5 31.9 %collective-permute-start.86 = (bf16[704,256]{1,0:T(8,128)(2,1)}, bf16[704,256]{1,0:T(8,128)(2,1)}, u32[]{:S(2)}, u32[]{:S(2)}) collective-permute-start(bf16[704,256]{1,0:T(8,128)(2,1)} %fusion.71), channel_id=1, source_target_pairs={{0,8},{8,16},{16,24},{24,28},{28,20},{20,12},{12,4},{4,0},{1,9},{9... | collective-permute-start | bytes 1081352 | tf_op jit(solution)/shard_map/ppermute | solution.py:72
  727.0 31.2 %collective-permute-start.93 = (bf16[704,256]{1,0:T(8,128)(2,1)}, bf16[704,256]{1,0:T(8,128)(2,1)S(1)}, u32[]{:S(2)}, u32[]{:S(2)}) collective-permute-start(bf16[704,256]{1,0:T(8,128)(2,1)} %add_convert_fusion.11), channel_id=1, source_target_pairs={{0,4},{8,0},{16,8},{24,16},{28,24},{20,28},{12,20},{4,12},{1,5},{9... | collective-permute-start | bytes 1081352 | tf_op jit(solution)/shard_map/ppermute | solution.py:72
  728.4 27.4 %collective-permute-start.85 = (bf16[704,256]{1,0:T(8,128)(2,1)}, bf16[704,256]{1,0:T(8,128)(2,1)}, u32[]{:S(2)}, u32[]{:S(2)}) collective-permute-start(bf16[704,256]{1,0:T(8,128)(2,1)} %add_convert_fusion.16), channel_id=1, source_target_pairs={{0,8},{8,16},{16,24},{24,28},{28,20},{20,12},{12,4},{4,0},{1,9},{9... | collective-permute-start | bytes 1081352 | tf_op jit(solution)/shard_map/ppermute | solution.py:72
  758.2 35.7 %collective-permute-start.76 = (bf16[512,2048]{1,0:T(8,128)(2,1)S(1)}, bf16[512,2048]{1,0:T(8,128)(2,1)}, u32[]{:S(2)}, u32[]{:S(2)}) collective-permute-start(bf16[512,2048]{1,0:T(8,128)(2,1)S(1)} %get-tuple-element.439), channel_id=1, source_target_pairs={{0,1},{1,0},{2,3},{3,2},{4,5},{5,4},{6,7},{7,6},{8,9},{9,8},{10,11... | collective-permute-start | bytes 6291464 | tf_op jit(solution)/shard_map/ppermute | solution.py:175
  767.0 23.0 %collective-permute-start.97 = (bf16[704,256]{1,0:T(8,128)(2,1)}, bf16[704,256]{1,0:T(8,128)(2,1)}, u32[]{:S(2)}, u32[]{:S(2)}) collective-permute-start(bf16[704,256]{1,0:T(8,128)(2,1)} %fusion.73), channel_id=1, source_target_pairs={{0,8},{8,16},{16,24},{24,28},{28,20},{20,12},{12,4},{4,0},{1,9},{9... | collective-permute-start | bytes 1081352 | tf_op jit(solution)/shard_map/ppermute | solution.py:72
  (185 other events, 2511.1 us)
Sparse Core Ops, SparseCore 0:
  524.7 82.9 all-reduce.15
  650.2 74.9 all-reduce.17

commit v4 on v3

--- a/solution.py
+++ b/solution.py
@@ -182,7 +182,8 @@
 
 def tp_sum(part, others=lambda v: v, chips=lambda v: v, totals=lambda v: v):
     got = core_swap(others(part(1).astype(bf16)))
-    chip = chips((part(0) + got.astype(f32)).astype(bf16))
+    own = lax.optimization_barrier(part(0).astype(bf16))
+    chip = chips((own.astype(f32) + got.astype(f32)).astype(bf16))
     far = chip_swap(chip)
     total = totals((chip.astype(f32) + far.astype(f32)).astype(bf16))
     return total, core_swap(total)
@@ -455,13 +456,13 @@
     return [*done[:count], *(a + b for a, b in zip(ready[count:], done[count:]))]
 
 
-def enter_kernel(sequence, chunk, *refs):
-    count = len(refs) // 2
-    part = refs[0].shape[1] // chunk.shape[0]
+def enter_kernel(sequence, chunk, tokens, cotangent, x, cot, turned):
+    part = x.shape[1] // chunk.shape[0]
+    turned[...] = cotangent[...]
     for k in range(chunk.shape[0]):
         at = pl.ds(pl.multiple_of(chunk[k] * part, part), part)
-        for i in range(count):
-            refs[count + i][:, k * part : (k + 1) * part] = refs[i][:, at]
+        x[:, k * part : (k + 1) * part] = tokens[:, at]
+        cot[:, k * part : (k + 1) * part] = cotangent[:, at]
 
 
 def norm_kernel(x, added, gain, middle, normed):
@@ -509,7 +510,11 @@
 
 
 def output_kernel(sequence, chunk, middle, added, output):
-    put_chunks(chunk, output, (middle[...] + added[...].astype(f32)).astype(bf16))
+    part = middle.shape[1] // chunk.shape[0]
+    for k in range(chunk.shape[0]):
+        at = pl.ds(pl.multiple_of(chunk[k] * part, part), part)
+        total = middle[:, k * part : (k + 1) * part] + added[:, at].astype(f32)
+        output[:, at] = total.astype(bf16)
 
 
 def own_order(array, order, back=False):
@@ -616,24 +621,31 @@
         jnp.concatenate([w_in[1], out_weight[half_lanes:], own_gain], axis=0), -1, n, chunk
     )
     mlp = [Gather(mlp_weight[:, 0], 1, n, chunk), Gather(mlp_weight[:, 1], -1, n, chunk)]
-    downs = Gather(down_weight, 1, n, chunk)
     ring.add([first, second])
-    ring.add([*mlp, downs], [0, 0, 2])
+    ring.add(mlp)
     ring.issue()
 
     tokens, cotangent = ring.land((tokens, cotangent))
     if tiled:
-        x, cot = by_rows(enter_kernel, [tokens, cotangent], [], [bf16, bf16], 0, move)
+        x, cot, cot_turned = by_rows(enter_kernel, [tokens, cotangent], [], [bf16] * 3, 0, move)
     else:
         x, cot = own_order(tokens, move), own_order(cotangent, move)
+        cot_turned = cotangent[sequence]
     full = x.shape
     part_full = (seqs // 2, piece, width)
-    x, cot = ring.land((x, cot))
-    grad_low = cot.reshape(rows, width)
+    x, cot, cot_turned, down_weight, tail_rows = ring.land(
+        (x, cot, cot_turned, down_weight, tokens[:, piece - taps + 1 :])
+    )
+    behind_rows = lax.ppermute(tail_rows, "seq", [(i, i + 1) for i in range(n - 1)])
+    w_down = lax.all_gather(down_weight, "seq", axis=1, tiled=True)
+    cot_turned = cot_turned.reshape(rows, width)
     start = x.reshape(rows, width).astype(f32)
     inverse1 = lax.rsqrt(jnp.mean(start * start, axis=-1, keepdims=True) + eps)
-    for _ in range(n - 3):
-        ring.land()
+    for turn in range(n - 3):
+        if turn == 3:
+            behind_rows = ring.land(behind_rows)
+        else:
+            ring.land()
     first, second = first.slots(), second.slots()
     in0 = [p[:lanes] for p in first]
     in1 = [p[:lanes] for p in second]
@@ -646,13 +658,22 @@
     ]
     inner = sum(across(normed1[k], in0[k]) for k in range(n)).astype(bf16)
     gate_in = sum(across(normed1[k], in1[k]) for k in range(n)).astype(bf16)
-    inner = ring.land(inner)
+    count = seqs * (taps - 1)
+    start_before = behind_rows[sequence].reshape(count, n, part)[:, chunk].reshape(count, width)
+    start_before = jnp.pad(start_before.astype(f32), ((0, -count % 16), (0, 0)))
+    inverse_before = lax.rsqrt(
+        jnp.mean(start_before * start_before, axis=-1, keepdims=True) + eps
+    )
+    normed_before = [
+        (sl(start_before, k) * inverse_before * gains[k][:1].astype(f32)).astype(bf16)
+        for k in range(n)
+    ]
+    before = sum(across(normed_before[k], in0[k]) for k in range(n)).astype(bf16)
+    before = before[:count].astype(f32).reshape(seqs, taps - 1, lanes)
+    before = jnp.pad(before, ((0, 0), (pad_rows - taps + 1, 0), (0, 0)))
     inner = inner.reshape(seqs, piece, lanes)
     gate_in = gate_in.reshape(seqs, piece, lanes)
-    before = lax.ppermute(
-        inner[:, piece - taps + 1 :], "seq", [(i, i + 1) for i in range(n - 1)]
-    ).astype(f32)
-    before = ring.land(jnp.pad(before, ((0, 0), (pad_rows - taps + 1, 0), (0, 0))))
+    inner = ring.land(inner)
     conv_w = conv_weight.astype(f32)
     rate = decay_rate.astype(f32)[None]
     gate_m = dense_heads(gate_matrix)
@@ -675,7 +696,7 @@
         [pltpu.VMEM((piece + pad_rows, lanes), f32), pltpu.VMEM((2, piece, lanes), f32)],
         gate_flops,
     )
-    entry = ring.land(carried(ring.land(ends), 1, n, ring.land))
+    entry = ring.land(carried(ring.land(ends), 1, n))
     states = local + cum * entry[:, :1]
     product = (states * gelu_parts(gate_in.astype(f32))[0]).astype(bf16).reshape(rows, lanes)
     w_out = jnp.concatenate(
@@ -691,45 +712,44 @@
         return a[h * block : (h + 1) * block]
 
     def lands(values, count):
-        for _ in range(count):
+        for _ in range(count - 1):
             ring.land()
-        return ring.resume(values)
+        return ring.land(values)
 
     chips = []
 
     def keep(chip):
-        chips.append(ring.land(chip))
-        return chips[0]
+        chips.append(chip)
+        return chip
 
     recurrent = tp_sum(
         lambda h: dot(half_of(product, h), w_out),
         chips=keep,
-        totals=lambda v: lands(v, 3),
+        totals=lambda v: lands(v, 4),
     )
     gate_act, gate_slope = gelu_parts(after(gate_in, chips[0]).astype(f32))
 
     middle, normed2 = in_halves(
         norm_kernel, [x], [r.reshape(part_full) for r in recurrent], [gain2], [f32, bf16], 0
     )
-    normed2 = ring.land(normed2.reshape(rows, width))
+    normed2 = normed2.reshape(rows, width)
     w_mlp = jnp.concatenate([jnp.concatenate(w.slots(), axis=0) for w in mlp], axis=1)
     both = dot(normed2, w_mlp).astype(bf16)
     both0, both1 = both[:, :units].astype(f32), both[:, units:].astype(f32)
     act, slope = gelu_parts(both0)
     hidden = (act * both1).astype(bf16)
-    hidden, act, slope = ring.land((hidden, act.astype(bf16), (slope * both1).astype(bf16)))
+    act, slope = act.astype(bf16), (slope * both1).astype(bf16)
     ring.drain()
-    w_down = jnp.concatenate(downs.slots(), axis=1)
     ring.token = None
+    grad_down = down(hidden, cot_turned).astype(bf16)
+    act, slope = after((act, slope), grad_down)
+    grad_down = lax.psum_scatter(grad_down, "seq", scatter_dimension=1, tiled=True).astype(f32)
     grad_both = []
-    grad_down = Scatter(lambda k: down(hidden, sl(grad_low, k)), 1, n, chunk)
     grad_mlp = [
-        Scatter(lambda k: down(sl(normed2, k), grad_both[0][:, :units]), -1, n, chunk),
-        Scatter(lambda k: down(sl(normed2, k), grad_both[0][:, units:]), 1, n, chunk),
+        Scatter(lambda k: down(sl(normed2, k), grad_both[0][:, :units]), 1, n, chunk),
+        Scatter(lambda k: down(sl(normed2, k), grad_both[0][:, units:]), -1, n, chunk),
     ]
-    ring.add([grad_down, *grad_mlp])
-    ring.issue(1)
-    act, slope, w_down = ring.hold((act, slope, w_down))
+    ring.add(grad_mlp)
     grad_both.append(
         pl.pallas_call(
             hidden_back_kernel,
@@ -745,21 +765,18 @@
             compiler_params=pltpu.CompilerParams(vmem_limit_bytes=vmem_bytes),
             cost_estimate=pl.CostEstimate(
                 flops=2 * rows * width * units,
-                bytes_accessed=moved_bytes(grad_low, w_down, act, slope, both),
+                bytes_accessed=moved_bytes(cot_turned, w_down, act, slope, both),
                 transcendentals=0,
             ),
-        )(grad_low, w_down, act, slope)
+        )(cot_turned, w_down, act, slope)
     )
     ring.issue()
     grad_normed2 = tp_sum(
         lambda h: across(half_of(grad_both[0], h), w_mlp),
-        others=ring.land,
-        chips=ring.land,
-        totals=lambda v: lands(v, 3),
+        totals=lambda v: lands(v, 2),
     )
     turned = jnp.concatenate([half_of(hidden, 1), half_of(hidden, 0)], axis=0)
     turned = jnp.where(odd == 1, turned, hidden)
-    mlp_out = lax.psum(dot(after(turned, grad_normed2[0]), w_down).astype(bf16), "tp")
 
     grad_middle, grad_rec, sum_gain2 = in_halves(
         middle_back_kernel,
@@ -769,7 +786,10 @@
         [f32, bf16],
         1,
     )
+    grad_out = Scatter(lambda k: down(product, sl(grad_rec, k)), -1, n, chunk)
+    ring.add([grad_out])
     grad_rec = ring.land(grad_rec.reshape(rows, width))
+    mlp_out = lax.psum(dot(after(turned, grad_middle), w_down).astype(bf16), "tp")
 
     grad_product = across(grad_rec, w_out).reshape(wide)
     tail, local_grad, early = per_sequence(
@@ -780,7 +800,7 @@
         [pltpu.VMEM((piece, lanes), f32)],
         rows * lanes * 50,
     )
-    incoming = ring.land(carried(ring.land(early), -1, n, ring.land))
+    incoming = ring.land(after(carried(early, -1, n), grad_down), 2)
     grad_gates, grad_inner, grad_gate_in, head, last, sums = per_sequence(
         gates_back_kernel,
         seqs,
@@ -832,7 +852,6 @@
     grads = [
         Scatter(lambda k: down(back0, normed1[k]), 1, n, chunk),
         Scatter(lambda k: down(back1, normed1[k]), -1, n, chunk),
-        Scatter(lambda k: down(product, sl(grad_rec, k)), -1, n, chunk),
     ]
     ring.add(grads)
     ring.issue()
@@ -848,6 +867,23 @@
         totals=lambda v: lands(v, 4),
     )
     mlp_out = late[0]
+    ready = None
+    if tiled:
+        summed1 = [g.reshape(part_full) for g in grad_normed1]
+        ready = by_rows(
+            start_back_kernel,
+            [x, summed1[0], grad_middle],
+            [gain1],
+            [f32],
+            0,
+            move,
+            back=True,
+            half=0,
+        )
+        ring.resume(ready[0])
+        total1 = after(grad_normed1[0], ready[0])
+    else:
+        total1 = grad_normed1[0]
     ring.drain()
     grads = [g.total() for g in grads]
     low_mixed = mixed.astype(bf16).reshape(rows, lanes)
@@ -873,26 +909,27 @@
             back=True,
             moved=(1,),
         )[0]
-        grad_tokens = in_halves(
+        grad_tokens = by_rows(
             start_back_kernel,
-            [x, grad_middle],
-            [g.reshape(part_full) for g in grad_normed1],
+            [x, summed1[1], grad_middle],
             [gain1],
             [f32],
             0,
             move,
             back=True,
+            half=1,
+            earlier=ready,
         )[0]
     else:
-        mlp_out = mlp_out.reshape(full)[sequence].astype(f32)
-        output = own_order((middle + mlp_out).astype(bf16), move, True)
+        mlp_out = mlp_out.reshape(full).astype(f32)
+        output = (own_order(middle, move, True) + mlp_out).astype(bf16)
         grad_normed1_all = jnp.concatenate(grad_normed1, axis=0).reshape(full).astype(f32)
         grad_start = norm_back(x.astype(f32), grad_normed1_all, gain1)[0]
         grad_tokens = own_order(grad_middle + grad_start, move, True)
     mine = lax.axis_index("seq")
     slots = (me - jnp.asarray(place, jnp.int32)) % n
     scaled1 = start[:block] * inverse1[:block]
-    sum_gain1 = jnp.sum(grad_normed1[0].astype(f32) * scaled1, axis=0)
+    sum_gain1 = jnp.sum(total1.astype(f32) * scaled1, axis=0)
     grad_gains = jnp.stack([sum_gain1, 0.5 * jnp.sum(sum_gain2, axis=0)])
     grad_gains = grad_gains + core_swap(grad_gains)
     grad_gains = seq_sum(grad_gains.reshape(2, n, part)[:, slots], n)
@@ -913,10 +950,10 @@
         grad_matrix,
         small[1:3],
         small[0],
-        grads[2],
+        grad_out.total(),
         grad_gains[1],
         jnp.stack([g.total() for g in grad_mlp], axis=1),
-        grad_down.total(),
+        grad_down,
     )
 
 

time: 818 us -> 911 us (1.11)
  waiting for transfers between devices: 205 us -> 271 us
  other arithmetic: 39.3 us -> 65 us
  starting transfers between devices: 127 us -> 111 us
  local copies, waits for them, and re-layouts: 106 us -> 120 us
    ppermute x77 -> x63, waiting for transfers between devices: 150 us -> 188 us  [issue(): flying.append((flow, lax.ppermute(message, 'seq', self.pairs[way])))]
    ppermute x3, waiting for transfers between devices: 12.6 us -> 36.4 us  [chip_swap(): return lax.ppermute(values, 'tp', [(i, i ^ 2) for i in range(size)])]
    dot_general x19 -> x27, matrix products: 48.6 us -> 71.9 us  [across(): lax.dot_general(a, b, (((1,), (1,)), ((), ())), preferred_element_type=f32)]
    dot_general x50 -> x43, matrix products: 109 us -> 90 us  [down(): lax.dot_general(a, b, (((0,), (0,)), ((), ())), preferred_element_type=f32)]
    ppermute x77 -> x63, starting transfers between devices: 91.2 us -> 72.7 us  [issue(): flying.append((flow, lax.ppermute(message, 'seq', self.pairs[way])))]
    ppermute x3, waiting for transfers between devices: 0.33 us -> 16.8 us  [seq_sum(): lax.ppermute(values, 'seq', [(i, i ^ by) for i in range(n)])]
    unnamed x352 -> x323, local copies, waits for them, and re-layouts: 67 us -> 81.2 us
    ppermute x1, waiting for transfers between devices: 12.2 us -> 0.01 us  [shards(): lax.ppermute(tail_rows, 'seq', [(i, i + 1) for i in range(n - 1)])]
  transfers between devices with their start and end apart: 102 -> 90, of which waited for: 26 -> 31; matrix products, arithmetic and copies ran while one was open for 38% -> 40% of each run, Pallas kernels for 13% -> 10%
where the time goes in v4:
time: 911 us; the launch traced here: 902 us
  waiting for transfers between devices  271 us (30%)
  matrix products  205 us (23%)
  local copies, waits for them, and re-layouts  120 us (13%)
  Pallas kernels  114 us (13%)
  starting transfers between devices  111 us (12%)
  other arithmetic  65 us (7%)
  between operations  16.4 us (2%)
    ppermute x63, waiting for transfers between devices, issue(): flying.append((flow, lax.ppermute(message, 'seq', self.pairs[way])))  188 us
    dot_general x43, matrix products, down(): lax.dot_general(a, b, (((0,), (0,)), ((), ())), preferred_element_type=f32)  90 us
    unnamed x323, local copies, waits for them, and re-layouts  81.2 us
    ppermute x63, starting transfers between devices, issue(): flying.append((flow, lax.ppermute(message, 'seq', self.pairs[way])))  72.7 us
    dot_general x27, matrix products, across(): lax.dot_general(a, b, (((1,), (1,)), ((), ())), preferred_element_type=f32)  71.9 us
    pallas_call x8, Pallas kernels, by_rows(): pl.pallas_call(body, grid_spec=pltpu.PrefetchScalarGridSpec(num_scalar_pr...  58.3 us
    dot_general x6, matrix products, dot(): return jnp.dot(a, b, preferred_element_type=f32)  43.1 us
    pallas_call x3, Pallas kernels, per_sequence(): pl.pallas_call(kernel, grid=(seqs,), in_specs=[spec(a.shape, kind) for a,...  42.9 us
  transfers between devices with their start and end apart: 90, of which 31 were waited for; matrix products, arithmetic and copies ran while one was open for 40% of the time, Pallas kernels for 10%

profile of v4, /device:TPU:0, one launch (start us, length us, event | category | flops | bytes accessed | tf_op | source)
XLA Modules:
  0.0 902.2 jit_solution(2241890948878149042)
XLA Ops:
  19.9 3.1 fusion.268
  32.8 9.8 %shard_map.255 = (bf16[4,256,2048]{2,1,0:T(8,128)(2,1)S(1)}, bf16[4,256,2048]{2,1,0:T(8,128)(2,1)}, bf16[4,256,2048]{2,1,0:T(8,128)(2,1)}) custom-call(s32[4]{0:T(128)S(1)} %and_select_fusion.3.refs_0_, s32[8]{0:T(128)S(1)} %gather_fusion, bf16[4,256,2048]{2,1,0:T(8,128)(2,1)} %refs_2_, bf16[4,256,2048]{2,1,0:T(8,128)(2,1)} %refs_3_), custom_call_target="tpu_custom_call" | custom-call | flops 16777216 | bytes 20971520 | tf_op jit(solution)/shard_map/pallas_call | solution.py:411
  57.5 6.7 convert_element_type.462
  74.9 16.3 %collective-permute-done.10 = bf16[1056,256]{1,0:T(8,128)(2,1)} collective-permute-done((bf16[1056,256]{1,0:T(8,128)(2,1)S(1)}, bf16[1056,256]{1,0:T(8,128)(2,1)}, u32[]{:S(2)}, u32[]{:S(2)}) %collective-permute-start.10) | collective-permute-done | bytes 540704 | tf_op jit(solution)/shard_map/ppermute | solution.py:72
  91.2 3.5 collective-permute-start.14
  96.4 18.2 %collective-permute-done.7 = bf16[1072,256]{1,0:T(8,128)(2,1)} collective-permute-done((bf16[1072,256]{1,0:T(8,128)(2,1)}, bf16[1072,256]{1,0:T(8,128)(2,1)}, u32[]{:S(2)}, u32[]{:S(2)}) %collective-permute-start.7) | collective-permute-done | bytes 548896 | tf_op jit(solution)/shard_map/ppermute | solution.py:72
  138.4 17.7 %collective-permute-done.13 = bf16[1072,256]{1,0:T(8,128)(2,1)S(1)} collective-permute-done((bf16[1072,256]{1,0:T(8,128)(2,1)}, bf16[1072,256]{1,0:T(8,128)(2,1)S(1)}, u32[]{:S(2)}, u32[]{:S(2)}) %collective-permute-start.13) | collective-permute-done | bytes 548896 | tf_op jit(solution)/shard_map/ppermute | solution.py:72
  160.7 4.0 fusion.59
  168.1 3.2 fusion.165
  173.1 3.2 fusion.161
  176.3 3.1 fusion.163
  186.4 3.3 add_convert_fusion.7
  206.6 3.8 add_convert_fusion.6
  212.5 16.1 %shard_map.256 = (f32[4,256,704]{2,1,0:T(8,128)}, f32[4,256,704]{2,1,0:T(8,128)}, f32[4,256,704]{2,1,0:T(8,128)}, f32[4,256,704]{2,1,0:T(8,128)}, f32[4,256,704]...) custom-call(bf16[4,256,704]{2,1,0:T(8,128)(2,1)S(1)} %bitcast.194, ...), custom_call_target="tpu_custom_call" | custom-call | flops 2030043136 | bytes 23812096 | tf_op jit(solution)/shard_map/pallas_call | solution.py:374
  232.1 8.7 collective-permute-start.20
  244.0 6.6 collective-permute-start.22
  254.8 6.0 fusion.30
  262.7 3.2 convolution_convert_fusion.3
  279.3 3.2 convolution_convert_fusion.4
  295.3 4.4 collective-permute-done.29
  312.9 13.8 %collective-permute-done.27 = bf16[256,1536]{1,0:T(8,128)(2,1)S(1)} collective-permute-done((bf16[256,1536]{1,0:T(8,128)(2,1)}, bf16[256,1536]{1,0:T(8,128)(2,1)S(1)}, u32[]{:S(2)}, u32[]{:S(2)}) %collective-permute-start.27) | collective-permute-done | bytes 786464 | tf_op jit(solution)/shard_map/ppermute | solution.py:72
  328.9 4.1 collective-permute-done.30
  335.1 24.7 %collective-permute-done.28 = bf16[256,1536]{1,0:T(8,128)(2,1)S(1)} collective-permute-done((bf16[256,1536]{1,0:T(8,128)(2,1)S(1)}, bf16[256,1536]{1,0:T(8,128)(2,1)S(1)}, u32[]{:S(2)}, u32[]{:S(2)}) %collective-permute-start.28) | collective-permute-done | bytes 786464 | tf_op jit(solution)/shard_map/ppermute | solution.py:72
  360.9 5.5 shard_map.257
  375.3 5.1 shard_map.258
  380.3 20.3 %convolution_convert_fusion.1 = bf16[1024,3072]{1,0:T(8,128)(2,1)} fusion(bf16[1024,2048]{1,0:T(8,128)(2,1)} %bitcast.227, bf16[2048,1536]{1,0:T(8,128)(2,1)} %constant_dynamic-update-slice_fusion.18, bf16[2048,1536]{1,0:T(8,128)(2,1)} %constant_dynamic-update-slice_fusion.10), kind=kOutput, calls=%fused_computation.43 | convolution fusion | flops 12913213440 | bytes 23068672 | tf_op jit(solution)/shard_map/dot_general | solution.py:576
  400.6 8.1 fusion.6
  410.3 8.9 convolution_convert_fusion
  419.2 12.3 %shard_map.259 = bf16[1024,3072]{1,0:T(8,128)(2,1)} custom-call(bf16[1024,2048]{1,0:T(8,128)(2,1)} %bitcast.309, bf16[1536,2048]{1,0:T(8,128)(2,1)} %all-gather.2.cloned.1.call-done.w_down, bf16[1024,1536]{1,0:T(8,128)(2,1)S(1)} %get-tuple-element.224.act, bf16[1024,1536]{1,0:T(8,128)(2,1)} %get-tuple-element.225.slope), custom_call_target="tpu_custom_call" | custom-call | flops 6442450944 | bytes 23068672 | tf_op jit(solution)/shard_map/pallas_call | solution.py:754
  431.6 11.9 %fusion.44 = bf16[512,2048]{1,0:T(8,128)(2,1)} fusion(bf16[2048,1536]{1,0:T(8,128)(2,1)} %constant_dynamic-update-slice_fusion.18, bf16[2048,1536]{1,0:T(8,128)(2,1)} %constant_dynamic-update-slice_fusion.10, bf16[1024,3072]{1,0:T(8,128)(2,1)} %shard_map.259), kind=kOutput, calls=%fused_computation.91 | convolution fusion | flops 6468665344 | bytes 17825792 | tf_op jit(solution)/shard_map/dot_general | solution.py:568
  443.8 4.8 fusion.19
  450.8 10.9 %fusion.41 = bf16[512,2048]{1,0:T(8,128)(2,1)S(1)} fusion(bf16[2048,1536]{1,0:T(8,128)(2,1)} %constant_dynamic-update-slice_fusion.18, bf16[2048,1536]{1,0:T(8,128)(2,1)} %constant_dynamic-update-slice_fusion.10, bf16[1024,3072]{1,0:T(8,128)(2,1)} %shard_map.259), kind=kOutput, calls=%fused_computation.90 | convolution fusion | flops 6468665344 | bytes 17825792 | tf_op jit(solution)/shard_map/dot_general | solution.py:568
  478.8 33.4 %collective-permute-done.37 = bf16[512,2048]{1,0:T(8,128)(2,1)S(1)} collective-permute-done((bf16[512,2048]{1,0:T(8,128)(2,1)S(1)}, bf16[512,2048]{1,0:T(8,128)(2,1)S(1)}, u32[]{:S(2)}, u32[]{:S(2)}) %collective-permute-start.37) | collective-permute-done | bytes 2097184 | tf_op jit(solution)/shard_map/ppermute | solution.py:180
  513.0 6.5 collective-permute-done.39
  519.4 19.3 %collective-permute-done.41 = bf16[256,1536]{1,0:T(8,128)(2,1)S(1)} collective-permute-done((bf16[256,1536]{1,0:T(8,128)(2,1)S(1)}, bf16[256,1536]{1,0:T(8,128)(2,1)S(1)}, u32[]{:S(2)}, u32[]{:S(2)}) %collective-permute-start.41) | collective-permute-done | bytes 786464 | tf_op jit(solution)/shard_map/ppermute | solution.py:72
  548.7 7.4 shard_map.260
  556.1 37.7 %collective-permute-done.51 = bf16[256,1536]{1,0:T(8,128)(2,1)S(1)} collective-permute-done((bf16[256,1536]{1,0:T(8,128)(2,1)S(1)}, bf16[256,1536]{1,0:T(8,128)(2,1)S(1)}, u32[]{:S(2)}, u32[]{:S(2)}) %collective-permute-start.51) | collective-permute-done | bytes 786464 | tf_op jit(solution)/shard_map/ppermute | solution.py:72
  593.8 3.8 add_convert_fusion.12
  597.5 3.8 add_convert_fusion.10
  603.4 7.5 shard_map.261
  610.8 7.8 fusion.74
  618.6 7.7 shard_map.262
  628.3 3.9 add_convert_fusion.15
  639.6 8.2 convolution_convert_fusion.2
  647.8 3.9 add_convert_fusion.14
  653.6 15.9 %collective-permute-done.46 = f32[4,2,704]{2,1,0:T(2,128)S(1)} collective-permute-done((f32[4,2,704]{2,1,0:T(2,128)S(1)}, f32[4,2,704]{2,1,0:T(2,128)S(1)}, u32[]{:S(2)}, u32[]{:S(2)}) %collective-permute-start.46) | collective-permute-done | bytes 22560 | tf_op jit(solution)/shard_map/ppermute | solution.py:533
  670.8 4.4 collective-permute-done.47
  676.7 6.1 collective-permute-done.48
  686.4 19.1 %shard_map.263 = (bf16[2,4,256,704]{3,2,1,0:T(8,128)(2,1)}, bf16[4,256,704]{2,1,0:T(8,128)(2,1)S(1)}, bf16[4,256,704]{2,1,0:T(8,128)(2,1)S(1)}, f32[4,8,704]{2,1...) custom-call(f32[4,256,704]{2,1,0:T(8,128)} %bitcast.221, f32[4,256,704]{2,1,0:T(8,128)} %get-tuple-element.381.slope, ...), custom_call_target="tpu_custom_call" | custom-call | flops 2030043136 | bytes 38514432 | tf_op jit(solution)/shard_map/pallas_call | solution.py:374
  706.9 3.2 add_convert_fusion.9
  723.9 5.2 collective-permute-done.56
  730.0 3.3 collective-permute-done.57
  733.3 4.7 fusion.40
  747.8 3.6 fusion.39
  751.4 3.7 add_convert_fusion.1
  764.8 3.1 collective-permute-done.65
  780.6 4.1 copy.79
  786.9 8.7 shard_map.264
  804.9 3.1 collective-permute-done.61
  811.1 7.3 shard_map.265.refs_6_
  831.7 7.8 collective-permute-done.71
  843.4 9.0 collective-permute-done.72
  870.3 4.4 collective-permute-done.78
  888.0 7.2 shard_map.266
  (658 shorter events, 336.7 us)
Async XLA Ops:
  7.2 412.0 %all-gather.2.cloned.1.call-start = ((), (), s32[]{:S(2)}) async-start(), calls=%async_computation.1 | async-start | bytes 7077888 | tf_op jit(solution)/shard_map/all_gather | solution.py:640
  11.2 17.8 %collective-permute-start = (bf16[1056,256]{1,0:T(8,128)(2,1)}, bf16[1056,256]{1,0:T(8,128)(2,1)S(1)}, u32[]{:S(2)}, u32[]{:S(2)}) collective-permute-start(bf16[1056,256]{1,0:T(8,128)(2,1)} %pad_maximum_fusion.22), channel_id=1, source_target_pairs={{0,8},{8,16},{16,24},{24,28},{28,20},{20,12},{12,4},{4,0},{1,9},{9... | collective-permute-start | bytes 1622024 | tf_op jit(solution)/shard_map/ppermute | solution.py:72
  15.1 29.5 %collective-permute-start.2 = (bf16[1072,256]{1,0:T(8,128)(2,1)}, bf16[1072,256]{1,0:T(8,128)(2,1)}, u32[]{:S(2)}, u32[]{:S(2)}) collective-permute-start(bf16[1072,256]{1,0:T(8,128)(2,1)} %pad_maximum_fusion.21), channel_id=1, source_target_pairs={{0,8},{8,16},{16,24},{24,28},{28,20},{20,12},{12,4},{4,0},{1,9},{9... | collective-permute-start | bytes 1646600 | tf_op jit(solution)/shard_map/ppermute | solution.py:72
  17.1 27.5 %collective-permute-start.3 = (bf16[1072,256]{1,0:T(8,128)(2,1)}, bf16[1072,256]{1,0:T(8,128)(2,1)}, u32[]{:S(2)}, u32[]{:S(2)}) collective-permute-start(bf16[1072,256]{1,0:T(8,128)(2,1)} %pad_maximum_fusion.21), channel_id=1, source_target_pairs={{0,4},{8,0},{16,8},{24,16},{28,24},{20,28},{12,20},{4,12},{1,5},{9... | collective-permute-start | bytes 1646600 | tf_op jit(solution)/shard_map/ppermute | solution.py:72
  30.7 36.6 %collective-permute-start.11 = (bf16[1056,256]{1,0:T(8,128)(2,1)}, bf16[1056,256]{1,0:T(8,128)(2,1)}, u32[]{:S(2)}, u32[]{:S(2)}) collective-permute-start(bf16[1056,256]{1,0:T(8,128)(2,1)} %collective-permute-done.1), channel_id=1, source_target_pairs={{0,4},{8,0},{16,8},{24,16},{28,24},{20,28},{12,20},{4,12},{1,5},{9... | collective-permute-start | bytes 1622024 | tf_op jit(solution)/shard_map/ppermute | solution.py:72
  32.2 36.6 %collective-permute-start.5 = (bf16[1056,256]{1,0:T(8,128)(2,1)}, bf16[1056,256]{1,0:T(8,128)(2,1)S(1)}, u32[]{:S(2)}, u32[]{:S(2)}) collective-permute-start(bf16[1056,256]{1,0:T(8,128)(2,1)} %copy-done.72), channel_id=1, source_target_pairs={{0,8},{8,16},{16,24},{24,28},{28,20},{20,12},{12,4},{4,0},{1,9},{9... | collective-permute-start | bytes 1622024 | tf_op jit(solution)/shard_map/ppermute | solution.py:72
  48.0 22.0 %collective-permute-start.4 = (bf16[1072,256]{1,0:T(8,128)(2,1)}, bf16[1072,256]{1,0:T(8,128)(2,1)}, u32[]{:S(2)}, u32[]{:S(2)}) collective-permute-start(bf16[1072,256]{1,0:T(8,128)(2,1)} %collective-permute-done.2), channel_id=1, source_target_pairs={{0,8},{8,16},{16,24},{24,28},{28,20},{20,12},{12,4},{4,0},{1,9},{9... | collective-permute-start | bytes 1646600 | tf_op jit(solution)/shard_map/ppermute | solution.py:72
  49.6 46.8 %collective-permute-start.6 = (bf16[4,3,2048]{2,1,0:T(4,128)(2,1)S(1)}, bf16[4,3,2048]{2,1,0:T(4,128)(2,1)}, u32[]{:S(2)}, u32[]{:S(2)}) collective-permute-start(bf16[4,3,2048]{2,1,0:T(4,128)(2,1)S(1)} %slice.518), channel_id=1, source_target_pairs={{0,4},{4,8},{8,12},{12,16},{16,20},{20,24},{24,28},{1,5},{5,9},{9,... | collective-permute-start | bytes 147464 | tf_op jit(solution)/shard_map/ppermute | solution.py:639
  52.5 17.5 %collective-permute-start.8 = (bf16[1072,256]{1,0:T(8,128)(2,1)}, bf16[1072,256]{1,0:T(8,128)(2,1)}, u32[]{:S(2)}, u32[]{:S(2)}) collective-permute-start(bf16[1072,256]{1,0:T(8,128)(2,1)} %collective-permute-done.3), channel_id=1, source_target_pairs={{0,4},{8,0},{16,8},{24,16},{28,24},{20,28},{12,20},{4,12},{1,5},{9... | collective-permute-start | bytes 1646600 | tf_op jit(solution)/shard_map/ppermute | solution.py:72
  56.2 626.7 %reduce-scatter.2.cloned.1.call-start = ((), (), s32[]{:S(2)}) async-start(), calls=%async_computation.3 | async-start | bytes 7077888 | tf_op jit(solution)/shard_map/reduce_scatter | solution.py:746
  67.2 53.4 %collective-permute-start.12 = (bf16[1056,256]{1,0:T(8,128)(2,1)}, bf16[1056,256]{1,0:T(8,128)(2,1)}, u32[]{:S(2)}, u32[]{:S(2)}) collective-permute-start(bf16[1056,256]{1,0:T(8,128)(2,1)} %collective-permute-done.11), channel_id=1, source_target_pairs={{0,4},{8,0},{16,8},{24,16},{28,24},{20,28},{12,20},{4,12},{1,5},{9... | collective-permute-start | bytes 1622024 | tf_op jit(solution)/shard_map/ppermute | solution.py:72
  68.8 22.4 %collective-permute-start.10 = (bf16[1056,256]{1,0:T(8,128)(2,1)S(1)}, bf16[1056,256]{1,0:T(8,128)(2,1)}, u32[]{:S(2)}, u32[]{:S(2)}) collective-permute-start(bf16[1056,256]{1,0:T(8,128)(2,1)S(1)} %collective-permute-done.5), channel_id=1, source_target_pairs={{0,8},{8,16},{16,24},{24,28},{28,20},{20,12},{12,4},{4,0},{1,9},{9... | collective-permute-start | bytes 1622024 | tf_op jit(solution)/shard_map/ppermute | solution.py:72
  70.0 44.6 %collective-permute-start.7 = (bf16[1072,256]{1,0:T(8,128)(2,1)}, bf16[1072,256]{1,0:T(8,128)(2,1)}, u32[]{:S(2)}, u32[]{:S(2)}) collective-permute-start(bf16[1072,256]{1,0:T(8,128)(2,1)} %collective-permute-done.4), channel_id=1, source_target_pairs={{0,8},{8,16},{16,24},{24,28},{28,20},{20,12},{12,4},{4,0},{1,9},{9... | collective-permute-start | bytes 1646600 | tf_op jit(solution)/shard_map/ppermute | solution.py:72
  70.0 45.4 %collective-permute-start.9 = (bf16[1072,256]{1,0:T(8,128)(2,1)}, bf16[1072,256]{1,0:T(8,128)(2,1)}, u32[]{:S(2)}, u32[]{:S(2)}) collective-permute-start(bf16[1072,256]{1,0:T(8,128)(2,1)} %collective-permute-done.8), channel_id=1, source_target_pairs={{0,4},{8,0},{16,8},{24,16},{28,24},{20,28},{12,20},{4,12},{1,5},{9... | collective-permute-start | bytes 1646600 | tf_op jit(solution)/shard_map/ppermute | solution.py:72
  91.2 40.4 %collective-permute-start.14 = (bf16[1056,256]{1,0:T(8,128)(2,1)}, bf16[1056,256]{1,0:T(8,128)(2,1)}, u32[]{:S(2)}, u32[]{:S(2)}) collective-permute-start(bf16[1056,256]{1,0:T(8,128)(2,1)} %collective-permute-done.10), channel_id=1, source_target_pairs={{0,8},{8,16},{16,24},{24,28},{28,20},{20,12},{12,4},{4,0},{1,9},{9... | collective-permute-start | bytes 1622024 | tf_op jit(solution)/shard_map/ppermute | solution.py:72
  120.7 35.3 %collective-permute-start.13 = (bf16[1072,256]{1,0:T(8,128)(2,1)}, bf16[1072,256]{1,0:T(8,128)(2,1)S(1)}, u32[]{:S(2)}, u32[]{:S(2)}) collective-permute-start(bf16[1072,256]{1,0:T(8,128)(2,1)} %collective-permute-done.9), channel_id=1, source_target_pairs={{0,4},{8,0},{16,8},{24,16},{28,24},{20,28},{12,20},{4,12},{1,5},{9... | collective-permute-start | bytes 1646600 | tf_op jit(solution)/shard_map/ppermute | solution.py:72
  123.2 87.2 %collective-permute-start.15 = (bf16[256,1536]{1,0:T(8,128)(2,1)}, bf16[256,1536]{1,0:T(8,128)(2,1)}, u32[]{:S(2)}, u32[]{:S(2)}) collective-permute-start(bf16[256,1536]{1,0:T(8,128)(2,1)} %get-tuple-element.189), channel_id=1, source_target_pairs={{0,8},{8,16},{16,24},{24,28},{28,20},{20,12},{12,4},{4,0},{1,9},{9... | collective-permute-start | bytes 2359304 | tf_op jit(solution)/shard_map/ppermute | solution.py:72
  123.2 87.2 %collective-permute-start.16 = (bf16[256,1536]{1,0:T(8,128)(2,1)}, bf16[256,1536]{1,0:T(8,128)(2,1)}, u32[]{:S(2)}, u32[]{:S(2)}) collective-permute-start(bf16[256,1536]{1,0:T(8,128)(2,1)} %get-tuple-element.189), channel_id=1, source_target_pairs={{0,4},{8,0},{16,8},{24,16},{28,24},{20,28},{12,20},{4,12},{1,5},{9... | collective-permute-start | bytes 2359304 | tf_op jit(solution)/shard_map/ppermute | solution.py:72
  131.6 96.9 %collective-permute-start.17 = (bf16[256,1536]{1,0:T(8,128)(2,1)}, bf16[256,1536]{1,0:T(8,128)(2,1)}, u32[]{:S(2)}, u32[]{:S(2)}) collective-permute-start(bf16[256,1536]{1,0:T(8,128)(2,1)} %get-tuple-element.196), channel_id=1, source_target_pairs={{0,8},{8,16},{16,24},{24,28},{28,20},{20,12},{12,4},{4,0},{1,9},{9... | collective-permute-start | bytes 2359304 | tf_op jit(solution)/shard_map/ppermute | solution.py:72
  196.1 32.4 %collective-permute-start.18 = (bf16[256,1536]{1,0:T(8,128)(2,1)}, bf16[256,1536]{1,0:T(8,128)(2,1)S(1)}, u32[]{:S(2)}, u32[]{:S(2)}) collective-permute-start(bf16[256,1536]{1,0:T(8,128)(2,1)} %get-tuple-element.196), channel_id=1, source_target_pairs={{0,4},{8,0},{16,8},{24,16},{28,24},{20,28},{12,20},{4,12},{1,5},{9... | collective-permute-start | bytes 2359304 | tf_op jit(solution)/shard_map/ppermute | solution.py:72
  210.4 43.6 %collective-permute-start.23 = (bf16[256,1536]{1,0:T(8,128)(2,1)}, bf16[256,1536]{1,0:T(8,128)(2,1)}, u32[]{:S(2)}, u32[]{:S(2)}) collective-permute-start(bf16[256,1536]{1,0:T(8,128)(2,1)} %collective-permute-done.15), channel_id=1, source_target_pairs={{0,8},{8,16},{16,24},{24,28},{28,20},{20,12},{12,4},{4,0},{1,9},{9... | collective-permute-start | bytes 2359304 | tf_op jit(solution)/shard_map/ppermute | solution.py:72
  212.4 41.6 %collective-permute-start.24 = (bf16[256,1536]{1,0:T(8,128)(2,1)}, bf16[256,1536]{1,0:T(8,128)(2,1)S(1)}, u32[]{:S(2)}, u32[]{:S(2)}) collective-permute-start(bf16[256,1536]{1,0:T(8,128)(2,1)} %collective-permute-done.16), channel_id=1, source_target_pairs={{0,4},{8,0},{16,8},{24,16},{28,24},{20,28},{12,20},{4,12},{1,5},{9... | collective-permute-start | bytes 2359304 | tf_op jit(solution)/shard_map/ppermute | solution.py:72
  279.3 20.3 %collective-permute-start.29 = (bf16[256,1536]{1,0:T(8,128)(2,1)S(1)}, bf16[256,1536]{1,0:T(8,128)(2,1)S(1)}, u32[]{:S(2)}, u32[]{:S(2)}) collective-permute-start(bf16[256,1536]{1,0:T(8,128)(2,1)S(1)} %copy-done.81), channel_id=1, source_target_pairs={{0,4},{8,0},{16,8},{24,16},{28,24},{20,28},{12,20},{4,12},{1,5},{9... | collective-permute-start | bytes 2359304 | tf_op jit(solution)/shard_map/ppermute | solution.py:72
  283.4 50.8 %collective-permute-start.26 = (bf16[512,2048]{1,0:T(8,128)(2,1)S(1)}, bf16[512,2048]{1,0:T(8,128)(2,1)S(1)}, u32[]{:S(2)}, u32[]{:S(2)}) collective-permute-start(bf16[512,2048]{1,0:T(8,128)(2,1)S(1)} %add_convert_fusion.5), channel_id=1, source_target_pairs={{0,2},{1,3},{2,0},{3,1},{4,6},{5,7},{6,4},{7,5},{8,10},{9,11},{10,... | collective-permute-start | bytes 6291464 | tf_op jit(solution)/shard_map/ppermute | solution.py:180
  289.3 20.6 %collective-permute-start.34 = (bf16[256,1536]{1,0:T(8,128)(2,1)}, bf16[256,1536]{1,0:T(8,128)(2,1)S(1)}, u32[]{:S(2)}, u32[]{:S(2)}) collective-permute-start(bf16[256,1536]{1,0:T(8,128)(2,1)} %collective-permute-done.17), channel_id=1, source_target_pairs={{0,8},{8,16},{16,24},{24,28},{28,20},{20,12},{12,4},{4,0},{1,9},{9... | collective-permute-start | bytes 2359304 | tf_op jit(solution)/shard_map/ppermute | solution.py:72
  293.2 33.6 %collective-permute-start.27 = (bf16[256,1536]{1,0:T(8,128)(2,1)}, bf16[256,1536]{1,0:T(8,128)(2,1)S(1)}, u32[]{:S(2)}, u32[]{:S(2)}) collective-permute-start(bf16[256,1536]{1,0:T(8,128)(2,1)} %collective-permute-done.23), channel_id=1, source_target_pairs={{0,8},{8,16},{16,24},{24,28},{28,20},{20,12},{12,4},{4,0},{1,9},{9... | collective-permute-start | bytes 2359304 | tf_op jit(solution)/shard_map/ppermute | solution.py:72
  293.3 35.6 %collective-permute-start.31 = (bf16[256,1536]{1,0:T(8,128)(2,1)S(1)}, bf16[256,1536]{1,0:T(8,128)(2,1)S(1)}, u32[]{:S(2)}, u32[]{:S(2)}) collective-permute-start(bf16[256,1536]{1,0:T(8,128)(2,1)S(1)} %collective-permute-done.24), channel_id=1, source_target_pairs={{0,4},{8,0},{16,8},{24,16},{28,24},{20,28},{12,20},{4,12},{1,5},{9... | collective-permute-start | bytes 2359304 | tf_op jit(solution)/shard_map/ppermute | solution.py:72
  299.7 33.3 %collective-permute-start.30 = (bf16[256,1536]{1,0:T(8,128)(2,1)S(1)}, bf16[256,1536]{1,0:T(8,128)(2,1)S(1)}, u32[]{:S(2)}, u32[]{:S(2)}) collective-permute-start(bf16[256,1536]{1,0:T(8,128)(2,1)S(1)} %collective-permute-done.29), channel_id=1, source_target_pairs={{0,4},{8,0},{16,8},{24,16},{28,24},{20,28},{12,20},{4,12},{1,5},{9... | collective-permute-start | bytes 2359304 | tf_op jit(solution)/shard_map/ppermute | solution.py:72
  309.9 49.8 %collective-permute-start.35 = (bf16[256,1536]{1,0:T(8,128)(2,1)S(1)}, bf16[256,1536]{1,0:T(8,128)(2,1)S(1)}, u32[]{:S(2)}, u32[]{:S(2)}) collective-permute-start(bf16[256,1536]{1,0:T(8,128)(2,1)S(1)} %collective-permute-done.34), channel_id=1, source_target_pairs={{0,8},{8,16},{16,24},{24,28},{28,20},{20,12},{12,4},{4,0},{1,9},{9... | collective-permute-start | bytes 2359304 | tf_op jit(solution)/shard_map/ppermute | solution.py:72
  326.8 33.0 %collective-permute-start.28 = (bf16[256,1536]{1,0:T(8,128)(2,1)S(1)}, bf16[256,1536]{1,0:T(8,128)(2,1)S(1)}, u32[]{:S(2)}, u32[]{:S(2)}) collective-permute-start(bf16[256,1536]{1,0:T(8,128)(2,1)S(1)} %collective-permute-done.27), channel_id=1, source_target_pairs={{0,8},{8,16},{16,24},{24,28},{28,20},{20,12},{12,4},{4,0},{1,9},{9... | collective-permute-start | bytes 2359304 | tf_op jit(solution)/shard_map/ppermute | solution.py:72
  333.0 26.8 %collective-permute-start.32 = (bf16[256,1536]{1,0:T(8,128)(2,1)S(1)}, bf16[256,1536]{1,0:T(8,128)(2,1)S(1)}, u32[]{:S(2)}, u32[]{:S(2)}) collective-permute-start(bf16[256,1536]{1,0:T(8,128)(2,1)S(1)} %collective-permute-done.30), channel_id=1, source_target_pairs={{0,4},{8,0},{16,8},{24,16},{28,24},{20,28},{12,20},{4,12},{1,5},{9... | collective-permute-start | bytes 2359304 | tf_op jit(solution)/shard_map/ppermute | solution.py:72
  443.5 18.2 %collective-permute-start.36 = (bf16[512,2048]{1,0:T(8,128)(2,1)}, bf16[512,2048]{1,0:T(8,128)(2,1)}, u32[]{:S(2)}, u32[]{:S(2)}) collective-permute-start(bf16[512,2048]{1,0:T(8,128)(2,1)} %fusion.44), channel_id=1, source_target_pairs={{0,1},{1,0},{2,3},{3,2},{4,5},{5,4},{6,7},{7,6},{8,9},{9,8},{10,11... | collective-permute-start | bytes 6291464 | tf_op jit(solution)/shard_map/ppermute | solution.py:175
  448.7 336.0 %all-reduce.17.cloned.1.call-start = ((), (), s32[]{:S(2)}) async-start(), calls=%async_computation.2 | async-start | bytes 8388608 | tf_op jit(solution)/shard_map/psum | solution.py:792
  464.4 47.8 %collective-permute-start.37 = (bf16[512,2048]{1,0:T(8,128)(2,1)S(1)}, bf16[512,2048]{1,0:T(8,128)(2,1)S(1)}, u32[]{:S(2)}, u32[]{:S(2)}) collective-permute-start(bf16[512,2048]{1,0:T(8,128)(2,1)S(1)} %add_convert_fusion.3), channel_id=1, source_target_pairs={{0,2},{1,3},{2,0},{3,1},{4,6},{5,7},{6,4},{7,5},{8,10},{9,11},{10,... | collective-permute-start | bytes 6291464 | tf_op jit(solution)/shard_map/ppermute | solution.py:180
  471.3 41.7 %collective-permute-start.38 = (bf16[256,1536]{1,0:T(8,128)(2,1)S(1)}, bf16[256,1536]{1,0:T(8,128)(2,1)S(1)}, u32[]{:S(2)}, u32[]{:S(2)}) collective-permute-start(bf16[256,1536]{1,0:T(8,128)(2,1)S(1)} %convolution_convert_fusion.8), channel_id=1, source_target_pairs={{0,8},{8,16},{16,24},{24,28},{28,20},{20,12},{12,4},{4,0},{1,9},{9... | collective-permute-start | bytes 2359304 | tf_op jit(solution)/shard_map/ppermute | solution.py:72
  473.9 45.5 %collective-permute-start.39 = (bf16[256,1536]{1,0:T(8,128)(2,1)S(1)}, bf16[256,1536]{1,0:T(8,128)(2,1)S(1)}, u32[]{:S(2)}, u32[]{:S(2)}) collective-permute-start(bf16[256,1536]{1,0:T(8,128)(2,1)S(1)} %convolution_convert_fusion.7), channel_id=1, source_target_pairs={{0,4},{8,0},{16,8},{24,16},{28,24},{20,28},{12,20},{4,12},{1,5},{9... | collective-permute-start | bytes 2359304 | tf_op jit(solution)/shard_map/ppermute | solution.py:72
  475.4 63.3 %collective-permute-start.41 = (bf16[256,1536]{1,0:T(8,128)(2,1)S(1)}, bf16[256,1536]{1,0:T(8,128)(2,1)S(1)}, u32[]{:S(2)}, u32[]{:S(2)}) collective-permute-start(bf16[256,1536]{1,0:T(8,128)(2,1)S(1)} %convolution_convert_fusion.6), channel_id=1, source_target_pairs={{0,8},{8,16},{16,24},{24,28},{28,20},{20,12},{12,4},{4,0},{1,9},{9... | collective-permute-start | bytes 2359304 | tf_op jit(solution)/shard_map/ppermute | solution.py:72
  478.3 68.2 %collective-permute-start.43 = (bf16[256,1536]{1,0:T(8,128)(2,1)S(1)}, bf16[256,1536]{1,0:T(8,128)(2,1)S(1)}, u32[]{:S(2)}, u32[]{:S(2)}) collective-permute-start(bf16[256,1536]{1,0:T(8,128)(2,1)S(1)} %convolution_convert_fusion.5), channel_id=1, source_target_pairs={{0,4},{8,0},{16,8},{24,16},{28,24},{20,28},{12,20},{4,12},{1,5},{9... | collective-permute-start | bytes 2359304 | tf_op jit(solution)/shard_map/ppermute | solution.py:72
  519.4 84.0 %collective-permute-start.40 = (bf16[512,2048]{1,0:T(8,128)(2,1)S(1)}, bf16[512,2048]{1,0:T(8,128)(2,1)S(1)}, u32[]{:S(2)}, u32[]{:S(2)}) collective-permute-start(bf16[512,2048]{1,0:T(8,128)(2,1)S(1)} %add_convert_fusion.2), channel_id=1, source_target_pairs={{0,1},{1,0},{2,3},{3,2},{4,5},{5,4},{6,7},{7,6},{8,9},{9,8},{10,11... | collective-permute-start | bytes 6291464 | tf_op jit(solution)/shard_map/ppermute | solution.py:175
  539.7 71.1 %collective-permute-start.42 = (bf16[256,1536]{1,0:T(8,128)(2,1)S(1)}, bf16[256,1536]{1,0:T(8,128)(2,1)S(1)}, u32[]{:S(2)}, u32[]{:S(2)}) collective-permute-start(bf16[256,1536]{1,0:T(8,128)(2,1)S(1)} %add_convert_fusion.17), channel_id=1, source_target_pairs={{0,8},{8,16},{16,24},{24,28},{28,20},{20,12},{12,4},{4,0},{1,9},{9... | collective-permute-start | bytes 2359304 | tf_op jit(solution)/shard_map/ppermute | solution.py:72
  543.3 50.5 %collective-permute-start.51 = (bf16[256,1536]{1,0:T(8,128)(2,1)S(1)}, bf16[256,1536]{1,0:T(8,128)(2,1)S(1)}, u32[]{:S(2)}, u32[]{:S(2)}) collective-permute-start(bf16[256,1536]{1,0:T(8,128)(2,1)S(1)} %add_convert_fusion.13), channel_id=1, source_target_pairs={{0,8},{8,16},{16,24},{24,28},{28,20},{20,12},{12,4},{4,0},{1,9},{9... | collective-permute-start | bytes 2359304 | tf_op jit(solution)/shard_map/ppermute | solution.py:72
  545.8 51.7 %collective-permute-start.53 = (bf16[256,1536]{1,0:T(8,128)(2,1)S(1)}, bf16[256,1536]{1,0:T(8,128)(2,1)S(1)}, u32[]{:S(2)}, u32[]{:S(2)}) collective-permute-start(bf16[256,1536]{1,0:T(8,128)(2,1)S(1)} %add_convert_fusion.11), channel_id=1, source_target_pairs={{0,4},{8,0},{16,8},{24,16},{28,24},{20,28},{12,20},{4,12},{1,5},{9... | collective-permute-start | bytes 2359304 | tf_op jit(solution)/shard_map/ppermute | solution.py:72
  547.5 63.3 %collective-permute-start.44 = (bf16[256,1536]{1,0:T(8,128)(2,1)S(1)}, bf16[256,1536]{1,0:T(8,128)(2,1)S(1)}, u32[]{:S(2)}, u32[]{:S(2)}) collective-permute-start(bf16[256,1536]{1,0:T(8,128)(2,1)S(1)} %add_convert_fusion.16), channel_id=1, source_target_pairs={{0,4},{8,0},{16,8},{24,16},{28,24},{20,28},{12,20},{4,12},{1,5},{9... | collective-permute-start | bytes 2359304 | tf_op jit(solution)/shard_map/ppermute | solution.py:72
  597.5 108.0 %collective-permute-start.52 = (bf16[256,1536]{1,0:T(8,128)(2,1)}, bf16[256,1536]{1,0:T(8,128)(2,1)}, u32[]{:S(2)}, u32[]{:S(2)}) collective-permute-start(bf16[256,1536]{1,0:T(8,128)(2,1)} %add_convert_fusion.12), channel_id=1, source_target_pairs={{0,8},{8,16},{16,24},{24,28},{28,20},{20,12},{12,4},{4,0},{1,9},{9... | collective-permute-start | bytes 2359304 | tf_op jit(solution)/shard_map/ppermute | solution.py:72
  601.3 104.2 %collective-permute-start.54 = (bf16[256,1536]{1,0:T(8,128)(2,1)}, bf16[256,1536]{1,0:T(8,128)(2,1)}, u32[]{:S(2)}, u32[]{:S(2)}) collective-permute-start(bf16[256,1536]{1,0:T(8,128)(2,1)} %add_convert_fusion.10), channel_id=1, source_target_pairs={{0,4},{8,0},{16,8},{24,16},{28,24},{20,28},{12,20},{4,12},{1,5},{9... | collective-permute-start | bytes 2359304 | tf_op jit(solution)/shard_map/ppermute | solution.py:72
  626.3 25.9 %collective-permute-start.45 = (f32[4,2,704]{2,1,0:T(2,128)S(1)}, f32[4,2,704]{2,1,0:T(2,128)S(1)}, u32[]{:S(2)}, u32[]{:S(2)}) collective-permute-start(f32[4,2,704]{2,1,0:T(2,128)S(1)} %slice.612), channel_id=1, source_target_pairs={{4,0},{8,4},{12,8},{16,12},{20,16},{24,20},{28,24},{5,1},{9,5},{13... | collective-permute-start | bytes 67592 | tf_op jit(solution)/shard_map/ppermute | solution.py:533
  632.3 53.2 %collective-permute-start.49 = (bf16[256,1536]{1,0:T(8,128)(2,1)}, bf16[256,1536]{1,0:T(8,128)(2,1)}, u32[]{:S(2)}, u32[]{:S(2)}) collective-permute-start(bf16[256,1536]{1,0:T(8,128)(2,1)} %add_convert_fusion.15), channel_id=1, source_target_pairs={{0,8},{8,16},{16,24},{24,28},{28,20},{20,12},{12,4},{4,0},{1,9},{9... | collective-permute-start | bytes 2359304 | tf_op jit(solution)/shard_map/ppermute | solution.py:72
  651.8 33.6 %collective-permute-start.50 = (bf16[256,1536]{1,0:T(8,128)(2,1)}, bf16[256,1536]{1,0:T(8,128)(2,1)S(1)}, u32[]{:S(2)}, u32[]{:S(2)}) collective-permute-start(bf16[256,1536]{1,0:T(8,128)(2,1)} %add_convert_fusion.14), channel_id=1, source_target_pairs={{0,4},{8,0},{16,8},{24,16},{28,24},{20,28},{12,20},{4,12},{1,5},{9... | collective-permute-start | bytes 2359304 | tf_op jit(solution)/shard_map/ppermute | solution.py:72
  652.3 17.2 %collective-permute-start.46 = (f32[4,2,704]{2,1,0:T(2,128)S(1)}, f32[4,2,704]{2,1,0:T(2,128)S(1)}, u32[]{:S(2)}, u32[]{:S(2)}) collective-permute-start(f32[4,2,704]{2,1,0:T(2,128)S(1)} %pad_add_fusion.1), channel_id=1, source_target_pairs={{8,0},{12,4},{16,8},{20,12},{24,16},{28,20},{9,1},{13,5},{17,9},{2... | collective-permute-start | bytes 67592 | tf_op jit(solution)/shard_map/ppermute | solution.py:533
  676.6 177.7 %all-reduce.19.cloned.1.call-start = ((), (), s32[]{:S(2)}) async-start(), calls=%async_computation.4 | async-start | bytes 1081344 | tf_op jit(solution)/shard_map/psum | solution.py:899
  710.1 19.0 %collective-permute-start.56 = (bf16[256,1536]{1,0:T(8,128)(2,1)S(1)}, bf16[256,1536]{1,0:T(8,128)(2,1)S(1)}, u32[]{:S(2)}, u32[]{:S(2)}) collective-permute-start(bf16[256,1536]{1,0:T(8,128)(2,1)S(1)} %add_convert_fusion.9), channel_id=1, source_target_pairs={{0,8},{8,16},{16,24},{24,28},{28,20},{20,12},{12,4},{4,0},{1,9},{9... | collective-permute-start | bytes 2359304 | tf_op jit(solution)/shard_map/ppermute | solution.py:72
  715.1 18.2 %collective-permute-start.57 = (bf16[256,1536]{1,0:T(8,128)(2,1)S(1)}, bf16[256,1536]{1,0:T(8,128)(2,1)S(1)}, u32[]{:S(2)}, u32[]{:S(2)}) collective-permute-start(bf16[256,1536]{1,0:T(8,128)(2,1)S(1)} %add_convert_fusion.8), channel_id=1, source_target_pairs={{0,4},{8,0},{16,8},{24,16},{28,24},{20,28},{12,20},{4,12},{1,5},{9... | collective-permute-start | bytes 2359304 | tf_op jit(solution)/shard_map/ppermute | solution.py:72
  715.4 39.8 %collective-permute-start.59 = (bf16[704,256]{1,0:T(8,128)(2,1)}, bf16[704,256]{1,0:T(8,128)(2,1)}, u32[]{:S(2)}, u32[]{:S(2)}) collective-permute-start(bf16[704,256]{1,0:T(8,128)(2,1)} %convolution_convert_fusion.16), channel_id=1, source_target_pairs={{0,8},{8,16},{16,24},{24,28},{28,20},{20,12},{12,4},{4,0},{1,9},{9... | collective-permute-start | bytes 1081352 | tf_op jit(solution)/shard_map/ppermute | solution.py:72
  717.2 38.0 %collective-permute-start.60 = (bf16[704,256]{1,0:T(8,128)(2,1)}, bf16[704,256]{1,0:T(8,128)(2,1)}, u32[]{:S(2)}, u32[]{:S(2)}) collective-permute-start(bf16[704,256]{1,0:T(8,128)(2,1)} %convolution_convert_fusion.15), channel_id=1, source_target_pairs={{0,4},{8,0},{16,8},{24,16},{28,24},{20,28},{12,20},{4,12},{1,5},{9... | collective-permute-start | bytes 1081352 | tf_op jit(solution)/shard_map/ppermute | solution.py:72
  759.9 48.1 %collective-permute-start.61 = (bf16[512,2048]{1,0:T(8,128)(2,1)}, bf16[512,2048]{1,0:T(8,128)(2,1)}, u32[]{:S(2)}, u32[]{:S(2)}) collective-permute-start(bf16[512,2048]{1,0:T(8,128)(2,1)} %add_convert_fusion.1), channel_id=1, source_target_pairs={{0,2},{1,3},{2,0},{3,1},{4,6},{5,7},{6,4},{7,5},{8,10},{9,11},{10,... | collective-permute-start | bytes 6291464 | tf_op jit(solution)/shard_map/ppermute | solution.py:180
  774.7 21.0 %collective-permute-start.63 = (bf16[704,256]{1,0:T(8,128)(2,1)}, bf16[704,256]{1,0:T(8,128)(2,1)S(1)}, u32[]{:S(2)}, u32[]{:S(2)}) collective-permute-start(bf16[704,256]{1,0:T(8,128)(2,1)} %fusion.53), channel_id=1, source_target_pairs={{0,8},{8,16},{16,24},{24,28},{28,20},{20,12},{12,4},{4,0},{1,9},{9... | collective-permute-start | bytes 1081352 | tf_op jit(solution)/shard_map/ppermute | solution.py:72
  776.4 21.4 %collective-permute-start.73 = (bf16[704,256]{1,0:T(8,128)(2,1)S(1)}, bf16[704,256]{1,0:T(8,128)(2,1)}, u32[]{:S(2)}, u32[]{:S(2)}) collective-permute-start(bf16[704,256]{1,0:T(8,128)(2,1)S(1)} %convolution_convert_fusion.12), channel_id=1, source_target_pairs={{0,8},{8,16},{16,24},{24,28},{28,20},{20,12},{12,4},{4,0},{1,9},{9... | collective-permute-start | bytes 1081352 | tf_op jit(solution)/shard_map/ppermute | solution.py:72
  780.1 22.0 %collective-permute-start.81 = (bf16[704,256]{1,0:T(8,128)(2,1)}, bf16[704,256]{1,0:T(8,128)(2,1)}, u32[]{:S(2)}, u32[]{:S(2)}) collective-permute-start(bf16[704,256]{1,0:T(8,128)(2,1)} %fusion.57), channel_id=1, source_target_pairs={{0,4},{8,0},{16,8},{24,16},{28,24},{20,28},{12,20},{4,12},{1,5},{9... | collective-permute-start | bytes 1081352 | tf_op jit(solution)/shard_map/ppermute | solution.py:72
  799.4 19.8 %collective-permute-start.74 = (bf16[704,256]{1,0:T(8,128)(2,1)S(1)}, bf16[704,256]{1,0:T(8,128)(2,1)S(1)}, u32[]{:S(2)}, u32[]{:S(2)}) collective-permute-start(bf16[704,256]{1,0:T(8,128)(2,1)S(1)} %add_convert_fusion.27), channel_id=1, source_target_pairs={{0,8},{8,16},{16,24},{24,28},{28,20},{20,12},{12,4},{4,0},{1,9},{9... | collective-permute-start | bytes 1081352 | tf_op jit(solution)/shard_map/ppermute | solution.py:72
  802.1 21.5 %collective-permute-start.82 = (bf16[704,256]{1,0:T(8,128)(2,1)}, bf16[704,256]{1,0:T(8,128)(2,1)}, u32[]{:S(2)}, u32[]{:S(2)}) collective-permute-start(bf16[704,256]{1,0:T(8,128)(2,1)} %convolution_convert_fusion.11), channel_id=1, source_target_pairs={{0,4},{8,0},{16,8},{24,16},{28,24},{20,28},{12,20},{4,12},{1,5},{9... | collective-permute-start | bytes 1081352 | tf_op jit(solution)/shard_map/ppermute | solution.py:72
  826.6 61.4 %collective-permute-start.68 = (bf16[512,2048]{1,0:T(8,128)(2,1)S(1)}, bf16[512,2048]{1,0:T(8,128)(2,1)}, u32[]{:S(2)}, u32[]{:S(2)}) collective-permute-start(bf16[512,2048]{1,0:T(8,128)(2,1)S(1)} %add_convert_fusion), channel_id=1, source_target_pairs={{0,1},{1,0},{2,3},{3,2},{4,5},{5,4},{6,7},{7,6},{8,9},{9,8},{10,11... | collective-permute-start | bytes 6291464 | tf_op jit(solution)/shard_map/ppermute | solution.py:175
  826.6 28.6 %collective-permute-start.83 = (bf16[704,256]{1,0:T(8,128)(2,1)}, bf16[704,256]{1,0:T(8,128)(2,1)}, u32[]{:S(2)}, u32[]{:S(2)}) collective-permute-start(bf16[704,256]{1,0:T(8,128)(2,1)} %add_convert_fusion.20), channel_id=1, source_target_pairs={{0,4},{8,0},{16,8},{24,16},{28,24},{20,28},{12,20},{4,12},{1,5},{9... | collective-permute-start | bytes 1081352 | tf_op jit(solution)/shard_map/ppermute | solution.py:72
  830.1 27.6 %collective-permute-start.77 = (bf16[704,256]{1,0:T(8,128)(2,1)}, bf16[704,256]{1,0:T(8,128)(2,1)}, u32[]{:S(2)}, u32[]{:S(2)}) collective-permute-start(bf16[704,256]{1,0:T(8,128)(2,1)} %add_convert_fusion.24), channel_id=1, source_target_pairs={{0,4},{8,0},{16,8},{24,16},{28,24},{20,28},{12,20},{4,12},{1,5},{9... | collective-permute-start | bytes 1081352 | tf_op jit(solution)/shard_map/ppermute | solution.py:72
  864.7 20.4 %collective-permute-start.80 = (bf16[704,256]{1,0:T(8,128)(2,1)}, bf16[704,256]{1,0:T(8,128)(2,1)}, u32[]{:S(2)}, u32[]{:S(2)}) collective-permute-start(bf16[704,256]{1,0:T(8,128)(2,1)} %add_convert_fusion.21), channel_id=1, source_target_pairs={{0,8},{8,16},{16,24},{24,28},{28,20},{20,12},{12,4},{4,0},{1,9},{9... | collective-permute-start | bytes 1081352 | tf_op jit(solution)/shard_map/ppermute | solution.py:72
  (161 other events, 2071.8 us)
Sparse Core Ops, SparseCore 0:
  56.3 156.6 all-gather.1
  448.8 168.3 reduce-scatter.1
  676.7 86.6 all-reduce.16
  767.7 82.9 all-reduce.18

commit v5 on v4

--- a/solution.py
+++ b/solution.py
@@ -17,6 +17,7 @@
 vmem_bytes = 48 * 2**20
 ring_most = 8
 lane_depth = 2
+landings = (3, 1, 1, 1, 1, 1, 0, 4, 1, 1, 1, 1, 0, 0, 2, 1, 1, 0, 1, 1, 1, 0, 0, 4)
 norm_rows = 128
 
 
@@ -101,6 +102,11 @@
             self.issue()
         return values
 
+    def need(self, weights):
+        flows = [flow for w in weights for flow in w.flows.values()]
+        while any(len(flow.got) < flow.count for flow in flows):
+            self.land()
+
     def drain(self):
         while self.queue[1] or self.queue[-1] or self.flying[1] or self.flying[-1]:
             self.land()
@@ -180,9 +186,9 @@
     return lax.ppermute(values, "tp", [(i, i ^ 2) for i in range(size)])
 
 
-def tp_sum(part, others=lambda v: v, chips=lambda v: v, totals=lambda v: v):
+def tp_sum(part, others=lambda v: v, owns=lambda v: v, chips=lambda v: v, totals=lambda v: v):
     got = core_swap(others(part(1).astype(bf16)))
-    own = lax.optimization_barrier(part(0).astype(bf16))
+    own = owns(lax.optimization_barrier(part(0).astype(bf16)))
     chip = chips((own.astype(f32) + got.astype(f32)).astype(bf16))
     far = chip_swap(chip)
     total = totals((chip.astype(f32) + far.astype(f32)).astype(bf16))
@@ -456,9 +462,8 @@
     return [*done[:count], *(a + b for a, b in zip(ready[count:], done[count:]))]
 
 
-def enter_kernel(sequence, chunk, tokens, cotangent, x, cot, turned):
+def enter_kernel(sequence, chunk, tokens, cotangent, x, cot):
     part = x.shape[1] // chunk.shape[0]
-    turned[...] = cotangent[...]
     for k in range(chunk.shape[0]):
         at = pl.ds(pl.multiple_of(chunk[k] * part, part), part)
         x[:, k * part : (k + 1) * part] = tokens[:, at]
@@ -513,8 +518,8 @@
     part = middle.shape[1] // chunk.shape[0]
     for k in range(chunk.shape[0]):
         at = pl.ds(pl.multiple_of(chunk[k] * part, part), part)
-        total = middle[:, k * part : (k + 1) * part] + added[:, at].astype(f32)
-        output[:, at] = total.astype(bf16)
+        near = slice(k * part, (k + 1) * part)
+        output[:, at] = (middle[:, near] + added[:, near].astype(f32)).astype(bf16)
 
 
 def own_order(array, order, back=False):
@@ -621,59 +626,65 @@
         jnp.concatenate([w_in[1], out_weight[half_lanes:], own_gain], axis=0), -1, n, chunk
     )
     mlp = [Gather(mlp_weight[:, 0], 1, n, chunk), Gather(mlp_weight[:, 1], -1, n, chunk)]
+    downs = Gather(down_weight, 1, n, chunk)
     ring.add([first, second])
-    ring.add(mlp)
+    ring.add([*mlp, downs], [0, 0, 3])
     ring.issue()
 
     tokens, cotangent = ring.land((tokens, cotangent))
     if tiled:
-        x, cot, cot_turned = by_rows(enter_kernel, [tokens, cotangent], [], [bf16] * 3, 0, move)
+        x, cot = by_rows(enter_kernel, [tokens, cotangent], [], [bf16] * 2, 0, move)
     else:
         x, cot = own_order(tokens, move), own_order(cotangent, move)
-        cot_turned = cotangent[sequence]
     full = x.shape
     part_full = (seqs // 2, piece, width)
-    x, cot, cot_turned, down_weight, tail_rows = ring.land(
-        (x, cot, cot_turned, down_weight, tokens[:, piece - taps + 1 :])
-    )
+    x, cot, tail_rows = ring.land((x, cot, tokens[:, piece - taps + 1 :]))
     behind_rows = lax.ppermute(tail_rows, "seq", [(i, i + 1) for i in range(n - 1)])
-    w_down = lax.all_gather(down_weight, "seq", axis=1, tiled=True)
-    cot_turned = cot_turned.reshape(rows, width)
+    grad_low = cot.reshape(rows, width)
     start = x.reshape(rows, width).astype(f32)
     inverse1 = lax.rsqrt(jnp.mean(start * start, axis=-1, keepdims=True) + eps)
+    count = seqs * (taps - 1)
+
+    def start_of(behind):
+        values = behind[sequence].reshape(count, n, part)[:, chunk].reshape(count, width)
+        values = jnp.pad(values.astype(f32), ((0, -count % 16), (0, 0)))
+        return values, lax.rsqrt(jnp.mean(values * values, axis=-1, keepdims=True) + eps)
+
+    normed1, pieces0, pieces1, gains = {}, {}, {}, {}
+    totals = None
+
+    def use(k, piece0, piece1):
+        nonlocal totals
+        pieces0[k], pieces1[k] = piece0, piece1
+        gains[k] = piece1[lanes + half_lanes : lanes + half_lanes + 2]
+        normed1[k] = (sl(start, k) * inverse1 * gains[k][:1].astype(f32)).astype(bf16)
+        shares = across(normed1[k], piece0[:lanes]), across(normed1[k], piece1[:lanes])
+        totals = shares if totals is None else tuple(t + s for t, s in zip(totals, shares))
+
     for turn in range(n - 3):
-        if turn == 3:
+        if turn == landings[0]:
             behind_rows = ring.land(behind_rows)
         else:
             ring.land()
-    first, second = first.slots(), second.slots()
+    for k, (piece0, piece1) in enumerate(zip(first.slots(), second.slots())):
+        use(k, piece0, piece1)
+    inner, gate_in = (t.astype(bf16) for t in totals)
+    first, second = ([pieces[k] for k in range(n)] for pieces in (pieces0, pieces1))
     in0 = [p[:lanes] for p in first]
     in1 = [p[:lanes] for p in second]
-    gains = [p[lanes + half_lanes : lanes + half_lanes + 2] for p in second]
     gain1, gain2 = (
-        jnp.concatenate([g[i : i + 1] for g in gains], axis=1).astype(f32) for i in range(2)
-    )
-    normed1 = [
-        (sl(start, k) * inverse1 * gains[k][:1].astype(f32)).astype(bf16) for k in range(n)
-    ]
-    inner = sum(across(normed1[k], in0[k]) for k in range(n)).astype(bf16)
-    gate_in = sum(across(normed1[k], in1[k]) for k in range(n)).astype(bf16)
-    count = seqs * (taps - 1)
-    start_before = behind_rows[sequence].reshape(count, n, part)[:, chunk].reshape(count, width)
-    start_before = jnp.pad(start_before.astype(f32), ((0, -count % 16), (0, 0)))
-    inverse_before = lax.rsqrt(
-        jnp.mean(start_before * start_before, axis=-1, keepdims=True) + eps
-    )
-    normed_before = [
-        (sl(start_before, k) * inverse_before * gains[k][:1].astype(f32)).astype(bf16)
-        for k in range(n)
-    ]
-    before = sum(across(normed_before[k], in0[k]) for k in range(n)).astype(bf16)
+        jnp.concatenate([gains[k][i : i + 1] for k in range(n)], axis=1).astype(f32)
+        for i in range(2)
+    )
+    w_both = jnp.concatenate([jnp.concatenate(in0, axis=1), jnp.concatenate(in1, axis=1)], axis=0)
+    start_before, inverse_before = start_of(behind_rows)
+    normed_before = (start_before * inverse_before * gain1).astype(bf16)
+    before = across(normed_before, w_both[:lanes]).astype(bf16)
     before = before[:count].astype(f32).reshape(seqs, taps - 1, lanes)
     before = jnp.pad(before, ((0, 0), (pad_rows - taps + 1, 0), (0, 0)))
     inner = inner.reshape(seqs, piece, lanes)
     gate_in = gate_in.reshape(seqs, piece, lanes)
-    inner = ring.land(inner)
+    inner = ring.land(inner, landings[1])
     conv_w = conv_weight.astype(f32)
     rate = decay_rate.astype(f32)[None]
     gate_m = dense_heads(gate_matrix)
@@ -696,7 +707,9 @@
         [pltpu.VMEM((piece + pad_rows, lanes), f32), pltpu.VMEM((2, piece, lanes), f32)],
         gate_flops,
     )
-    entry = ring.land(carried(ring.land(ends), 1, n))
+    ends = ring.land(ends, landings[2])
+    entry = carried(ends, 1, n, lambda v: ring.land(v, landings[3]))
+    entry = ring.land(entry, landings[4])
     states = local + cum * entry[:, :1]
     product = (states * gelu_parts(gate_in.astype(f32))[0]).astype(bf16).reshape(rows, lanes)
     w_out = jnp.concatenate(
@@ -719,37 +732,38 @@
     chips = []
 
     def keep(chip):
-        chips.append(chip)
-        return chip
+        chips.append(ring.land(chip, landings[6]))
+        return chips[0]
 
     recurrent = tp_sum(
         lambda h: dot(half_of(product, h), w_out),
+        others=lambda v: ring.land(v, landings[5]),
         chips=keep,
-        totals=lambda v: lands(v, 4),
+        totals=lambda v: lands(v, landings[7]),
     )
     gate_act, gate_slope = gelu_parts(after(gate_in, chips[0]).astype(f32))
 
     middle, normed2 = in_halves(
         norm_kernel, [x], [r.reshape(part_full) for r in recurrent], [gain2], [f32, bf16], 0
     )
-    normed2 = normed2.reshape(rows, width)
+    normed2 = ring.land(normed2.reshape(rows, width), landings[8])
+    ring.need(mlp)
     w_mlp = jnp.concatenate([jnp.concatenate(w.slots(), axis=0) for w in mlp], axis=1)
     both = dot(normed2, w_mlp).astype(bf16)
     both0, both1 = both[:, :units].astype(f32), both[:, units:].astype(f32)
     act, slope = gelu_parts(both0)
     hidden = (act * both1).astype(bf16)
-    act, slope = act.astype(bf16), (slope * both1).astype(bf16)
+    hidden, act, slope = ring.land(
+        (hidden, act.astype(bf16), (slope * both1).astype(bf16)), landings[9]
+    )
     ring.drain()
-    ring.token = None
-    grad_down = down(hidden, cot_turned).astype(bf16)
-    act, slope = after((act, slope), grad_down)
-    grad_down = lax.psum_scatter(grad_down, "seq", scatter_dimension=1, tiled=True).astype(f32)
+    w_down = jnp.concatenate(downs.slots(), axis=1)
     grad_both = []
-    grad_mlp = [
-        Scatter(lambda k: down(sl(normed2, k), grad_both[0][:, :units]), 1, n, chunk),
-        Scatter(lambda k: down(sl(normed2, k), grad_both[0][:, units:]), -1, n, chunk),
-    ]
-    ring.add(grad_mlp)
+    grad_down = Scatter(lambda k: down(hidden, sl(grad_low, k)), 1, n, chunk)
+    grad_mlp = Scatter(lambda k: down(sl(normed2, k), grad_both[0]), -1, n, chunk)
+    ring.add([grad_down, grad_mlp])
+    ring.issue(landings[10])
+    act, slope, w_down = ring.hold((act, slope, w_down))
     grad_both.append(
         pl.pallas_call(
             hidden_back_kernel,
@@ -765,15 +779,18 @@
             compiler_params=pltpu.CompilerParams(vmem_limit_bytes=vmem_bytes),
             cost_estimate=pl.CostEstimate(
                 flops=2 * rows * width * units,
-                bytes_accessed=moved_bytes(cot_turned, w_down, act, slope, both),
+                bytes_accessed=moved_bytes(grad_low, w_down, act, slope, both),
                 transcendentals=0,
             ),
-        )(cot_turned, w_down, act, slope)
+        )(grad_low, w_down, act, slope)
     )
     ring.issue()
     grad_normed2 = tp_sum(
         lambda h: across(half_of(grad_both[0], h), w_mlp),
-        totals=lambda v: lands(v, 2),
+        others=lambda v: ring.land(v, landings[11]),
+        owns=lambda v: ring.land(v, landings[12]),
+        chips=lambda v: ring.land(v, landings[13]),
+        totals=lambda v: lands(v, landings[14]),
     )
     turned = jnp.concatenate([half_of(hidden, 1), half_of(hidden, 0)], axis=0)
     turned = jnp.where(odd == 1, turned, hidden)
@@ -786,9 +803,9 @@
         [f32, bf16],
         1,
     )
-    grad_out = Scatter(lambda k: down(product, sl(grad_rec, k)), -1, n, chunk)
+    grad_out = Scatter(lambda k: down(product, sl(grad_rec, k)), 1, n, chunk)
     ring.add([grad_out])
-    grad_rec = ring.land(grad_rec.reshape(rows, width))
+    grad_rec = ring.land(grad_rec.reshape(rows, width), landings[15])
     mlp_out = lax.psum(dot(after(turned, grad_middle), w_down).astype(bf16), "tp")
 
     grad_product = across(grad_rec, w_out).reshape(wide)
@@ -800,7 +817,9 @@
         [pltpu.VMEM((piece, lanes), f32)],
         rows * lanes * 50,
     )
-    incoming = ring.land(after(carried(early, -1, n), grad_down), 2)
+    early = ring.land(early, landings[16])
+    incoming = carried(early, -1, n, lambda v: ring.land(v, landings[17]))
+    incoming = ring.land(incoming, landings[18])
     grad_gates, grad_inner, grad_gate_in, head, last, sums = per_sequence(
         gates_back_kernel,
         seqs,
@@ -834,7 +853,7 @@
         [pltpu.VMEM((piece, lanes), f32)] + [pltpu.VMEM((piece + pad_rows, lanes), f32)] * 2,
         gate_flops,
     )
-    head = ring.land(head)
+    head = ring.land(head, landings[19])
     behind = lax.ppermute(
         head[:, : taps - 1].astype(bf16), "seq", [(i + 1, i) for i in range(n - 1)]
     ).astype(f32)
@@ -847,8 +866,7 @@
     )
     back0 = grad_inner.reshape(rows, lanes)
     back1 = grad_gate_in.reshape(rows, lanes)
-    back = ring.land(jnp.concatenate([back0, back1], axis=1))
-    w_both = jnp.concatenate([jnp.concatenate(in0, axis=1), jnp.concatenate(in1, axis=1)], axis=0)
+    back = ring.land(jnp.concatenate([back0, back1], axis=1), landings[20])
     grads = [
         Scatter(lambda k: down(back0, normed1[k]), 1, n, chunk),
         Scatter(lambda k: down(back1, normed1[k]), -1, n, chunk),
@@ -859,12 +877,13 @@
 
     def hold_output(chip):
         late.append(after(mlp_out, chip))
-        return ring.land(chip)
+        return ring.land(chip, landings[22])
 
     grad_normed1 = tp_sum(
         lambda h: dot(half_of(back, h), w_both),
+        others=lambda v: ring.land(v, landings[21]),
         chips=hold_output,
-        totals=lambda v: lands(v, 4),
+        totals=lambda v: lands(v, landings[23]),
     )
     mlp_out = late[0]
     ready = None
@@ -880,7 +899,18 @@
             back=True,
             half=0,
         )
-        ring.resume(ready[0])
+        grad_tokens = by_rows(
+            start_back_kernel,
+            [x, summed1[1], grad_middle],
+            [gain1],
+            [f32],
+            0,
+            move,
+            back=True,
+            half=1,
+            earlier=ready,
+        )[0]
+        ring.resume(grad_tokens)
         total1 = after(grad_normed1[0], ready[0])
     else:
         total1 = grad_normed1[0]
@@ -909,20 +939,9 @@
             back=True,
             moved=(1,),
         )[0]
-        grad_tokens = by_rows(
-            start_back_kernel,
-            [x, summed1[1], grad_middle],
-            [gain1],
-            [f32],
-            0,
-            move,
-            back=True,
-            half=1,
-            earlier=ready,
-        )[0]
     else:
-        mlp_out = mlp_out.reshape(full).astype(f32)
-        output = (own_order(middle, move, True) + mlp_out).astype(bf16)
+        mlp_out = mlp_out.reshape(full)[sequence].astype(f32)
+        output = own_order((middle + mlp_out).astype(bf16), move, True)
         grad_normed1_all = jnp.concatenate(grad_normed1, axis=0).reshape(full).astype(f32)
         grad_start = norm_back(x.astype(f32), grad_normed1_all, gain1)[0]
         grad_tokens = own_order(grad_middle + grad_start, move, True)
@@ -952,8 +971,8 @@
         small[0],
         grad_out.total(),
         grad_gains[1],
-        jnp.stack([g.total() for g in grad_mlp], axis=1),
-        grad_down,
+        grad_mlp.total().reshape(part, 2, units),
+        grad_down.total(),
     )
 
 

time: 911 us -> 857 us (0.941)
  waiting for transfers between devices: 271 us -> 204 us
  local copies, waits for them, and re-layouts: 120 us -> 139 us
  other arithmetic: 65 us -> 55.3 us
    ppermute x63 -> x70, waiting for transfers between devices: 188 us -> 138 us  [issue(): flying.append((flow, lax.ppermute(message, 'seq', self.pairs[way])))]
    ppermute x3, waiting for transfers between devices: 16.8 us -> 4.11 us  [seq_sum(): lax.ppermute(values, 'seq', [(i, i ^ by) for i in range(n)])]
    ppermute x3, waiting for transfers between devices: 36.4 us -> 25.3 us  [chip_swap(): return lax.ppermute(values, 'tp', [(i, i ^ 2) for i in range(size)])]
    dot_general x27 -> x20, matrix products: 71.9 us -> 61.8 us  [across(): lax.dot_general(a, b, (((1,), (1,)), ((), ())), preferred_element_type=f32)]
    ppermute x63 -> x70, starting transfers between devices: 72.7 us -> 77.8 us  [issue(): flying.append((flow, lax.ppermute(message, 'seq', self.pairs[way])))]
    dot_general x43 -> x42, matrix products: 90 us -> 94.6 us  [down(): lax.dot_general(a, b, (((0,), (0,)), ((), ())), preferred_element_type=f32)]
    unnamed x323 -> x336, local copies, waits for them, and re-layouts: 81.2 us -> 85.8 us
  transfers between devices with their start and end apart: 90 -> 95, of which waited for: 31 -> 27; matrix products, arithmetic and copies ran while one was open for 40% -> 43% of each run, Pallas kernels for 10% -> 13%
where the time goes in v5:
time: 857 us; the launch traced here: 845 us
  waiting for transfers between devices  204 us (24%)
  matrix products  204 us (24%)
  local copies, waits for them, and re-layouts  139 us (16%)
  starting transfers between devices  115 us (13%)
  Pallas kernels  111 us (13%)
  other arithmetic  55.3 us (6%)
  between operations  16.8 us (2%)
    ppermute x70, waiting for transfers between devices, issue(): flying.append((flow, lax.ppermute(message, 'seq', self.pairs[way])))  138 us
    dot_general x42, matrix products, down(): lax.dot_general(a, b, (((0,), (0,)), ((), ())), preferred_element_type=f32)  94.6 us
    unnamed x336, local copies, waits for them, and re-layouts  85.8 us
    ppermute x70, starting transfers between devices, issue(): flying.append((flow, lax.ppermute(message, 'seq', self.pairs[way])))  77.8 us
    dot_general x20, matrix products, across(): lax.dot_general(a, b, (((1,), (1,)), ((), ())), preferred_element_type=f32)  61.8 us
    pallas_call x8, Pallas kernels, by_rows(): pl.pallas_call(body, grid_spec=pltpu.PrefetchScalarGridSpec(num_scalar_pr...  56.2 us
    dot_general x6, matrix products, dot(): return jnp.dot(a, b, preferred_element_type=f32)  47.4 us
    pallas_call x3, Pallas kernels, per_sequence(): pl.pallas_call(kernel, grid=(seqs,), in_specs=[spec(a.shape, kind) for a,...  42.8 us
  transfers between devices with their start and end apart: 95, of which 27 were waited for; matrix products, arithmetic and copies ran while one was open for 43% of the time, Pallas kernels for 13%

profile of v5, /device:TPU:0, one launch (start us, length us, event | category | flops | bytes accessed | tf_op | source)
XLA Modules:
  0.0 844.8 jit_solution(7081894514530652649)
XLA Ops:
  29.7 3.5 constant_dynamic-update-slice_fusion.26
  36.4 8.5 %shard_map.255 = (bf16[4,256,2048]{2,1,0:T(8,128)(2,1)S(1)}, bf16[4,256,2048]{2,1,0:T(8,128)(2,1)}) custom-call(s32[4]{0:T(128)S(1)} %and_select_fusion.3.refs_0_, s32[8]{0:T(128)S(1)} %gather_fusion, bf16[4,256,2048]{2,1,0:T(8,128)(2,1)} %refs_2_, bf16[4,256,2048]{2,1,0:T(8,128)(2,1)} %refs_3_), custom_call_target="tpu_custom_call" | custom-call | flops 16777216 | bytes 16777216 | tf_op jit(solution)/shard_map/pallas_call | solution.py:417
  48.9 4.4 collective-permute-start.6
  56.6 4.5 convert_element_type.429
  74.3 4.6 collective-permute-done.10
  81.5 9.3 %collective-permute-done.7 = bf16[1072,256]{1,0:T(8,128)(2,1)} collective-permute-done((bf16[1072,256]{1,0:T(8,128)(2,1)}, bf16[1072,256]{1,0:T(8,128)(2,1)}, u32[]{:S(2)}, u32[]{:S(2)}) %collective-permute-start.7) | collective-permute-done | bytes 548896 | tf_op jit(solution)/shard_map/ppermute | solution.py:73
  122.1 4.1 fusion.71
  144.9 5.5 add_convert_fusion.7
  155.2 3.3 add_convert_fusion.6
  172.8 16.1 %shard_map.256 = (f32[4,256,704]{2,1,0:T(8,128)}, f32[4,256,704]{2,1,0:T(8,128)}, f32[4,256,704]{2,1,0:T(8,128)}, f32[4,256,704]{2,1,0:T(8,128)}, f32[4,256,704]...) custom-call(bf16[4,256,704]{2,1,0:T(8,128)(2,1)S(1)} %bitcast.198, ...), custom_call_target="tpu_custom_call" | custom-call | flops 2030043136 | bytes 23812096 | tf_op jit(solution)/shard_map/pallas_call | solution.py:380
  188.9 3.5 collective-permute-start.19
  194.6 3.7 collective-permute-start.22
  198.3 6.0 collective-permute-done.22
  204.3 3.9 collective-permute-start.23
  208.2 6.1 collective-permute-start.24
  221.1 5.9 fusion.36
  229.2 4.6 convolution_convert_fusion.4
  236.3 4.2 slice.715
  246.3 3.3 convolution_convert_fusion.5
  264.3 13.8 %collective-permute-done.39 = bf16[256,1536]{1,0:T(8,128)(2,1)S(1)} collective-permute-done((bf16[256,1536]{1,0:T(8,128)(2,1)S(1)}, bf16[256,1536]{1,0:T(8,128)(2,1)S(1)}, u32[]{:S(2)}, u32[]{:S(2)}) %collective-permute-start.39) | collective-permute-done | bytes 786464 | tf_op jit(solution)/shard_map/ppermute | solution.py:73
  280.1 16.7 %collective-permute-done.31 = bf16[1536,256]{1,0:T(8,128)(2,1)S(1)} collective-permute-done((bf16[1536,256]{1,0:T(8,128)(2,1)S(1)}, bf16[1536,256]{1,0:T(8,128)(2,1)S(1)}, u32[]{:S(2)}, u32[]{:S(2)}) %collective-permute-start.31) | collective-permute-done | bytes 786464 | tf_op jit(solution)/shard_map/ppermute | solution.py:73
  300.8 28.8 %collective-permute-done.32 = bf16[1536,256]{1,0:T(8,128)(2,1)S(1)} collective-permute-done((bf16[1536,256]{1,0:T(8,128)(2,1)S(1)}, bf16[1536,256]{1,0:T(8,128)(2,1)S(1)}, u32[]{:S(2)}, u32[]{:S(2)}) %collective-permute-start.32) | collective-permute-done | bytes 786464 | tf_op jit(solution)/shard_map/ppermute | solution.py:73
  339.9 5.0 shard_map.257
  345.9 5.0 shard_map.258
  355.3 20.2 %convolution_convert_fusion = bf16[1024,3072]{1,0:T(8,128)(2,1)} fusion(bf16[1024,2048]{1,0:T(8,128)(2,1)} %bitcast.224, bf16[2048,1536]{1,0:T(8,128)(2,1)} %copy-done.94, bf16[2048,1536]{1,0:T(8,128)(2,1)} %copy-done.93), kind=kOutput, calls=%fused_computation.42 | convolution fusion | flops 12913213440 | bytes 23068672 | tf_op jit(solution)/shard_map/dot_general | solution.py:581
  375.4 7.9 fusion.6
  386.1 3.3 convolution_convert_fusion.6
  400.0 12.4 %shard_map.259 = bf16[1024,3072]{1,0:T(8,128)(2,1)} custom-call(bf16[1024,2048]{1,0:T(8,128)(2,1)} %bitcast.235, bf16[1536,2048]{1,0:T(8,128)(2,1)} %constant_dynamic-update-slice_fusion.27.w_down, bf16[1024,1536]{1,0:T(8,128)(2,1)S(1)} %get-tuple-element.265.act, bf16[1024,1536]{1,0:T(8,128)(2,1)} %get-tuple-element.266.slope), custom_call_target="tpu_custom_call" | custom-call | flops 6442450944 | bytes 23068672 | tf_op jit(solution)/shard_map/pallas_call | solution.py:768
  412.4 11.8 %fusion.50 = bf16[512,2048]{1,0:T(8,128)(2,1)} fusion(bf16[2048,1536]{1,0:T(8,128)(2,1)} %copy-done.94, bf16[2048,1536]{1,0:T(8,128)(2,1)} %copy-done.93, bf16[1024,3072]{1,0:T(8,128)(2,1)} %shard_map.259), kind=kOutput, calls=%fused_computation.103 | convolution fusion | flops 6468665344 | bytes 17825792 | tf_op jit(solution)/shard_map/dot_general | solution.py:573
  432.7 10.7 %fusion.47 = bf16[512,2048]{1,0:T(8,128)(2,1)} fusion(bf16[2048,1536]{1,0:T(8,128)(2,1)} %copy-done.94, bf16[2048,1536]{1,0:T(8,128)(2,1)} %copy-done.93, bf16[1024,3072]{1,0:T(8,128)(2,1)S(1)} %copy-done.25), kind=kOutput, calls=%fused_computation.102 | convolution fusion | flops 6468665344 | bytes 17825792 | tf_op jit(solution)/shard_map/dot_general | solution.py:573
  447.4 4.7 fusion.25
  458.5 6.2 collective-permute-done.52
  464.8 4.4 fusion.21
  470.3 4.4 fusion.20
  475.8 18.4 %collective-permute-done.46 = bf16[512,2048]{1,0:T(8,128)(2,1)S(1)} collective-permute-done((bf16[512,2048]{1,0:T(8,128)(2,1)S(1)}, bf16[512,2048]{1,0:T(8,128)(2,1)S(1)}, u32[]{:S(2)}, u32[]{:S(2)}) %collective-permute-start.46) | collective-permute-done | bytes 2097184 | tf_op jit(solution)/shard_map/ppermute | solution.py:186
  503.7 7.3 shard_map.260
  511.0 7.3 shard_map.261
  519.9 4.0 fusion.23
  524.3 4.7 fusion.22
  531.2 6.4 fusion.86
  537.7 7.7 shard_map.262
  545.4 4.4 fusion.58
  552.2 11.0 %convolution_convert_fusion.3 = bf16[1024,2048]{1,0:T(8,128)(2,1)} fusion(bf16[1024,1536]{1,0:T(8,128)(2,1)S(1)} %copy-done.67, bf16[1536,2048]{1,0:T(8,128)(2,1)} %constant_dynamic-update-slice_fusion.27.w_down), kind=kOutput, calls=%fused_computation.75 | convolution fusion | flops 6444548096 | bytes 13631488 | tf_op jit(solution)/shard_map/dot_general | solution.py:581
  567.0 19.9 %collective-permute-done.56 = f32[4,2,704]{2,1,0:T(2,128)S(1)} collective-permute-done((f32[4,2,704]{2,1,0:T(2,128)S(1)}, f32[4,2,704]{2,1,0:T(2,128)S(1)}, u32[]{:S(2)}, u32[]{:S(2)}) %collective-permute-start.56) | collective-permute-done | bytes 22560 | tf_op jit(solution)/shard_map/ppermute | solution.py:538
  588.4 4.4 collective-permute-done.57
  601.7 6.1 fusion.24
  613.2 19.1 %shard_map.263 = (bf16[2,4,256,704]{3,2,1,0:T(8,128)(2,1)}, bf16[4,256,704]{2,1,0:T(8,128)(2,1)S(1)}, bf16[4,256,704]{2,1,0:T(8,128)(2,1)S(1)}, f32[4,8,704]{2,1...) custom-call(f32[4,256,704]{2,1,0:T(8,128)} %bitcast.245, f32[4,256,704]{2,1,0:T(8,128)} %get-tuple-element.421.slope, ...), custom_call_target="tpu_custom_call" | custom-call | flops 2030043136 | bytes 38514432 | tf_op jit(solution)/shard_map/pallas_call | solution.py:380
  641.4 4.5 collective-permute-done.63
  658.6 4.7 fusion.46
  663.3 5.4 fusion.19
  668.7 5.6 reshape.524
  674.3 4.8 fusion.53
  680.9 4.6 collective-permute-start.69
  685.5 3.6 fusion.45
  698.7 10.2 %collective-permute-done.72 = bf16[704,256]{1,0:T(8,128)(2,1)S(1)} collective-permute-done((bf16[704,256]{1,0:T(8,128)(2,1)S(1)}, bf16[704,256]{1,0:T(8,128)(2,1)S(1)}, u32[]{:S(2)}, u32[]{:S(2)}) %collective-permute-start.72) | collective-permute-done | bytes 360480 | tf_op jit(solution)/shard_map/ppermute | solution.py:73
  713.1 8.9 %collective-permute-done.73 = bf16[704,256]{1,0:T(8,128)(2,1)S(1)} collective-permute-done((bf16[704,256]{1,0:T(8,128)(2,1)S(1)}, bf16[704,256]{1,0:T(8,128)(2,1)S(1)}, u32[]{:S(2)}, u32[]{:S(2)}) %collective-permute-start.73) | collective-permute-done | bytes 360480 | tf_op jit(solution)/shard_map/ppermute | solution.py:73
  724.0 6.2 collective-permute-done.83
  732.4 6.9 collective-permute-done.68
  741.0 7.0 shard_map.265.refs_6_
  753.7 11.0 %collective-permute-done.87 = bf16[704,256]{1,0:T(8,128)(2,1)} collective-permute-done((bf16[704,256]{1,0:T(8,128)(2,1)}, bf16[704,256]{1,0:T(8,128)(2,1)}, u32[]{:S(2)}, u32[]{:S(2)}) %collective-permute-start.87) | collective-permute-done | bytes 360480 | tf_op jit(solution)/shard_map/ppermute | solution.py:73
  769.8 8.6 %shard_map.264 = bf16[4,256,2048]{2,1,0:T(8,128)(2,1)} custom-call(s32[4]{0:T(128)S(1)} %copy-done.24, s32[8]{0:T(128)S(1)} %copy-done.20, f32[4,256,2048]{2,1,0:T(8,128)} %get-tuple-element.241.refs_0_.refs_2_, bf16[4,256,2048]{2,1,0:T(8,128)(2,1)S(1)} %bitcast.200), custom_call_target="tpu_custom_call" | custom-call | flops 16777216 | bytes 16777216 | tf_op jit(solution)/shard_map/pallas_call | solution.py:417
  793.8 7.5 shard_map.266
  807.4 5.2 collective-permute-done.81
  814.7 5.6 collective-permute-done.88
  (672 shorter events, 336.7 us)
Async XLA Ops:
  7.2 760.4 %all-reduce.17.cloned.1.call-start = ((), (), s32[]{:S(2)}) async-start(), calls=%async_computation | async-start | bytes 8388608 | tf_op jit(solution)/shard_map/psum | solution.py:809
  11.3 21.9 %collective-permute-start = (bf16[1056,256]{1,0:T(8,128)(2,1)}, bf16[1056,256]{1,0:T(8,128)(2,1)S(1)}, u32[]{:S(2)}, u32[]{:S(2)}) collective-permute-start(bf16[1056,256]{1,0:T(8,128)(2,1)} %pad_maximum_fusion.21), channel_id=1, source_target_pairs={{0,8},{8,16},{16,24},{24,28},{28,20},{20,12},{12,4},{4,0},{1,9},{9... | collective-permute-start | bytes 1622024 | tf_op jit(solution)/shard_map/ppermute | solution.py:73
  14.3 18.9 %collective-permute-start.1 = (bf16[1056,256]{1,0:T(8,128)(2,1)}, bf16[1056,256]{1,0:T(8,128)(2,1)}, u32[]{:S(2)}, u32[]{:S(2)}) collective-permute-start(bf16[1056,256]{1,0:T(8,128)(2,1)} %pad_maximum_fusion.21), channel_id=1, source_target_pairs={{0,4},{8,0},{16,8},{24,16},{28,24},{20,28},{12,20},{4,12},{1,5},{9... | collective-permute-start | bytes 1622024 | tf_op jit(solution)/shard_map/ppermute | solution.py:73
  15.2 31.7 %collective-permute-start.2 = (bf16[1072,256]{1,0:T(8,128)(2,1)}, bf16[1072,256]{1,0:T(8,128)(2,1)}, u32[]{:S(2)}, u32[]{:S(2)}) collective-permute-start(bf16[1072,256]{1,0:T(8,128)(2,1)} %pad_maximum_fusion.20), channel_id=1, source_target_pairs={{0,8},{8,16},{16,24},{24,28},{28,20},{20,12},{12,4},{4,0},{1,9},{9... | collective-permute-start | bytes 1646600 | tf_op jit(solution)/shard_map/ppermute | solution.py:73
  17.2 29.7 %collective-permute-start.3 = (bf16[1072,256]{1,0:T(8,128)(2,1)}, bf16[1072,256]{1,0:T(8,128)(2,1)}, u32[]{:S(2)}, u32[]{:S(2)}) collective-permute-start(bf16[1072,256]{1,0:T(8,128)(2,1)} %pad_maximum_fusion.20), channel_id=1, source_target_pairs={{0,4},{8,0},{16,8},{24,16},{28,24},{20,28},{12,20},{4,12},{1,5},{9... | collective-permute-start | bytes 1646600 | tf_op jit(solution)/shard_map/ppermute | solution.py:73
  34.3 28.2 %collective-permute-start.11 = (bf16[1056,256]{1,0:T(8,128)(2,1)}, bf16[1056,256]{1,0:T(8,128)(2,1)}, u32[]{:S(2)}, u32[]{:S(2)}) collective-permute-start(bf16[1056,256]{1,0:T(8,128)(2,1)} %collective-permute-done.1), channel_id=1, source_target_pairs={{0,4},{8,0},{16,8},{24,16},{28,24},{20,28},{12,20},{4,12},{1,5},{9... | collective-permute-start | bytes 1622024 | tf_op jit(solution)/shard_map/ppermute | solution.py:73
  36.3 27.2 %collective-permute-start.5 = (bf16[1056,256]{1,0:T(8,128)(2,1)S(1)}, bf16[1056,256]{1,0:T(8,128)(2,1)}, u32[]{:S(2)}, u32[]{:S(2)}) collective-permute-start(bf16[1056,256]{1,0:T(8,128)(2,1)S(1)} %collective-permute-done), channel_id=1, source_target_pairs={{0,8},{8,16},{16,24},{24,28},{28,20},{20,12},{12,4},{4,0},{1,9},{9... | collective-permute-start | bytes 1622024 | tf_op jit(solution)/shard_map/ppermute | solution.py:73
  46.9 21.1 %collective-permute-start.4 = (bf16[1072,256]{1,0:T(8,128)(2,1)}, bf16[1072,256]{1,0:T(8,128)(2,1)}, u32[]{:S(2)}, u32[]{:S(2)}) collective-permute-start(bf16[1072,256]{1,0:T(8,128)(2,1)} %collective-permute-done.2), channel_id=1, source_target_pairs={{0,8},{8,16},{16,24},{24,28},{28,20},{20,12},{12,4},{4,0},{1,9},{9... | collective-permute-start | bytes 1646600 | tf_op jit(solution)/shard_map/ppermute | solution.py:73
  48.9 20.1 %collective-permute-start.8 = (bf16[1072,256]{1,0:T(8,128)(2,1)}, bf16[1072,256]{1,0:T(8,128)(2,1)}, u32[]{:S(2)}, u32[]{:S(2)}) collective-permute-start(bf16[1072,256]{1,0:T(8,128)(2,1)} %collective-permute-done.3), channel_id=1, source_target_pairs={{0,4},{8,0},{16,8},{24,16},{28,24},{20,28},{12,20},{4,12},{1,5},{9... | collective-permute-start | bytes 1646600 | tf_op jit(solution)/shard_map/ppermute | solution.py:73
  48.9 32.6 %collective-permute-start.6 = (bf16[4,3,2048]{2,1,0:T(4,128)(2,1)S(1)}, bf16[4,3,2048]{2,1,0:T(4,128)(2,1)}, u32[]{:S(2)}, u32[]{:S(2)}) collective-permute-start(bf16[4,3,2048]{2,1,0:T(4,128)(2,1)S(1)} %slice.496), channel_id=1, source_target_pairs={{0,4},{4,8},{8,12},{12,16},{16,20},{20,24},{24,28},{1,5},{5,9},{9,... | collective-permute-start | bytes 147464 | tf_op jit(solution)/shard_map/ppermute | solution.py:642
  62.5 29.6 %collective-permute-start.12 = (bf16[1056,256]{1,0:T(8,128)(2,1)}, bf16[1056,256]{1,0:T(8,128)(2,1)}, u32[]{:S(2)}, u32[]{:S(2)}) collective-permute-start(bf16[1056,256]{1,0:T(8,128)(2,1)} %collective-permute-done.11), channel_id=1, source_target_pairs={{0,4},{8,0},{16,8},{24,16},{28,24},{20,28},{12,20},{4,12},{1,5},{9... | collective-permute-start | bytes 1622024 | tf_op jit(solution)/shard_map/ppermute | solution.py:73
  68.0 22.8 %collective-permute-start.7 = (bf16[1072,256]{1,0:T(8,128)(2,1)}, bf16[1072,256]{1,0:T(8,128)(2,1)}, u32[]{:S(2)}, u32[]{:S(2)}) collective-permute-start(bf16[1072,256]{1,0:T(8,128)(2,1)} %collective-permute-done.4), channel_id=1, source_target_pairs={{0,8},{8,16},{16,24},{24,28},{28,20},{20,12},{12,4},{4,0},{1,9},{9... | collective-permute-start | bytes 1646600 | tf_op jit(solution)/shard_map/ppermute | solution.py:73
  69.0 21.8 %collective-permute-start.9 = (bf16[1072,256]{1,0:T(8,128)(2,1)}, bf16[1072,256]{1,0:T(8,128)(2,1)}, u32[]{:S(2)}, u32[]{:S(2)}) collective-permute-start(bf16[1072,256]{1,0:T(8,128)(2,1)} %collective-permute-done.8), channel_id=1, source_target_pairs={{0,4},{8,0},{16,8},{24,16},{28,24},{20,28},{12,20},{4,12},{1,5},{9... | collective-permute-start | bytes 1646600 | tf_op jit(solution)/shard_map/ppermute | solution.py:73
  78.9 26.1 %collective-permute-start.14 = (bf16[1056,256]{1,0:T(8,128)(2,1)S(1)}, bf16[1056,256]{1,0:T(8,128)(2,1)}, u32[]{:S(2)}, u32[]{:S(2)}) collective-permute-start(bf16[1056,256]{1,0:T(8,128)(2,1)S(1)} %collective-permute-done.10), channel_id=1, source_target_pairs={{0,8},{8,16},{16,24},{24,28},{28,20},{20,12},{12,4},{4,0},{1,9},{9... | collective-permute-start | bytes 1622024 | tf_op jit(solution)/shard_map/ppermute | solution.py:73
  92.1 26.9 %collective-permute-start.13 = (bf16[1072,256]{1,0:T(8,128)(2,1)}, bf16[1072,256]{1,0:T(8,128)(2,1)}, u32[]{:S(2)}, u32[]{:S(2)}) collective-permute-start(bf16[1072,256]{1,0:T(8,128)(2,1)} %collective-permute-done.9), channel_id=1, source_target_pairs={{0,4},{8,0},{16,8},{24,16},{28,24},{20,28},{12,20},{4,12},{1,5},{9... | collective-permute-start | bytes 1646600 | tf_op jit(solution)/shard_map/ppermute | solution.py:73
  99.9 67.8 %collective-permute-start.15 = (bf16[256,1536]{1,0:T(8,128)(2,1)}, bf16[256,1536]{1,0:T(8,128)(2,1)}, u32[]{:S(2)}, u32[]{:S(2)}) collective-permute-start(bf16[256,1536]{1,0:T(8,128)(2,1)} %get-tuple-element.208), channel_id=1, source_target_pairs={{0,8},{8,16},{16,24},{24,28},{28,20},{20,12},{12,4},{4,0},{1,9},{9... | collective-permute-start | bytes 2359304 | tf_op jit(solution)/shard_map/ppermute | solution.py:73
  100.3 67.3 %collective-permute-start.16 = (bf16[256,1536]{1,0:T(8,128)(2,1)}, bf16[256,1536]{1,0:T(8,128)(2,1)}, u32[]{:S(2)}, u32[]{:S(2)}) collective-permute-start(bf16[256,1536]{1,0:T(8,128)(2,1)} %get-tuple-element.208), channel_id=1, source_target_pairs={{0,4},{8,0},{16,8},{24,16},{28,24},{20,28},{12,20},{4,12},{1,5},{9... | collective-permute-start | bytes 2359304 | tf_op jit(solution)/shard_map/ppermute | solution.py:73
  105.0 83.9 %collective-permute-start.17 = (bf16[256,1536]{1,0:T(8,128)(2,1)}, bf16[256,1536]{1,0:T(8,128)(2,1)}, u32[]{:S(2)}, u32[]{:S(2)}) collective-permute-start(bf16[256,1536]{1,0:T(8,128)(2,1)} %get-tuple-element.215), channel_id=1, source_target_pairs={{0,8},{8,16},{16,24},{24,28},{28,20},{20,12},{12,4},{4,0},{1,9},{9... | collective-permute-start | bytes 2359304 | tf_op jit(solution)/shard_map/ppermute | solution.py:73
  129.9 59.0 %collective-permute-start.18 = (bf16[256,1536]{1,0:T(8,128)(2,1)}, bf16[256,1536]{1,0:T(8,128)(2,1)}, u32[]{:S(2)}, u32[]{:S(2)}) collective-permute-start(bf16[256,1536]{1,0:T(8,128)(2,1)} %get-tuple-element.215), channel_id=1, source_target_pairs={{0,4},{8,0},{16,8},{24,16},{28,24},{20,28},{12,20},{4,12},{1,5},{9... | collective-permute-start | bytes 2359304 | tf_op jit(solution)/shard_map/ppermute | solution.py:73
  167.7 26.9 %collective-permute-start.20 = (bf16[256,1536]{1,0:T(8,128)(2,1)}, bf16[256,1536]{1,0:T(8,128)(2,1)}, u32[]{:S(2)}, u32[]{:S(2)}) collective-permute-start(bf16[256,1536]{1,0:T(8,128)(2,1)} %collective-permute-done.15), channel_id=1, source_target_pairs={{0,8},{8,16},{16,24},{24,28},{28,20},{20,12},{12,4},{4,0},{1,9},{9... | collective-permute-start | bytes 2359304 | tf_op jit(solution)/shard_map/ppermute | solution.py:73
  168.1 26.4 %collective-permute-start.21 = (bf16[256,1536]{1,0:T(8,128)(2,1)}, bf16[256,1536]{1,0:T(8,128)(2,1)}, u32[]{:S(2)}, u32[]{:S(2)}) collective-permute-start(bf16[256,1536]{1,0:T(8,128)(2,1)} %collective-permute-done.16), channel_id=1, source_target_pairs={{0,4},{8,0},{16,8},{24,16},{28,24},{20,28},{12,20},{4,12},{1,5},{9... | collective-permute-start | bytes 2359304 | tf_op jit(solution)/shard_map/ppermute | solution.py:73
  192.5 27.8 %collective-permute-start.25 = (bf16[256,1536]{1,0:T(8,128)(2,1)}, bf16[256,1536]{1,0:T(8,128)(2,1)S(1)}, u32[]{:S(2)}, u32[]{:S(2)}) collective-permute-start(bf16[256,1536]{1,0:T(8,128)(2,1)} %collective-permute-done.17), channel_id=1, source_target_pairs={{0,8},{8,16},{16,24},{24,28},{28,20},{20,12},{12,4},{4,0},{1,9},{9... | collective-permute-start | bytes 2359304 | tf_op jit(solution)/shard_map/ppermute | solution.py:73
  192.6 27.7 %collective-permute-start.26 = (bf16[256,1536]{1,0:T(8,128)(2,1)}, bf16[256,1536]{1,0:T(8,128)(2,1)S(1)}, u32[]{:S(2)}, u32[]{:S(2)}) collective-permute-start(bf16[256,1536]{1,0:T(8,128)(2,1)} %collective-permute-done.18), channel_id=1, source_target_pairs={{0,4},{8,0},{16,8},{24,16},{28,24},{20,28},{12,20},{4,12},{1,5},{9... | collective-permute-start | bytes 2359304 | tf_op jit(solution)/shard_map/ppermute | solution.py:73
  250.6 49.2 %collective-permute-start.30 = (bf16[512,2048]{1,0:T(8,128)(2,1)S(1)}, bf16[512,2048]{1,0:T(8,128)(2,1)S(1)}, u32[]{:S(2)}, u32[]{:S(2)}) collective-permute-start(bf16[512,2048]{1,0:T(8,128)(2,1)S(1)} %add_convert_fusion.5), channel_id=1, source_target_pairs={{0,2},{1,3},{2,0},{3,1},{4,6},{5,7},{6,4},{7,5},{8,10},{9,11},{10,... | collective-permute-start | bytes 6291464 | tf_op jit(solution)/shard_map/ppermute | solution.py:186
  257.6 20.4 %collective-permute-start.39 = (bf16[256,1536]{1,0:T(8,128)(2,1)S(1)}, bf16[256,1536]{1,0:T(8,128)(2,1)S(1)}, u32[]{:S(2)}, u32[]{:S(2)}) collective-permute-start(bf16[256,1536]{1,0:T(8,128)(2,1)S(1)} %copy-done.79), channel_id=1, source_target_pairs={{0,4},{8,0},{16,8},{24,16},{28,24},{20,28},{12,20},{4,12},{1,5},{9... | collective-permute-start | bytes 2359304 | tf_op jit(solution)/shard_map/ppermute | solution.py:73
  259.6 20.4 %collective-permute-start.36 = (bf16[256,1536]{1,0:T(8,128)(2,1)S(1)}, bf16[256,1536]{1,0:T(8,128)(2,1)S(1)}, u32[]{:S(2)}, u32[]{:S(2)}) collective-permute-start(bf16[256,1536]{1,0:T(8,128)(2,1)S(1)} %copy-done.81), channel_id=1, source_target_pairs={{0,8},{8,16},{16,24},{24,28},{28,20},{20,12},{12,4},{4,0},{1,9},{9... | collective-permute-start | bytes 2359304 | tf_op jit(solution)/shard_map/ppermute | solution.py:73
  260.9 36.0 %collective-permute-start.31 = (bf16[1536,256]{1,0:T(8,128)(2,1)S(1)}, bf16[1536,256]{1,0:T(8,128)(2,1)S(1)}, u32[]{:S(2)}, u32[]{:S(2)}) collective-permute-start(bf16[1536,256]{1,0:T(8,128)(2,1)S(1)} %copy-done.77), channel_id=1, source_target_pairs={{0,8},{8,16},{16,24},{24,28},{28,20},{20,12},{12,4},{4,0},{1,9},{9... | collective-permute-start | bytes 2359304 | tf_op jit(solution)/shard_map/ppermute | solution.py:73
  260.9 36.0 %collective-permute-start.33 = (bf16[1536,256]{1,0:T(8,128)(2,1)S(1)}, bf16[1536,256]{1,0:T(8,128)(2,1)S(1)}, u32[]{:S(2)}, u32[]{:S(2)}) collective-permute-start(bf16[1536,256]{1,0:T(8,128)(2,1)S(1)} %copy-done.77), channel_id=1, source_target_pairs={{0,4},{8,0},{16,8},{24,16},{28,24},{20,28},{12,20},{4,12},{1,5},{9... | collective-permute-start | bytes 2359304 | tf_op jit(solution)/shard_map/ppermute | solution.py:73
  278.0 55.4 %collective-permute-start.40 = (bf16[256,1536]{1,0:T(8,128)(2,1)S(1)}, bf16[256,1536]{1,0:T(8,128)(2,1)S(1)}, u32[]{:S(2)}, u32[]{:S(2)}) collective-permute-start(bf16[256,1536]{1,0:T(8,128)(2,1)S(1)} %collective-permute-done.39), channel_id=1, source_target_pairs={{0,4},{8,0},{16,8},{24,16},{28,24},{20,28},{12,20},{4,12},{1,5},{9... | collective-permute-start | bytes 2359304 | tf_op jit(solution)/shard_map/ppermute | solution.py:73
  280.0 49.6 %collective-permute-start.37 = (bf16[256,1536]{1,0:T(8,128)(2,1)S(1)}, bf16[256,1536]{1,0:T(8,128)(2,1)S(1)}, u32[]{:S(2)}, u32[]{:S(2)}) collective-permute-start(bf16[256,1536]{1,0:T(8,128)(2,1)S(1)} %copy-done.83), channel_id=1, source_target_pairs={{0,8},{8,16},{16,24},{24,28},{28,20},{20,12},{12,4},{4,0},{1,9},{9... | collective-permute-start | bytes 2359304 | tf_op jit(solution)/shard_map/ppermute | solution.py:73
  296.8 32.7 %collective-permute-start.32 = (bf16[1536,256]{1,0:T(8,128)(2,1)S(1)}, bf16[1536,256]{1,0:T(8,128)(2,1)S(1)}, u32[]{:S(2)}, u32[]{:S(2)}) collective-permute-start(bf16[1536,256]{1,0:T(8,128)(2,1)S(1)} %collective-permute-done.31), channel_id=1, source_target_pairs={{0,8},{8,16},{16,24},{24,28},{28,20},{20,12},{12,4},{4,0},{1,9},{9... | collective-permute-start | bytes 2359304 | tf_op jit(solution)/shard_map/ppermute | solution.py:73
  296.9 32.6 %collective-permute-start.34 = (bf16[1536,256]{1,0:T(8,128)(2,1)S(1)}, bf16[1536,256]{1,0:T(8,128)(2,1)S(1)}, u32[]{:S(2)}, u32[]{:S(2)}) collective-permute-start(bf16[1536,256]{1,0:T(8,128)(2,1)S(1)} %collective-permute-done.33), channel_id=1, source_target_pairs={{0,4},{8,0},{16,8},{24,16},{28,24},{20,28},{12,20},{4,12},{1,5},{9... | collective-permute-start | bytes 2359304 | tf_op jit(solution)/shard_map/ppermute | solution.py:73
  333.5 19.8 %collective-permute-start.41 = (bf16[1536,256]{1,0:T(8,128)(2,1)S(1)}, bf16[1536,256]{1,0:T(8,128)(2,1)S(1)}, u32[]{:S(2)}, u32[]{:S(2)}) collective-permute-start(bf16[1536,256]{1,0:T(8,128)(2,1)S(1)} %collective-permute-done.34), channel_id=1, source_target_pairs={{0,4},{8,0},{16,8},{24,16},{28,24},{20,28},{12,20},{4,12},{1,5},{9... | collective-permute-start | bytes 2359304 | tf_op jit(solution)/shard_map/ppermute | solution.py:73
  333.9 19.5 %collective-permute-start.38 = (bf16[1536,256]{1,0:T(8,128)(2,1)S(1)}, bf16[1536,256]{1,0:T(8,128)(2,1)}, u32[]{:S(2)}, u32[]{:S(2)}) collective-permute-start(bf16[1536,256]{1,0:T(8,128)(2,1)S(1)} %collective-permute-done.32), channel_id=1, source_target_pairs={{0,8},{8,16},{16,24},{24,28},{28,20},{20,12},{12,4},{4,0},{1,9},{9... | collective-permute-start | bytes 2359304 | tf_op jit(solution)/shard_map/ppermute | solution.py:73
  354.2 32.0 %collective-permute-start.42 = (bf16[1536,256]{1,0:T(8,128)(2,1)}, bf16[1536,256]{1,0:T(8,128)(2,1)S(1)}, u32[]{:S(2)}, u32[]{:S(2)}) collective-permute-start(bf16[1536,256]{1,0:T(8,128)(2,1)} %collective-permute-done.38), channel_id=1, source_target_pairs={{0,8},{8,16},{16,24},{24,28},{28,20},{20,12},{12,4},{4,0},{1,9},{9... | collective-permute-start | bytes 2359304 | tf_op jit(solution)/shard_map/ppermute | solution.py:73
  396.8 27.4 %collective-permute-start.44 = (bf16[1536,256]{1,0:T(8,128)(2,1)}, bf16[1536,256]{1,0:T(8,128)(2,1)}, u32[]{:S(2)}, u32[]{:S(2)}) collective-permute-start(bf16[1536,256]{1,0:T(8,128)(2,1)} %convolution_convert_fusion.6), channel_id=1, source_target_pairs={{0,4},{8,0},{16,8},{24,16},{28,24},{20,28},{12,20},{4,12},{1,5},{9... | collective-permute-start | bytes 2359304 | tf_op jit(solution)/shard_map/ppermute | solution.py:73
  397.8 26.3 %collective-permute-start.43 = (bf16[1536,256]{1,0:T(8,128)(2,1)}, bf16[1536,256]{1,0:T(8,128)(2,1)}, u32[]{:S(2)}, u32[]{:S(2)}) collective-permute-start(bf16[1536,256]{1,0:T(8,128)(2,1)} %convolution_convert_fusion.7), channel_id=1, source_target_pairs={{0,8},{8,16},{16,24},{24,28},{28,20},{20,12},{12,4},{4,0},{1,9},{9... | collective-permute-start | bytes 2359304 | tf_op jit(solution)/shard_map/ppermute | solution.py:73
  424.2 19.3 %collective-permute-start.45 = (bf16[512,2048]{1,0:T(8,128)(2,1)}, bf16[512,2048]{1,0:T(8,128)(2,1)}, u32[]{:S(2)}, u32[]{:S(2)}) collective-permute-start(bf16[512,2048]{1,0:T(8,128)(2,1)} %fusion.50), channel_id=1, source_target_pairs={{0,1},{1,0},{2,3},{3,2},{4,5},{5,4},{6,7},{7,6},{8,9},{9,8},{10,11... | collective-permute-start | bytes 6291464 | tf_op jit(solution)/shard_map/ppermute | solution.py:181
  427.3 37.5 %collective-permute-start.52 = (bf16[256,3072]{1,0:T(8,128)(2,1)}, bf16[256,3072]{1,0:T(8,128)(2,1)}, u32[]{:S(2)}, u32[]{:S(2)}) collective-permute-start(bf16[256,3072]{1,0:T(8,128)(2,1)} %convolution_convert_fusion.1), channel_id=1, source_target_pairs={{0,4},{8,0},{16,8},{24,16},{28,24},{20,28},{12,20},{4,12},{1,5},{9... | collective-permute-start | bytes 4718600 | tf_op jit(solution)/shard_map/ppermute | solution.py:73
  431.4 38.9 %collective-permute-start.50 = (bf16[256,3072]{1,0:T(8,128)(2,1)}, bf16[256,3072]{1,0:T(8,128)(2,1)}, u32[]{:S(2)}, u32[]{:S(2)}) collective-permute-start(bf16[256,3072]{1,0:T(8,128)(2,1)} %convolution_convert_fusion.2), channel_id=1, source_target_pairs={{0,8},{8,16},{16,24},{24,28},{28,20},{20,12},{12,4},{4,0},{1,9},{9... | collective-permute-start | bytes 4718600 | tf_op jit(solution)/shard_map/ppermute | solution.py:73
  446.6 47.5 %collective-permute-start.46 = (bf16[512,2048]{1,0:T(8,128)(2,1)S(1)}, bf16[512,2048]{1,0:T(8,128)(2,1)S(1)}, u32[]{:S(2)}, u32[]{:S(2)}) collective-permute-start(bf16[512,2048]{1,0:T(8,128)(2,1)S(1)} %add_convert_fusion.3), channel_id=1, source_target_pairs={{0,2},{1,3},{2,0},{3,1},{4,6},{5,7},{6,4},{7,5},{8,10},{9,11},{10,... | collective-permute-start | bytes 6291464 | tf_op jit(solution)/shard_map/ppermute | solution.py:186
  454.2 40.7 %collective-permute-start.48 = (bf16[1536,256]{1,0:T(8,128)(2,1)S(1)}, bf16[1536,256]{1,0:T(8,128)(2,1)S(1)}, u32[]{:S(2)}, u32[]{:S(2)}) collective-permute-start(bf16[1536,256]{1,0:T(8,128)(2,1)S(1)} %fusion.55), channel_id=1, source_target_pairs={{0,4},{8,0},{16,8},{24,16},{28,24},{20,28},{12,20},{4,12},{1,5},{9... | collective-permute-start | bytes 2359304 | tf_op jit(solution)/shard_map/ppermute | solution.py:73
  457.5 37.4 %collective-permute-start.47 = (bf16[1536,256]{1,0:T(8,128)(2,1)S(1)}, bf16[1536,256]{1,0:T(8,128)(2,1)S(1)}, u32[]{:S(2)}, u32[]{:S(2)}) collective-permute-start(bf16[1536,256]{1,0:T(8,128)(2,1)S(1)} %fusion.54), channel_id=1, source_target_pairs={{0,8},{8,16},{16,24},{24,28},{28,20},{20,12},{12,4},{4,0},{1,9},{9... | collective-permute-start | bytes 2359304 | tf_op jit(solution)/shard_map/ppermute | solution.py:73
  469.2 49.2 %collective-permute-start.53 = (bf16[256,3072]{1,0:T(8,128)(2,1)}, bf16[256,3072]{1,0:T(8,128)(2,1)S(1)}, u32[]{:S(2)}, u32[]{:S(2)}) collective-permute-start(bf16[256,3072]{1,0:T(8,128)(2,1)} %fusion.21), channel_id=1, source_target_pairs={{0,4},{8,0},{16,8},{24,16},{28,24},{20,28},{12,20},{4,12},{1,5},{9... | collective-permute-start | bytes 4718600 | tf_op jit(solution)/shard_map/ppermute | solution.py:73
  474.7 45.2 %collective-permute-start.51 = (bf16[256,3072]{1,0:T(8,128)(2,1)}, bf16[256,3072]{1,0:T(8,128)(2,1)}, u32[]{:S(2)}, u32[]{:S(2)}) collective-permute-start(bf16[256,3072]{1,0:T(8,128)(2,1)} %fusion.20), channel_id=1, source_target_pairs={{0,8},{8,16},{16,24},{24,28},{28,20},{20,12},{12,4},{4,0},{1,9},{9... | collective-permute-start | bytes 4718600 | tf_op jit(solution)/shard_map/ppermute | solution.py:73
  499.7 45.6 %collective-permute-start.55 = (bf16[1536,256]{1,0:T(8,128)(2,1)}, bf16[1536,256]{1,0:T(8,128)(2,1)}, u32[]{:S(2)}, u32[]{:S(2)}) collective-permute-start(bf16[1536,256]{1,0:T(8,128)(2,1)} %fusion.57), channel_id=1, source_target_pairs={{0,4},{8,0},{16,8},{24,16},{28,24},{20,28},{12,20},{4,12},{1,5},{9... | collective-permute-start | bytes 2359304 | tf_op jit(solution)/shard_map/ppermute | solution.py:73
  502.8 42.6 %collective-permute-start.54 = (bf16[1536,256]{1,0:T(8,128)(2,1)}, bf16[1536,256]{1,0:T(8,128)(2,1)}, u32[]{:S(2)}, u32[]{:S(2)}) collective-permute-start(bf16[1536,256]{1,0:T(8,128)(2,1)} %fusion.56), channel_id=1, source_target_pairs={{0,8},{8,16},{16,24},{24,28},{28,20},{20,12},{12,4},{4,0},{1,9},{9... | collective-permute-start | bytes 2359304 | tf_op jit(solution)/shard_map/ppermute | solution.py:73
  523.9 77.8 %collective-permute-start.61 = (bf16[256,3072]{1,0:T(8,128)(2,1)}, bf16[256,3072]{1,0:T(8,128)(2,1)}, u32[]{:S(2)}, u32[]{:S(2)}) collective-permute-start(bf16[256,3072]{1,0:T(8,128)(2,1)} %fusion.23), channel_id=1, source_target_pairs={{0,4},{8,0},{16,8},{24,16},{28,24},{20,28},{12,20},{4,12},{1,5},{9... | collective-permute-start | bytes 4718600 | tf_op jit(solution)/shard_map/ppermute | solution.py:73
  529.0 72.7 %collective-permute-start.60 = (bf16[256,3072]{1,0:T(8,128)(2,1)}, bf16[256,3072]{1,0:T(8,128)(2,1)}, u32[]{:S(2)}, u32[]{:S(2)}) collective-permute-start(bf16[256,3072]{1,0:T(8,128)(2,1)} %fusion.22), channel_id=1, source_target_pairs={{0,8},{8,16},{16,24},{24,28},{28,20},{20,12},{12,4},{4,0},{1,9},{9... | collective-permute-start | bytes 4718600 | tf_op jit(solution)/shard_map/ppermute | solution.py:73
  549.7 91.6 %collective-permute-start.62 = (bf16[1536,256]{1,0:T(8,128)(2,1)}, bf16[1536,256]{1,0:T(8,128)(2,1)}, u32[]{:S(2)}, u32[]{:S(2)}) collective-permute-start(bf16[1536,256]{1,0:T(8,128)(2,1)} %fusion.58), channel_id=1, source_target_pairs={{0,8},{8,16},{16,24},{24,28},{28,20},{20,12},{12,4},{4,0},{1,9},{9... | collective-permute-start | bytes 2359304 | tf_op jit(solution)/shard_map/ppermute | solution.py:73
  563.3 23.7 %collective-permute-start.56 = (f32[4,2,704]{2,1,0:T(2,128)S(1)}, f32[4,2,704]{2,1,0:T(2,128)S(1)}, u32[]{:S(2)}, u32[]{:S(2)}) collective-permute-start(f32[4,2,704]{2,1,0:T(2,128)S(1)} %slice.586), channel_id=1, source_target_pairs={{4,0},{8,4},{12,8},{16,12},{20,16},{24,20},{28,24},{5,1},{9,5},{13... | collective-permute-start | bytes 67592 | tf_op jit(solution)/shard_map/ppermute | solution.py:538
  595.4 194.5 %all-reduce.19.cloned.1.call-start = ((), (), s32[]{:S(2)}) async-start(), calls=%async_computation.1 | async-start | bytes 1081344 | tf_op jit(solution)/shard_map/psum | solution.py:929
  607.8 38.0 %collective-permute-start.63 = (bf16[256,3072]{1,0:T(8,128)(2,1)S(1)}, bf16[256,3072]{1,0:T(8,128)(2,1)S(1)}, u32[]{:S(2)}, u32[]{:S(2)}) collective-permute-start(bf16[256,3072]{1,0:T(8,128)(2,1)S(1)} %fusion.24), channel_id=1, source_target_pairs={{0,4},{8,0},{16,8},{24,16},{28,24},{20,28},{12,20},{4,12},{1,5},{9... | collective-permute-start | bytes 4718600 | tf_op jit(solution)/shard_map/ppermute | solution.py:73
  610.8 45.3 %collective-permute-start.66 = (bf16[704,256]{1,0:T(8,128)(2,1)}, bf16[704,256]{1,0:T(8,128)(2,1)}, u32[]{:S(2)}, u32[]{:S(2)}) collective-permute-start(bf16[704,256]{1,0:T(8,128)(2,1)} %convolution_convert_fusion.14), channel_id=1, source_target_pairs={{0,4},{8,0},{16,8},{24,16},{28,24},{20,28},{12,20},{4,12},{1,5},{9... | collective-permute-start | bytes 1081352 | tf_op jit(solution)/shard_map/ppermute | solution.py:73
  610.9 45.3 %collective-permute-start.65 = (bf16[704,256]{1,0:T(8,128)(2,1)}, bf16[704,256]{1,0:T(8,128)(2,1)}, u32[]{:S(2)}, u32[]{:S(2)}) collective-permute-start(bf16[704,256]{1,0:T(8,128)(2,1)} %convolution_convert_fusion.15), channel_id=1, source_target_pairs={{0,8},{8,16},{16,24},{24,28},{28,20},{20,12},{12,4},{4,0},{1,9},{9... | collective-permute-start | bytes 1081352 | tf_op jit(solution)/shard_map/ppermute | solution.py:73
  663.3 25.9 %collective-permute-start.67 = (bf16[512,2048]{1,0:T(8,128)(2,1)}, bf16[512,2048]{1,0:T(8,128)(2,1)}, u32[]{:S(2)}, u32[]{:S(2)}) collective-permute-start(bf16[512,2048]{1,0:T(8,128)(2,1)} %fusion.46), channel_id=1, source_target_pairs={{0,1},{1,0},{2,3},{3,2},{4,5},{5,4},{6,7},{7,6},{8,9},{9,8},{10,11... | collective-permute-start | bytes 6291464 | tf_op jit(solution)/shard_map/ppermute | solution.py:181
  691.5 47.8 %collective-permute-start.68 = (bf16[512,2048]{1,0:T(8,128)(2,1)S(1)}, bf16[512,2048]{1,0:T(8,128)(2,1)S(1)}, u32[]{:S(2)}, u32[]{:S(2)}) collective-permute-start(bf16[512,2048]{1,0:T(8,128)(2,1)S(1)} %add_convert_fusion.1), channel_id=1, source_target_pairs={{0,2},{1,3},{2,0},{3,1},{4,6},{5,7},{6,4},{7,5},{8,10},{9,11},{10,... | collective-permute-start | bytes 6291464 | tf_op jit(solution)/shard_map/ppermute | solution.py:186
  709.6 20.6 %collective-permute-start.83 = (bf16[704,256]{1,0:T(8,128)(2,1)S(1)}, bf16[704,256]{1,0:T(8,128)(2,1)S(1)}, u32[]{:S(2)}, u32[]{:S(2)}) collective-permute-start(bf16[704,256]{1,0:T(8,128)(2,1)S(1)} %convolution_convert_fusion.11), channel_id=1, source_target_pairs={{0,4},{8,0},{16,8},{24,16},{28,24},{20,28},{12,20},{4,12},{1,5},{9... | collective-permute-start | bytes 1081352 | tf_op jit(solution)/shard_map/ppermute | solution.py:73
  711.7 19.2 %collective-permute-start.86 = (bf16[704,256]{1,0:T(8,128)(2,1)S(1)}, bf16[704,256]{1,0:T(8,128)(2,1)S(1)}, u32[]{:S(2)}, u32[]{:S(2)}) collective-permute-start(bf16[704,256]{1,0:T(8,128)(2,1)S(1)} %fusion.69), channel_id=1, source_target_pairs={{0,8},{8,16},{16,24},{24,28},{28,20},{20,12},{12,4},{4,0},{1,9},{9... | collective-permute-start | bytes 1081352 | tf_op jit(solution)/shard_map/ppermute | solution.py:73
  740.2 53.5 %collective-permute-start.75 = (bf16[512,2048]{1,0:T(8,128)(2,1)S(1)}, bf16[512,2048]{1,0:T(8,128)(2,1)}, u32[]{:S(2)}, u32[]{:S(2)}) collective-permute-start(bf16[512,2048]{1,0:T(8,128)(2,1)S(1)} %add_convert_fusion), channel_id=1, source_target_pairs={{0,1},{1,0},{2,3},{3,2},{4,5},{5,4},{6,7},{7,6},{8,9},{9,8},{10,11... | collective-permute-start | bytes 6291464 | tf_op jit(solution)/shard_map/ppermute | solution.py:181
  753.0 25.4 %collective-permute-start.77 = (f32[2,8,256]{2,0,1:T(2,128)S(1)}, f32[2,8,256]{2,0,1:T(2,128)S(1)}, u32[]{:S(2)}, u32[]{:S(2)}) collective-permute-start(f32[2,8,256]{2,0,1:T(2,128)S(1)} %bitcast.287), channel_id=1, source_target_pairs={{0,4},{4,0},{8,12},{12,8},{16,20},{20,16},{24,28},{28,24},{1,5},{5... | collective-permute-start | bytes 49160 | tf_op jit(solution)/shard_map/ppermute | solution.py:558
  802.0 18.3 %collective-permute-start.88 = (bf16[704,256]{1,0:T(8,128)(2,1)S(1)}, bf16[704,256]{1,0:T(8,128)(2,1)S(1)}, u32[]{:S(2)}, u32[]{:S(2)}) collective-permute-start(bf16[704,256]{1,0:T(8,128)(2,1)S(1)} %copy-done.120), channel_id=1, source_target_pairs={{0,8},{8,16},{16,24},{24,28},{28,20},{20,12},{12,4},{4,0},{1,9},{9... | collective-permute-start | bytes 1081352 | tf_op jit(solution)/shard_map/ppermute | solution.py:73
  805.3 18.5 %collective-permute-start.85 = (bf16[704,256]{1,0:T(8,128)(2,1)S(1)}, bf16[704,256]{1,0:T(8,128)(2,1)S(1)}, u32[]{:S(2)}, u32[]{:S(2)}) collective-permute-start(bf16[704,256]{1,0:T(8,128)(2,1)S(1)} %copy-done.117), channel_id=1, source_target_pairs={{0,4},{8,0},{16,8},{24,16},{28,24},{20,28},{12,20},{4,12},{1,5},{9... | collective-permute-start | bytes 1081352 | tf_op jit(solution)/shard_map/ppermute | solution.py:73
  814.0 18.6 %collective-permute-start.82 = (bf16[704,256]{1,0:T(8,128)(2,1)}, bf16[704,256]{1,0:T(8,128)(2,1)}, u32[]{:S(2)}, u32[]{:S(2)}) collective-permute-start(bf16[704,256]{1,0:T(8,128)(2,1)} %add_convert_fusion.15), channel_id=1, source_target_pairs={{0,8},{8,16},{16,24},{24,28},{28,20},{20,12},{12,4},{4,0},{1,9},{9... | collective-permute-start | bytes 1081352 | tf_op jit(solution)/shard_map/ppermute | solution.py:73
  (163 other events, 2029.9 us)
Sparse Core Ops, SparseCore 0:
  595.5 87.8 all-reduce.16
  687.8 76.5 all-reduce.18

commit v6 on v3

--- a/solution.py
+++ b/solution.py
@@ -182,7 +182,8 @@
 
 def tp_sum(part, others=lambda v: v, chips=lambda v: v, totals=lambda v: v):
     got = core_swap(others(part(1).astype(bf16)))
-    chip = chips((part(0) + got.astype(f32)).astype(bf16))
+    own = lax.optimization_barrier(part(0).astype(bf16))
+    chip = chips((own.astype(f32) + got.astype(f32)).astype(bf16))
     far = chip_swap(chip)
     total = totals((chip.astype(f32) + far.astype(f32)).astype(bf16))
     return total, core_swap(total)
@@ -723,11 +724,8 @@
     ring.token = None
     grad_both = []
     grad_down = Scatter(lambda k: down(hidden, sl(grad_low, k)), 1, n, chunk)
-    grad_mlp = [
-        Scatter(lambda k: down(sl(normed2, k), grad_both[0][:, :units]), -1, n, chunk),
-        Scatter(lambda k: down(sl(normed2, k), grad_both[0][:, units:]), 1, n, chunk),
-    ]
-    ring.add([grad_down, *grad_mlp])
+    grad_mlp = Scatter(lambda k: down(sl(normed2, k), grad_both[0]), -1, n, chunk)
+    ring.add([grad_down, grad_mlp])
     ring.issue(1)
     act, slope, w_down = ring.hold((act, slope, w_down))
     grad_both.append(
@@ -754,12 +752,10 @@
     grad_normed2 = tp_sum(
         lambda h: across(half_of(grad_both[0], h), w_mlp),
         others=ring.land,
-        chips=ring.land,
-        totals=lambda v: lands(v, 3),
+        totals=lambda v: ring.land((ring.land(), v)[1]),
     )
     turned = jnp.concatenate([half_of(hidden, 1), half_of(hidden, 0)], axis=0)
     turned = jnp.where(odd == 1, turned, hidden)
-    mlp_out = lax.psum(dot(after(turned, grad_normed2[0]), w_down).astype(bf16), "tp")
 
     grad_middle, grad_rec, sum_gain2 = in_halves(
         middle_back_kernel,
@@ -769,6 +765,8 @@
         [f32, bf16],
         1,
     )
+    grad_out = Scatter(lambda k: down(product, sl(grad_rec, k)), 1, n, chunk)
+    ring.add([grad_out])
     grad_rec = ring.land(grad_rec.reshape(rows, width))
 
     grad_product = across(grad_rec, w_out).reshape(wide)
@@ -780,7 +778,14 @@
         [pltpu.VMEM((piece, lanes), f32)],
         rows * lanes * 50,
     )
-    incoming = ring.land(carried(ring.land(early), -1, n, ring.land))
+    rounds = []
+
+    def keep_round(ends):
+        rounds.append(ends)
+        return ends
+
+    incoming = ring.land(carried(ring.land(early), -1, n, keep_round))
+    mlp_out = lax.psum(dot(after(turned, *rounds), w_down).astype(bf16), "tp")
     grad_gates, grad_inner, grad_gate_in, head, last, sums = per_sequence(
         gates_back_kernel,
         seqs,
@@ -814,7 +819,6 @@
         [pltpu.VMEM((piece, lanes), f32)] + [pltpu.VMEM((piece + pad_rows, lanes), f32)] * 2,
         gate_flops,
     )
-    head = ring.land(head)
     behind = lax.ppermute(
         head[:, : taps - 1].astype(bf16), "seq", [(i + 1, i) for i in range(n - 1)]
     ).astype(f32)
@@ -832,7 +836,6 @@
     grads = [
         Scatter(lambda k: down(back0, normed1[k]), 1, n, chunk),
         Scatter(lambda k: down(back1, normed1[k]), -1, n, chunk),
-        Scatter(lambda k: down(product, sl(grad_rec, k)), -1, n, chunk),
     ]
     ring.add(grads)
     ring.issue()
@@ -907,15 +910,15 @@
         output,
         grad_tokens,
         grad_gains[0],
-        jnp.transpose(jnp.stack(grads[:2]), (2, 0, 1)),
+        jnp.transpose(jnp.stack(grads), (2, 0, 1)),
         small[4:],
         small[3],
         grad_matrix,
         small[1:3],
         small[0],
-        grads[2],
+        grad_out.total(),
         grad_gains[1],
-        jnp.stack([g.total() for g in grad_mlp], axis=1),
+        grad_mlp.total().reshape(part, 2, units),
         grad_down.total(),
     )
 

time: 818 us -> 821 us (level)
    ppermute x77 -> x70, waiting for transfers between devices: 150 us -> 107 us  [issue(): flying.append((flow, lax.ppermute(message, 'seq', self.pairs[way])))]
    ppermute x8, waiting for transfers between devices: 30.3 us -> 45.9 us  [shifted(): return lax.ppermute(values, 'seq', pairs)]
    ppermute x3, waiting for transfers between devices: 12.6 us -> 27 us  [chip_swap(): return lax.ppermute(values, 'tp', [(i, i ^ 2) for i in range(size)])]
    unnamed x352 -> x351, local copies, waits for them, and re-layouts: 67 us -> 63.4 us
    ppermute x77 -> x70, starting transfers between devices: 91.2 us -> 94.7 us  [issue(): flying.append((flow, lax.ppermute(message, 'seq', self.pairs[way])))]
    dot_general x50 -> x42, matrix products: 109 us -> 108 us  [down(): lax.dot_general(a, b, (((0,), (0,)), ((), ())), preferred_element_type=f32)]
  transfers between devices with their start and end apart: 102 -> 95, of which waited for: 26 -> 28; matrix products, arithmetic and copies ran while one was open for 38% -> 38% of each run, Pallas kernels for 13% -> 13%
where the time goes in v6:
time: 821 us; the launch traced here: 811 us
  waiting for transfers between devices  197 us (24%)
  matrix products  196 us (24%)
  starting transfers between devices  134 us (16%)
  Pallas kernels  112 us (14%)
  local copies, waits for them, and re-layouts  109 us (13%)
  other arithmetic  46.6 us (6%)
  between operations  16.7 us (2%)
    dot_general x42, matrix products, down(): lax.dot_general(a, b, (((0,), (0,)), ((), ())), preferred_element_type=f32)  108 us
    ppermute x70, waiting for transfers between devices, issue(): flying.append((flow, lax.ppermute(message, 'seq', self.pairs[way])))  107 us
    ppermute x70, starting transfers between devices, issue(): flying.append((flow, lax.ppermute(message, 'seq', self.pairs[way])))  94.7 us
    unnamed x351, local copies, waits for them, and re-layouts  63.4 us
    pallas_call x8, Pallas kernels, by_rows(): pl.pallas_call(body, grid_spec=pltpu.PrefetchScalarGridSpec(num_scalar_pr...  55.8 us
    dot_general x19, matrix products, across(): lax.dot_general(a, b, (((1,), (1,)), ((), ())), preferred_element_type=f32)  47.2 us
    ppermute x8, waiting for transfers between devices, shifted(): return lax.ppermute(values, 'seq', pairs)  45.9 us
    pallas_call x3, Pallas kernels, per_sequence(): pl.pallas_call(kernel, grid=(seqs,), in_specs=[spec(a.shape, kind) for a,...  43.6 us
  transfers between devices with their start and end apart: 95, of which 28 were waited for; matrix products, arithmetic and copies ran while one was open for 38% of the time, Pallas kernels for 13%

profile of v6, /device:TPU:0, one launch (start us, length us, event | category | flops | bytes accessed | tf_op | source)
XLA Modules:
  0.0 811.5 jit_solution(3338069519194819628)
XLA Ops:
  31.0 3.4 constant_dynamic-update-slice_fusion.25
  36.6 8.5 %shard_map.255 = (bf16[4,256,2048]{2,1,0:T(8,128)(2,1)S(1)}, bf16[4,256,2048]{2,1,0:T(8,128)(2,1)}) custom-call(s32[4]{0:T(128)S(1)} %and_select_fusion.2.refs_0_, s32[8]{0:T(128)S(1)} %gather_fusion, bf16[4,256,2048]{2,1,0:T(8,128)(2,1)} %refs_2_, bf16[4,256,2048]{2,1,0:T(8,128)(2,1)} %refs_3_), custom_call_target="tpu_custom_call" | custom-call | flops 16777216 | bytes 16777216 | tf_op jit(solution)/shard_map/pallas_call | solution.py:411
  67.6 8.3 %collective-permute-done.7 = bf16[1056,256]{1,0:T(8,128)(2,1)S(1)} collective-permute-done((bf16[1056,256]{1,0:T(8,128)(2,1)}, bf16[1056,256]{1,0:T(8,128)(2,1)S(1)}, u32[]{:S(2)}, u32[]{:S(2)}) %collective-permute-start.7) | collective-permute-done | bytes 540704 | tf_op jit(solution)/shard_map/ppermute | solution.py:72
  77.0 9.6 %collective-permute-done.9 = bf16[1072,256]{1,0:T(8,128)(2,1)S(1)} collective-permute-done((bf16[1072,256]{1,0:T(8,128)(2,1)S(1)}, bf16[1072,256]{1,0:T(8,128)(2,1)S(1)}, u32[]{:S(2)}, u32[]{:S(2)}) %collective-permute-start.9) | collective-permute-done | bytes 548896 | tf_op jit(solution)/shard_map/ppermute | solution.py:72
  89.7 9.5 %collective-permute-done.13 = bf16[1056,256]{1,0:T(8,128)(2,1)S(1)} collective-permute-done((bf16[1056,256]{1,0:T(8,128)(2,1)S(1)}, bf16[1056,256]{1,0:T(8,128)(2,1)S(1)}, u32[]{:S(2)}, u32[]{:S(2)}) %collective-permute-start.13) | collective-permute-done | bytes 540704 | tf_op jit(solution)/shard_map/ppermute | solution.py:72
  115.1 3.4 add_convert_fusion.7
  131.5 3.5 collective-permute-start.16
  136.7 12.2 %collective-permute-done.16 = bf16[4,3,704]{2,1,0:T(4,128)(2,1)S(1)} collective-permute-done((bf16[4,3,704]{2,1,0:T(4,128)(2,1)S(1)}, bf16[4,3,704]{2,1,0:T(4,128)(2,1)S(1)}, u32[]{:S(2)}, u32[]{:S(2)}) %collective-permute-start.16) | collective-permute-done | bytes 16928 | tf_op jit(solution)/shard_map/ppermute | solution.py:653
  155.2 16.0 %shard_map.256 = (f32[4,256,704]{2,1,0:T(8,128)}, f32[4,256,704]{2,1,0:T(8,128)}, f32[4,256,704]{2,1,0:T(8,128)}, f32[4,256,704]{2,1,0:T(8,128)}, f32[4,256,704]...) custom-call(bf16[4,256,704]{2,1,0:T(8,128)(2,1)S(1)} %bitcast.194, ...), custom_call_target="tpu_custom_call" | custom-call | flops 2030043136 | bytes 23812096 | tf_op jit(solution)/shard_map/pallas_call | solution.py:374
  176.9 5.3 collective-permute-start.24
  182.3 7.6 collective-permute-done.24
  189.9 5.3 collective-permute-start.25
  195.3 5.0 collective-permute-start.26
  204.5 6.0 fusion.36
  212.4 3.3 convolution_convert_fusion.4
  226.9 3.4 convolution_convert_fusion.5
  233.3 11.5 %collective-permute-done.31 = bf16[256,1536]{1,0:T(8,128)(2,1)S(1)} collective-permute-done((bf16[256,1536]{1,0:T(8,128)(2,1)S(1)}, bf16[256,1536]{1,0:T(8,128)(2,1)S(1)}, u32[]{:S(2)}, u32[]{:S(2)}) %collective-permute-start.31) | collective-permute-done | bytes 786464 | tf_op jit(solution)/shard_map/ppermute | solution.py:72
  254.9 6.3 collective-permute-done.40
  267.1 3.6 collective-permute-done.38
  270.7 9.6 %collective-permute-done.41 = bf16[256,1536]{1,0:T(8,128)(2,1)S(1)} collective-permute-done((bf16[256,1536]{1,0:T(8,128)(2,1)S(1)}, bf16[256,1536]{1,0:T(8,128)(2,1)S(1)}, u32[]{:S(2)}, u32[]{:S(2)}) %collective-permute-start.41) | collective-permute-done | bytes 786464 | tf_op jit(solution)/shard_map/ppermute | solution.py:72
  284.3 9.4 %collective-permute-done.32 = bf16[512,2048]{1,0:T(8,128)(2,1)S(1)} collective-permute-done((bf16[512,2048]{1,0:T(8,128)(2,1)S(1)}, bf16[512,2048]{1,0:T(8,128)(2,1)S(1)}, u32[]{:S(2)}, u32[]{:S(2)}) %collective-permute-start.32) | collective-permute-done | bytes 2097184 | tf_op jit(solution)/shard_map/ppermute | solution.py:180
  295.9 4.9 collective-permute-done.36
  301.3 15.0 %collective-permute-done.34 = bf16[1536,256]{1,0:T(8,128)(2,1)S(1)} collective-permute-done((bf16[1536,256]{1,0:T(8,128)(2,1)}, bf16[1536,256]{1,0:T(8,128)(2,1)S(1)}, u32[]{:S(2)}, u32[]{:S(2)}) %collective-permute-start.34) | collective-permute-done | bytes 786464 | tf_op jit(solution)/shard_map/ppermute | solution.py:72
  322.2 5.1 shard_map.257
  327.2 5.1 shard_map.258
  336.1 17.5 %convolution_convert_fusion = bf16[1024,3072]{1,0:T(8,128)(2,1)S(1)} fusion(bf16[1024,2048]{1,0:T(8,128)(2,1)} %bitcast.220, bf16[2048,1536]{1,0:T(8,128)(2,1)} %copy-done.111, bf16[2048,1536]{1,0:T(8,128)(2,1)} %copy-done.110), kind=kOutput, calls=%fused_computation.40 | convolution fusion | flops 12913213440 | bytes 23068672 | tf_op jit(solution)/shard_map/dot_general | solution.py:572
  353.6 6.4 fusion.6
  376.2 12.4 %shard_map.259 = bf16[1024,3072]{1,0:T(8,128)(2,1)} custom-call(bf16[1024,2048]{1,0:T(8,128)(2,1)} %bitcast.231, bf16[1536,2048]{1,0:T(8,128)(2,1)} %constant_dynamic-update-slice_fusion.26.w_down, bf16[1024,1536]{1,0:T(8,128)(2,1)S(1)} %get-tuple-element.255.act, bf16[1024,1536]{1,0:T(8,128)(2,1)} %get-tuple-element.256.slope), custom_call_target="tpu_custom_call" | custom-call | flops 6442450944 | bytes 23068672 | tf_op jit(solution)/shard_map/pallas_call | solution.py:732
  388.6 11.8 %fusion.50 = bf16[512,2048]{1,0:T(8,128)(2,1)} fusion(bf16[2048,1536]{1,0:T(8,128)(2,1)} %copy-done.111, bf16[2048,1536]{1,0:T(8,128)(2,1)} %copy-done.110, bf16[1024,3072]{1,0:T(8,128)(2,1)} %shard_map.259), kind=kOutput, calls=%fused_computation.101 | convolution fusion | flops 6468665344 | bytes 17825792 | tf_op jit(solution)/shard_map/dot_general | solution.py:564
  401.4 4.4 convolution_convert_fusion.1
  405.9 4.1 convolution_convert_fusion.2
  412.1 10.7 %fusion.47 = bf16[512,2048]{1,0:T(8,128)(2,1)} fusion(bf16[2048,1536]{1,0:T(8,128)(2,1)} %copy-done.111, bf16[2048,1536]{1,0:T(8,128)(2,1)} %copy-done.110, bf16[1024,3072]{1,0:T(8,128)(2,1)S(1)} %copy-done.24), kind=kOutput, calls=%fused_computation.100 | convolution fusion | flops 6468665344 | bytes 17825792 | tf_op jit(solution)/shard_map/dot_general | solution.py:564
  426.8 4.6 fusion.33
  435.7 7.6 collective-permute-done.52
  443.3 4.6 fusion.21
  448.1 4.7 fusion.20
  454.9 17.6 %collective-permute-done.46 = bf16[512,2048]{1,0:T(8,128)(2,1)S(1)} collective-permute-done((bf16[512,2048]{1,0:T(8,128)(2,1)S(1)}, bf16[512,2048]{1,0:T(8,128)(2,1)S(1)}, u32[]{:S(2)}, u32[]{:S(2)}) %collective-permute-start.46) | collective-permute-done | bytes 2097184 | tf_op jit(solution)/shard_map/ppermute | solution.py:180
  482.2 7.3 shard_map.260
  489.5 7.5 shard_map.261
  498.3 7.7 fusion.86
  506.0 7.8 shard_map.262
  519.7 4.4 fusion.23
  525.8 4.7 fusion.22
  539.2 29.4 %collective-permute-done.56 = f32[4,2,704]{2,1,0:T(2,128)S(1)} collective-permute-done((f32[4,2,704]{2,1,0:T(2,128)S(1)}, f32[4,2,704]{2,1,0:T(2,128)S(1)}, u32[]{:S(2)}, u32[]{:S(2)}) %collective-permute-start.56) | collective-permute-done | bytes 22560 | tf_op jit(solution)/shard_map/ppermute | solution.py:529
  569.9 4.4 collective-permute-done.57
  577.0 8.3 %convolution_convert_fusion.3 = bf16[1024,2048]{1,0:T(8,128)(2,1)} fusion(bf16[1024,1536]{1,0:T(8,128)(2,1)S(1)} %copy-done.61, bf16[1536,2048]{1,0:T(8,128)(2,1)S(1)} %bitcast.271), kind=kOutput, calls=%fused_computation.73 | convolution fusion | flops 6444548096 | bytes 13631488 | tf_op jit(solution)/shard_map/dot_general | solution.py:572
  590.0 5.4 fusion.24
  595.4 5.9 collective-permute-start.64
  601.4 19.8 %shard_map.263 = (bf16[2,4,256,704]{3,2,1,0:T(8,128)(2,1)}, bf16[4,256,704]{2,1,0:T(8,128)(2,1)S(1)}, bf16[4,256,704]{2,1,0:T(8,128)(2,1)S(1)}, f32[4,8,704]{2,1...) custom-call(f32[4,256,704]{2,1,0:T(8,128)} %bitcast.241, f32[4,256,704]{2,1,0:T(8,128)} %get-tuple-element.395.slope, ...), custom_call_target="tpu_custom_call" | custom-call | flops 2030043136 | bytes 38514432 | tf_op jit(solution)/shard_map/pallas_call | solution.py:374
  632.5 5.6 collective-permute-done.64
  638.1 4.6 fusion.46
  657.1 3.6 fusion.45
  660.7 3.8 add_convert_fusion.1
  666.4 4.6 collective-permute-start.74
  675.0 4.9 fusion.19
  686.4 3.5 fusion.53
  689.9 5.6 reshape.426
  697.7 8.5 %shard_map.264 = bf16[4,256,2048]{2,1,0:T(8,128)(2,1)} custom-call(s32[4]{0:T(128)S(1)} %copy-done.23, s32[8]{0:T(128)S(1)} %copy-done.19, f32[4,256,2048]{2,1,0:T(8,128)} %get-tuple-element.228.refs_0_.refs_2_, bf16[4,256,2048]{2,1,0:T(8,128)(2,1)S(1)} %bitcast.196), custom_call_target="tpu_custom_call" | custom-call | flops 16777216 | bytes 16777216 | tf_op jit(solution)/shard_map/pallas_call | solution.py:411
  716.2 4.4 collective-permute-done.88
  724.7 4.1 collective-permute-done.82
  735.3 4.0 fusion.18
  746.3 5.4 collective-permute-done.71
  763.9 6.7 shard_map.265.refs_6_
  797.0 7.2 shard_map.266
  (671 shorter events, 318.2 us)
Async XLA Ops:
  7.2 688.3 %all-reduce.16.cloned.1.call-start = ((), (), s32[]{:S(2)}) async-start(), calls=%async_computation | async-start | bytes 8388608 | tf_op jit(solution)/shard_map/psum | solution.py:788
  11.2 23.3 %collective-permute-start = (bf16[1056,256]{1,0:T(8,128)(2,1)}, bf16[1056,256]{1,0:T(8,128)(2,1)S(1)}, u32[]{:S(2)}, u32[]{:S(2)}) collective-permute-start(bf16[1056,256]{1,0:T(8,128)(2,1)} %pad_maximum_fusion.21), channel_id=1, source_target_pairs={{0,8},{8,16},{16,24},{24,28},{28,20},{20,12},{12,4},{4,0},{1,9},{9... | collective-permute-start | bytes 1622024 | tf_op jit(solution)/shard_map/ppermute | solution.py:72
  14.2 20.3 %collective-permute-start.1 = (bf16[1056,256]{1,0:T(8,128)(2,1)}, bf16[1056,256]{1,0:T(8,128)(2,1)}, u32[]{:S(2)}, u32[]{:S(2)}) collective-permute-start(bf16[1056,256]{1,0:T(8,128)(2,1)} %pad_maximum_fusion.21), channel_id=1, source_target_pairs={{0,4},{8,0},{16,8},{24,16},{28,24},{20,28},{12,20},{4,12},{1,5},{9... | collective-permute-start | bytes 1622024 | tf_op jit(solution)/shard_map/ppermute | solution.py:72
  15.1 32.0 %collective-permute-start.2 = (bf16[1072,256]{1,0:T(8,128)(2,1)}, bf16[1072,256]{1,0:T(8,128)(2,1)}, u32[]{:S(2)}, u32[]{:S(2)}) collective-permute-start(bf16[1072,256]{1,0:T(8,128)(2,1)} %pad_maximum_fusion.20), channel_id=1, source_target_pairs={{0,8},{8,16},{16,24},{24,28},{28,20},{20,12},{12,4},{4,0},{1,9},{9... | collective-permute-start | bytes 1646600 | tf_op jit(solution)/shard_map/ppermute | solution.py:72
  17.1 30.0 %collective-permute-start.3 = (bf16[1072,256]{1,0:T(8,128)(2,1)}, bf16[1072,256]{1,0:T(8,128)(2,1)}, u32[]{:S(2)}, u32[]{:S(2)}) collective-permute-start(bf16[1072,256]{1,0:T(8,128)(2,1)} %pad_maximum_fusion.20), channel_id=1, source_target_pairs={{0,4},{8,0},{16,8},{24,16},{28,24},{20,28},{12,20},{4,12},{1,5},{9... | collective-permute-start | bytes 1646600 | tf_op jit(solution)/shard_map/ppermute | solution.py:72
  34.5 24.0 %collective-permute-start.10 = (bf16[1056,256]{1,0:T(8,128)(2,1)}, bf16[1056,256]{1,0:T(8,128)(2,1)S(1)}, u32[]{:S(2)}, u32[]{:S(2)}) collective-permute-start(bf16[1056,256]{1,0:T(8,128)(2,1)} %collective-permute-done.1), channel_id=1, source_target_pairs={{0,4},{8,0},{16,8},{24,16},{28,24},{20,28},{12,20},{4,12},{1,5},{9... | collective-permute-start | bytes 1622024 | tf_op jit(solution)/shard_map/ppermute | solution.py:72
  36.5 23.9 %collective-permute-start.5 = (bf16[1056,256]{1,0:T(8,128)(2,1)S(1)}, bf16[1056,256]{1,0:T(8,128)(2,1)}, u32[]{:S(2)}, u32[]{:S(2)}) collective-permute-start(bf16[1056,256]{1,0:T(8,128)(2,1)S(1)} %collective-permute-done), channel_id=1, source_target_pairs={{0,8},{8,16},{16,24},{24,28},{28,20},{20,12},{12,4},{4,0},{1,9},{9... | collective-permute-start | bytes 1622024 | tf_op jit(solution)/shard_map/ppermute | solution.py:72
  58.5 18.5 %collective-permute-start.11 = (bf16[1056,256]{1,0:T(8,128)(2,1)S(1)}, bf16[1056,256]{1,0:T(8,128)(2,1)S(1)}, u32[]{:S(2)}, u32[]{:S(2)}) collective-permute-start(bf16[1056,256]{1,0:T(8,128)(2,1)S(1)} %collective-permute-done.10), channel_id=1, source_target_pairs={{0,4},{8,0},{16,8},{24,16},{28,24},{20,28},{12,20},{4,12},{1,5},{9... | collective-permute-start | bytes 1622024 | tf_op jit(solution)/shard_map/ppermute | solution.py:72
  63.9 24.7 %collective-permute-start.6 = (bf16[1072,256]{1,0:T(8,128)(2,1)S(1)}, bf16[1072,256]{1,0:T(8,128)(2,1)S(1)}, u32[]{:S(2)}, u32[]{:S(2)}) collective-permute-start(bf16[1072,256]{1,0:T(8,128)(2,1)S(1)} %collective-permute-done.4), channel_id=1, source_target_pairs={{0,8},{8,16},{16,24},{24,28},{28,20},{20,12},{12,4},{4,0},{1,9},{9... | collective-permute-start | bytes 1646600 | tf_op jit(solution)/shard_map/ppermute | solution.py:72
  65.9 20.7 %collective-permute-start.9 = (bf16[1072,256]{1,0:T(8,128)(2,1)S(1)}, bf16[1072,256]{1,0:T(8,128)(2,1)S(1)}, u32[]{:S(2)}, u32[]{:S(2)}) collective-permute-start(bf16[1072,256]{1,0:T(8,128)(2,1)S(1)} %collective-permute-done.8), channel_id=1, source_target_pairs={{0,4},{8,0},{16,8},{24,16},{28,24},{20,28},{12,20},{4,12},{1,5},{9... | collective-permute-start | bytes 1646600 | tf_op jit(solution)/shard_map/ppermute | solution.py:72
  75.8 23.3 %collective-permute-start.13 = (bf16[1056,256]{1,0:T(8,128)(2,1)S(1)}, bf16[1056,256]{1,0:T(8,128)(2,1)S(1)}, u32[]{:S(2)}, u32[]{:S(2)}) collective-permute-start(bf16[1056,256]{1,0:T(8,128)(2,1)S(1)} %collective-permute-done.7), channel_id=1, source_target_pairs={{0,8},{8,16},{16,24},{24,28},{28,20},{20,12},{12,4},{4,0},{1,9},{9... | collective-permute-start | bytes 1622024 | tf_op jit(solution)/shard_map/ppermute | solution.py:72
  86.9 38.5 %collective-permute-start.15 = (bf16[256,1536]{1,0:T(8,128)(2,1)}, bf16[256,1536]{1,0:T(8,128)(2,1)}, u32[]{:S(2)}, u32[]{:S(2)}) collective-permute-start(bf16[256,1536]{1,0:T(8,128)(2,1)} %get-tuple-element.198), channel_id=1, source_target_pairs={{0,4},{8,0},{16,8},{24,16},{28,24},{20,28},{12,20},{4,12},{1,5},{9... | collective-permute-start | bytes 2359304 | tf_op jit(solution)/shard_map/ppermute | solution.py:72
  88.6 36.9 %collective-permute-start.14 = (bf16[256,1536]{1,0:T(8,128)(2,1)}, bf16[256,1536]{1,0:T(8,128)(2,1)}, u32[]{:S(2)}, u32[]{:S(2)}) collective-permute-start(bf16[256,1536]{1,0:T(8,128)(2,1)} %get-tuple-element.198), channel_id=1, source_target_pairs={{0,8},{8,16},{16,24},{24,28},{28,20},{20,12},{12,4},{4,0},{1,9},{9... | collective-permute-start | bytes 2359304 | tf_op jit(solution)/shard_map/ppermute | solution.py:72
  99.2 49.7 %collective-permute-start.17 = (bf16[256,1536]{1,0:T(8,128)(2,1)}, bf16[256,1536]{1,0:T(8,128)(2,1)}, u32[]{:S(2)}, u32[]{:S(2)}) collective-permute-start(bf16[256,1536]{1,0:T(8,128)(2,1)} %get-tuple-element.201), channel_id=1, source_target_pairs={{0,8},{8,16},{16,24},{24,28},{28,20},{20,12},{12,4},{4,0},{1,9},{9... | collective-permute-start | bytes 2359304 | tf_op jit(solution)/shard_map/ppermute | solution.py:72
  109.0 39.9 %collective-permute-start.18 = (bf16[256,1536]{1,0:T(8,128)(2,1)}, bf16[256,1536]{1,0:T(8,128)(2,1)}, u32[]{:S(2)}, u32[]{:S(2)}) collective-permute-start(bf16[256,1536]{1,0:T(8,128)(2,1)} %get-tuple-element.201), channel_id=1, source_target_pairs={{0,4},{8,0},{16,8},{24,16},{28,24},{20,28},{12,20},{4,12},{1,5},{9... | collective-permute-start | bytes 2359304 | tf_op jit(solution)/shard_map/ppermute | solution.py:72
  125.5 45.8 %collective-permute-start.19 = (bf16[256,1536]{1,0:T(8,128)(2,1)}, bf16[256,1536]{1,0:T(8,128)(2,1)}, u32[]{:S(2)}, u32[]{:S(2)}) collective-permute-start(bf16[256,1536]{1,0:T(8,128)(2,1)} %collective-permute-done.14), channel_id=1, source_target_pairs={{0,8},{8,16},{16,24},{24,28},{28,20},{20,12},{12,4},{4,0},{1,9},{9... | collective-permute-start | bytes 2359304 | tf_op jit(solution)/shard_map/ppermute | solution.py:72
  125.9 45.3 %collective-permute-start.20 = (bf16[256,1536]{1,0:T(8,128)(2,1)}, bf16[256,1536]{1,0:T(8,128)(2,1)S(1)}, u32[]{:S(2)}, u32[]{:S(2)}) collective-permute-start(bf16[256,1536]{1,0:T(8,128)(2,1)} %collective-permute-done.15), channel_id=1, source_target_pairs={{0,4},{8,0},{16,8},{24,16},{28,24},{20,28},{12,20},{4,12},{1,5},{9... | collective-permute-start | bytes 2359304 | tf_op jit(solution)/shard_map/ppermute | solution.py:72
  148.9 28.0 %collective-permute-start.22 = (bf16[256,1536]{1,0:T(8,128)(2,1)}, bf16[256,1536]{1,0:T(8,128)(2,1)S(1)}, u32[]{:S(2)}, u32[]{:S(2)}) collective-permute-start(bf16[256,1536]{1,0:T(8,128)(2,1)} %collective-permute-done.17), channel_id=1, source_target_pairs={{0,8},{8,16},{16,24},{24,28},{28,20},{20,12},{12,4},{4,0},{1,9},{9... | collective-permute-start | bytes 2359304 | tf_op jit(solution)/shard_map/ppermute | solution.py:72
  152.2 24.7 %collective-permute-start.23 = (bf16[256,1536]{1,0:T(8,128)(2,1)}, bf16[256,1536]{1,0:T(8,128)(2,1)S(1)}, u32[]{:S(2)}, u32[]{:S(2)}) collective-permute-start(bf16[256,1536]{1,0:T(8,128)(2,1)} %collective-permute-done.18), channel_id=1, source_target_pairs={{0,4},{8,0},{16,8},{24,16},{28,24},{20,28},{12,20},{4,12},{1,5},{9... | collective-permute-start | bytes 2359304 | tf_op jit(solution)/shard_map/ppermute | solution.py:72
  174.5 29.2 %collective-permute-start.27 = (bf16[1536,256]{1,0:T(8,128)(2,1)}, bf16[1536,256]{1,0:T(8,128)(2,1)}, u32[]{:S(2)}, u32[]{:S(2)}) collective-permute-start(bf16[1536,256]{1,0:T(8,128)(2,1)} %param.27), channel_id=1, source_target_pairs={{0,8},{8,16},{16,24},{24,28},{28,20},{20,12},{12,4},{4,0},{1,9},{9... | collective-permute-start | bytes 2359304 | tf_op jit(solution)/shard_map/ppermute | solution.py:72
  175.3 28.4 %collective-permute-start.28 = (bf16[1536,256]{1,0:T(8,128)(2,1)}, bf16[1536,256]{1,0:T(8,128)(2,1)S(1)}, u32[]{:S(2)}, u32[]{:S(2)}) collective-permute-start(bf16[1536,256]{1,0:T(8,128)(2,1)} %param.27), channel_id=1, source_target_pairs={{0,4},{8,0},{16,8},{24,16},{28,24},{20,28},{12,20},{4,12},{1,5},{9... | collective-permute-start | bytes 2359304 | tf_op jit(solution)/shard_map/ppermute | solution.py:72
  223.8 20.9 %collective-permute-start.31 = (bf16[256,1536]{1,0:T(8,128)(2,1)S(1)}, bf16[256,1536]{1,0:T(8,128)(2,1)S(1)}, u32[]{:S(2)}, u32[]{:S(2)}) collective-permute-start(bf16[256,1536]{1,0:T(8,128)(2,1)S(1)} %copy-done.97), channel_id=1, source_target_pairs={{0,4},{8,0},{16,8},{24,16},{28,24},{20,28},{12,20},{4,12},{1,5},{9... | collective-permute-start | bytes 2359304 | tf_op jit(solution)/shard_map/ppermute | solution.py:72
  226.9 19.9 %collective-permute-start.30 = (bf16[256,1536]{1,0:T(8,128)(2,1)}, bf16[256,1536]{1,0:T(8,128)(2,1)S(1)}, u32[]{:S(2)}, u32[]{:S(2)}) collective-permute-start(bf16[256,1536]{1,0:T(8,128)(2,1)} %collective-permute-done.19), channel_id=1, source_target_pairs={{0,8},{8,16},{16,24},{24,28},{28,20},{20,12},{12,4},{4,0},{1,9},{9... | collective-permute-start | bytes 2359304 | tf_op jit(solution)/shard_map/ppermute | solution.py:72
  230.3 30.9 %collective-permute-start.40 = (bf16[256,1536]{1,0:T(8,128)(2,1)S(1)}, bf16[256,1536]{1,0:T(8,128)(2,1)S(1)}, u32[]{:S(2)}, u32[]{:S(2)}) collective-permute-start(bf16[256,1536]{1,0:T(8,128)(2,1)S(1)} %copy-done.102), channel_id=1, source_target_pairs={{0,4},{8,0},{16,8},{24,16},{28,24},{20,28},{12,20},{4,12},{1,5},{9... | collective-permute-start | bytes 2359304 | tf_op jit(solution)/shard_map/ppermute | solution.py:72
  246.7 46.9 %collective-permute-start.32 = (bf16[512,2048]{1,0:T(8,128)(2,1)S(1)}, bf16[512,2048]{1,0:T(8,128)(2,1)S(1)}, u32[]{:S(2)}, u32[]{:S(2)}) collective-permute-start(bf16[512,2048]{1,0:T(8,128)(2,1)S(1)} %add_convert_fusion.5), channel_id=1, source_target_pairs={{0,2},{1,3},{2,0},{3,1},{4,6},{5,7},{6,4},{7,5},{8,10},{9,11},{10,... | collective-permute-start | bytes 6291464 | tf_op jit(solution)/shard_map/ppermute | solution.py:180
  252.0 18.6 %collective-permute-start.38 = (bf16[256,1536]{1,0:T(8,128)(2,1)S(1)}, bf16[256,1536]{1,0:T(8,128)(2,1)S(1)}, u32[]{:S(2)}, u32[]{:S(2)}) collective-permute-start(bf16[256,1536]{1,0:T(8,128)(2,1)S(1)} %copy-done.104), channel_id=1, source_target_pairs={{0,8},{8,16},{16,24},{24,28},{28,20},{20,12},{12,4},{4,0},{1,9},{9... | collective-permute-start | bytes 2359304 | tf_op jit(solution)/shard_map/ppermute | solution.py:72
  261.2 19.2 %collective-permute-start.41 = (bf16[256,1536]{1,0:T(8,128)(2,1)S(1)}, bf16[256,1536]{1,0:T(8,128)(2,1)S(1)}, u32[]{:S(2)}, u32[]{:S(2)}) collective-permute-start(bf16[256,1536]{1,0:T(8,128)(2,1)S(1)} %collective-permute-done.40), channel_id=1, source_target_pairs={{0,4},{8,0},{16,8},{24,16},{28,24},{20,28},{12,20},{4,12},{1,5},{9... | collective-permute-start | bytes 2359304 | tf_op jit(solution)/shard_map/ppermute | solution.py:72
  280.4 37.6 %collective-permute-start.39 = (bf16[256,1536]{1,0:T(8,128)(2,1)S(1)}, bf16[256,1536]{1,0:T(8,128)(2,1)S(1)}, u32[]{:S(2)}, u32[]{:S(2)}) collective-permute-start(bf16[256,1536]{1,0:T(8,128)(2,1)S(1)} %collective-permute-done.30), channel_id=1, source_target_pairs={{0,8},{8,16},{16,24},{24,28},{28,20},{20,12},{12,4},{4,0},{1,9},{9... | collective-permute-start | bytes 2359304 | tf_op jit(solution)/shard_map/ppermute | solution.py:72
  282.3 18.5 %collective-permute-start.36 = (bf16[1536,256]{1,0:T(8,128)(2,1)S(1)}, bf16[1536,256]{1,0:T(8,128)(2,1)S(1)}, u32[]{:S(2)}, u32[]{:S(2)}) collective-permute-start(bf16[1536,256]{1,0:T(8,128)(2,1)S(1)} %copy-done.99), channel_id=1, source_target_pairs={{0,4},{8,0},{16,8},{24,16},{28,24},{20,28},{12,20},{4,12},{1,5},{9... | collective-permute-start | bytes 2359304 | tf_op jit(solution)/shard_map/ppermute | solution.py:72
  283.0 33.3 %collective-permute-start.34 = (bf16[1536,256]{1,0:T(8,128)(2,1)}, bf16[1536,256]{1,0:T(8,128)(2,1)S(1)}, u32[]{:S(2)}, u32[]{:S(2)}) collective-permute-start(bf16[1536,256]{1,0:T(8,128)(2,1)} %collective-permute-done.27), channel_id=1, source_target_pairs={{0,8},{8,16},{16,24},{24,28},{28,20},{20,12},{12,4},{4,0},{1,9},{9... | collective-permute-start | bytes 2359304 | tf_op jit(solution)/shard_map/ppermute | solution.py:72
  294.4 32.8 %collective-permute-start.33 = (bf16[512,2048]{1,0:T(8,128)(2,1)S(1)}, bf16[512,2048]{1,0:T(8,128)(2,1)S(1)}, u32[]{:S(2)}, u32[]{:S(2)}) collective-permute-start(bf16[512,2048]{1,0:T(8,128)(2,1)S(1)} %add_convert_fusion.4), channel_id=1, source_target_pairs={{0,1},{1,0},{2,3},{3,2},{4,5},{5,4},{6,7},{7,6},{8,9},{9,8},{10,11... | collective-permute-start | bytes 6291464 | tf_op jit(solution)/shard_map/ppermute | solution.py:175
  300.8 31.5 %collective-permute-start.37 = (bf16[1536,256]{1,0:T(8,128)(2,1)S(1)}, bf16[1536,256]{1,0:T(8,128)(2,1)S(1)}, u32[]{:S(2)}, u32[]{:S(2)}) collective-permute-start(bf16[1536,256]{1,0:T(8,128)(2,1)S(1)} %collective-permute-done.36), channel_id=1, source_target_pairs={{0,4},{8,0},{16,8},{24,16},{28,24},{20,28},{12,20},{4,12},{1,5},{9... | collective-permute-start | bytes 2359304 | tf_op jit(solution)/shard_map/ppermute | solution.py:72
  334.0 28.6 %collective-permute-start.42 = (bf16[1536,256]{1,0:T(8,128)(2,1)}, bf16[1536,256]{1,0:T(8,128)(2,1)}, u32[]{:S(2)}, u32[]{:S(2)}) collective-permute-start(bf16[1536,256]{1,0:T(8,128)(2,1)} %collective-permute-done.35), channel_id=1, source_target_pairs={{0,8},{8,16},{16,24},{24,28},{28,20},{20,12},{12,4},{4,0},{1,9},{9... | collective-permute-start | bytes 2359304 | tf_op jit(solution)/shard_map/ppermute | solution.py:72
  373.8 26.7 %collective-permute-start.44 = (bf16[1536,256]{1,0:T(8,128)(2,1)}, bf16[1536,256]{1,0:T(8,128)(2,1)S(1)}, u32[]{:S(2)}, u32[]{:S(2)}) collective-permute-start(bf16[1536,256]{1,0:T(8,128)(2,1)} %convolution_convert_fusion.6), channel_id=1, source_target_pairs={{0,4},{8,0},{16,8},{24,16},{28,24},{20,28},{12,20},{4,12},{1,5},{9... | collective-permute-start | bytes 2359304 | tf_op jit(solution)/shard_map/ppermute | solution.py:72
  373.9 27.5 %collective-permute-start.43 = (bf16[1536,256]{1,0:T(8,128)(2,1)}, bf16[1536,256]{1,0:T(8,128)(2,1)S(1)}, u32[]{:S(2)}, u32[]{:S(2)}) collective-permute-start(bf16[1536,256]{1,0:T(8,128)(2,1)} %convolution_convert_fusion.7), channel_id=1, source_target_pairs={{0,8},{8,16},{16,24},{24,28},{28,20},{20,12},{12,4},{4,0},{1,9},{9... | collective-permute-start | bytes 2359304 | tf_op jit(solution)/shard_map/ppermute | solution.py:72
  401.4 21.4 %collective-permute-start.45 = (bf16[512,2048]{1,0:T(8,128)(2,1)}, bf16[512,2048]{1,0:T(8,128)(2,1)S(1)}, u32[]{:S(2)}, u32[]{:S(2)}) collective-permute-start(bf16[512,2048]{1,0:T(8,128)(2,1)} %fusion.50), channel_id=1, source_target_pairs={{0,1},{1,0},{2,3},{3,2},{4,5},{5,4},{6,7},{7,6},{8,9},{9,8},{10,11... | collective-permute-start | bytes 6291464 | tf_op jit(solution)/shard_map/ppermute | solution.py:175
  405.8 37.5 %collective-permute-start.52 = (bf16[256,3072]{1,0:T(8,128)(2,1)}, bf16[256,3072]{1,0:T(8,128)(2,1)}, u32[]{:S(2)}, u32[]{:S(2)}) collective-permute-start(bf16[256,3072]{1,0:T(8,128)(2,1)} %convolution_convert_fusion.1), channel_id=1, source_target_pairs={{0,4},{8,0},{16,8},{24,16},{28,24},{20,28},{12,20},{4,12},{1,5},{9... | collective-permute-start | bytes 4718600 | tf_op jit(solution)/shard_map/ppermute | solution.py:72
  410.0 38.1 %collective-permute-start.50 = (bf16[256,3072]{1,0:T(8,128)(2,1)}, bf16[256,3072]{1,0:T(8,128)(2,1)}, u32[]{:S(2)}, u32[]{:S(2)}) collective-permute-start(bf16[256,3072]{1,0:T(8,128)(2,1)} %convolution_convert_fusion.2), channel_id=1, source_target_pairs={{0,8},{8,16},{16,24},{24,28},{28,20},{20,12},{12,4},{4,0},{1,9},{9... | collective-permute-start | bytes 4718600 | tf_op jit(solution)/shard_map/ppermute | solution.py:72
  425.2 47.3 %collective-permute-start.46 = (bf16[512,2048]{1,0:T(8,128)(2,1)S(1)}, bf16[512,2048]{1,0:T(8,128)(2,1)S(1)}, u32[]{:S(2)}, u32[]{:S(2)}) collective-permute-start(bf16[512,2048]{1,0:T(8,128)(2,1)S(1)} %add_convert_fusion.3), channel_id=1, source_target_pairs={{0,2},{1,3},{2,0},{3,1},{4,6},{5,7},{6,4},{7,5},{8,10},{9,11},{10,... | collective-permute-start | bytes 6291464 | tf_op jit(solution)/shard_map/ppermute | solution.py:180
  432.5 40.8 %collective-permute-start.48 = (bf16[1536,256]{1,0:T(8,128)(2,1)S(1)}, bf16[1536,256]{1,0:T(8,128)(2,1)S(1)}, u32[]{:S(2)}, u32[]{:S(2)}) collective-permute-start(bf16[1536,256]{1,0:T(8,128)(2,1)S(1)} %fusion.55), channel_id=1, source_target_pairs={{0,4},{8,0},{16,8},{24,16},{28,24},{20,28},{12,20},{4,12},{1,5},{9... | collective-permute-start | bytes 2359304 | tf_op jit(solution)/shard_map/ppermute | solution.py:72
  433.8 39.5 %collective-permute-start.47 = (bf16[1536,256]{1,0:T(8,128)(2,1)S(1)}, bf16[1536,256]{1,0:T(8,128)(2,1)S(1)}, u32[]{:S(2)}, u32[]{:S(2)}) collective-permute-start(bf16[1536,256]{1,0:T(8,128)(2,1)S(1)} %fusion.54), channel_id=1, source_target_pairs={{0,8},{8,16},{16,24},{24,28},{28,20},{20,12},{12,4},{4,0},{1,9},{9... | collective-permute-start | bytes 2359304 | tf_op jit(solution)/shard_map/ppermute | solution.py:72
  448.0 49.0 %collective-permute-start.53 = (bf16[256,3072]{1,0:T(8,128)(2,1)}, bf16[256,3072]{1,0:T(8,128)(2,1)S(1)}, u32[]{:S(2)}, u32[]{:S(2)}) collective-permute-start(bf16[256,3072]{1,0:T(8,128)(2,1)} %fusion.21), channel_id=1, source_target_pairs={{0,4},{8,0},{16,8},{24,16},{28,24},{20,28},{12,20},{4,12},{1,5},{9... | collective-permute-start | bytes 4718600 | tf_op jit(solution)/shard_map/ppermute | solution.py:72
  452.7 45.5 %collective-permute-start.51 = (bf16[256,3072]{1,0:T(8,128)(2,1)}, bf16[256,3072]{1,0:T(8,128)(2,1)}, u32[]{:S(2)}, u32[]{:S(2)}) collective-permute-start(bf16[256,3072]{1,0:T(8,128)(2,1)} %fusion.20), channel_id=1, source_target_pairs={{0,8},{8,16},{16,24},{24,28},{28,20},{20,12},{12,4},{4,0},{1,9},{9... | collective-permute-start | bytes 4718600 | tf_op jit(solution)/shard_map/ppermute | solution.py:72
  478.2 35.6 %collective-permute-start.55 = (bf16[1536,256]{1,0:T(8,128)(2,1)}, bf16[1536,256]{1,0:T(8,128)(2,1)S(1)}, u32[]{:S(2)}, u32[]{:S(2)}) collective-permute-start(bf16[1536,256]{1,0:T(8,128)(2,1)} %fusion.57), channel_id=1, source_target_pairs={{0,4},{8,0},{16,8},{24,16},{28,24},{20,28},{12,20},{4,12},{1,5},{9... | collective-permute-start | bytes 2359304 | tf_op jit(solution)/shard_map/ppermute | solution.py:72
  480.5 33.8 %collective-permute-start.54 = (bf16[1536,256]{1,0:T(8,128)(2,1)}, bf16[1536,256]{1,0:T(8,128)(2,1)}, u32[]{:S(2)}, u32[]{:S(2)}) collective-permute-start(bf16[1536,256]{1,0:T(8,128)(2,1)} %fusion.56), channel_id=1, source_target_pairs={{0,8},{8,16},{16,24},{24,28},{28,20},{20,12},{12,4},{4,0},{1,9},{9... | collective-permute-start | bytes 2359304 | tf_op jit(solution)/shard_map/ppermute | solution.py:72
  524.1 65.8 %collective-permute-start.61 = (bf16[256,3072]{1,0:T(8,128)(2,1)}, bf16[256,3072]{1,0:T(8,128)(2,1)S(1)}, u32[]{:S(2)}, u32[]{:S(2)}) collective-permute-start(bf16[256,3072]{1,0:T(8,128)(2,1)} %fusion.23), channel_id=1, source_target_pairs={{0,4},{8,0},{16,8},{24,16},{28,24},{20,28},{12,20},{4,12},{1,5},{9... | collective-permute-start | bytes 4718600 | tf_op jit(solution)/shard_map/ppermute | solution.py:72
  530.5 59.5 %collective-permute-start.60 = (bf16[256,3072]{1,0:T(8,128)(2,1)}, bf16[256,3072]{1,0:T(8,128)(2,1)S(1)}, u32[]{:S(2)}, u32[]{:S(2)}) collective-permute-start(bf16[256,3072]{1,0:T(8,128)(2,1)} %fusion.22), channel_id=1, source_target_pairs={{0,8},{8,16},{16,24},{24,28},{28,20},{20,12},{12,4},{4,0},{1,9},{9... | collective-permute-start | bytes 4718600 | tf_op jit(solution)/shard_map/ppermute | solution.py:72
  531.2 37.3 %collective-permute-start.56 = (f32[4,2,704]{2,1,0:T(2,128)S(1)}, f32[4,2,704]{2,1,0:T(2,128)S(1)}, u32[]{:S(2)}, u32[]{:S(2)}) collective-permute-start(f32[4,2,704]{2,1,0:T(2,128)S(1)} %slice.568), channel_id=1, source_target_pairs={{4,0},{8,4},{12,8},{16,12},{20,16},{24,20},{28,24},{5,1},{9,5},{13... | collective-permute-start | bytes 67592 | tf_op jit(solution)/shard_map/ppermute | solution.py:529
  535.9 96.7 %collective-permute-start.63 = (bf16[1536,256]{1,0:T(8,128)(2,1)}, bf16[1536,256]{1,0:T(8,128)(2,1)}, u32[]{:S(2)}, u32[]{:S(2)}) collective-permute-start(bf16[1536,256]{1,0:T(8,128)(2,1)} %fusion.58), channel_id=1, source_target_pairs={{0,8},{8,16},{16,24},{24,28},{28,20},{20,12},{12,4},{4,0},{1,9},{9... | collective-permute-start | bytes 2359304 | tf_op jit(solution)/shard_map/ppermute | solution.py:72
  585.3 186.1 %all-reduce.18.cloned.1.call-start = ((), (), s32[]{:S(2)}) async-start(), calls=%async_computation.1 | async-start | bytes 1081344 | tf_op jit(solution)/shard_map/psum | solution.py:866
  595.4 42.7 %collective-permute-start.64 = (bf16[256,3072]{1,0:T(8,128)(2,1)S(1)}, bf16[256,3072]{1,0:T(8,128)(2,1)S(1)}, u32[]{:S(2)}, u32[]{:S(2)}) collective-permute-start(bf16[256,3072]{1,0:T(8,128)(2,1)S(1)} %fusion.24), channel_id=1, source_target_pairs={{0,4},{8,0},{16,8},{24,16},{28,24},{20,28},{12,20},{4,12},{1,5},{9... | collective-permute-start | bytes 4718600 | tf_op jit(solution)/shard_map/ppermute | solution.py:72
  622.5 42.0 %collective-permute-start.67 = (bf16[704,256]{1,0:T(8,128)(2,1)}, bf16[704,256]{1,0:T(8,128)(2,1)}, u32[]{:S(2)}, u32[]{:S(2)}) collective-permute-start(bf16[704,256]{1,0:T(8,128)(2,1)} %convolution_convert_fusion.14), channel_id=1, source_target_pairs={{0,4},{8,0},{16,8},{24,16},{28,24},{20,28},{12,20},{4,12},{1,5},{9... | collective-permute-start | bytes 1081352 | tf_op jit(solution)/shard_map/ppermute | solution.py:72
  625.2 39.3 %collective-permute-start.66 = (bf16[704,256]{1,0:T(8,128)(2,1)}, bf16[704,256]{1,0:T(8,128)(2,1)}, u32[]{:S(2)}, u32[]{:S(2)}) collective-permute-start(bf16[704,256]{1,0:T(8,128)(2,1)} %convolution_convert_fusion.15), channel_id=1, source_target_pairs={{0,8},{8,16},{16,24},{24,28},{28,20},{20,12},{12,4},{4,0},{1,9},{9... | collective-permute-start | bytes 1081352 | tf_op jit(solution)/shard_map/ppermute | solution.py:72
  642.8 17.9 %collective-permute-start.65 = (bf16[512,2048]{1,0:T(8,128)(2,1)}, bf16[512,2048]{1,0:T(8,128)(2,1)}, u32[]{:S(2)}, u32[]{:S(2)}) collective-permute-start(bf16[512,2048]{1,0:T(8,128)(2,1)} %fusion.46), channel_id=1, source_target_pairs={{0,1},{1,0},{2,3},{3,2},{4,5},{5,4},{6,7},{7,6},{8,9},{9,8},{10,11... | collective-permute-start | bytes 6291464 | tf_op jit(solution)/shard_map/ppermute | solution.py:175
  680.0 55.3 %collective-permute-start.68 = (bf16[512,2048]{1,0:T(8,128)(2,1)}, bf16[512,2048]{1,0:T(8,128)(2,1)}, u32[]{:S(2)}, u32[]{:S(2)}) collective-permute-start(bf16[512,2048]{1,0:T(8,128)(2,1)} %add_convert_fusion.1), channel_id=1, source_target_pairs={{0,2},{1,3},{2,0},{3,1},{4,6},{5,7},{6,4},{7,5},{8,10},{9,11},{10,... | collective-permute-start | bytes 6291464 | tf_op jit(solution)/shard_map/ppermute | solution.py:180
  684.3 25.7 %collective-permute-start.75 = (bf16[704,256]{1,0:T(8,128)(2,1)}, bf16[704,256]{1,0:T(8,128)(2,1)}, u32[]{:S(2)}, u32[]{:S(2)}) collective-permute-start(bf16[704,256]{1,0:T(8,128)(2,1)} %fusion.65), channel_id=1, source_target_pairs={{0,8},{8,16},{16,24},{24,28},{28,20},{20,12},{12,4},{4,0},{1,9},{9... | collective-permute-start | bytes 1081352 | tf_op jit(solution)/shard_map/ppermute | solution.py:72
  684.3 26.0 %collective-permute-start.81 = (bf16[704,256]{1,0:T(8,128)(2,1)}, bf16[704,256]{1,0:T(8,128)(2,1)}, u32[]{:S(2)}, u32[]{:S(2)}) collective-permute-start(bf16[704,256]{1,0:T(8,128)(2,1)} %convolution_convert_fusion.12), channel_id=1, source_target_pairs={{0,4},{8,0},{16,8},{24,16},{28,24},{20,28},{12,20},{4,12},{1,5},{9... | collective-permute-start | bytes 1081352 | tf_op jit(solution)/shard_map/ppermute | solution.py:72
  720.6 18.9 %collective-permute-start.89 = (bf16[704,256]{1,0:T(8,128)(2,1)}, bf16[704,256]{1,0:T(8,128)(2,1)S(1)}, u32[]{:S(2)}, u32[]{:S(2)}) collective-permute-start(bf16[704,256]{1,0:T(8,128)(2,1)} %convolution_convert_fusion.10), channel_id=1, source_target_pairs={{0,4},{8,0},{16,8},{24,16},{28,24},{20,28},{12,20},{4,12},{1,5},{9... | collective-permute-start | bytes 1081352 | tf_op jit(solution)/shard_map/ppermute | solution.py:72
  723.5 20.0 %collective-permute-start.77 = (bf16[704,256]{1,0:T(8,128)(2,1)}, bf16[704,256]{1,0:T(8,128)(2,1)}, u32[]{:S(2)}, u32[]{:S(2)}) collective-permute-start(bf16[704,256]{1,0:T(8,128)(2,1)} %add_convert_fusion.17), channel_id=1, source_target_pairs={{0,8},{8,16},{16,24},{24,28},{28,20},{20,12},{12,4},{4,0},{1,9},{9... | collective-permute-start | bytes 1081352 | tf_op jit(solution)/shard_map/ppermute | solution.py:72
  730.2 21.7 %collective-permute-start.85 = (bf16[704,256]{1,0:T(8,128)(2,1)}, bf16[704,256]{1,0:T(8,128)(2,1)}, u32[]{:S(2)}, u32[]{:S(2)}) collective-permute-start(bf16[704,256]{1,0:T(8,128)(2,1)} %convolution_convert_fusion.11), channel_id=1, source_target_pairs={{0,8},{8,16},{16,24},{24,28},{28,20},{20,12},{12,4},{4,0},{1,9},{9... | collective-permute-start | bytes 1081352 | tf_op jit(solution)/shard_map/ppermute | solution.py:72
  740.9 18.7 %collective-permute-start.90 = (bf16[704,256]{1,0:T(8,128)(2,1)}, bf16[704,256]{1,0:T(8,128)(2,1)}, u32[]{:S(2)}, u32[]{:S(2)}) collective-permute-start(bf16[704,256]{1,0:T(8,128)(2,1)} %add_convert_fusion.10), channel_id=1, source_target_pairs={{0,4},{8,0},{16,8},{24,16},{28,24},{20,28},{12,20},{4,12},{1,5},{9... | collective-permute-start | bytes 1081352 | tf_op jit(solution)/shard_map/ppermute | solution.py:72
  754.3 18.1 %collective-permute-start.78 = (bf16[704,256]{1,0:T(8,128)(2,1)}, bf16[704,256]{1,0:T(8,128)(2,1)}, u32[]{:S(2)}, u32[]{:S(2)}) collective-permute-start(bf16[704,256]{1,0:T(8,128)(2,1)} %add_convert_fusion.16), channel_id=1, source_target_pairs={{0,8},{8,16},{16,24},{24,28},{28,20},{20,12},{12,4},{4,0},{1,9},{9... | collective-permute-start | bytes 1081352 | tf_op jit(solution)/shard_map/ppermute | solution.py:72
  761.9 35.1 %collective-permute-start.69 = (bf16[512,2048]{1,0:T(8,128)(2,1)S(1)}, bf16[512,2048]{1,0:T(8,128)(2,1)}, u32[]{:S(2)}, u32[]{:S(2)}) collective-permute-start(bf16[512,2048]{1,0:T(8,128)(2,1)S(1)} %get-tuple-element.373), channel_id=1, source_target_pairs={{0,1},{1,0},{2,3},{3,2},{4,5},{5,4},{6,7},{7,6},{8,9},{9,8},{10,11... | collective-permute-start | bytes 6291464 | tf_op jit(solution)/shard_map/ppermute | solution.py:175
  761.9 21.7 %collective-permute-start.83 = (bf16[704,256]{1,0:T(8,128)(2,1)S(1)}, bf16[704,256]{1,0:T(8,128)(2,1)}, u32[]{:S(2)}, u32[]{:S(2)}) collective-permute-start(bf16[704,256]{1,0:T(8,128)(2,1)S(1)} %copy-done.134), channel_id=1, source_target_pairs={{0,4},{8,0},{16,8},{24,16},{28,24},{20,28},{12,20},{4,12},{1,5},{9... | collective-permute-start | bytes 1081352 | tf_op jit(solution)/shard_map/ppermute | solution.py:72
  (178 other events, 2448.6 us)
Sparse Core Ops, SparseCore 0:
  585.4 97.8 all-reduce.15
  687.6 74.6 all-reduce.17

commit v7 on v6

--- a/solution.py
+++ b/solution.py
@@ -87,6 +87,14 @@
             values = self.land(values)
         self.queue = waiting
         return values
+
+    def pause(self):
+        waiting, self.queue = self.queue, {1: [], -1: []}
+        return waiting
+
+    def go(self, waiting, token):
+        self.queue = waiting
+        self.resume(token)
 
     def land(self, values=None, count=1):
         for turn in range(count):
@@ -767,6 +775,7 @@
     )
     grad_out = Scatter(lambda k: down(product, sl(grad_rec, k)), 1, n, chunk)
     ring.add([grad_out])
+    waiting = ring.pause()
     grad_rec = ring.land(grad_rec.reshape(rows, width))
 
     grad_product = across(grad_rec, w_out).reshape(wide)
@@ -784,7 +793,8 @@
         rounds.append(ends)
         return ends
 
-    incoming = ring.land(carried(ring.land(early), -1, n, keep_round))
+    incoming = carried(ring.land(early), -1, n, keep_round)
+    ring.go(waiting, incoming)
     mlp_out = lax.psum(dot(after(turned, *rounds), w_down).astype(bf16), "tp")
     grad_gates, grad_inner, grad_gate_in, head, last, sums = per_sequence(
         gates_back_kernel,

time: 821 us -> 796 us (0.970)
  starting transfers between devices: 134 us -> 123 us
  matrix products: 196 us -> 187 us
    ppermute x8, waiting for transfers between devices: 45.9 us -> 13.4 us  [shifted(): return lax.ppermute(values, 'seq', pairs)]
    ppermute x70, waiting for transfers between devices: 107 us -> 139 us  [issue(): flying.append((flow, lax.ppermute(message, 'seq', self.pairs[way])))]
    ppermute x70, starting transfers between devices: 94.7 us -> 86 us  [issue(): flying.append((flow, lax.ppermute(message, 'seq', self.pairs[way])))]
    unnamed x351 -> x343, local copies, waits for them, and re-layouts: 63.4 us -> 62.7 us
  transfers between devices with their start and end apart: 95 -> 95, of which waited for: 28 -> 30; matrix products, arithmetic and copies ran while one was open for 38% -> 38% of each run, Pallas kernels for 13% -> 13%
where the time goes in v7:
time: 796 us; the launch traced here: 786 us
  waiting for transfers between devices  194 us (24%)
  matrix products  187 us (23%)
  starting transfers between devices  123 us (15%)
  Pallas kernels  111 us (14%)
  local copies, waits for them, and re-layouts  109 us (14%)
  other arithmetic  46.4 us (6%)
  between operations  16.8 us (2%)
    ppermute x70, waiting for transfers between devices, issue(): flying.append((flow, lax.ppermute(message, 'seq', self.pairs[way])))  139 us
    dot_general x42, matrix products, down(): lax.dot_general(a, b, (((0,), (0,)), ((), ())), preferred_element_type=f32)  99.8 us
    ppermute x70, starting transfers between devices, issue(): flying.append((flow, lax.ppermute(message, 'seq', self.pairs[way])))  86 us
    unnamed x343, local copies, waits for them, and re-layouts  62.7 us
    pallas_call x8, Pallas kernels, by_rows(): pl.pallas_call(body, grid_spec=pltpu.PrefetchScalarGridSpec(num_scalar_pr...  55.9 us
    dot_general x19, matrix products, across(): lax.dot_general(a, b, (((1,), (1,)), ((), ())), preferred_element_type=f32)  47.2 us
    pallas_call x3, Pallas kernels, per_sequence(): pl.pallas_call(kernel, grid=(seqs,), in_specs=[spec(a.shape, kind) for a,...  42.8 us
    dot_general x6, matrix products, dot(): return jnp.dot(a, b, preferred_element_type=f32)  39.7 us
  transfers between devices with their start and end apart: 95, of which 30 were waited for; matrix products, arithmetic and copies ran while one was open for 38% of the time, Pallas kernels for 13%

profile of v7, /device:TPU:0, one launch (start us, length us, event | category | flops | bytes accessed | tf_op | source)
XLA Modules:
  0.0 786.1 jit_solution(12693353752773876180)
XLA Ops:
  31.0 3.4 constant_dynamic-update-slice_fusion.25
  36.6 8.5 %shard_map.255 = (bf16[4,256,2048]{2,1,0:T(8,128)(2,1)S(1)}, bf16[4,256,2048]{2,1,0:T(8,128)(2,1)}) custom-call(s32[4]{0:T(128)S(1)} %and_select_fusion.2.refs_0_, s32[8]{0:T(128)S(1)} %gather_fusion, bf16[4,256,2048]{2,1,0:T(8,128)(2,1)} %refs_2_, bf16[4,256,2048]{2,1,0:T(8,128)(2,1)} %refs_3_), custom_call_target="tpu_custom_call" | custom-call | flops 16777216 | bytes 16777216 | tf_op jit(solution)/shard_map/pallas_call | solution.py:419
  67.4 8.2 %collective-permute-done.7 = bf16[1056,256]{1,0:T(8,128)(2,1)S(1)} collective-permute-done((bf16[1056,256]{1,0:T(8,128)(2,1)}, bf16[1056,256]{1,0:T(8,128)(2,1)S(1)}, u32[]{:S(2)}, u32[]{:S(2)}) %collective-permute-start.7) | collective-permute-done | bytes 540704 | tf_op jit(solution)/shard_map/ppermute | solution.py:72
  77.0 9.6 %collective-permute-done.9 = bf16[1072,256]{1,0:T(8,128)(2,1)S(1)} collective-permute-done((bf16[1072,256]{1,0:T(8,128)(2,1)S(1)}, bf16[1072,256]{1,0:T(8,128)(2,1)S(1)}, u32[]{:S(2)}, u32[]{:S(2)}) %collective-permute-start.9) | collective-permute-done | bytes 548896 | tf_op jit(solution)/shard_map/ppermute | solution.py:72
  89.7 9.4 %collective-permute-done.13 = bf16[1056,256]{1,0:T(8,128)(2,1)S(1)} collective-permute-done((bf16[1056,256]{1,0:T(8,128)(2,1)S(1)}, bf16[1056,256]{1,0:T(8,128)(2,1)S(1)}, u32[]{:S(2)}, u32[]{:S(2)}) %collective-permute-start.13) | collective-permute-done | bytes 540704 | tf_op jit(solution)/shard_map/ppermute | solution.py:72
  115.0 3.4 add_convert_fusion.7
  122.1 3.3 add_convert_fusion.6
  131.5 3.5 collective-permute-start.16
  136.6 12.3 %collective-permute-done.16 = bf16[4,3,704]{2,1,0:T(4,128)(2,1)S(1)} collective-permute-done((bf16[4,3,704]{2,1,0:T(4,128)(2,1)S(1)}, bf16[4,3,704]{2,1,0:T(4,128)(2,1)S(1)}, u32[]{:S(2)}, u32[]{:S(2)}) %collective-permute-start.16) | collective-permute-done | bytes 16928 | tf_op jit(solution)/shard_map/ppermute | solution.py:661
  148.9 3.3 collective-permute-start.22
  155.2 16.0 %shard_map.256 = (f32[4,256,704]{2,1,0:T(8,128)}, f32[4,256,704]{2,1,0:T(8,128)}, f32[4,256,704]{2,1,0:T(8,128)}, f32[4,256,704]{2,1,0:T(8,128)}, f32[4,256,704]...) custom-call(bf16[4,256,704]{2,1,0:T(8,128)(2,1)S(1)} %bitcast.194, ...), custom_call_target="tpu_custom_call" | custom-call | flops 2030043136 | bytes 23812096 | tf_op jit(solution)/shard_map/pallas_call | solution.py:382
  176.9 5.3 collective-permute-start.24
  182.3 7.6 collective-permute-done.24
  190.0 5.3 collective-permute-start.25
  195.3 5.0 collective-permute-start.26
  204.5 6.0 fusion.36
  212.4 3.3 convolution_convert_fusion.4
  226.8 3.4 convolution_convert_fusion.5
  233.2 11.4 %collective-permute-done.31 = bf16[256,1536]{1,0:T(8,128)(2,1)S(1)} collective-permute-done((bf16[256,1536]{1,0:T(8,128)(2,1)S(1)}, bf16[256,1536]{1,0:T(8,128)(2,1)S(1)}, u32[]{:S(2)}, u32[]{:S(2)}) %collective-permute-start.31) | collective-permute-done | bytes 786464 | tf_op jit(solution)/shard_map/ppermute | solution.py:72
  254.8 6.3 collective-permute-done.40
  267.0 3.6 collective-permute-done.38
  270.6 9.6 %collective-permute-done.41 = bf16[256,1536]{1,0:T(8,128)(2,1)S(1)} collective-permute-done((bf16[256,1536]{1,0:T(8,128)(2,1)S(1)}, bf16[256,1536]{1,0:T(8,128)(2,1)S(1)}, u32[]{:S(2)}, u32[]{:S(2)}) %collective-permute-start.41) | collective-permute-done | bytes 786464 | tf_op jit(solution)/shard_map/ppermute | solution.py:72
  284.2 9.4 %collective-permute-done.32 = bf16[512,2048]{1,0:T(8,128)(2,1)S(1)} collective-permute-done((bf16[512,2048]{1,0:T(8,128)(2,1)S(1)}, bf16[512,2048]{1,0:T(8,128)(2,1)S(1)}, u32[]{:S(2)}, u32[]{:S(2)}) %collective-permute-start.32) | collective-permute-done | bytes 2097184 | tf_op jit(solution)/shard_map/ppermute | solution.py:188
  295.8 4.9 collective-permute-done.36
  301.2 15.0 %collective-permute-done.34 = bf16[1536,256]{1,0:T(8,128)(2,1)S(1)} collective-permute-done((bf16[1536,256]{1,0:T(8,128)(2,1)}, bf16[1536,256]{1,0:T(8,128)(2,1)S(1)}, u32[]{:S(2)}, u32[]{:S(2)}) %collective-permute-start.34) | collective-permute-done | bytes 786464 | tf_op jit(solution)/shard_map/ppermute | solution.py:72
  322.1 5.0 shard_map.257
  327.1 5.1 shard_map.258
  336.0 17.5 %convolution_convert_fusion = bf16[1024,3072]{1,0:T(8,128)(2,1)S(1)} fusion(bf16[1024,2048]{1,0:T(8,128)(2,1)} %bitcast.220, bf16[2048,1536]{1,0:T(8,128)(2,1)} %copy-done.109, bf16[2048,1536]{1,0:T(8,128)(2,1)} %copy-done.108), kind=kOutput, calls=%fused_computation.40 | convolution fusion | flops 12913213440 | bytes 23068672 | tf_op jit(solution)/shard_map/dot_general | solution.py:580
  353.5 6.4 fusion.6
  376.1 12.5 %shard_map.259 = bf16[1024,3072]{1,0:T(8,128)(2,1)} custom-call(bf16[1024,2048]{1,0:T(8,128)(2,1)} %bitcast.231, bf16[1536,2048]{1,0:T(8,128)(2,1)} %constant_dynamic-update-slice_fusion.26.w_down, bf16[1024,1536]{1,0:T(8,128)(2,1)S(1)} %get-tuple-element.270.act, bf16[1024,1536]{1,0:T(8,128)(2,1)} %get-tuple-element.271.slope), custom_call_target="tpu_custom_call" | custom-call | flops 6442450944 | bytes 23068672 | tf_op jit(solution)/shard_map/pallas_call | solution.py:740
  388.6 11.9 %fusion.50 = bf16[512,2048]{1,0:T(8,128)(2,1)} fusion(bf16[2048,1536]{1,0:T(8,128)(2,1)} %copy-done.109, bf16[2048,1536]{1,0:T(8,128)(2,1)} %copy-done.108, bf16[1024,3072]{1,0:T(8,128)(2,1)} %shard_map.259), kind=kOutput, calls=%fused_computation.101 | convolution fusion | flops 6468665344 | bytes 17825792 | tf_op jit(solution)/shard_map/dot_general | solution.py:572
  401.4 4.4 convolution_convert_fusion.1
  406.0 4.1 convolution_convert_fusion.2
  412.2 10.8 %fusion.47 = bf16[512,2048]{1,0:T(8,128)(2,1)} fusion(bf16[2048,1536]{1,0:T(8,128)(2,1)} %copy-done.109, bf16[2048,1536]{1,0:T(8,128)(2,1)} %copy-done.108, bf16[1024,3072]{1,0:T(8,128)(2,1)S(1)} %copy-done.27), kind=kOutput, calls=%fused_computation.100 | convolution fusion | flops 6468665344 | bytes 17825792 | tf_op jit(solution)/shard_map/dot_general | solution.py:572
  426.9 4.7 fusion.33
  435.9 7.5 collective-permute-done.52
  443.4 4.7 fusion.21
  448.2 4.7 fusion.20
  455.0 17.6 %collective-permute-done.46 = bf16[512,2048]{1,0:T(8,128)(2,1)S(1)} collective-permute-done((bf16[512,2048]{1,0:T(8,128)(2,1)S(1)}, bf16[512,2048]{1,0:T(8,128)(2,1)S(1)}, u32[]{:S(2)}, u32[]{:S(2)}) %collective-permute-start.46) | collective-permute-done | bytes 2097184 | tf_op jit(solution)/shard_map/ppermute | solution.py:188
  482.2 7.3 shard_map.260
  489.5 7.5 shard_map.261
  498.4 7.7 fusion.86
  506.1 7.8 shard_map.262
  519.8 4.3 fusion.23
  526.0 4.7 fusion.22
  530.7 3.4 fusion.58
  535.5 5.7 collective-permute-done.57
  543.9 8.3 %convolution_convert_fusion.3 = bf16[1024,2048]{1,0:T(8,128)(2,1)} fusion(bf16[1024,1536]{1,0:T(8,128)(2,1)S(1)} %copy-done.65, bf16[1536,2048]{1,0:T(8,128)(2,1)S(1)} %bitcast.271), kind=kOutput, calls=%fused_computation.73 | convolution fusion | flops 6444548096 | bytes 13631488 | tf_op jit(solution)/shard_map/dot_general | solution.py:580
  555.8 19.0 %shard_map.263 = (bf16[2,4,256,704]{3,2,1,0:T(8,128)(2,1)}, bf16[4,256,704]{2,1,0:T(8,128)(2,1)S(1)}, bf16[4,256,704]{2,1,0:T(8,128)(2,1)S(1)}, f32[4,8,704]{2,1...) custom-call(f32[4,256,704]{2,1,0:T(8,128)} %bitcast.241, f32[4,256,704]{2,1,0:T(8,128)} %get-tuple-element.425.slope, ...), custom_call_target="tpu_custom_call" | custom-call | flops 2030043136 | bytes 38514432 | tf_op jit(solution)/shard_map/pallas_call | solution.py:382
  576.8 3.6 collective-permute-start.64
  597.3 3.6 fusion.46
  602.4 3.4 fusion.24
  609.4 3.6 fusion.45
  613.1 5.1 collective-permute-done.72
  621.0 22.1 %collective-permute-done.65 = bf16[256,3072]{1,0:T(8,128)(2,1)S(1)} collective-permute-done((bf16[256,3072]{1,0:T(8,128)(2,1)S(1)}, bf16[256,3072]{1,0:T(8,128)(2,1)S(1)}, u32[]{:S(2)}, u32[]{:S(2)}) %collective-permute-start.65) | collective-permute-done | bytes 1572896 | tf_op jit(solution)/shard_map/ppermute | solution.py:72
  646.4 4.0 collective-permute-done.79
  658.2 5.3 fusion.19
  671.5 3.5 fusion.53
  675.0 5.6 reshape.426
  682.9 8.5 %shard_map.264 = bf16[4,256,2048]{2,1,0:T(8,128)(2,1)} custom-call(s32[4]{0:T(128)S(1)} %copy-done.26, s32[8]{0:T(128)S(1)} %copy-done.22, f32[4,256,2048]{2,1,0:T(8,128)} %get-tuple-element.243.refs_0_.refs_2_, bf16[4,256,2048]{2,1,0:T(8,128)(2,1)S(1)} %bitcast.196), custom_call_target="tpu_custom_call" | custom-call | flops 16777216 | bytes 16777216 | tf_op jit(solution)/shard_map/pallas_call | solution.py:419
  700.9 4.0 fusion.18
  727.0 6.7 shard_map.265.refs_6_
  739.0 5.5 collective-permute-done.90
  771.6 7.2 shard_map.266
  (663 shorter events, 307.9 us)
Async XLA Ops:
  7.2 673.4 %all-reduce.16.cloned.1.call-start = ((), (), s32[]{:S(2)}) async-start(), calls=%async_computation | async-start | bytes 8388608 | tf_op jit(solution)/shard_map/psum | solution.py:798
  11.2 23.2 %collective-permute-start = (bf16[1056,256]{1,0:T(8,128)(2,1)}, bf16[1056,256]{1,0:T(8,128)(2,1)S(1)}, u32[]{:S(2)}, u32[]{:S(2)}) collective-permute-start(bf16[1056,256]{1,0:T(8,128)(2,1)} %pad_maximum_fusion.21), channel_id=1, source_target_pairs={{0,8},{8,16},{16,24},{24,28},{28,20},{20,12},{12,4},{4,0},{1,9},{9... | collective-permute-start | bytes 1622024 | tf_op jit(solution)/shard_map/ppermute | solution.py:72
  14.2 20.2 %collective-permute-start.1 = (bf16[1056,256]{1,0:T(8,128)(2,1)}, bf16[1056,256]{1,0:T(8,128)(2,1)}, u32[]{:S(2)}, u32[]{:S(2)}) collective-permute-start(bf16[1056,256]{1,0:T(8,128)(2,1)} %pad_maximum_fusion.21), channel_id=1, source_target_pairs={{0,4},{8,0},{16,8},{24,16},{28,24},{20,28},{12,20},{4,12},{1,5},{9... | collective-permute-start | bytes 1622024 | tf_op jit(solution)/shard_map/ppermute | solution.py:72
  15.1 31.9 %collective-permute-start.2 = (bf16[1072,256]{1,0:T(8,128)(2,1)}, bf16[1072,256]{1,0:T(8,128)(2,1)}, u32[]{:S(2)}, u32[]{:S(2)}) collective-permute-start(bf16[1072,256]{1,0:T(8,128)(2,1)} %pad_maximum_fusion.20), channel_id=1, source_target_pairs={{0,8},{8,16},{16,24},{24,28},{28,20},{20,12},{12,4},{4,0},{1,9},{9... | collective-permute-start | bytes 1646600 | tf_op jit(solution)/shard_map/ppermute | solution.py:72
  17.1 29.9 %collective-permute-start.3 = (bf16[1072,256]{1,0:T(8,128)(2,1)}, bf16[1072,256]{1,0:T(8,128)(2,1)}, u32[]{:S(2)}, u32[]{:S(2)}) collective-permute-start(bf16[1072,256]{1,0:T(8,128)(2,1)} %pad_maximum_fusion.20), channel_id=1, source_target_pairs={{0,4},{8,0},{16,8},{24,16},{28,24},{20,28},{12,20},{4,12},{1,5},{9... | collective-permute-start | bytes 1646600 | tf_op jit(solution)/shard_map/ppermute | solution.py:72
  34.5 23.9 %collective-permute-start.10 = (bf16[1056,256]{1,0:T(8,128)(2,1)}, bf16[1056,256]{1,0:T(8,128)(2,1)S(1)}, u32[]{:S(2)}, u32[]{:S(2)}) collective-permute-start(bf16[1056,256]{1,0:T(8,128)(2,1)} %collective-permute-done.1), channel_id=1, source_target_pairs={{0,4},{8,0},{16,8},{24,16},{28,24},{20,28},{12,20},{4,12},{1,5},{9... | collective-permute-start | bytes 1622024 | tf_op jit(solution)/shard_map/ppermute | solution.py:72
  36.5 23.8 %collective-permute-start.5 = (bf16[1056,256]{1,0:T(8,128)(2,1)S(1)}, bf16[1056,256]{1,0:T(8,128)(2,1)}, u32[]{:S(2)}, u32[]{:S(2)}) collective-permute-start(bf16[1056,256]{1,0:T(8,128)(2,1)S(1)} %collective-permute-done), channel_id=1, source_target_pairs={{0,8},{8,16},{16,24},{24,28},{28,20},{20,12},{12,4},{4,0},{1,9},{9... | collective-permute-start | bytes 1622024 | tf_op jit(solution)/shard_map/ppermute | solution.py:72
  58.4 18.6 %collective-permute-start.11 = (bf16[1056,256]{1,0:T(8,128)(2,1)S(1)}, bf16[1056,256]{1,0:T(8,128)(2,1)S(1)}, u32[]{:S(2)}, u32[]{:S(2)}) collective-permute-start(bf16[1056,256]{1,0:T(8,128)(2,1)S(1)} %collective-permute-done.10), channel_id=1, source_target_pairs={{0,4},{8,0},{16,8},{24,16},{28,24},{20,28},{12,20},{4,12},{1,5},{9... | collective-permute-start | bytes 1622024 | tf_op jit(solution)/shard_map/ppermute | solution.py:72
  63.8 24.8 %collective-permute-start.6 = (bf16[1072,256]{1,0:T(8,128)(2,1)S(1)}, bf16[1072,256]{1,0:T(8,128)(2,1)S(1)}, u32[]{:S(2)}, u32[]{:S(2)}) collective-permute-start(bf16[1072,256]{1,0:T(8,128)(2,1)S(1)} %collective-permute-done.4), channel_id=1, source_target_pairs={{0,8},{8,16},{16,24},{24,28},{28,20},{20,12},{12,4},{4,0},{1,9},{9... | collective-permute-start | bytes 1646600 | tf_op jit(solution)/shard_map/ppermute | solution.py:72
  65.8 20.8 %collective-permute-start.9 = (bf16[1072,256]{1,0:T(8,128)(2,1)S(1)}, bf16[1072,256]{1,0:T(8,128)(2,1)S(1)}, u32[]{:S(2)}, u32[]{:S(2)}) collective-permute-start(bf16[1072,256]{1,0:T(8,128)(2,1)S(1)} %collective-permute-done.8), channel_id=1, source_target_pairs={{0,4},{8,0},{16,8},{24,16},{28,24},{20,28},{12,20},{4,12},{1,5},{9... | collective-permute-start | bytes 1646600 | tf_op jit(solution)/shard_map/ppermute | solution.py:72
  75.7 23.3 %collective-permute-start.13 = (bf16[1056,256]{1,0:T(8,128)(2,1)S(1)}, bf16[1056,256]{1,0:T(8,128)(2,1)S(1)}, u32[]{:S(2)}, u32[]{:S(2)}) collective-permute-start(bf16[1056,256]{1,0:T(8,128)(2,1)S(1)} %collective-permute-done.7), channel_id=1, source_target_pairs={{0,8},{8,16},{16,24},{24,28},{28,20},{20,12},{12,4},{4,0},{1,9},{9... | collective-permute-start | bytes 1622024 | tf_op jit(solution)/shard_map/ppermute | solution.py:72
  86.9 38.4 %collective-permute-start.15 = (bf16[256,1536]{1,0:T(8,128)(2,1)}, bf16[256,1536]{1,0:T(8,128)(2,1)}, u32[]{:S(2)}, u32[]{:S(2)}) collective-permute-start(bf16[256,1536]{1,0:T(8,128)(2,1)} %get-tuple-element.213), channel_id=1, source_target_pairs={{0,4},{8,0},{16,8},{24,16},{28,24},{20,28},{12,20},{4,12},{1,5},{9... | collective-permute-start | bytes 2359304 | tf_op jit(solution)/shard_map/ppermute | solution.py:72
  88.6 36.8 %collective-permute-start.14 = (bf16[256,1536]{1,0:T(8,128)(2,1)}, bf16[256,1536]{1,0:T(8,128)(2,1)}, u32[]{:S(2)}, u32[]{:S(2)}) collective-permute-start(bf16[256,1536]{1,0:T(8,128)(2,1)} %get-tuple-element.213), channel_id=1, source_target_pairs={{0,8},{8,16},{16,24},{24,28},{28,20},{20,12},{12,4},{4,0},{1,9},{9... | collective-permute-start | bytes 2359304 | tf_op jit(solution)/shard_map/ppermute | solution.py:72
  99.0 49.9 %collective-permute-start.17 = (bf16[256,1536]{1,0:T(8,128)(2,1)}, bf16[256,1536]{1,0:T(8,128)(2,1)}, u32[]{:S(2)}, u32[]{:S(2)}) collective-permute-start(bf16[256,1536]{1,0:T(8,128)(2,1)} %get-tuple-element.216), channel_id=1, source_target_pairs={{0,8},{8,16},{16,24},{24,28},{28,20},{20,12},{12,4},{4,0},{1,9},{9... | collective-permute-start | bytes 2359304 | tf_op jit(solution)/shard_map/ppermute | solution.py:72
  109.0 39.9 %collective-permute-start.18 = (bf16[256,1536]{1,0:T(8,128)(2,1)}, bf16[256,1536]{1,0:T(8,128)(2,1)}, u32[]{:S(2)}, u32[]{:S(2)}) collective-permute-start(bf16[256,1536]{1,0:T(8,128)(2,1)} %get-tuple-element.216), channel_id=1, source_target_pairs={{0,4},{8,0},{16,8},{24,16},{28,24},{20,28},{12,20},{4,12},{1,5},{9... | collective-permute-start | bytes 2359304 | tf_op jit(solution)/shard_map/ppermute | solution.py:72
  125.4 45.9 %collective-permute-start.19 = (bf16[256,1536]{1,0:T(8,128)(2,1)}, bf16[256,1536]{1,0:T(8,128)(2,1)}, u32[]{:S(2)}, u32[]{:S(2)}) collective-permute-start(bf16[256,1536]{1,0:T(8,128)(2,1)} %collective-permute-done.14), channel_id=1, source_target_pairs={{0,8},{8,16},{16,24},{24,28},{28,20},{20,12},{12,4},{4,0},{1,9},{9... | collective-permute-start | bytes 2359304 | tf_op jit(solution)/shard_map/ppermute | solution.py:72
  126.0 45.3 %collective-permute-start.20 = (bf16[256,1536]{1,0:T(8,128)(2,1)}, bf16[256,1536]{1,0:T(8,128)(2,1)S(1)}, u32[]{:S(2)}, u32[]{:S(2)}) collective-permute-start(bf16[256,1536]{1,0:T(8,128)(2,1)} %collective-permute-done.15), channel_id=1, source_target_pairs={{0,4},{8,0},{16,8},{24,16},{28,24},{20,28},{12,20},{4,12},{1,5},{9... | collective-permute-start | bytes 2359304 | tf_op jit(solution)/shard_map/ppermute | solution.py:72
  148.9 28.0 %collective-permute-start.22 = (bf16[256,1536]{1,0:T(8,128)(2,1)}, bf16[256,1536]{1,0:T(8,128)(2,1)S(1)}, u32[]{:S(2)}, u32[]{:S(2)}) collective-permute-start(bf16[256,1536]{1,0:T(8,128)(2,1)} %collective-permute-done.17), channel_id=1, source_target_pairs={{0,8},{8,16},{16,24},{24,28},{28,20},{20,12},{12,4},{4,0},{1,9},{9... | collective-permute-start | bytes 2359304 | tf_op jit(solution)/shard_map/ppermute | solution.py:72
  152.2 24.7 %collective-permute-start.23 = (bf16[256,1536]{1,0:T(8,128)(2,1)}, bf16[256,1536]{1,0:T(8,128)(2,1)S(1)}, u32[]{:S(2)}, u32[]{:S(2)}) collective-permute-start(bf16[256,1536]{1,0:T(8,128)(2,1)} %collective-permute-done.18), channel_id=1, source_target_pairs={{0,4},{8,0},{16,8},{24,16},{28,24},{20,28},{12,20},{4,12},{1,5},{9... | collective-permute-start | bytes 2359304 | tf_op jit(solution)/shard_map/ppermute | solution.py:72
  174.5 29.2 %collective-permute-start.27 = (bf16[1536,256]{1,0:T(8,128)(2,1)}, bf16[1536,256]{1,0:T(8,128)(2,1)}, u32[]{:S(2)}, u32[]{:S(2)}) collective-permute-start(bf16[1536,256]{1,0:T(8,128)(2,1)} %param.27), channel_id=1, source_target_pairs={{0,8},{8,16},{16,24},{24,28},{28,20},{20,12},{12,4},{4,0},{1,9},{9... | collective-permute-start | bytes 2359304 | tf_op jit(solution)/shard_map/ppermute | solution.py:72
  175.3 28.4 %collective-permute-start.28 = (bf16[1536,256]{1,0:T(8,128)(2,1)}, bf16[1536,256]{1,0:T(8,128)(2,1)S(1)}, u32[]{:S(2)}, u32[]{:S(2)}) collective-permute-start(bf16[1536,256]{1,0:T(8,128)(2,1)} %param.27), channel_id=1, source_target_pairs={{0,4},{8,0},{16,8},{24,16},{28,24},{20,28},{12,20},{4,12},{1,5},{9... | collective-permute-start | bytes 2359304 | tf_op jit(solution)/shard_map/ppermute | solution.py:72
  223.7 20.9 %collective-permute-start.31 = (bf16[256,1536]{1,0:T(8,128)(2,1)S(1)}, bf16[256,1536]{1,0:T(8,128)(2,1)S(1)}, u32[]{:S(2)}, u32[]{:S(2)}) collective-permute-start(bf16[256,1536]{1,0:T(8,128)(2,1)S(1)} %copy-done.95), channel_id=1, source_target_pairs={{0,4},{8,0},{16,8},{24,16},{28,24},{20,28},{12,20},{4,12},{1,5},{9... | collective-permute-start | bytes 2359304 | tf_op jit(solution)/shard_map/ppermute | solution.py:72
  226.8 19.9 %collective-permute-start.30 = (bf16[256,1536]{1,0:T(8,128)(2,1)}, bf16[256,1536]{1,0:T(8,128)(2,1)S(1)}, u32[]{:S(2)}, u32[]{:S(2)}) collective-permute-start(bf16[256,1536]{1,0:T(8,128)(2,1)} %collective-permute-done.19), channel_id=1, source_target_pairs={{0,8},{8,16},{16,24},{24,28},{28,20},{20,12},{12,4},{4,0},{1,9},{9... | collective-permute-start | bytes 2359304 | tf_op jit(solution)/shard_map/ppermute | solution.py:72
  230.2 30.9 %collective-permute-start.40 = (bf16[256,1536]{1,0:T(8,128)(2,1)S(1)}, bf16[256,1536]{1,0:T(8,128)(2,1)S(1)}, u32[]{:S(2)}, u32[]{:S(2)}) collective-permute-start(bf16[256,1536]{1,0:T(8,128)(2,1)S(1)} %copy-done.100), channel_id=1, source_target_pairs={{0,4},{8,0},{16,8},{24,16},{28,24},{20,28},{12,20},{4,12},{1,5},{9... | collective-permute-start | bytes 2359304 | tf_op jit(solution)/shard_map/ppermute | solution.py:72
  246.6 46.9 %collective-permute-start.32 = (bf16[512,2048]{1,0:T(8,128)(2,1)S(1)}, bf16[512,2048]{1,0:T(8,128)(2,1)S(1)}, u32[]{:S(2)}, u32[]{:S(2)}) collective-permute-start(bf16[512,2048]{1,0:T(8,128)(2,1)S(1)} %add_convert_fusion.5), channel_id=1, source_target_pairs={{0,2},{1,3},{2,0},{3,1},{4,6},{5,7},{6,4},{7,5},{8,10},{9,11},{10,... | collective-permute-start | bytes 6291464 | tf_op jit(solution)/shard_map/ppermute | solution.py:188
  252.0 18.6 %collective-permute-start.38 = (bf16[256,1536]{1,0:T(8,128)(2,1)S(1)}, bf16[256,1536]{1,0:T(8,128)(2,1)S(1)}, u32[]{:S(2)}, u32[]{:S(2)}) collective-permute-start(bf16[256,1536]{1,0:T(8,128)(2,1)S(1)} %copy-done.102), channel_id=1, source_target_pairs={{0,8},{8,16},{16,24},{24,28},{28,20},{20,12},{12,4},{4,0},{1,9},{9... | collective-permute-start | bytes 2359304 | tf_op jit(solution)/shard_map/ppermute | solution.py:72
  261.1 19.2 %collective-permute-start.41 = (bf16[256,1536]{1,0:T(8,128)(2,1)S(1)}, bf16[256,1536]{1,0:T(8,128)(2,1)S(1)}, u32[]{:S(2)}, u32[]{:S(2)}) collective-permute-start(bf16[256,1536]{1,0:T(8,128)(2,1)S(1)} %collective-permute-done.40), channel_id=1, source_target_pairs={{0,4},{8,0},{16,8},{24,16},{28,24},{20,28},{12,20},{4,12},{1,5},{9... | collective-permute-start | bytes 2359304 | tf_op jit(solution)/shard_map/ppermute | solution.py:72
  280.3 37.6 %collective-permute-start.39 = (bf16[256,1536]{1,0:T(8,128)(2,1)S(1)}, bf16[256,1536]{1,0:T(8,128)(2,1)S(1)}, u32[]{:S(2)}, u32[]{:S(2)}) collective-permute-start(bf16[256,1536]{1,0:T(8,128)(2,1)S(1)} %collective-permute-done.30), channel_id=1, source_target_pairs={{0,8},{8,16},{16,24},{24,28},{28,20},{20,12},{12,4},{4,0},{1,9},{9... | collective-permute-start | bytes 2359304 | tf_op jit(solution)/shard_map/ppermute | solution.py:72
  282.2 18.5 %collective-permute-start.36 = (bf16[1536,256]{1,0:T(8,128)(2,1)S(1)}, bf16[1536,256]{1,0:T(8,128)(2,1)S(1)}, u32[]{:S(2)}, u32[]{:S(2)}) collective-permute-start(bf16[1536,256]{1,0:T(8,128)(2,1)S(1)} %copy-done.97), channel_id=1, source_target_pairs={{0,4},{8,0},{16,8},{24,16},{28,24},{20,28},{12,20},{4,12},{1,5},{9... | collective-permute-start | bytes 2359304 | tf_op jit(solution)/shard_map/ppermute | solution.py:72
  282.9 33.3 %collective-permute-start.34 = (bf16[1536,256]{1,0:T(8,128)(2,1)}, bf16[1536,256]{1,0:T(8,128)(2,1)S(1)}, u32[]{:S(2)}, u32[]{:S(2)}) collective-permute-start(bf16[1536,256]{1,0:T(8,128)(2,1)} %collective-permute-done.27), channel_id=1, source_target_pairs={{0,8},{8,16},{16,24},{24,28},{28,20},{20,12},{12,4},{4,0},{1,9},{9... | collective-permute-start | bytes 2359304 | tf_op jit(solution)/shard_map/ppermute | solution.py:72
  294.4 32.8 %collective-permute-start.33 = (bf16[512,2048]{1,0:T(8,128)(2,1)S(1)}, bf16[512,2048]{1,0:T(8,128)(2,1)S(1)}, u32[]{:S(2)}, u32[]{:S(2)}) collective-permute-start(bf16[512,2048]{1,0:T(8,128)(2,1)S(1)} %add_convert_fusion.4), channel_id=1, source_target_pairs={{0,1},{1,0},{2,3},{3,2},{4,5},{5,4},{6,7},{7,6},{8,9},{9,8},{10,11... | collective-permute-start | bytes 6291464 | tf_op jit(solution)/shard_map/ppermute | solution.py:183
  300.7 31.5 %collective-permute-start.37 = (bf16[1536,256]{1,0:T(8,128)(2,1)S(1)}, bf16[1536,256]{1,0:T(8,128)(2,1)S(1)}, u32[]{:S(2)}, u32[]{:S(2)}) collective-permute-start(bf16[1536,256]{1,0:T(8,128)(2,1)S(1)} %collective-permute-done.36), channel_id=1, source_target_pairs={{0,4},{8,0},{16,8},{24,16},{28,24},{20,28},{12,20},{4,12},{1,5},{9... | collective-permute-start | bytes 2359304 | tf_op jit(solution)/shard_map/ppermute | solution.py:72
  316.2 17.7 %collective-permute-start.35 = (bf16[1536,256]{1,0:T(8,128)(2,1)S(1)}, bf16[1536,256]{1,0:T(8,128)(2,1)}, u32[]{:S(2)}, u32[]{:S(2)}) collective-permute-start(bf16[1536,256]{1,0:T(8,128)(2,1)S(1)} %collective-permute-done.34), channel_id=1, source_target_pairs={{0,8},{8,16},{16,24},{24,28},{28,20},{20,12},{12,4},{4,0},{1,9},{9... | collective-permute-start | bytes 2359304 | tf_op jit(solution)/shard_map/ppermute | solution.py:72
  333.9 28.6 %collective-permute-start.42 = (bf16[1536,256]{1,0:T(8,128)(2,1)}, bf16[1536,256]{1,0:T(8,128)(2,1)}, u32[]{:S(2)}, u32[]{:S(2)}) collective-permute-start(bf16[1536,256]{1,0:T(8,128)(2,1)} %collective-permute-done.35), channel_id=1, source_target_pairs={{0,8},{8,16},{16,24},{24,28},{28,20},{20,12},{12,4},{4,0},{1,9},{9... | collective-permute-start | bytes 2359304 | tf_op jit(solution)/shard_map/ppermute | solution.py:72
  373.7 26.7 %collective-permute-start.44 = (bf16[1536,256]{1,0:T(8,128)(2,1)}, bf16[1536,256]{1,0:T(8,128)(2,1)S(1)}, u32[]{:S(2)}, u32[]{:S(2)}) collective-permute-start(bf16[1536,256]{1,0:T(8,128)(2,1)} %convolution_convert_fusion.6), channel_id=1, source_target_pairs={{0,4},{8,0},{16,8},{24,16},{28,24},{20,28},{12,20},{4,12},{1,5},{9... | collective-permute-start | bytes 2359304 | tf_op jit(solution)/shard_map/ppermute | solution.py:72
  373.8 27.6 %collective-permute-start.43 = (bf16[1536,256]{1,0:T(8,128)(2,1)}, bf16[1536,256]{1,0:T(8,128)(2,1)S(1)}, u32[]{:S(2)}, u32[]{:S(2)}) collective-permute-start(bf16[1536,256]{1,0:T(8,128)(2,1)} %convolution_convert_fusion.7), channel_id=1, source_target_pairs={{0,8},{8,16},{16,24},{24,28},{28,20},{20,12},{12,4},{4,0},{1,9},{9... | collective-permute-start | bytes 2359304 | tf_op jit(solution)/shard_map/ppermute | solution.py:72
  401.4 21.5 %collective-permute-start.45 = (bf16[512,2048]{1,0:T(8,128)(2,1)}, bf16[512,2048]{1,0:T(8,128)(2,1)S(1)}, u32[]{:S(2)}, u32[]{:S(2)}) collective-permute-start(bf16[512,2048]{1,0:T(8,128)(2,1)} %fusion.50), channel_id=1, source_target_pairs={{0,1},{1,0},{2,3},{3,2},{4,5},{5,4},{6,7},{7,6},{8,9},{9,8},{10,11... | collective-permute-start | bytes 6291464 | tf_op jit(solution)/shard_map/ppermute | solution.py:183
  405.9 37.5 %collective-permute-start.52 = (bf16[256,3072]{1,0:T(8,128)(2,1)}, bf16[256,3072]{1,0:T(8,128)(2,1)}, u32[]{:S(2)}, u32[]{:S(2)}) collective-permute-start(bf16[256,3072]{1,0:T(8,128)(2,1)} %convolution_convert_fusion.1), channel_id=1, source_target_pairs={{0,4},{8,0},{16,8},{24,16},{28,24},{20,28},{12,20},{4,12},{1,5},{9... | collective-permute-start | bytes 4718600 | tf_op jit(solution)/shard_map/ppermute | solution.py:72
  410.1 38.1 %collective-permute-start.50 = (bf16[256,3072]{1,0:T(8,128)(2,1)}, bf16[256,3072]{1,0:T(8,128)(2,1)}, u32[]{:S(2)}, u32[]{:S(2)}) collective-permute-start(bf16[256,3072]{1,0:T(8,128)(2,1)} %convolution_convert_fusion.2), channel_id=1, source_target_pairs={{0,8},{8,16},{16,24},{24,28},{28,20},{20,12},{12,4},{4,0},{1,9},{9... | collective-permute-start | bytes 4718600 | tf_op jit(solution)/shard_map/ppermute | solution.py:72
  425.3 47.3 %collective-permute-start.46 = (bf16[512,2048]{1,0:T(8,128)(2,1)S(1)}, bf16[512,2048]{1,0:T(8,128)(2,1)S(1)}, u32[]{:S(2)}, u32[]{:S(2)}) collective-permute-start(bf16[512,2048]{1,0:T(8,128)(2,1)S(1)} %add_convert_fusion.3), channel_id=1, source_target_pairs={{0,2},{1,3},{2,0},{3,1},{4,6},{5,7},{6,4},{7,5},{8,10},{9,11},{10,... | collective-permute-start | bytes 6291464 | tf_op jit(solution)/shard_map/ppermute | solution.py:188
  432.6 40.8 %collective-permute-start.48 = (bf16[1536,256]{1,0:T(8,128)(2,1)S(1)}, bf16[1536,256]{1,0:T(8,128)(2,1)S(1)}, u32[]{:S(2)}, u32[]{:S(2)}) collective-permute-start(bf16[1536,256]{1,0:T(8,128)(2,1)S(1)} %fusion.55), channel_id=1, source_target_pairs={{0,4},{8,0},{16,8},{24,16},{28,24},{20,28},{12,20},{4,12},{1,5},{9... | collective-permute-start | bytes 2359304 | tf_op jit(solution)/shard_map/ppermute | solution.py:72
  433.9 39.5 %collective-permute-start.47 = (bf16[1536,256]{1,0:T(8,128)(2,1)S(1)}, bf16[1536,256]{1,0:T(8,128)(2,1)S(1)}, u32[]{:S(2)}, u32[]{:S(2)}) collective-permute-start(bf16[1536,256]{1,0:T(8,128)(2,1)S(1)} %fusion.54), channel_id=1, source_target_pairs={{0,8},{8,16},{16,24},{24,28},{28,20},{20,12},{12,4},{4,0},{1,9},{9... | collective-permute-start | bytes 2359304 | tf_op jit(solution)/shard_map/ppermute | solution.py:72
  448.1 48.9 %collective-permute-start.53 = (bf16[256,3072]{1,0:T(8,128)(2,1)}, bf16[256,3072]{1,0:T(8,128)(2,1)S(1)}, u32[]{:S(2)}, u32[]{:S(2)}) collective-permute-start(bf16[256,3072]{1,0:T(8,128)(2,1)} %fusion.21), channel_id=1, source_target_pairs={{0,4},{8,0},{16,8},{24,16},{28,24},{20,28},{12,20},{4,12},{1,5},{9... | collective-permute-start | bytes 4718600 | tf_op jit(solution)/shard_map/ppermute | solution.py:72
  452.9 45.5 %collective-permute-start.51 = (bf16[256,3072]{1,0:T(8,128)(2,1)}, bf16[256,3072]{1,0:T(8,128)(2,1)}, u32[]{:S(2)}, u32[]{:S(2)}) collective-permute-start(bf16[256,3072]{1,0:T(8,128)(2,1)} %fusion.20), channel_id=1, source_target_pairs={{0,8},{8,16},{16,24},{24,28},{28,20},{20,12},{12,4},{4,0},{1,9},{9... | collective-permute-start | bytes 4718600 | tf_op jit(solution)/shard_map/ppermute | solution.py:72
  478.2 35.7 %collective-permute-start.55 = (bf16[1536,256]{1,0:T(8,128)(2,1)}, bf16[1536,256]{1,0:T(8,128)(2,1)S(1)}, u32[]{:S(2)}, u32[]{:S(2)}) collective-permute-start(bf16[1536,256]{1,0:T(8,128)(2,1)} %fusion.57), channel_id=1, source_target_pairs={{0,4},{8,0},{16,8},{24,16},{28,24},{20,28},{12,20},{4,12},{1,5},{9... | collective-permute-start | bytes 2359304 | tf_op jit(solution)/shard_map/ppermute | solution.py:72
  480.4 33.9 %collective-permute-start.54 = (bf16[1536,256]{1,0:T(8,128)(2,1)}, bf16[1536,256]{1,0:T(8,128)(2,1)}, u32[]{:S(2)}, u32[]{:S(2)}) collective-permute-start(bf16[1536,256]{1,0:T(8,128)(2,1)} %fusion.56), channel_id=1, source_target_pairs={{0,8},{8,16},{16,24},{24,28},{28,20},{20,12},{12,4},{4,0},{1,9},{9... | collective-permute-start | bytes 2359304 | tf_op jit(solution)/shard_map/ppermute | solution.py:72
  552.2 181.9 %all-reduce.18.cloned.1.call-start = ((), (), s32[]{:S(2)}) async-start(), calls=%async_computation.1 | async-start | bytes 1081344 | tf_op jit(solution)/shard_map/psum | solution.py:876
  552.3 43.5 %collective-permute-start.62 = (bf16[256,3072]{1,0:T(8,128)(2,1)}, bf16[256,3072]{1,0:T(8,128)(2,1)}, u32[]{:S(2)}, u32[]{:S(2)}) collective-permute-start(bf16[256,3072]{1,0:T(8,128)(2,1)} %fusion.23), channel_id=1, source_target_pairs={{0,4},{8,0},{16,8},{24,16},{28,24},{20,28},{12,20},{4,12},{1,5},{9... | collective-permute-start | bytes 4718600 | tf_op jit(solution)/shard_map/ppermute | solution.py:72
  555.0 40.8 %collective-permute-start.61 = (bf16[256,3072]{1,0:T(8,128)(2,1)}, bf16[256,3072]{1,0:T(8,128)(2,1)}, u32[]{:S(2)}, u32[]{:S(2)}) collective-permute-start(bf16[256,3072]{1,0:T(8,128)(2,1)} %fusion.22), channel_id=1, source_target_pairs={{0,8},{8,16},{16,24},{24,28},{28,20},{20,12},{12,4},{4,0},{1,9},{9... | collective-permute-start | bytes 4718600 | tf_op jit(solution)/shard_map/ppermute | solution.py:72
  575.5 17.7 %collective-permute-start.60 = (bf16[4,3,704]{2,1,0:T(4,128)(2,1)}, bf16[4,3,704]{2,1,0:T(4,128)(2,1)}, u32[]{:S(2)}, u32[]{:S(2)}) collective-permute-start(bf16[4,3,704]{2,1,0:T(4,128)(2,1)} %slice.945), channel_id=1, source_target_pairs={{4,0},{8,4},{12,8},{16,12},{20,16},{24,20},{28,24},{5,1},{9,5},{13... | collective-permute-start | bytes 50696 | tf_op jit(solution)/shard_map/ppermute | solution.py:832
  576.8 44.2 %collective-permute-start.64 = (bf16[1536,256]{1,0:T(8,128)(2,1)}, bf16[1536,256]{1,0:T(8,128)(2,1)}, u32[]{:S(2)}, u32[]{:S(2)}) collective-permute-start(bf16[1536,256]{1,0:T(8,128)(2,1)} %fusion.58), channel_id=1, source_target_pairs={{0,8},{8,16},{16,24},{24,28},{28,20},{20,12},{12,4},{4,0},{1,9},{9... | collective-permute-start | bytes 2359304 | tf_op jit(solution)/shard_map/ppermute | solution.py:72
  600.9 17.9 %collective-permute-start.63 = (bf16[512,2048]{1,0:T(8,128)(2,1)S(1)}, bf16[512,2048]{1,0:T(8,128)(2,1)S(1)}, u32[]{:S(2)}, u32[]{:S(2)}) collective-permute-start(bf16[512,2048]{1,0:T(8,128)(2,1)S(1)} %fusion.46), channel_id=1, source_target_pairs={{0,1},{1,0},{2,3},{3,2},{4,5},{5,4},{6,7},{7,6},{8,9},{9,8},{10,11... | collective-permute-start | bytes 6291464 | tf_op jit(solution)/shard_map/ppermute | solution.py:183
  605.8 37.2 %collective-permute-start.65 = (bf16[256,3072]{1,0:T(8,128)(2,1)S(1)}, bf16[256,3072]{1,0:T(8,128)(2,1)S(1)}, u32[]{:S(2)}, u32[]{:S(2)}) collective-permute-start(bf16[256,3072]{1,0:T(8,128)(2,1)S(1)} %fusion.24), channel_id=1, source_target_pairs={{0,4},{8,0},{16,8},{24,16},{28,24},{20,28},{12,20},{4,12},{1,5},{9... | collective-permute-start | bytes 4718600 | tf_op jit(solution)/shard_map/ppermute | solution.py:72
  613.0 37.4 %collective-permute-start.79 = (bf16[704,256]{1,0:T(8,128)(2,1)S(1)}, bf16[704,256]{1,0:T(8,128)(2,1)S(1)}, u32[]{:S(2)}, u32[]{:S(2)}) collective-permute-start(bf16[704,256]{1,0:T(8,128)(2,1)S(1)} %copy-done.129), channel_id=1, source_target_pairs={{0,4},{8,0},{16,8},{24,16},{28,24},{20,28},{12,20},{4,12},{1,5},{9... | collective-permute-start | bytes 1081352 | tf_op jit(solution)/shard_map/ppermute | solution.py:72
  651.4 49.5 %collective-permute-start.66 = (bf16[512,2048]{1,0:T(8,128)(2,1)}, bf16[512,2048]{1,0:T(8,128)(2,1)}, u32[]{:S(2)}, u32[]{:S(2)}) collective-permute-start(bf16[512,2048]{1,0:T(8,128)(2,1)} %add_convert_fusion.1), channel_id=1, source_target_pairs={{0,2},{1,3},{2,0},{3,1},{4,6},{5,7},{6,4},{7,5},{8,10},{9,11},{10,... | collective-permute-start | bytes 6291464 | tf_op jit(solution)/shard_map/ppermute | solution.py:188
  668.1 27.8 %collective-permute-start.88 = (bf16[704,256]{1,0:T(8,128)(2,1)}, bf16[704,256]{1,0:T(8,128)(2,1)}, u32[]{:S(2)}, u32[]{:S(2)}) collective-permute-start(bf16[704,256]{1,0:T(8,128)(2,1)} %fusion.69), channel_id=1, source_target_pairs={{0,4},{8,0},{16,8},{24,16},{28,24},{20,28},{12,20},{4,12},{1,5},{9... | collective-permute-start | bytes 1081352 | tf_op jit(solution)/shard_map/ppermute | solution.py:72
  668.1 25.3 %collective-permute-start.81 = (bf16[704,256]{1,0:T(8,128)(2,1)}, bf16[704,256]{1,0:T(8,128)(2,1)}, u32[]{:S(2)}, u32[]{:S(2)}) collective-permute-start(bf16[704,256]{1,0:T(8,128)(2,1)} %convolution_convert_fusion.13), channel_id=1, source_target_pairs={{0,4},{8,0},{16,8},{24,16},{28,24},{20,28},{12,20},{4,12},{1,5},{9... | collective-permute-start | bytes 1081352 | tf_op jit(solution)/shard_map/ppermute | solution.py:72
  670.5 26.8 %collective-permute-start.84 = (bf16[704,256]{1,0:T(8,128)(2,1)}, bf16[704,256]{1,0:T(8,128)(2,1)}, u32[]{:S(2)}, u32[]{:S(2)}) collective-permute-start(bf16[704,256]{1,0:T(8,128)(2,1)} %fusion.68), channel_id=1, source_target_pairs={{0,8},{8,16},{16,24},{24,28},{28,20},{20,12},{12,4},{4,0},{1,9},{9... | collective-permute-start | bytes 1081352 | tf_op jit(solution)/shard_map/ppermute | solution.py:72
  695.8 21.0 %collective-permute-start.89 = (bf16[704,256]{1,0:T(8,128)(2,1)S(1)}, bf16[704,256]{1,0:T(8,128)(2,1)}, u32[]{:S(2)}, u32[]{:S(2)}) collective-permute-start(bf16[704,256]{1,0:T(8,128)(2,1)S(1)} %copy-done.131), channel_id=1, source_target_pairs={{0,4},{8,0},{16,8},{24,16},{28,24},{20,28},{12,20},{4,12},{1,5},{9... | collective-permute-start | bytes 1081352 | tf_op jit(solution)/shard_map/ppermute | solution.py:72
  697.3 23.2 %collective-permute-start.85 = (bf16[704,256]{1,0:T(8,128)(2,1)}, bf16[704,256]{1,0:T(8,128)(2,1)}, u32[]{:S(2)}, u32[]{:S(2)}) collective-permute-start(bf16[704,256]{1,0:T(8,128)(2,1)} %convolution_convert_fusion.11), channel_id=1, source_target_pairs={{0,8},{8,16},{16,24},{24,28},{28,20},{20,12},{12,4},{4,0},{1,9},{9... | collective-permute-start | bytes 1081352 | tf_op jit(solution)/shard_map/ppermute | solution.py:72
  722.9 48.7 %collective-permute-start.67 = (bf16[512,2048]{1,0:T(8,128)(2,1)S(1)}, bf16[512,2048]{1,0:T(8,128)(2,1)}, u32[]{:S(2)}, u32[]{:S(2)}) collective-permute-start(bf16[512,2048]{1,0:T(8,128)(2,1)S(1)} %get-tuple-element.403), channel_id=1, source_target_pairs={{0,1},{1,0},{2,3},{3,2},{4,5},{5,4},{6,7},{7,6},{8,9},{9,8},{10,11... | collective-permute-start | bytes 6291464 | tf_op jit(solution)/shard_map/ppermute | solution.py:183
  722.9 34.5 %collective-permute-start.83 = (bf16[704,256]{1,0:T(8,128)(2,1)}, bf16[704,256]{1,0:T(8,128)(2,1)}, u32[]{:S(2)}, u32[]{:S(2)}) collective-permute-start(bf16[704,256]{1,0:T(8,128)(2,1)} %add_convert_fusion.13), channel_id=1, source_target_pairs={{0,4},{8,0},{16,8},{24,16},{28,24},{20,28},{12,20},{4,12},{1,5},{9... | collective-permute-start | bytes 1081352 | tf_op jit(solution)/shard_map/ppermute | solution.py:72
  725.4 21.1 %collective-permute-start.86 = (bf16[704,256]{1,0:T(8,128)(2,1)}, bf16[704,256]{1,0:T(8,128)(2,1)}, u32[]{:S(2)}, u32[]{:S(2)}) collective-permute-start(bf16[704,256]{1,0:T(8,128)(2,1)} %add_convert_fusion.12), channel_id=1, source_target_pairs={{0,8},{8,16},{16,24},{24,28},{28,20},{20,12},{12,4},{4,0},{1,9},{9... | collective-permute-start | bytes 1081352 | tf_op jit(solution)/shard_map/ppermute | solution.py:72
  749.0 19.7 %collective-permute-start.87 = (bf16[704,256]{1,0:T(8,128)(2,1)}, bf16[704,256]{1,0:T(8,128)(2,1)}, u32[]{:S(2)}, u32[]{:S(2)}) collective-permute-start(bf16[704,256]{1,0:T(8,128)(2,1)} %add_convert_fusion.11), channel_id=1, source_target_pairs={{0,8},{8,16},{16,24},{24,28},{28,20},{20,12},{12,4},{4,0},{1,9},{9... | collective-permute-start | bytes 1081352 | tf_op jit(solution)/shard_map/ppermute | solution.py:72
  (174 other events, 2291.6 us)
Sparse Core Ops, SparseCore 0:
  552.3 89.4 all-reduce.15
  645.6 77.0 all-reduce.17

commit v8 on v7

--- a/solution.py
+++ b/solution.py
@@ -655,13 +655,13 @@
     ]
     inner = sum(across(normed1[k], in0[k]) for k in range(n)).astype(bf16)
     gate_in = sum(across(normed1[k], in1[k]) for k in range(n)).astype(bf16)
-    inner = ring.land(inner)
     inner = inner.reshape(seqs, piece, lanes)
     gate_in = gate_in.reshape(seqs, piece, lanes)
     before = lax.ppermute(
         inner[:, piece - taps + 1 :], "seq", [(i, i + 1) for i in range(n - 1)]
     ).astype(f32)
-    before = ring.land(jnp.pad(before, ((0, 0), (pad_rows - taps + 1, 0), (0, 0))))
+    before = jnp.pad(before, ((0, 0), (pad_rows - taps + 1, 0), (0, 0)))
+    before, inner = ring.land((before, inner), 2)
     conv_w = conv_weight.astype(f32)
     rate = decay_rate.astype(f32)[None]
     gate_m = dense_heads(gate_matrix)
@@ -844,8 +844,7 @@
     back = ring.land(jnp.concatenate([back0, back1], axis=1))
     w_both = jnp.concatenate([jnp.concatenate(in0, axis=1), jnp.concatenate(in1, axis=1)], axis=0)
     grads = [
-        Scatter(lambda k: down(back0, normed1[k]), 1, n, chunk),
-        Scatter(lambda k: down(back1, normed1[k]), -1, n, chunk),
+        Scatter(lambda k: down(back, normed1[k]), -1, n, chunk),
     ]
     ring.add(grads)
     ring.issue()
@@ -920,7 +919,7 @@
         output,
         grad_tokens,
         grad_gains[0],
-        jnp.transpose(jnp.stack(grads), (2, 0, 1)),
+        jnp.transpose(grads[0].reshape(2, lanes, part), (2, 0, 1)),
         small[4:],
         small[3],
         grad_matrix,

time: 796 us -> 805 us (1.011)
  waiting for transfers between devices: 194 us -> 228 us
  local copies, waits for them, and re-layouts: 109 us -> 97.1 us
  starting transfers between devices: 123 us -> 113 us
    ppermute x70 -> x63, waiting for transfers between devices: 139 us -> 167 us  [issue(): flying.append((flow, lax.ppermute(message, 'seq', self.pairs[way])))]
    unnamed x343 -> x335, local copies, waits for them, and re-layouts: 62.7 us -> 49 us
    ppermute x1, waiting for transfers between devices: 12.3 us -> 0.01 us  [shards(): lax.ppermute(inner[:, piece - taps + 1:], 'seq', [(i, i + 1) for i in ran...]
    ppermute x70 -> x63, starting transfers between devices: 86 us -> 73.9 us  [issue(): flying.append((flow, lax.ppermute(message, 'seq', self.pairs[way])))]
    dot_general x42 -> x34, matrix products: 99.8 us -> 89.1 us  [down(): lax.dot_general(a, b, (((0,), (0,)), ((), ())), preferred_element_type=f32)]
  transfers between devices with their start and end apart: 95 -> 88, of which waited for: 30 -> 32; matrix products, arithmetic and copies ran while one was open for 38% -> 36% of each run, Pallas kernels for 13% -> 13%
where the time goes in v8:
time: 805 us; the launch traced here: 797 us
  waiting for transfers between devices  228 us (28%)
  matrix products  186 us (23%)
  starting transfers between devices  113 us (14%)
  Pallas kernels  111 us (14%)
  local copies, waits for them, and re-layouts  97.1 us (12%)
  other arithmetic  44 us (5%)
  between operations  16.9 us (2%)
    ppermute x63, waiting for transfers between devices, issue(): flying.append((flow, lax.ppermute(message, 'seq', self.pairs[way])))  167 us
    dot_general x34, matrix products, down(): lax.dot_general(a, b, (((0,), (0,)), ((), ())), preferred_element_type=f32)  89.1 us
    ppermute x63, starting transfers between devices, issue(): flying.append((flow, lax.ppermute(message, 'seq', self.pairs[way])))  73.9 us
    pallas_call x8, Pallas kernels, by_rows(): pl.pallas_call(body, grid_spec=pltpu.PrefetchScalarGridSpec(num_scalar_pr...  56.1 us
    dot_general x19, matrix products, across(): lax.dot_general(a, b, (((1,), (1,)), ((), ())), preferred_element_type=f32)  51.2 us
    unnamed x335, local copies, waits for them, and re-layouts  49 us
    dot_general x6, matrix products, dot(): return jnp.dot(a, b, preferred_element_type=f32)  46.1 us
    pallas_call x3, Pallas kernels, per_sequence(): pl.pallas_call(kernel, grid=(seqs,), in_specs=[spec(a.shape, kind) for a,...  42.9 us
  transfers between devices with their start and end apart: 88, of which 32 were waited for; matrix products, arithmetic and copies ran while one was open for 36% of the time, Pallas kernels for 13%

profile of v8, /device:TPU:0, one launch (start us, length us, event | category | flops | bytes accessed | tf_op | source)
XLA Modules:
  0.0 797.1 jit_solution(12143606709782584143)
XLA Ops:
  35.5 8.5 %shard_map.255 = (bf16[4,256,2048]{2,1,0:T(8,128)(2,1)S(1)}, bf16[4,256,2048]{2,1,0:T(8,128)(2,1)}) custom-call(s32[4]{0:T(128)S(1)} %and_select_fusion.2.refs_0_, s32[8]{0:T(128)S(1)} %gather_fusion, bf16[4,256,2048]{2,1,0:T(8,128)(2,1)} %refs_2_, bf16[4,256,2048]{2,1,0:T(8,128)(2,1)} %refs_3_), custom_call_target="tpu_custom_call" | custom-call | flops 16777216 | bytes 16777216 | tf_op jit(solution)/shard_map/pallas_call | solution.py:419
  59.1 3.5 collective-permute-done.4
  66.3 7.9 collective-permute-done.7
  76.3 10.3 %collective-permute-done.9 = bf16[1072,256]{1,0:T(8,128)(2,1)S(1)} collective-permute-done((bf16[1072,256]{1,0:T(8,128)(2,1)S(1)}, bf16[1072,256]{1,0:T(8,128)(2,1)S(1)}, u32[]{:S(2)}, u32[]{:S(2)}) %collective-permute-start.9) | collective-permute-done | bytes 548896 | tf_op jit(solution)/shard_map/ppermute | solution.py:72
  89.7 7.8 collective-permute-done.13
  131.4 4.0 add_convert_fusion.6
  138.8 5.3 collective-permute-done.16
  147.4 16.0 %shard_map.256 = (f32[4,256,704]{2,1,0:T(8,128)}, f32[4,256,704]{2,1,0:T(8,128)}, f32[4,256,704]{2,1,0:T(8,128)}, f32[4,256,704]{2,1,0:T(8,128)}, f32[4,256,704]...) custom-call(bf16[4,256,704]{2,1,0:T(8,128)(2,1)S(1)} %bitcast.175, ...), custom_call_target="tpu_custom_call" | custom-call | flops 2030043136 | bytes 23812096 | tf_op jit(solution)/shard_map/pallas_call | solution.py:382
  163.5 3.9 collective-permute-start.21
  169.7 8.6 %collective-permute-done.21 = f32[4,2,704]{2,1,0:T(2,128)S(1)} collective-permute-done((f32[4,2,704]{2,1,0:T(2,128)S(1)}, f32[4,2,704]{2,1,0:T(2,128)S(1)}, u32[]{:S(2)}, u32[]{:S(2)}) %collective-permute-start.21) | collective-permute-done | bytes 22560 | tf_op jit(solution)/shard_map/ppermute | solution.py:537
  178.4 5.4 collective-permute-start.24
  185.3 9.7 %collective-permute-start.25 = (f32[4,2,704]{2,1,0:T(2,128)S(1)}, f32[4,2,704]{2,1,0:T(2,128)S(1)}, u32[]{:S(2)}, u32[]{:S(2)}) collective-permute-start(f32[4,2,704]{2,1,0:T(2,128)S(1)} %pad_add_fusion.2), channel_id=1, source_target_pairs={{0,4},{4,8},{8,12},{12,16},{16,20},{20,24},{24,28},{1,5},{5,9},{9,... | collective-permute-start | bytes 67592 | tf_op jit(solution)/shard_map/ppermute | solution.py:537
  195.0 4.8 collective-permute-start.26
  204.0 6.0 fusion.36
  230.7 12.5 %collective-permute-done.31 = bf16[256,1536]{1,0:T(8,128)(2,1)S(1)} collective-permute-done((bf16[256,1536]{1,0:T(8,128)(2,1)S(1)}, bf16[256,1536]{1,0:T(8,128)(2,1)S(1)}, u32[]{:S(2)}, u32[]{:S(2)}) %collective-permute-start.31) | collective-permute-done | bytes 786464 | tf_op jit(solution)/shard_map/ppermute | solution.py:72
  252.4 7.2 collective-permute-done.40
  263.3 4.6 collective-permute-done.38
  267.9 10.8 %collective-permute-done.41 = bf16[256,1536]{1,0:T(8,128)(2,1)S(1)} collective-permute-done((bf16[256,1536]{1,0:T(8,128)(2,1)S(1)}, bf16[256,1536]{1,0:T(8,128)(2,1)S(1)}, u32[]{:S(2)}, u32[]{:S(2)}) %collective-permute-start.41) | collective-permute-done | bytes 786464 | tf_op jit(solution)/shard_map/ppermute | solution.py:72
  281.9 9.0 %collective-permute-done.32 = bf16[512,2048]{1,0:T(8,128)(2,1)S(1)} collective-permute-done((bf16[512,2048]{1,0:T(8,128)(2,1)S(1)}, bf16[512,2048]{1,0:T(8,128)(2,1)S(1)}, u32[]{:S(2)}, u32[]{:S(2)}) %collective-permute-start.32) | collective-permute-done | bytes 2097184 | tf_op jit(solution)/shard_map/ppermute | solution.py:188
  293.2 5.4 collective-permute-done.36
  299.1 14.9 %collective-permute-done.34 = bf16[1536,256]{1,0:T(8,128)(2,1)S(1)} collective-permute-done((bf16[1536,256]{1,0:T(8,128)(2,1)}, bf16[1536,256]{1,0:T(8,128)(2,1)S(1)}, u32[]{:S(2)}, u32[]{:S(2)}) %collective-permute-start.34) | collective-permute-done | bytes 786464 | tf_op jit(solution)/shard_map/ppermute | solution.py:72
  319.8 5.0 shard_map.257
  324.9 5.1 shard_map.258
  333.7 20.2 %convolution_convert_fusion = bf16[1024,3072]{1,0:T(8,128)(2,1)} fusion(bf16[1024,2048]{1,0:T(8,128)(2,1)} %bitcast.185, bf16[2048,1536]{1,0:T(8,128)(2,1)} %copy-done.100, bf16[2048,1536]{1,0:T(8,128)(2,1)} %copy-done.101), kind=kOutput, calls=%fused_computation.40 | convolution fusion | flops 12913213440 | bytes 23068672 | tf_op jit(solution)/shard_map/dot_general | solution.py:580
  353.9 8.0 %fusion.6 = (bf16[1024,1536]{1,0:T(8,128)(2,1)}, bf16[1024,1536]{1,0:T(8,128)(2,1)S(1)}, bf16[1024,1536]{1,0:T(8,128)(2,1)S(1)}) fusion(bf16[1024,3072]{1,0:T(8,128)(2,1)} %convolution_convert_fusion), kind=kLoop, calls=%fused_computation.30 | loop fusion | flops 39321600 | bytes 15728640 | tf_op jit(solution)/shard_map/convert_element_type | solution.py:729
  378.0 12.4 %shard_map.259 = bf16[1024,3072]{1,0:T(8,128)(2,1)} custom-call(bf16[1024,2048]{1,0:T(8,128)(2,1)} %bitcast.196, bf16[1536,2048]{1,0:T(8,128)(2,1)} %constant_dynamic-update-slice_fusion.26.w_down, bf16[1024,1536]{1,0:T(8,128)(2,1)S(1)} %get-tuple-element.252.act, bf16[1024,1536]{1,0:T(8,128)(2,1)} %get-tuple-element.253.slope), custom_call_target="tpu_custom_call" | custom-call | flops 6442450944 | bytes 23068672 | tf_op jit(solution)/shard_map/pallas_call | solution.py:740
  390.4 11.8 %fusion.50 = bf16[512,2048]{1,0:T(8,128)(2,1)} fusion(bf16[2048,1536]{1,0:T(8,128)(2,1)} %copy-done.100, bf16[2048,1536]{1,0:T(8,128)(2,1)} %copy-done.101, bf16[1024,3072]{1,0:T(8,128)(2,1)} %shard_map.259), kind=kOutput, calls=%fused_computation.101 | convolution fusion | flops 6468665344 | bytes 17825792 | tf_op jit(solution)/shard_map/dot_general | solution.py:572
  402.4 4.6 convolution_convert_fusion.1
  412.1 10.8 %fusion.47 = bf16[512,2048]{1,0:T(8,128)(2,1)} fusion(bf16[2048,1536]{1,0:T(8,128)(2,1)} %copy-done.100, bf16[2048,1536]{1,0:T(8,128)(2,1)} %copy-done.101, bf16[1024,3072]{1,0:T(8,128)(2,1)S(1)} %copy-done.20), kind=kOutput, calls=%fused_computation.100 | convolution fusion | flops 6468665344 | bytes 17825792 | tf_op jit(solution)/shard_map/dot_general | solution.py:572
  427.5 4.6 fusion.33
  436.4 8.1 %collective-permute-done.52 = bf16[256,3072]{1,0:T(8,128)(2,1)} collective-permute-done((bf16[256,3072]{1,0:T(8,128)(2,1)}, bf16[256,3072]{1,0:T(8,128)(2,1)}, u32[]{:S(2)}, u32[]{:S(2)}) %collective-permute-start.52) | collective-permute-done | bytes 1572896 | tf_op jit(solution)/shard_map/ppermute | solution.py:72
  444.5 4.7 fusion.21
  449.2 4.1 fusion.20
  455.5 17.6 %collective-permute-done.46 = bf16[512,2048]{1,0:T(8,128)(2,1)S(1)} collective-permute-done((bf16[512,2048]{1,0:T(8,128)(2,1)S(1)}, bf16[512,2048]{1,0:T(8,128)(2,1)S(1)}, u32[]{:S(2)}, u32[]{:S(2)}) %collective-permute-start.46) | collective-permute-done | bytes 2097184 | tf_op jit(solution)/shard_map/ppermute | solution.py:188
  482.8 7.4 shard_map.260
  490.1 7.5 shard_map.261
  498.0 7.9 fusion.92
  506.0 7.9 shard_map.262
  519.4 4.2 fusion.23
  525.3 4.7 fusion.22
  534.9 5.6 collective-permute-done.57
  543.1 10.9 %convolution_convert_fusion.3 = bf16[1024,2048]{1,0:T(8,128)(2,1)} fusion(bf16[1024,1536]{1,0:T(8,128)(2,1)S(1)} %copy-done.57, bf16[1536,2048]{1,0:T(8,128)(2,1)} %constant_dynamic-update-slice_fusion.26.w_down), kind=kOutput, calls=%fused_computation.73 | convolution fusion | flops 6444548096 | bytes 13631488 | tf_op jit(solution)/shard_map/dot_general | solution.py:580
  557.9 19.0 %shard_map.263 = (bf16[2,4,256,704]{3,2,1,0:T(8,128)(2,1)}, bf16[4,256,704]{2,1,0:T(8,128)(2,1)S(1)}, bf16[4,256,704]{2,1,0:T(8,128)(2,1)S(1)}, f32[4,8,704]{2,1...) custom-call(f32[4,256,704]{2,1,0:T(8,128)} %bitcast.206, f32[4,256,704]{2,1,0:T(8,128)} %get-tuple-element.393.slope, ...), custom_call_target="tpu_custom_call" | custom-call | flops 2030043136 | bytes 38514432 | tf_op jit(solution)/shard_map/pallas_call | solution.py:382
  591.1 4.0 collective-permute-done.60
  598.6 4.6 fusion.46
  605.7 6.2 fusion.24
  614.1 3.7 fusion.45
  618.9 4.0 collective-permute-done.72
  624.4 24.9 %collective-permute-done.65 = bf16[256,3072]{1,0:T(8,128)(2,1)S(1)} collective-permute-done((bf16[256,3072]{1,0:T(8,128)(2,1)S(1)}, bf16[256,3072]{1,0:T(8,128)(2,1)S(1)}, u32[]{:S(2)}, u32[]{:S(2)}) %collective-permute-start.65) | collective-permute-done | bytes 1572896 | tf_op jit(solution)/shard_map/ppermute | solution.py:72
  649.2 9.3 %collective-permute-done.79 = bf16[704,256]{1,0:T(8,128)(2,1)S(1)} collective-permute-done((bf16[704,256]{1,0:T(8,128)(2,1)S(1)}, bf16[704,256]{1,0:T(8,128)(2,1)S(1)}, u32[]{:S(2)}, u32[]{:S(2)}) %collective-permute-start.79) | collective-permute-done | bytes 360480 | tf_op jit(solution)/shard_map/ppermute | solution.py:72
  664.6 6.7 collective-permute-done.80
  671.4 5.4 fusion.19
  682.3 9.7 %collective-permute-done.81 = bf16[1408,256]{1,0:T(8,128)(2,1)S(1)} collective-permute-done((bf16[1408,256]{1,0:T(8,128)(2,1)S(1)}, bf16[1408,256]{1,0:T(8,128)(2,1)S(1)}, u32[]{:S(2)}, u32[]{:S(2)}) %collective-permute-start.81) | collective-permute-done | bytes 720928 | tf_op jit(solution)/shard_map/ppermute | solution.py:72
  693.8 4.3 collective-permute-done.82
  698.2 7.2 collective-permute-done.66
  711.1 6.0 collective-permute-done.83
  717.1 3.8 fusion.63
  721.2 7.8 collective-permute-done.69
  729.1 3.5 fusion.54
  732.6 5.6 reshape.430
  740.5 8.8 %shard_map.264 = bf16[4,256,2048]{2,1,0:T(8,128)(2,1)} custom-call(s32[4]{0:T(128)S(1)} %copy-done.19, s32[8]{0:T(128)S(1)} %copy-done.15, f32[4,256,2048]{2,1,0:T(8,128)} %get-tuple-element.225.refs_0_.refs_2_, bf16[4,256,2048]{2,1,0:T(8,128)(2,1)S(1)} %bitcast.177), custom_call_target="tpu_custom_call" | custom-call | flops 16777216 | bytes 16777216 | tf_op jit(solution)/shard_map/pallas_call | solution.py:419
  760.5 6.7 shard_map.265.refs_6_
  778.4 4.3 fusion.53
  782.6 7.2 shard_map.266
  (631 shorter events, 278.4 us)
Async XLA Ops:
  7.2 731.0 %all-reduce.16.cloned.1.call-start = ((), (), s32[]{:S(2)}) async-start(), calls=%async_computation | async-start | bytes 8388608 | tf_op jit(solution)/shard_map/psum | solution.py:798
  11.2 22.2 %collective-permute-start = (bf16[1056,256]{1,0:T(8,128)(2,1)}, bf16[1056,256]{1,0:T(8,128)(2,1)S(1)}, u32[]{:S(2)}, u32[]{:S(2)}) collective-permute-start(bf16[1056,256]{1,0:T(8,128)(2,1)} %pad_maximum_fusion.21), channel_id=1, source_target_pairs={{0,8},{8,16},{16,24},{24,28},{28,20},{20,12},{12,4},{4,0},{1,9},{9... | collective-permute-start | bytes 1622024 | tf_op jit(solution)/shard_map/ppermute | solution.py:72
  14.2 19.2 %collective-permute-start.1 = (bf16[1056,256]{1,0:T(8,128)(2,1)}, bf16[1056,256]{1,0:T(8,128)(2,1)}, u32[]{:S(2)}, u32[]{:S(2)}) collective-permute-start(bf16[1056,256]{1,0:T(8,128)(2,1)} %pad_maximum_fusion.21), channel_id=1, source_target_pairs={{0,4},{8,0},{16,8},{24,16},{28,24},{20,28},{12,20},{4,12},{1,5},{9... | collective-permute-start | bytes 1622024 | tf_op jit(solution)/shard_map/ppermute | solution.py:72
  15.1 29.9 %collective-permute-start.2 = (bf16[1072,256]{1,0:T(8,128)(2,1)}, bf16[1072,256]{1,0:T(8,128)(2,1)}, u32[]{:S(2)}, u32[]{:S(2)}) collective-permute-start(bf16[1072,256]{1,0:T(8,128)(2,1)} %pad_maximum_fusion.20), channel_id=1, source_target_pairs={{0,8},{8,16},{16,24},{24,28},{28,20},{20,12},{12,4},{4,0},{1,9},{9... | collective-permute-start | bytes 1646600 | tf_op jit(solution)/shard_map/ppermute | solution.py:72
  17.1 27.9 %collective-permute-start.3 = (bf16[1072,256]{1,0:T(8,128)(2,1)}, bf16[1072,256]{1,0:T(8,128)(2,1)}, u32[]{:S(2)}, u32[]{:S(2)}) collective-permute-start(bf16[1072,256]{1,0:T(8,128)(2,1)} %pad_maximum_fusion.20), channel_id=1, source_target_pairs={{0,4},{8,0},{16,8},{24,16},{28,24},{20,28},{12,20},{4,12},{1,5},{9... | collective-permute-start | bytes 1646600 | tf_op jit(solution)/shard_map/ppermute | solution.py:72
  33.4 22.8 %collective-permute-start.10 = (bf16[1056,256]{1,0:T(8,128)(2,1)}, bf16[1056,256]{1,0:T(8,128)(2,1)S(1)}, u32[]{:S(2)}, u32[]{:S(2)}) collective-permute-start(bf16[1056,256]{1,0:T(8,128)(2,1)} %collective-permute-done.1), channel_id=1, source_target_pairs={{0,4},{8,0},{16,8},{24,16},{28,24},{20,28},{12,20},{4,12},{1,5},{9... | collective-permute-start | bytes 1622024 | tf_op jit(solution)/shard_map/ppermute | solution.py:72
  35.4 22.7 %collective-permute-start.5 = (bf16[1056,256]{1,0:T(8,128)(2,1)S(1)}, bf16[1056,256]{1,0:T(8,128)(2,1)S(1)}, u32[]{:S(2)}, u32[]{:S(2)}) collective-permute-start(bf16[1056,256]{1,0:T(8,128)(2,1)S(1)} %collective-permute-done), channel_id=1, source_target_pairs={{0,8},{8,16},{16,24},{24,28},{28,20},{20,12},{12,4},{4,0},{1,9},{9... | collective-permute-start | bytes 1622024 | tf_op jit(solution)/shard_map/ppermute | solution.py:72
  56.2 20.1 %collective-permute-start.11 = (bf16[1056,256]{1,0:T(8,128)(2,1)S(1)}, bf16[1056,256]{1,0:T(8,128)(2,1)S(1)}, u32[]{:S(2)}, u32[]{:S(2)}) collective-permute-start(bf16[1056,256]{1,0:T(8,128)(2,1)S(1)} %collective-permute-done.10), channel_id=1, source_target_pairs={{0,4},{8,0},{16,8},{24,16},{28,24},{20,28},{12,20},{4,12},{1,5},{9... | collective-permute-start | bytes 1622024 | tf_op jit(solution)/shard_map/ppermute | solution.py:72
  62.6 26.0 %collective-permute-start.6 = (bf16[1072,256]{1,0:T(8,128)(2,1)S(1)}, bf16[1072,256]{1,0:T(8,128)(2,1)S(1)}, u32[]{:S(2)}, u32[]{:S(2)}) collective-permute-start(bf16[1072,256]{1,0:T(8,128)(2,1)S(1)} %collective-permute-done.4), channel_id=1, source_target_pairs={{0,8},{8,16},{16,24},{24,28},{28,20},{20,12},{12,4},{4,0},{1,9},{9... | collective-permute-start | bytes 1646600 | tf_op jit(solution)/shard_map/ppermute | solution.py:72
  64.7 21.9 %collective-permute-start.9 = (bf16[1072,256]{1,0:T(8,128)(2,1)S(1)}, bf16[1072,256]{1,0:T(8,128)(2,1)S(1)}, u32[]{:S(2)}, u32[]{:S(2)}) collective-permute-start(bf16[1072,256]{1,0:T(8,128)(2,1)S(1)} %collective-permute-done.8), channel_id=1, source_target_pairs={{0,4},{8,0},{16,8},{24,16},{28,24},{20,28},{12,20},{4,12},{1,5},{9... | collective-permute-start | bytes 1646600 | tf_op jit(solution)/shard_map/ppermute | solution.py:72
  74.2 23.3 %collective-permute-start.13 = (bf16[1056,256]{1,0:T(8,128)(2,1)S(1)}, bf16[1056,256]{1,0:T(8,128)(2,1)S(1)}, u32[]{:S(2)}, u32[]{:S(2)}) collective-permute-start(bf16[1056,256]{1,0:T(8,128)(2,1)S(1)} %collective-permute-done.7), channel_id=1, source_target_pairs={{0,8},{8,16},{16,24},{24,28},{28,20},{20,12},{12,4},{4,0},{1,9},{9... | collective-permute-start | bytes 1622024 | tf_op jit(solution)/shard_map/ppermute | solution.py:72
  86.9 48.5 %collective-permute-start.19 = (bf16[256,1536]{1,0:T(8,128)(2,1)}, bf16[256,1536]{1,0:T(8,128)(2,1)}, u32[]{:S(2)}, u32[]{:S(2)}) collective-permute-start(bf16[256,1536]{1,0:T(8,128)(2,1)} %get-tuple-element.205), channel_id=1, source_target_pairs={{0,4},{8,0},{16,8},{24,16},{28,24},{20,28},{12,20},{4,12},{1,5},{9... | collective-permute-start | bytes 2359304 | tf_op jit(solution)/shard_map/ppermute | solution.py:72
  88.6 48.4 %collective-permute-start.17 = (bf16[256,1536]{1,0:T(8,128)(2,1)}, bf16[256,1536]{1,0:T(8,128)(2,1)}, u32[]{:S(2)}, u32[]{:S(2)}) collective-permute-start(bf16[256,1536]{1,0:T(8,128)(2,1)} %get-tuple-element.205), channel_id=1, source_target_pairs={{0,8},{8,16},{16,24},{24,28},{28,20},{20,12},{12,4},{4,0},{1,9},{9... | collective-permute-start | bytes 2359304 | tf_op jit(solution)/shard_map/ppermute | solution.py:72
  97.5 41.3 %collective-permute-start.15 = (bf16[256,1536]{1,0:T(8,128)(2,1)}, bf16[256,1536]{1,0:T(8,128)(2,1)}, u32[]{:S(2)}, u32[]{:S(2)}) collective-permute-start(bf16[256,1536]{1,0:T(8,128)(2,1)} %get-tuple-element.197), channel_id=1, source_target_pairs={{0,8},{8,16},{16,24},{24,28},{28,20},{20,12},{12,4},{4,0},{1,9},{9... | collective-permute-start | bytes 2359304 | tf_op jit(solution)/shard_map/ppermute | solution.py:72
  123.1 21.1 %collective-permute-start.16 = (bf16[256,1536]{1,0:T(8,128)(2,1)}, bf16[256,1536]{1,0:T(8,128)(2,1)}, u32[]{:S(2)}, u32[]{:S(2)}) collective-permute-start(bf16[256,1536]{1,0:T(8,128)(2,1)} %get-tuple-element.197), channel_id=1, source_target_pairs={{0,4},{8,0},{16,8},{24,16},{28,24},{20,28},{12,20},{4,12},{1,5},{9... | collective-permute-start | bytes 2359304 | tf_op jit(solution)/shard_map/ppermute | solution.py:72
  135.4 28.0 %collective-permute-start.20 = (bf16[256,1536]{1,0:T(8,128)(2,1)}, bf16[256,1536]{1,0:T(8,128)(2,1)S(1)}, u32[]{:S(2)}, u32[]{:S(2)}) collective-permute-start(bf16[256,1536]{1,0:T(8,128)(2,1)} %collective-permute-done.19), channel_id=1, source_target_pairs={{0,4},{8,0},{16,8},{24,16},{28,24},{20,28},{12,20},{4,12},{1,5},{9... | collective-permute-start | bytes 2359304 | tf_op jit(solution)/shard_map/ppermute | solution.py:72
  137.0 26.5 %collective-permute-start.18 = (bf16[256,1536]{1,0:T(8,128)(2,1)}, bf16[256,1536]{1,0:T(8,128)(2,1)S(1)}, u32[]{:S(2)}, u32[]{:S(2)}) collective-permute-start(bf16[256,1536]{1,0:T(8,128)(2,1)} %collective-permute-done.17), channel_id=1, source_target_pairs={{0,8},{8,16},{16,24},{24,28},{28,20},{20,12},{12,4},{4,0},{1,9},{9... | collective-permute-start | bytes 2359304 | tf_op jit(solution)/shard_map/ppermute | solution.py:72
  144.2 34.2 %collective-permute-start.22 = (bf16[256,1536]{1,0:T(8,128)(2,1)}, bf16[256,1536]{1,0:T(8,128)(2,1)S(1)}, u32[]{:S(2)}, u32[]{:S(2)}) collective-permute-start(bf16[256,1536]{1,0:T(8,128)(2,1)} %collective-permute-done.15), channel_id=1, source_target_pairs={{0,8},{8,16},{16,24},{24,28},{28,20},{20,12},{12,4},{4,0},{1,9},{9... | collective-permute-start | bytes 2359304 | tf_op jit(solution)/shard_map/ppermute | solution.py:72
  145.6 32.8 %collective-permute-start.23 = (bf16[256,1536]{1,0:T(8,128)(2,1)}, bf16[256,1536]{1,0:T(8,128)(2,1)S(1)}, u32[]{:S(2)}, u32[]{:S(2)}) collective-permute-start(bf16[256,1536]{1,0:T(8,128)(2,1)} %collective-permute-done.16), channel_id=1, source_target_pairs={{0,4},{8,0},{16,8},{24,16},{28,24},{20,28},{12,20},{4,12},{1,5},{9... | collective-permute-start | bytes 2359304 | tf_op jit(solution)/shard_map/ppermute | solution.py:72
  167.4 35.8 %collective-permute-start.27 = (bf16[1536,256]{1,0:T(8,128)(2,1)S(1)}, bf16[1536,256]{1,0:T(8,128)(2,1)}, u32[]{:S(2)}, u32[]{:S(2)}) collective-permute-start(bf16[1536,256]{1,0:T(8,128)(2,1)S(1)} %copy-done.88), channel_id=1, source_target_pairs={{0,8},{8,16},{16,24},{24,28},{28,20},{20,12},{12,4},{4,0},{1,9},{9... | collective-permute-start | bytes 2359304 | tf_op jit(solution)/shard_map/ppermute | solution.py:72
  169.1 34.2 %collective-permute-start.28 = (bf16[1536,256]{1,0:T(8,128)(2,1)S(1)}, bf16[1536,256]{1,0:T(8,128)(2,1)}, u32[]{:S(2)}, u32[]{:S(2)}) collective-permute-start(bf16[1536,256]{1,0:T(8,128)(2,1)S(1)} %copy-done.88), channel_id=1, source_target_pairs={{0,4},{8,0},{16,8},{24,16},{28,24},{20,28},{12,20},{4,12},{1,5},{9... | collective-permute-start | bytes 2359304 | tf_op jit(solution)/shard_map/ppermute | solution.py:72
  222.8 20.3 %collective-permute-start.31 = (bf16[256,1536]{1,0:T(8,128)(2,1)S(1)}, bf16[256,1536]{1,0:T(8,128)(2,1)S(1)}, u32[]{:S(2)}, u32[]{:S(2)}) collective-permute-start(bf16[256,1536]{1,0:T(8,128)(2,1)S(1)} %copy-done.90), channel_id=1, source_target_pairs={{0,4},{8,0},{16,8},{24,16},{28,24},{20,28},{12,20},{4,12},{1,5},{9... | collective-permute-start | bytes 2359304 | tf_op jit(solution)/shard_map/ppermute | solution.py:72
  224.3 19.7 %collective-permute-start.30 = (bf16[256,1536]{1,0:T(8,128)(2,1)S(1)}, bf16[256,1536]{1,0:T(8,128)(2,1)S(1)}, u32[]{:S(2)}, u32[]{:S(2)}) collective-permute-start(bf16[256,1536]{1,0:T(8,128)(2,1)S(1)} %copy-done.94), channel_id=1, source_target_pairs={{0,8},{8,16},{16,24},{24,28},{28,20},{20,12},{12,4},{4,0},{1,9},{9... | collective-permute-start | bytes 2359304 | tf_op jit(solution)/shard_map/ppermute | solution.py:72
  228.2 31.3 %collective-permute-start.40 = (bf16[256,1536]{1,0:T(8,128)(2,1)S(1)}, bf16[256,1536]{1,0:T(8,128)(2,1)S(1)}, u32[]{:S(2)}, u32[]{:S(2)}) collective-permute-start(bf16[256,1536]{1,0:T(8,128)(2,1)S(1)} %copy-done.92), channel_id=1, source_target_pairs={{0,4},{8,0},{16,8},{24,16},{28,24},{20,28},{12,20},{4,12},{1,5},{9... | collective-permute-start | bytes 2359304 | tf_op jit(solution)/shard_map/ppermute | solution.py:72
  243.9 46.9 %collective-permute-start.32 = (bf16[512,2048]{1,0:T(8,128)(2,1)S(1)}, bf16[512,2048]{1,0:T(8,128)(2,1)S(1)}, u32[]{:S(2)}, u32[]{:S(2)}) collective-permute-start(bf16[512,2048]{1,0:T(8,128)(2,1)S(1)} %add_convert_fusion.5), channel_id=1, source_target_pairs={{0,2},{1,3},{2,0},{3,1},{4,6},{5,7},{6,4},{7,5},{8,10},{9,11},{10,... | collective-permute-start | bytes 6291464 | tf_op jit(solution)/shard_map/ppermute | solution.py:188
  259.6 19.2 %collective-permute-start.41 = (bf16[256,1536]{1,0:T(8,128)(2,1)S(1)}, bf16[256,1536]{1,0:T(8,128)(2,1)S(1)}, u32[]{:S(2)}, u32[]{:S(2)}) collective-permute-start(bf16[256,1536]{1,0:T(8,128)(2,1)S(1)} %collective-permute-done.40), channel_id=1, source_target_pairs={{0,4},{8,0},{16,8},{24,16},{28,24},{20,28},{12,20},{4,12},{1,5},{9... | collective-permute-start | bytes 2359304 | tf_op jit(solution)/shard_map/ppermute | solution.py:72
  278.8 36.7 %collective-permute-start.39 = (bf16[256,1536]{1,0:T(8,128)(2,1)S(1)}, bf16[256,1536]{1,0:T(8,128)(2,1)S(1)}, u32[]{:S(2)}, u32[]{:S(2)}) collective-permute-start(bf16[256,1536]{1,0:T(8,128)(2,1)S(1)} %collective-permute-done.30), channel_id=1, source_target_pairs={{0,8},{8,16},{16,24},{24,28},{28,20},{20,12},{12,4},{4,0},{1,9},{9... | collective-permute-start | bytes 2359304 | tf_op jit(solution)/shard_map/ppermute | solution.py:72
  279.8 18.7 %collective-permute-start.36 = (bf16[1536,256]{1,0:T(8,128)(2,1)}, bf16[1536,256]{1,0:T(8,128)(2,1)S(1)}, u32[]{:S(2)}, u32[]{:S(2)}) collective-permute-start(bf16[1536,256]{1,0:T(8,128)(2,1)} %collective-permute-done.28), channel_id=1, source_target_pairs={{0,4},{8,0},{16,8},{24,16},{28,24},{20,28},{12,20},{4,12},{1,5},{9... | collective-permute-start | bytes 2359304 | tf_op jit(solution)/shard_map/ppermute | solution.py:72
  280.9 33.1 %collective-permute-start.34 = (bf16[1536,256]{1,0:T(8,128)(2,1)}, bf16[1536,256]{1,0:T(8,128)(2,1)S(1)}, u32[]{:S(2)}, u32[]{:S(2)}) collective-permute-start(bf16[1536,256]{1,0:T(8,128)(2,1)} %collective-permute-done.27), channel_id=1, source_target_pairs={{0,8},{8,16},{16,24},{24,28},{28,20},{20,12},{12,4},{4,0},{1,9},{9... | collective-permute-start | bytes 2359304 | tf_op jit(solution)/shard_map/ppermute | solution.py:72
  291.8 33.1 %collective-permute-start.33 = (bf16[512,2048]{1,0:T(8,128)(2,1)S(1)}, bf16[512,2048]{1,0:T(8,128)(2,1)S(1)}, u32[]{:S(2)}, u32[]{:S(2)}) collective-permute-start(bf16[512,2048]{1,0:T(8,128)(2,1)S(1)} %add_convert_fusion.4), channel_id=1, source_target_pairs={{0,1},{1,0},{2,3},{3,2},{4,5},{5,4},{6,7},{7,6},{8,9},{9,8},{10,11... | collective-permute-start | bytes 6291464 | tf_op jit(solution)/shard_map/ppermute | solution.py:183
  298.6 31.3 %collective-permute-start.37 = (bf16[1536,256]{1,0:T(8,128)(2,1)S(1)}, bf16[1536,256]{1,0:T(8,128)(2,1)S(1)}, u32[]{:S(2)}, u32[]{:S(2)}) collective-permute-start(bf16[1536,256]{1,0:T(8,128)(2,1)S(1)} %collective-permute-done.36), channel_id=1, source_target_pairs={{0,4},{8,0},{16,8},{24,16},{28,24},{20,28},{12,20},{4,12},{1,5},{9... | collective-permute-start | bytes 2359304 | tf_op jit(solution)/shard_map/ppermute | solution.py:72
  331.4 33.2 %collective-permute-start.42 = (bf16[1536,256]{1,0:T(8,128)(2,1)}, bf16[1536,256]{1,0:T(8,128)(2,1)S(1)}, u32[]{:S(2)}, u32[]{:S(2)}) collective-permute-start(bf16[1536,256]{1,0:T(8,128)(2,1)} %collective-permute-done.35), channel_id=1, source_target_pairs={{0,8},{8,16},{16,24},{24,28},{28,20},{20,12},{12,4},{4,0},{1,9},{9... | collective-permute-start | bytes 2359304 | tf_op jit(solution)/shard_map/ppermute | solution.py:72
  375.6 26.7 %collective-permute-start.44 = (bf16[1536,256]{1,0:T(8,128)(2,1)}, bf16[1536,256]{1,0:T(8,128)(2,1)S(1)}, u32[]{:S(2)}, u32[]{:S(2)}) collective-permute-start(bf16[1536,256]{1,0:T(8,128)(2,1)} %convolution_convert_fusion.8), channel_id=1, source_target_pairs={{0,4},{8,0},{16,8},{24,16},{28,24},{20,28},{12,20},{4,12},{1,5},{9... | collective-permute-start | bytes 2359304 | tf_op jit(solution)/shard_map/ppermute | solution.py:72
  375.6 26.7 %collective-permute-start.43 = (bf16[1536,256]{1,0:T(8,128)(2,1)}, bf16[1536,256]{1,0:T(8,128)(2,1)S(1)}, u32[]{:S(2)}, u32[]{:S(2)}) collective-permute-start(bf16[1536,256]{1,0:T(8,128)(2,1)} %convolution_convert_fusion.9), channel_id=1, source_target_pairs={{0,8},{8,16},{16,24},{24,28},{28,20},{20,12},{12,4},{4,0},{1,9},{9... | collective-permute-start | bytes 2359304 | tf_op jit(solution)/shard_map/ppermute | solution.py:72
  402.3 20.6 %collective-permute-start.45 = (bf16[512,2048]{1,0:T(8,128)(2,1)}, bf16[512,2048]{1,0:T(8,128)(2,1)}, u32[]{:S(2)}, u32[]{:S(2)}) collective-permute-start(bf16[512,2048]{1,0:T(8,128)(2,1)} %fusion.50), channel_id=1, source_target_pairs={{0,1},{1,0},{2,3},{3,2},{4,5},{5,4},{6,7},{7,6},{8,9},{9,8},{10,11... | collective-permute-start | bytes 6291464 | tf_op jit(solution)/shard_map/ppermute | solution.py:183
  407.0 37.6 %collective-permute-start.52 = (bf16[256,3072]{1,0:T(8,128)(2,1)}, bf16[256,3072]{1,0:T(8,128)(2,1)}, u32[]{:S(2)}, u32[]{:S(2)}) collective-permute-start(bf16[256,3072]{1,0:T(8,128)(2,1)} %convolution_convert_fusion.1), channel_id=1, source_target_pairs={{0,4},{8,0},{16,8},{24,16},{28,24},{20,28},{12,20},{4,12},{1,5},{9... | collective-permute-start | bytes 4718600 | tf_op jit(solution)/shard_map/ppermute | solution.py:72
  409.9 39.3 %collective-permute-start.50 = (bf16[256,3072]{1,0:T(8,128)(2,1)S(1)}, bf16[256,3072]{1,0:T(8,128)(2,1)S(1)}, u32[]{:S(2)}, u32[]{:S(2)}) collective-permute-start(bf16[256,3072]{1,0:T(8,128)(2,1)S(1)} %convolution_convert_fusion.2), channel_id=1, source_target_pairs={{0,8},{8,16},{16,24},{24,28},{28,20},{20,12},{12,4},{4,0},{1,9},{9... | collective-permute-start | bytes 4718600 | tf_op jit(solution)/shard_map/ppermute | solution.py:72
  426.0 47.1 %collective-permute-start.46 = (bf16[512,2048]{1,0:T(8,128)(2,1)S(1)}, bf16[512,2048]{1,0:T(8,128)(2,1)S(1)}, u32[]{:S(2)}, u32[]{:S(2)}) collective-permute-start(bf16[512,2048]{1,0:T(8,128)(2,1)S(1)} %add_convert_fusion.3), channel_id=1, source_target_pairs={{0,2},{1,3},{2,0},{3,1},{4,6},{5,7},{6,4},{7,5},{8,10},{9,11},{10,... | collective-permute-start | bytes 6291464 | tf_op jit(solution)/shard_map/ppermute | solution.py:188
  433.2 40.7 %collective-permute-start.48 = (bf16[1536,256]{1,0:T(8,128)(2,1)S(1)}, bf16[1536,256]{1,0:T(8,128)(2,1)S(1)}, u32[]{:S(2)}, u32[]{:S(2)}) collective-permute-start(bf16[1536,256]{1,0:T(8,128)(2,1)S(1)} %fusion.56), channel_id=1, source_target_pairs={{0,4},{8,0},{16,8},{24,16},{28,24},{20,28},{12,20},{4,12},{1,5},{9... | collective-permute-start | bytes 2359304 | tf_op jit(solution)/shard_map/ppermute | solution.py:72
  434.4 39.5 %collective-permute-start.47 = (bf16[1536,256]{1,0:T(8,128)(2,1)S(1)}, bf16[1536,256]{1,0:T(8,128)(2,1)S(1)}, u32[]{:S(2)}, u32[]{:S(2)}) collective-permute-start(bf16[1536,256]{1,0:T(8,128)(2,1)S(1)} %fusion.55), channel_id=1, source_target_pairs={{0,8},{8,16},{16,24},{24,28},{28,20},{20,12},{12,4},{4,0},{1,9},{9... | collective-permute-start | bytes 2359304 | tf_op jit(solution)/shard_map/ppermute | solution.py:72
  449.2 48.4 %collective-permute-start.53 = (bf16[256,3072]{1,0:T(8,128)(2,1)}, bf16[256,3072]{1,0:T(8,128)(2,1)S(1)}, u32[]{:S(2)}, u32[]{:S(2)}) collective-permute-start(bf16[256,3072]{1,0:T(8,128)(2,1)} %fusion.21), channel_id=1, source_target_pairs={{0,4},{8,0},{16,8},{24,16},{28,24},{20,28},{12,20},{4,12},{1,5},{9... | collective-permute-start | bytes 4718600 | tf_op jit(solution)/shard_map/ppermute | solution.py:72
  453.3 44.7 %collective-permute-start.51 = (bf16[256,3072]{1,0:T(8,128)(2,1)}, bf16[256,3072]{1,0:T(8,128)(2,1)}, u32[]{:S(2)}, u32[]{:S(2)}) collective-permute-start(bf16[256,3072]{1,0:T(8,128)(2,1)} %fusion.20), channel_id=1, source_target_pairs={{0,8},{8,16},{16,24},{24,28},{28,20},{20,12},{12,4},{4,0},{1,9},{9... | collective-permute-start | bytes 4718600 | tf_op jit(solution)/shard_map/ppermute | solution.py:72
  478.8 35.1 %collective-permute-start.55 = (bf16[1536,256]{1,0:T(8,128)(2,1)}, bf16[1536,256]{1,0:T(8,128)(2,1)S(1)}, u32[]{:S(2)}, u32[]{:S(2)}) collective-permute-start(bf16[1536,256]{1,0:T(8,128)(2,1)} %fusion.58), channel_id=1, source_target_pairs={{0,4},{8,0},{16,8},{24,16},{28,24},{20,28},{12,20},{4,12},{1,5},{9... | collective-permute-start | bytes 2359304 | tf_op jit(solution)/shard_map/ppermute | solution.py:72
  481.0 33.0 %collective-permute-start.54 = (bf16[1536,256]{1,0:T(8,128)(2,1)}, bf16[1536,256]{1,0:T(8,128)(2,1)}, u32[]{:S(2)}, u32[]{:S(2)}) collective-permute-start(bf16[1536,256]{1,0:T(8,128)(2,1)} %fusion.57), channel_id=1, source_target_pairs={{0,8},{8,16},{16,24},{24,28},{28,20},{20,12},{12,4},{4,0},{1,9},{9... | collective-permute-start | bytes 2359304 | tf_op jit(solution)/shard_map/ppermute | solution.py:72
  554.1 213.1 %all-reduce.18.cloned.1.call-start = ((), (), s32[]{:S(2)}) async-start(), calls=%async_computation.1 | async-start | bytes 1081344 | tf_op jit(solution)/shard_map/psum | solution.py:875
  554.2 43.5 %collective-permute-start.62 = (bf16[256,3072]{1,0:T(8,128)(2,1)}, bf16[256,3072]{1,0:T(8,128)(2,1)}, u32[]{:S(2)}, u32[]{:S(2)}) collective-permute-start(bf16[256,3072]{1,0:T(8,128)(2,1)} %fusion.23), channel_id=1, source_target_pairs={{0,4},{8,0},{16,8},{24,16},{28,24},{20,28},{12,20},{4,12},{1,5},{9... | collective-permute-start | bytes 4718600 | tf_op jit(solution)/shard_map/ppermute | solution.py:72
  556.9 40.8 %collective-permute-start.61 = (bf16[256,3072]{1,0:T(8,128)(2,1)}, bf16[256,3072]{1,0:T(8,128)(2,1)}, u32[]{:S(2)}, u32[]{:S(2)}) collective-permute-start(bf16[256,3072]{1,0:T(8,128)(2,1)} %fusion.22), channel_id=1, source_target_pairs={{0,8},{8,16},{16,24},{24,28},{28,20},{20,12},{12,4},{4,0},{1,9},{9... | collective-permute-start | bytes 4718600 | tf_op jit(solution)/shard_map/ppermute | solution.py:72
  578.8 45.6 %collective-permute-start.64 = (bf16[1536,256]{1,0:T(8,128)(2,1)}, bf16[1536,256]{1,0:T(8,128)(2,1)}, u32[]{:S(2)}, u32[]{:S(2)}) collective-permute-start(bf16[1536,256]{1,0:T(8,128)(2,1)} %fusion.59), channel_id=1, source_target_pairs={{0,8},{8,16},{16,24},{24,28},{28,20},{20,12},{12,4},{4,0},{1,9},{9... | collective-permute-start | bytes 2359304 | tf_op jit(solution)/shard_map/ppermute | solution.py:72
  603.2 20.3 %collective-permute-start.63 = (bf16[512,2048]{1,0:T(8,128)(2,1)}, bf16[512,2048]{1,0:T(8,128)(2,1)S(1)}, u32[]{:S(2)}, u32[]{:S(2)}) collective-permute-start(bf16[512,2048]{1,0:T(8,128)(2,1)} %fusion.46), channel_id=1, source_target_pairs={{0,1},{1,0},{2,3},{3,2},{4,5},{5,4},{6,7},{7,6},{8,9},{9,8},{10,11... | collective-permute-start | bytes 6291464 | tf_op jit(solution)/shard_map/ppermute | solution.py:183
  612.0 37.2 %collective-permute-start.65 = (bf16[256,3072]{1,0:T(8,128)(2,1)S(1)}, bf16[256,3072]{1,0:T(8,128)(2,1)S(1)}, u32[]{:S(2)}, u32[]{:S(2)}) collective-permute-start(bf16[256,3072]{1,0:T(8,128)(2,1)S(1)} %fusion.24), channel_id=1, source_target_pairs={{0,4},{8,0},{16,8},{24,16},{28,24},{20,28},{12,20},{4,12},{1,5},{9... | collective-permute-start | bytes 4718600 | tf_op jit(solution)/shard_map/ppermute | solution.py:72
  617.8 40.7 %collective-permute-start.79 = (bf16[704,256]{1,0:T(8,128)(2,1)S(1)}, bf16[704,256]{1,0:T(8,128)(2,1)S(1)}, u32[]{:S(2)}, u32[]{:S(2)}) collective-permute-start(bf16[704,256]{1,0:T(8,128)(2,1)S(1)} %copy-done.125), channel_id=1, source_target_pairs={{0,4},{8,0},{16,8},{24,16},{28,24},{20,28},{12,20},{4,12},{1,5},{9... | collective-permute-start | bytes 1081352 | tf_op jit(solution)/shard_map/ppermute | solution.py:72
  659.4 46.1 %collective-permute-start.66 = (bf16[512,2048]{1,0:T(8,128)(2,1)S(1)}, bf16[512,2048]{1,0:T(8,128)(2,1)S(1)}, u32[]{:S(2)}, u32[]{:S(2)}) collective-permute-start(bf16[512,2048]{1,0:T(8,128)(2,1)S(1)} %add_convert_fusion.1), channel_id=1, source_target_pairs={{0,2},{1,3},{2,0},{3,1},{4,6},{5,7},{6,4},{7,5},{8,10},{9,11},{10,... | collective-permute-start | bytes 6291464 | tf_op jit(solution)/shard_map/ppermute | solution.py:188
  671.3 20.7 %collective-permute-start.81 = (bf16[1408,256]{1,0:T(8,128)(2,1)S(1)}, bf16[1408,256]{1,0:T(8,128)(2,1)S(1)}, u32[]{:S(2)}, u32[]{:S(2)}) collective-permute-start(bf16[1408,256]{1,0:T(8,128)(2,1)S(1)} %convolution_convert_fusion.6), channel_id=1, source_target_pairs={{0,4},{8,0},{16,8},{24,16},{28,24},{20,28},{12,20},{4,12},{1,5},{9... | collective-permute-start | bytes 2162696 | tf_op jit(solution)/shard_map/ppermute | solution.py:72
  677.4 20.7 %collective-permute-start.82 = (bf16[704,256]{1,0:T(8,128)(2,1)S(1)}, bf16[704,256]{1,0:T(8,128)(2,1)S(1)}, u32[]{:S(2)}, u32[]{:S(2)}) collective-permute-start(bf16[704,256]{1,0:T(8,128)(2,1)S(1)} %fusion.75), channel_id=1, source_target_pairs={{0,4},{8,0},{16,8},{24,16},{28,24},{20,28},{12,20},{4,12},{1,5},{9... | collective-permute-start | bytes 1081352 | tf_op jit(solution)/shard_map/ppermute | solution.py:72
  679.5 28.7 %collective-permute-start.76 = (bf16[704,256]{1,0:T(8,128)(2,1)S(1)}, bf16[704,256]{1,0:T(8,128)(2,1)S(1)}, u32[]{:S(2)}, u32[]{:S(2)}) collective-permute-start(bf16[704,256]{1,0:T(8,128)(2,1)S(1)} %fusion.73), channel_id=1, source_target_pairs={{0,8},{8,16},{16,24},{24,28},{28,20},{20,12},{12,4},{4,0},{1,9},{9... | collective-permute-start | bytes 1081352 | tf_op jit(solution)/shard_map/ppermute | solution.py:72
  680.2 26.9 %collective-permute-start.75 = (bf16[1408,256]{1,0:T(8,128)(2,1)S(1)}, bf16[1408,256]{1,0:T(8,128)(2,1)S(1)}, u32[]{:S(2)}, u32[]{:S(2)}) collective-permute-start(bf16[1408,256]{1,0:T(8,128)(2,1)S(1)} %convolution_convert_fusion.7), channel_id=1, source_target_pairs={{0,8},{8,16},{16,24},{24,28},{28,20},{20,12},{12,4},{4,0},{1,9},{9... | collective-permute-start | bytes 2162696 | tf_op jit(solution)/shard_map/ppermute | solution.py:72
  698.1 19.0 %collective-permute-start.83 = (bf16[1408,256]{1,0:T(8,128)(2,1)}, bf16[1408,256]{1,0:T(8,128)(2,1)}, u32[]{:S(2)}, u32[]{:S(2)}) collective-permute-start(bf16[1408,256]{1,0:T(8,128)(2,1)} %fusion.64), channel_id=1, source_target_pairs={{0,4},{8,0},{16,8},{24,16},{28,24},{20,28},{12,20},{4,12},{1,5},{9... | collective-permute-start | bytes 2162696 | tf_op jit(solution)/shard_map/ppermute | solution.py:72
  708.2 41.2 %collective-permute-start.77 = (bf16[1408,256]{1,0:T(8,128)(2,1)S(1)}, bf16[1408,256]{1,0:T(8,128)(2,1)}, u32[]{:S(2)}, u32[]{:S(2)}) collective-permute-start(bf16[1408,256]{1,0:T(8,128)(2,1)S(1)} %fusion.61), channel_id=1, source_target_pairs={{0,8},{8,16},{16,24},{24,28},{28,20},{20,12},{12,4},{4,0},{1,9},{9... | collective-permute-start | bytes 2162696 | tf_op jit(solution)/shard_map/ppermute | solution.py:72
  710.4 18.6 %collective-permute-start.69 = (f32[2,8,256]{2,0,1:T(2,128)S(1)}, f32[2,8,256]{2,0,1:T(2,128)S(1)}, u32[]{:S(2)}, u32[]{:S(2)}) collective-permute-start(f32[2,8,256]{2,0,1:T(2,128)S(1)} %bitcast.243), channel_id=1, source_target_pairs={{0,4},{4,0},{8,12},{12,8},{16,20},{20,16},{24,28},{28,24},{1,5},{5... | collective-permute-start | bytes 49160 | tf_op jit(solution)/shard_map/ppermute | solution.py:557
  720.9 61.7 %collective-permute-start.67 = (bf16[512,2048]{1,0:T(8,128)(2,1)S(1)}, bf16[512,2048]{1,0:T(8,128)(2,1)}, u32[]{:S(2)}, u32[]{:S(2)}) collective-permute-start(bf16[512,2048]{1,0:T(8,128)(2,1)S(1)} %get-tuple-element.371), channel_id=1, source_target_pairs={{0,1},{1,0},{2,3},{3,2},{4,5},{5,4},{6,7},{7,6},{8,9},{9,8},{10,11... | collective-permute-start | bytes 6291464 | tf_op jit(solution)/shard_map/ppermute | solution.py:183
  720.9 33.5 %collective-permute-start.84 = (bf16[1408,256]{1,0:T(8,128)(2,1)}, bf16[1408,256]{1,0:T(8,128)(2,1)}, u32[]{:S(2)}, u32[]{:S(2)}) collective-permute-start(bf16[1408,256]{1,0:T(8,128)(2,1)} %fusion.63), channel_id=1, source_target_pairs={{0,4},{8,0},{16,8},{24,16},{28,24},{20,28},{12,20},{4,12},{1,5},{9... | collective-permute-start | bytes 2162696 | tf_op jit(solution)/shard_map/ppermute | solution.py:72
  729.0 20.2 %collective-permute-start.70 = (f32[2,8,256]{2,0,1:T(2,128)S(1)}, f32[2,8,256]{2,0,1:T(2,128)S(1)}, u32[]{:S(2)}, u32[]{:S(2)}) collective-permute-start(f32[2,8,256]{2,0,1:T(2,128)S(1)} %bitcast_add_fusion), channel_id=1, source_target_pairs={{0,8},{4,12},{8,0},{12,4},{16,24},{20,28},{24,16},{28,20},{1,9},{5... | collective-permute-start | bytes 49160 | tf_op jit(solution)/shard_map/ppermute | solution.py:557
  752.4 26.0 %collective-permute-start.78 = (bf16[1408,256]{1,0:T(8,128)(2,1)}, bf16[1408,256]{1,0:T(8,128)(2,1)}, u32[]{:S(2)}, u32[]{:S(2)}) collective-permute-start(bf16[1408,256]{1,0:T(8,128)(2,1)} %fusion.60), channel_id=1, source_target_pairs={{0,8},{8,16},{16,24},{24,28},{28,20},{20,12},{12,4},{4,0},{1,9},{9... | collective-permute-start | bytes 2162696 | tf_op jit(solution)/shard_map/ppermute | solution.py:72
  757.4 21.0 %collective-permute-start.85 = (bf16[1408,256]{1,0:T(8,128)(2,1)}, bf16[1408,256]{1,0:T(8,128)(2,1)}, u32[]{:S(2)}, u32[]{:S(2)}) collective-permute-start(bf16[1408,256]{1,0:T(8,128)(2,1)} %fusion.62), channel_id=1, source_target_pairs={{0,4},{8,0},{16,8},{24,16},{28,24},{20,28},{12,20},{4,12},{1,5},{9... | collective-permute-start | bytes 2162696 | tf_op jit(solution)/shard_map/ppermute | solution.py:72
  (163 other events, 2289.1 us)
Sparse Core Ops, SparseCore 0:
  554.2 89.5 all-reduce.15
  648.2 76.5 all-reduce.17

commit v9 on v7

--- a/solution.py
+++ b/solution.py
@@ -627,7 +627,7 @@
     mlp = [Gather(mlp_weight[:, 0], 1, n, chunk), Gather(mlp_weight[:, 1], -1, n, chunk)]
     downs = Gather(down_weight, 1, n, chunk)
     ring.add([first, second])
-    ring.add([*mlp, downs], [0, 0, 2])
+    ring.add([*mlp, downs], [0, 0, 3])
     ring.issue()
 
     tokens, cotangent = ring.land((tokens, cotangent))

time: 796 us -> 790 us (level)
  waiting for transfers between devices: 194 us -> 184 us
    ppermute x70, waiting for transfers between devices: 139 us -> 130 us  [issue(): flying.append((flow, lax.ppermute(message, 'seq', self.pairs[way])))]
    unnamed x343 -> x333, local copies, waits for them, and re-layouts: 62.7 us -> 65.7 us
  transfers between devices with their start and end apart: 95 -> 95, of which waited for: 30 -> 27; matrix products, arithmetic and copies ran while one was open for 38% -> 39% of each run, Pallas kernels for 13% -> 13%
where the time goes in v9:
time: 790 us; the launch traced here: 780 us
  matrix products  191 us (24%)
  waiting for transfers between devices  184 us (23%)
  starting transfers between devices  119 us (15%)
  local copies, waits for them, and re-layouts  112 us (14%)
  Pallas kernels  111 us (14%)
  other arithmetic  46.6 us (6%)
  between operations  16.8 us (2%)
    ppermute x70, waiting for transfers between devices, issue(): flying.append((flow, lax.ppermute(message, 'seq', self.pairs[way])))  130 us
    dot_general x42, matrix products, down(): lax.dot_general(a, b, (((0,), (0,)), ((), ())), preferred_element_type=f32)  102 us
    ppermute x70, starting transfers between devices, issue(): flying.append((flow, lax.ppermute(message, 'seq', self.pairs[way])))  82.2 us
    unnamed x333, local copies, waits for them, and re-layouts  65.7 us
    pallas_call x8, Pallas kernels, by_rows(): pl.pallas_call(body, grid_spec=pltpu.PrefetchScalarGridSpec(num_scalar_pr...  55.7 us
    dot_general x19, matrix products, across(): lax.dot_general(a, b, (((1,), (1,)), ((), ())), preferred_element_type=f32)  47.3 us
    pallas_call x3, Pallas kernels, per_sequence(): pl.pallas_call(kernel, grid=(seqs,), in_specs=[spec(a.shape, kind) for a,...  42.8 us
    dot_general x6, matrix products, dot(): return jnp.dot(a, b, preferred_element_type=f32)  42.4 us
  transfers between devices with their start and end apart: 95, of which 27 were waited for; matrix products, arithmetic and copies ran while one was open for 39% of the time, Pallas kernels for 13%

profile of v9, /device:TPU:0, one launch (start us, length us, event | category | flops | bytes accessed | tf_op | source)
XLA Modules:
  0.0 780.0 jit_solution(13857147054608561050)
XLA Ops:
  29.9 3.4 constant_dynamic-update-slice_fusion.25
  35.5 8.5 %shard_map.255 = (bf16[4,256,2048]{2,1,0:T(8,128)(2,1)S(1)}, bf16[4,256,2048]{2,1,0:T(8,128)(2,1)}) custom-call(s32[4]{0:T(128)S(1)} %and_select_fusion.2.refs_0_, s32[8]{0:T(128)S(1)} %gather_fusion, bf16[4,256,2048]{2,1,0:T(8,128)(2,1)} %refs_2_, bf16[4,256,2048]{2,1,0:T(8,128)(2,1)} %refs_3_), custom_call_target="tpu_custom_call" | custom-call | flops 16777216 | bytes 16777216 | tf_op jit(solution)/shard_map/pallas_call | solution.py:419
  66.3 8.2 %collective-permute-done.7 = bf16[1056,256]{1,0:T(8,128)(2,1)S(1)} collective-permute-done((bf16[1056,256]{1,0:T(8,128)(2,1)}, bf16[1056,256]{1,0:T(8,128)(2,1)S(1)}, u32[]{:S(2)}, u32[]{:S(2)}) %collective-permute-start.7) | collective-permute-done | bytes 540704 | tf_op jit(solution)/shard_map/ppermute | solution.py:72
  77.0 9.6 %collective-permute-done.9 = bf16[1072,256]{1,0:T(8,128)(2,1)S(1)} collective-permute-done((bf16[1072,256]{1,0:T(8,128)(2,1)S(1)}, bf16[1072,256]{1,0:T(8,128)(2,1)S(1)}, u32[]{:S(2)}, u32[]{:S(2)}) %collective-permute-start.9) | collective-permute-done | bytes 548896 | tf_op jit(solution)/shard_map/ppermute | solution.py:72
  89.7 8.2 %collective-permute-done.13 = bf16[1056,256]{1,0:T(8,128)(2,1)S(1)} collective-permute-done((bf16[1056,256]{1,0:T(8,128)(2,1)S(1)}, bf16[1056,256]{1,0:T(8,128)(2,1)S(1)}, u32[]{:S(2)}, u32[]{:S(2)}) %collective-permute-start.13) | collective-permute-done | bytes 540704 | tf_op jit(solution)/shard_map/ppermute | solution.py:72
  113.8 3.4 add_convert_fusion.7
  120.9 3.3 add_convert_fusion.6
  130.3 3.6 collective-permute-start.16
  135.6 13.3 %collective-permute-done.16 = bf16[4,3,704]{2,1,0:T(4,128)(2,1)S(1)} collective-permute-done((bf16[4,3,704]{2,1,0:T(4,128)(2,1)S(1)}, bf16[4,3,704]{2,1,0:T(4,128)(2,1)S(1)}, u32[]{:S(2)}, u32[]{:S(2)}) %collective-permute-start.16) | collective-permute-done | bytes 16928 | tf_op jit(solution)/shard_map/ppermute | solution.py:661
  148.9 3.3 collective-permute-start.22
  155.2 16.0 %shard_map.256 = (f32[4,256,704]{2,1,0:T(8,128)}, f32[4,256,704]{2,1,0:T(8,128)}, f32[4,256,704]{2,1,0:T(8,128)}, f32[4,256,704]{2,1,0:T(8,128)}, f32[4,256,704]...) custom-call(bf16[4,256,704]{2,1,0:T(8,128)(2,1)S(1)} %bitcast.194, ...), custom_call_target="tpu_custom_call" | custom-call | flops 2030043136 | bytes 23812096 | tf_op jit(solution)/shard_map/pallas_call | solution.py:382
  171.3 3.2 collective-permute-start.21
  176.9 5.3 collective-permute-start.24
  182.3 7.6 collective-permute-done.24
  189.9 5.3 collective-permute-start.25
  195.3 5.0 collective-permute-start.26
  204.5 6.0 fusion.36
  212.4 3.3 convolution_convert_fusion.4
  227.0 3.4 convolution_convert_fusion.5
  231.4 13.9 %collective-permute-done.30 = bf16[256,1536]{1,0:T(8,128)(2,1)S(1)} collective-permute-done((bf16[256,1536]{1,0:T(8,128)(2,1)S(1)}, bf16[256,1536]{1,0:T(8,128)(2,1)S(1)}, u32[]{:S(2)}, u32[]{:S(2)}) %collective-permute-start.30) | collective-permute-done | bytes 786464 | tf_op jit(solution)/shard_map/ppermute | solution.py:72
  255.1 6.8 collective-permute-done.34
  264.4 5.6 collective-permute-done.38
  272.1 9.2 %collective-permute-done.35 = bf16[1536,256]{1,0:T(8,128)(2,1)S(1)} collective-permute-done((bf16[1536,256]{1,0:T(8,128)(2,1)S(1)}, bf16[1536,256]{1,0:T(8,128)(2,1)S(1)}, u32[]{:S(2)}, u32[]{:S(2)}) %collective-permute-start.35) | collective-permute-done | bytes 786464 | tf_op jit(solution)/shard_map/ppermute | solution.py:72
  284.3 8.3 %collective-permute-done.32 = bf16[512,2048]{1,0:T(8,128)(2,1)S(1)} collective-permute-done((bf16[512,2048]{1,0:T(8,128)(2,1)S(1)}, bf16[512,2048]{1,0:T(8,128)(2,1)S(1)}, u32[]{:S(2)}, u32[]{:S(2)}) %collective-permute-start.32) | collective-permute-done | bytes 2097184 | tf_op jit(solution)/shard_map/ppermute | solution.py:188
  293.5 11.5 %collective-permute-done.40 = bf16[256,1536]{1,0:T(8,128)(2,1)S(1)} collective-permute-done((bf16[256,1536]{1,0:T(8,128)(2,1)S(1)}, bf16[256,1536]{1,0:T(8,128)(2,1)S(1)}, u32[]{:S(2)}, u32[]{:S(2)}) %collective-permute-start.40) | collective-permute-done | bytes 786464 | tf_op jit(solution)/shard_map/ppermute | solution.py:72
  316.2 5.0 shard_map.257
  321.2 5.1 shard_map.258
  328.7 17.5 %convolution_convert_fusion = bf16[1024,3072]{1,0:T(8,128)(2,1)S(1)} fusion(bf16[1024,2048]{1,0:T(8,128)(2,1)} %bitcast.220, bf16[2048,1536]{1,0:T(8,128)(2,1)} %copy-done.110, bf16[2048,1536]{1,0:T(8,128)(2,1)} %copy-done.109), kind=kOutput, calls=%fused_computation.40 | convolution fusion | flops 12913213440 | bytes 23068672 | tf_op jit(solution)/shard_map/dot_general | solution.py:580
  346.3 6.4 fusion.6
  368.9 12.4 %shard_map.259 = bf16[1024,3072]{1,0:T(8,128)(2,1)} custom-call(bf16[1024,2048]{1,0:T(8,128)(2,1)} %bitcast.231, bf16[1536,2048]{1,0:T(8,128)(2,1)} %constant_dynamic-update-slice_fusion.26.w_down, bf16[1024,1536]{1,0:T(8,128)(2,1)S(1)} %get-tuple-element.270.act, bf16[1024,1536]{1,0:T(8,128)(2,1)} %get-tuple-element.271.slope), custom_call_target="tpu_custom_call" | custom-call | flops 6442450944 | bytes 23068672 | tf_op jit(solution)/shard_map/pallas_call | solution.py:740
  381.3 11.9 %fusion.50 = bf16[512,2048]{1,0:T(8,128)(2,1)} fusion(bf16[2048,1536]{1,0:T(8,128)(2,1)} %copy-done.110, bf16[2048,1536]{1,0:T(8,128)(2,1)} %copy-done.109, bf16[1024,3072]{1,0:T(8,128)(2,1)} %shard_map.259), kind=kOutput, calls=%fused_computation.101 | convolution fusion | flops 6468665344 | bytes 17825792 | tf_op jit(solution)/shard_map/dot_general | solution.py:572
  393.2 4.1 convolution_convert_fusion.1
  397.9 4.1 convolution_convert_fusion.2
  403.6 10.8 %fusion.47 = bf16[512,2048]{1,0:T(8,128)(2,1)} fusion(bf16[2048,1536]{1,0:T(8,128)(2,1)} %copy-done.110, bf16[2048,1536]{1,0:T(8,128)(2,1)} %copy-done.109, bf16[1024,3072]{1,0:T(8,128)(2,1)S(1)} %copy-done.27), kind=kOutput, calls=%fused_computation.100 | convolution fusion | flops 6468665344 | bytes 17825792 | tf_op jit(solution)/shard_map/dot_general | solution.py:572
  417.3 4.7 fusion.33
  428.5 6.3 collective-permute-done.52
  434.8 4.7 fusion.21
  440.1 4.7 fusion.20
  446.4 17.9 %collective-permute-done.46 = bf16[512,2048]{1,0:T(8,128)(2,1)S(1)} collective-permute-done((bf16[512,2048]{1,0:T(8,128)(2,1)S(1)}, bf16[512,2048]{1,0:T(8,128)(2,1)S(1)}, u32[]{:S(2)}, u32[]{:S(2)}) %collective-permute-start.46) | collective-permute-done | bytes 2097184 | tf_op jit(solution)/shard_map/ppermute | solution.py:188
  473.9 7.3 shard_map.260
  481.2 7.5 shard_map.261
  490.2 7.8 fusion.86
  498.0 7.9 %shard_map.262 = (f32[4,256,704]{2,1,0:T(8,128)S(1)}, f32[4,256,704]{2,1,0:T(8,128)}, f32[4,8,704]{2,1,0:T(8,128)S(1)}) custom-call(f32[4,256,704]{2,1,0:T(8,128)} %bitcast.240, f32[4,256,704]{2,1,0:T(8,128)} %get-tuple-element.426.act, f32[4,256,704]{2,1,0:T(8,128)} %get-tuple-element.287.decay), custom_call_target="tpu_custom_call" | custom-call | flops 36044800 | bytes 14508032 | tf_op jit(solution)/shard_map/pallas_call | solution.py:382
  511.8 4.2 fusion.23
  517.7 4.7 fusion.22
  522.4 3.4 fusion.58
  527.2 5.0 collective-permute-done.57
  534.8 11.0 %convolution_convert_fusion.3 = bf16[1024,2048]{1,0:T(8,128)(2,1)} fusion(bf16[1024,1536]{1,0:T(8,128)(2,1)S(1)} %copy-done.65, bf16[1536,2048]{1,0:T(8,128)(2,1)} %constant_dynamic-update-slice_fusion.26.w_down), kind=kOutput, calls=%fused_computation.73 | convolution fusion | flops 6444548096 | bytes 13631488 | tf_op jit(solution)/shard_map/dot_general | solution.py:580
  550.2 18.9 %shard_map.263 = (bf16[2,4,256,704]{3,2,1,0:T(8,128)(2,1)}, bf16[4,256,704]{2,1,0:T(8,128)(2,1)S(1)}, bf16[4,256,704]{2,1,0:T(8,128)(2,1)S(1)}, f32[4,8,704]{2,1...) custom-call(f32[4,256,704]{2,1,0:T(8,128)} %bitcast.241, f32[4,256,704]{2,1,0:T(8,128)} %get-tuple-element.425.slope, ...), custom_call_target="tpu_custom_call" | custom-call | flops 2030043136 | bytes 38514432 | tf_op jit(solution)/shard_map/pallas_call | solution.py:382
  591.0 3.6 fusion.46
  596.0 3.5 fusion.24
  603.0 3.6 fusion.45
  606.7 5.1 collective-permute-done.72
  614.7 22.1 %collective-permute-done.65 = bf16[256,3072]{1,0:T(8,128)(2,1)S(1)} collective-permute-done((bf16[256,3072]{1,0:T(8,128)(2,1)S(1)}, bf16[256,3072]{1,0:T(8,128)(2,1)S(1)}, u32[]{:S(2)}, u32[]{:S(2)}) %collective-permute-start.65) | collective-permute-done | bytes 1572896 | tf_op jit(solution)/shard_map/ppermute | solution.py:72
  636.8 3.4 collective-permute-start.73
  645.6 5.8 collective-permute-done.73
  654.6 5.3 fusion.19
  665.5 3.5 fusion.53
  669.0 5.6 reshape.426
  676.8 8.5 %shard_map.264 = bf16[4,256,2048]{2,1,0:T(8,128)(2,1)} custom-call(s32[4]{0:T(128)S(1)} %copy-done.26, s32[8]{0:T(128)S(1)} %copy-done.22, f32[4,256,2048]{2,1,0:T(8,128)} %get-tuple-element.243.refs_0_.refs_2_, bf16[4,256,2048]{2,1,0:T(8,128)(2,1)S(1)} %bitcast.196), custom_call_target="tpu_custom_call" | custom-call | flops 16777216 | bytes 16777216 | tf_op jit(solution)/shard_map/pallas_call | solution.py:419
  694.9 4.0 fusion.18
  721.2 6.7 shard_map.265.refs_6_
  733.2 5.3 collective-permute-done.90
  765.5 7.2 shard_map.266
  (652 shorter events, 301.6 us)
Async XLA Ops:
  7.2 667.4 %all-reduce.16.cloned.1.call-start = ((), (), s32[]{:S(2)}) async-start(), calls=%async_computation | async-start | bytes 8388608 | tf_op jit(solution)/shard_map/psum | solution.py:798
  11.2 22.2 %collective-permute-start = (bf16[1056,256]{1,0:T(8,128)(2,1)}, bf16[1056,256]{1,0:T(8,128)(2,1)S(1)}, u32[]{:S(2)}, u32[]{:S(2)}) collective-permute-start(bf16[1056,256]{1,0:T(8,128)(2,1)} %pad_maximum_fusion.21), channel_id=1, source_target_pairs={{0,8},{8,16},{16,24},{24,28},{28,20},{20,12},{12,4},{4,0},{1,9},{9... | collective-permute-start | bytes 1622024 | tf_op jit(solution)/shard_map/ppermute | solution.py:72
  14.2 19.2 %collective-permute-start.1 = (bf16[1056,256]{1,0:T(8,128)(2,1)}, bf16[1056,256]{1,0:T(8,128)(2,1)}, u32[]{:S(2)}, u32[]{:S(2)}) collective-permute-start(bf16[1056,256]{1,0:T(8,128)(2,1)} %pad_maximum_fusion.21), channel_id=1, source_target_pairs={{0,4},{8,0},{16,8},{24,16},{28,24},{20,28},{12,20},{4,12},{1,5},{9... | collective-permute-start | bytes 1622024 | tf_op jit(solution)/shard_map/ppermute | solution.py:72
  15.1 30.9 %collective-permute-start.2 = (bf16[1072,256]{1,0:T(8,128)(2,1)}, bf16[1072,256]{1,0:T(8,128)(2,1)}, u32[]{:S(2)}, u32[]{:S(2)}) collective-permute-start(bf16[1072,256]{1,0:T(8,128)(2,1)} %pad_maximum_fusion.20), channel_id=1, source_target_pairs={{0,8},{8,16},{16,24},{24,28},{28,20},{20,12},{12,4},{4,0},{1,9},{9... | collective-permute-start | bytes 1646600 | tf_op jit(solution)/shard_map/ppermute | solution.py:72
  17.1 28.9 %collective-permute-start.3 = (bf16[1072,256]{1,0:T(8,128)(2,1)}, bf16[1072,256]{1,0:T(8,128)(2,1)}, u32[]{:S(2)}, u32[]{:S(2)}) collective-permute-start(bf16[1072,256]{1,0:T(8,128)(2,1)} %pad_maximum_fusion.20), channel_id=1, source_target_pairs={{0,4},{8,0},{16,8},{24,16},{28,24},{20,28},{12,20},{4,12},{1,5},{9... | collective-permute-start | bytes 1646600 | tf_op jit(solution)/shard_map/ppermute | solution.py:72
  33.4 23.8 %collective-permute-start.10 = (bf16[1056,256]{1,0:T(8,128)(2,1)}, bf16[1056,256]{1,0:T(8,128)(2,1)S(1)}, u32[]{:S(2)}, u32[]{:S(2)}) collective-permute-start(bf16[1056,256]{1,0:T(8,128)(2,1)} %collective-permute-done.1), channel_id=1, source_target_pairs={{0,4},{8,0},{16,8},{24,16},{28,24},{20,28},{12,20},{4,12},{1,5},{9... | collective-permute-start | bytes 1622024 | tf_op jit(solution)/shard_map/ppermute | solution.py:72
  35.4 23.7 %collective-permute-start.5 = (bf16[1056,256]{1,0:T(8,128)(2,1)S(1)}, bf16[1056,256]{1,0:T(8,128)(2,1)}, u32[]{:S(2)}, u32[]{:S(2)}) collective-permute-start(bf16[1056,256]{1,0:T(8,128)(2,1)S(1)} %collective-permute-done), channel_id=1, source_target_pairs={{0,8},{8,16},{16,24},{24,28},{28,20},{20,12},{12,4},{4,0},{1,9},{9... | collective-permute-start | bytes 1622024 | tf_op jit(solution)/shard_map/ppermute | solution.py:72
  57.2 19.8 %collective-permute-start.11 = (bf16[1056,256]{1,0:T(8,128)(2,1)S(1)}, bf16[1056,256]{1,0:T(8,128)(2,1)S(1)}, u32[]{:S(2)}, u32[]{:S(2)}) collective-permute-start(bf16[1056,256]{1,0:T(8,128)(2,1)S(1)} %collective-permute-done.10), channel_id=1, source_target_pairs={{0,4},{8,0},{16,8},{24,16},{28,24},{20,28},{12,20},{4,12},{1,5},{9... | collective-permute-start | bytes 1622024 | tf_op jit(solution)/shard_map/ppermute | solution.py:72
  62.6 26.0 %collective-permute-start.6 = (bf16[1072,256]{1,0:T(8,128)(2,1)S(1)}, bf16[1072,256]{1,0:T(8,128)(2,1)S(1)}, u32[]{:S(2)}, u32[]{:S(2)}) collective-permute-start(bf16[1072,256]{1,0:T(8,128)(2,1)S(1)} %collective-permute-done.4), channel_id=1, source_target_pairs={{0,8},{8,16},{16,24},{24,28},{28,20},{20,12},{12,4},{4,0},{1,9},{9... | collective-permute-start | bytes 1646600 | tf_op jit(solution)/shard_map/ppermute | solution.py:72
  64.7 21.9 %collective-permute-start.9 = (bf16[1072,256]{1,0:T(8,128)(2,1)S(1)}, bf16[1072,256]{1,0:T(8,128)(2,1)S(1)}, u32[]{:S(2)}, u32[]{:S(2)}) collective-permute-start(bf16[1072,256]{1,0:T(8,128)(2,1)S(1)} %collective-permute-done.8), channel_id=1, source_target_pairs={{0,4},{8,0},{16,8},{24,16},{28,24},{20,28},{12,20},{4,12},{1,5},{9... | collective-permute-start | bytes 1646600 | tf_op jit(solution)/shard_map/ppermute | solution.py:72
  74.5 23.3 %collective-permute-start.13 = (bf16[1056,256]{1,0:T(8,128)(2,1)S(1)}, bf16[1056,256]{1,0:T(8,128)(2,1)S(1)}, u32[]{:S(2)}, u32[]{:S(2)}) collective-permute-start(bf16[1056,256]{1,0:T(8,128)(2,1)S(1)} %collective-permute-done.7), channel_id=1, source_target_pairs={{0,8},{8,16},{16,24},{24,28},{28,20},{20,12},{12,4},{4,0},{1,9},{9... | collective-permute-start | bytes 1622024 | tf_op jit(solution)/shard_map/ppermute | solution.py:72
  86.9 37.3 %collective-permute-start.15 = (bf16[256,1536]{1,0:T(8,128)(2,1)}, bf16[256,1536]{1,0:T(8,128)(2,1)}, u32[]{:S(2)}, u32[]{:S(2)}) collective-permute-start(bf16[256,1536]{1,0:T(8,128)(2,1)} %get-tuple-element.213), channel_id=1, source_target_pairs={{0,4},{8,0},{16,8},{24,16},{28,24},{20,28},{12,20},{4,12},{1,5},{9... | collective-permute-start | bytes 2359304 | tf_op jit(solution)/shard_map/ppermute | solution.py:72
  88.6 35.6 %collective-permute-start.14 = (bf16[256,1536]{1,0:T(8,128)(2,1)}, bf16[256,1536]{1,0:T(8,128)(2,1)}, u32[]{:S(2)}, u32[]{:S(2)}) collective-permute-start(bf16[256,1536]{1,0:T(8,128)(2,1)} %get-tuple-element.213), channel_id=1, source_target_pairs={{0,8},{8,16},{16,24},{24,28},{28,20},{20,12},{12,4},{4,0},{1,9},{9... | collective-permute-start | bytes 2359304 | tf_op jit(solution)/shard_map/ppermute | solution.py:72
  97.8 51.0 %collective-permute-start.17 = (bf16[256,1536]{1,0:T(8,128)(2,1)}, bf16[256,1536]{1,0:T(8,128)(2,1)}, u32[]{:S(2)}, u32[]{:S(2)}) collective-permute-start(bf16[256,1536]{1,0:T(8,128)(2,1)} %get-tuple-element.216), channel_id=1, source_target_pairs={{0,8},{8,16},{16,24},{24,28},{28,20},{20,12},{12,4},{4,0},{1,9},{9... | collective-permute-start | bytes 2359304 | tf_op jit(solution)/shard_map/ppermute | solution.py:72
  109.0 39.9 %collective-permute-start.18 = (bf16[256,1536]{1,0:T(8,128)(2,1)}, bf16[256,1536]{1,0:T(8,128)(2,1)}, u32[]{:S(2)}, u32[]{:S(2)}) collective-permute-start(bf16[256,1536]{1,0:T(8,128)(2,1)} %get-tuple-element.216), channel_id=1, source_target_pairs={{0,4},{8,0},{16,8},{24,16},{28,24},{20,28},{12,20},{4,12},{1,5},{9... | collective-permute-start | bytes 2359304 | tf_op jit(solution)/shard_map/ppermute | solution.py:72
  124.2 47.0 %collective-permute-start.19 = (bf16[256,1536]{1,0:T(8,128)(2,1)}, bf16[256,1536]{1,0:T(8,128)(2,1)}, u32[]{:S(2)}, u32[]{:S(2)}) collective-permute-start(bf16[256,1536]{1,0:T(8,128)(2,1)} %collective-permute-done.14), channel_id=1, source_target_pairs={{0,8},{8,16},{16,24},{24,28},{28,20},{20,12},{12,4},{4,0},{1,9},{9... | collective-permute-start | bytes 2359304 | tf_op jit(solution)/shard_map/ppermute | solution.py:72
  126.0 45.3 %collective-permute-start.20 = (bf16[256,1536]{1,0:T(8,128)(2,1)}, bf16[256,1536]{1,0:T(8,128)(2,1)}, u32[]{:S(2)}, u32[]{:S(2)}) collective-permute-start(bf16[256,1536]{1,0:T(8,128)(2,1)} %collective-permute-done.15), channel_id=1, source_target_pairs={{0,4},{8,0},{16,8},{24,16},{28,24},{20,28},{12,20},{4,12},{1,5},{9... | collective-permute-start | bytes 2359304 | tf_op jit(solution)/shard_map/ppermute | solution.py:72
  130.3 18.6 %collective-permute-start.16 = (bf16[4,3,704]{2,1,0:T(4,128)(2,1)S(1)}, bf16[4,3,704]{2,1,0:T(4,128)(2,1)S(1)}, u32[]{:S(2)}, u32[]{:S(2)}) collective-permute-start(bf16[4,3,704]{2,1,0:T(4,128)(2,1)S(1)} %slice.644), channel_id=1, source_target_pairs={{0,4},{4,8},{8,12},{12,16},{16,20},{20,24},{24,28},{1,5},{5,9},{9,... | collective-permute-start | bytes 50696 | tf_op jit(solution)/shard_map/ppermute | solution.py:661
  148.9 28.0 %collective-permute-start.22 = (bf16[256,1536]{1,0:T(8,128)(2,1)}, bf16[256,1536]{1,0:T(8,128)(2,1)S(1)}, u32[]{:S(2)}, u32[]{:S(2)}) collective-permute-start(bf16[256,1536]{1,0:T(8,128)(2,1)} %collective-permute-done.17), channel_id=1, source_target_pairs={{0,8},{8,16},{16,24},{24,28},{28,20},{20,12},{12,4},{4,0},{1,9},{9... | collective-permute-start | bytes 2359304 | tf_op jit(solution)/shard_map/ppermute | solution.py:72
  152.2 24.7 %collective-permute-start.23 = (bf16[256,1536]{1,0:T(8,128)(2,1)}, bf16[256,1536]{1,0:T(8,128)(2,1)S(1)}, u32[]{:S(2)}, u32[]{:S(2)}) collective-permute-start(bf16[256,1536]{1,0:T(8,128)(2,1)} %collective-permute-done.18), channel_id=1, source_target_pairs={{0,4},{8,0},{16,8},{24,16},{28,24},{20,28},{12,20},{4,12},{1,5},{9... | collective-permute-start | bytes 2359304 | tf_op jit(solution)/shard_map/ppermute | solution.py:72
  174.5 29.2 %collective-permute-start.27 = (bf16[256,1536]{1,0:T(8,128)(2,1)}, bf16[256,1536]{1,0:T(8,128)(2,1)}, u32[]{:S(2)}, u32[]{:S(2)}) collective-permute-start(bf16[256,1536]{1,0:T(8,128)(2,1)} %collective-permute-done.19), channel_id=1, source_target_pairs={{0,8},{8,16},{16,24},{24,28},{28,20},{20,12},{12,4},{4,0},{1,9},{9... | collective-permute-start | bytes 2359304 | tf_op jit(solution)/shard_map/ppermute | solution.py:72
  175.3 28.4 %collective-permute-start.28 = (bf16[256,1536]{1,0:T(8,128)(2,1)}, bf16[256,1536]{1,0:T(8,128)(2,1)S(1)}, u32[]{:S(2)}, u32[]{:S(2)}) collective-permute-start(bf16[256,1536]{1,0:T(8,128)(2,1)} %collective-permute-done.20), channel_id=1, source_target_pairs={{0,4},{8,0},{16,8},{24,16},{28,24},{20,28},{12,20},{4,12},{1,5},{9... | collective-permute-start | bytes 2359304 | tf_op jit(solution)/shard_map/ppermute | solution.py:72
  223.9 21.4 %collective-permute-start.30 = (bf16[256,1536]{1,0:T(8,128)(2,1)S(1)}, bf16[256,1536]{1,0:T(8,128)(2,1)S(1)}, u32[]{:S(2)}, u32[]{:S(2)}) collective-permute-start(bf16[256,1536]{1,0:T(8,128)(2,1)S(1)} %copy-done.101), channel_id=1, source_target_pairs={{0,8},{8,16},{16,24},{24,28},{28,20},{20,12},{12,4},{4,0},{1,9},{9... | collective-permute-start | bytes 2359304 | tf_op jit(solution)/shard_map/ppermute | solution.py:72
  224.8 20.5 %collective-permute-start.31 = (bf16[256,1536]{1,0:T(8,128)(2,1)S(1)}, bf16[256,1536]{1,0:T(8,128)(2,1)S(1)}, u32[]{:S(2)}, u32[]{:S(2)}) collective-permute-start(bf16[256,1536]{1,0:T(8,128)(2,1)S(1)} %copy-done.97), channel_id=1, source_target_pairs={{0,4},{8,0},{16,8},{24,16},{28,24},{20,28},{12,20},{4,12},{1,5},{9... | collective-permute-start | bytes 2359304 | tf_op jit(solution)/shard_map/ppermute | solution.py:72
  230.4 31.6 %collective-permute-start.34 = (bf16[1536,256]{1,0:T(8,128)(2,1)S(1)}, bf16[1536,256]{1,0:T(8,128)(2,1)S(1)}, u32[]{:S(2)}, u32[]{:S(2)}) collective-permute-start(bf16[1536,256]{1,0:T(8,128)(2,1)S(1)} %copy-done.95), channel_id=1, source_target_pairs={{0,8},{8,16},{16,24},{24,28},{28,20},{20,12},{12,4},{4,0},{1,9},{9... | collective-permute-start | bytes 2359304 | tf_op jit(solution)/shard_map/ppermute | solution.py:72
  245.3 47.3 %collective-permute-start.32 = (bf16[512,2048]{1,0:T(8,128)(2,1)S(1)}, bf16[512,2048]{1,0:T(8,128)(2,1)S(1)}, u32[]{:S(2)}, u32[]{:S(2)}) collective-permute-start(bf16[512,2048]{1,0:T(8,128)(2,1)S(1)} %add_convert_fusion.5), channel_id=1, source_target_pairs={{0,2},{1,3},{2,0},{3,1},{4,6},{5,7},{6,4},{7,5},{8,10},{9,11},{10,... | collective-permute-start | bytes 6291464 | tf_op jit(solution)/shard_map/ppermute | solution.py:188
  250.6 19.4 %collective-permute-start.38 = (bf16[1536,256]{1,0:T(8,128)(2,1)S(1)}, bf16[1536,256]{1,0:T(8,128)(2,1)S(1)}, u32[]{:S(2)}, u32[]{:S(2)}) collective-permute-start(bf16[1536,256]{1,0:T(8,128)(2,1)S(1)} %copy-done.95), channel_id=1, source_target_pairs={{0,4},{8,0},{16,8},{24,16},{28,24},{20,28},{12,20},{4,12},{1,5},{9... | collective-permute-start | bytes 2359304 | tf_op jit(solution)/shard_map/ppermute | solution.py:72
  262.0 19.4 %collective-permute-start.35 = (bf16[1536,256]{1,0:T(8,128)(2,1)S(1)}, bf16[1536,256]{1,0:T(8,128)(2,1)S(1)}, u32[]{:S(2)}, u32[]{:S(2)}) collective-permute-start(bf16[1536,256]{1,0:T(8,128)(2,1)S(1)} %collective-permute-done.34), channel_id=1, source_target_pairs={{0,8},{8,16},{16,24},{24,28},{28,20},{20,12},{12,4},{4,0},{1,9},{9... | collective-permute-start | bytes 2359304 | tf_op jit(solution)/shard_map/ppermute | solution.py:72
  270.0 23.6 %collective-permute-start.39 = (bf16[1536,256]{1,0:T(8,128)(2,1)S(1)}, bf16[1536,256]{1,0:T(8,128)(2,1)S(1)}, u32[]{:S(2)}, u32[]{:S(2)}) collective-permute-start(bf16[1536,256]{1,0:T(8,128)(2,1)S(1)} %collective-permute-done.38), channel_id=1, source_target_pairs={{0,4},{8,0},{16,8},{24,16},{28,24},{20,28},{12,20},{4,12},{1,5},{9... | collective-permute-start | bytes 2359304 | tf_op jit(solution)/shard_map/ppermute | solution.py:72
  282.3 22.8 %collective-permute-start.40 = (bf16[256,1536]{1,0:T(8,128)(2,1)S(1)}, bf16[256,1536]{1,0:T(8,128)(2,1)S(1)}, u32[]{:S(2)}, u32[]{:S(2)}) collective-permute-start(bf16[256,1536]{1,0:T(8,128)(2,1)S(1)} %collective-permute-done.31), channel_id=1, source_target_pairs={{0,4},{8,0},{16,8},{24,16},{28,24},{20,28},{12,20},{4,12},{1,5},{9... | collective-permute-start | bytes 2359304 | tf_op jit(solution)/shard_map/ppermute | solution.py:72
  283.8 21.8 %collective-permute-start.36 = (bf16[256,1536]{1,0:T(8,128)(2,1)}, bf16[256,1536]{1,0:T(8,128)(2,1)S(1)}, u32[]{:S(2)}, u32[]{:S(2)}) collective-permute-start(bf16[256,1536]{1,0:T(8,128)(2,1)} %collective-permute-done.27), channel_id=1, source_target_pairs={{0,8},{8,16},{16,24},{24,28},{28,20},{20,12},{12,4},{4,0},{1,9},{9... | collective-permute-start | bytes 2359304 | tf_op jit(solution)/shard_map/ppermute | solution.py:72
  293.4 27.8 %collective-permute-start.33 = (bf16[512,2048]{1,0:T(8,128)(2,1)S(1)}, bf16[512,2048]{1,0:T(8,128)(2,1)S(1)}, u32[]{:S(2)}, u32[]{:S(2)}) collective-permute-start(bf16[512,2048]{1,0:T(8,128)(2,1)S(1)} %add_convert_fusion.4), channel_id=1, source_target_pairs={{0,1},{1,0},{2,3},{3,2},{4,5},{5,4},{6,7},{7,6},{8,9},{9,8},{10,11... | collective-permute-start | bytes 6291464 | tf_op jit(solution)/shard_map/ppermute | solution.py:183
  305.1 21.2 %collective-permute-start.41 = (bf16[1536,256]{1,0:T(8,128)(2,1)S(1)}, bf16[1536,256]{1,0:T(8,128)(2,1)S(1)}, u32[]{:S(2)}, u32[]{:S(2)}) collective-permute-start(bf16[1536,256]{1,0:T(8,128)(2,1)S(1)} %collective-permute-done.39), channel_id=1, source_target_pairs={{0,4},{8,0},{16,8},{24,16},{28,24},{20,28},{12,20},{4,12},{1,5},{9... | collective-permute-start | bytes 2359304 | tf_op jit(solution)/shard_map/ppermute | solution.py:72
  305.6 20.6 %collective-permute-start.37 = (bf16[1536,256]{1,0:T(8,128)(2,1)S(1)}, bf16[1536,256]{1,0:T(8,128)(2,1)}, u32[]{:S(2)}, u32[]{:S(2)}) collective-permute-start(bf16[1536,256]{1,0:T(8,128)(2,1)S(1)} %collective-permute-done.35), channel_id=1, source_target_pairs={{0,8},{8,16},{16,24},{24,28},{28,20},{20,12},{12,4},{4,0},{1,9},{9... | collective-permute-start | bytes 2359304 | tf_op jit(solution)/shard_map/ppermute | solution.py:72
  327.1 28.2 %collective-permute-start.42 = (bf16[1536,256]{1,0:T(8,128)(2,1)}, bf16[1536,256]{1,0:T(8,128)(2,1)}, u32[]{:S(2)}, u32[]{:S(2)}) collective-permute-start(bf16[1536,256]{1,0:T(8,128)(2,1)} %collective-permute-done.37), channel_id=1, source_target_pairs={{0,8},{8,16},{16,24},{24,28},{28,20},{20,12},{12,4},{4,0},{1,9},{9... | collective-permute-start | bytes 2359304 | tf_op jit(solution)/shard_map/ppermute | solution.py:72
  361.4 31.8 %collective-permute-start.44 = (bf16[1536,256]{1,0:T(8,128)(2,1)}, bf16[1536,256]{1,0:T(8,128)(2,1)}, u32[]{:S(2)}, u32[]{:S(2)}) collective-permute-start(bf16[1536,256]{1,0:T(8,128)(2,1)} %convolution_convert_fusion.6), channel_id=1, source_target_pairs={{0,4},{8,0},{16,8},{24,16},{28,24},{20,28},{12,20},{4,12},{1,5},{9... | collective-permute-start | bytes 2359304 | tf_op jit(solution)/shard_map/ppermute | solution.py:72
  362.0 31.2 %collective-permute-start.43 = (bf16[1536,256]{1,0:T(8,128)(2,1)}, bf16[1536,256]{1,0:T(8,128)(2,1)}, u32[]{:S(2)}, u32[]{:S(2)}) collective-permute-start(bf16[1536,256]{1,0:T(8,128)(2,1)} %convolution_convert_fusion.7), channel_id=1, source_target_pairs={{0,8},{8,16},{16,24},{24,28},{28,20},{20,12},{12,4},{4,0},{1,9},{9... | collective-permute-start | bytes 2359304 | tf_op jit(solution)/shard_map/ppermute | solution.py:72
  393.1 21.2 %collective-permute-start.45 = (bf16[512,2048]{1,0:T(8,128)(2,1)}, bf16[512,2048]{1,0:T(8,128)(2,1)S(1)}, u32[]{:S(2)}, u32[]{:S(2)}) collective-permute-start(bf16[512,2048]{1,0:T(8,128)(2,1)} %fusion.50), channel_id=1, source_target_pairs={{0,1},{1,0},{2,3},{3,2},{4,5},{5,4},{6,7},{7,6},{8,9},{9,8},{10,11... | collective-permute-start | bytes 6291464 | tf_op jit(solution)/shard_map/ppermute | solution.py:183
  397.3 37.5 %collective-permute-start.52 = (bf16[256,3072]{1,0:T(8,128)(2,1)}, bf16[256,3072]{1,0:T(8,128)(2,1)}, u32[]{:S(2)}, u32[]{:S(2)}) collective-permute-start(bf16[256,3072]{1,0:T(8,128)(2,1)} %convolution_convert_fusion.1), channel_id=1, source_target_pairs={{0,4},{8,0},{16,8},{24,16},{28,24},{20,28},{12,20},{4,12},{1,5},{9... | collective-permute-start | bytes 4718600 | tf_op jit(solution)/shard_map/ppermute | solution.py:72
  402.0 38.1 %collective-permute-start.50 = (bf16[256,3072]{1,0:T(8,128)(2,1)}, bf16[256,3072]{1,0:T(8,128)(2,1)}, u32[]{:S(2)}, u32[]{:S(2)}) collective-permute-start(bf16[256,3072]{1,0:T(8,128)(2,1)} %convolution_convert_fusion.2), channel_id=1, source_target_pairs={{0,8},{8,16},{16,24},{24,28},{28,20},{20,12},{12,4},{4,0},{1,9},{9... | collective-permute-start | bytes 4718600 | tf_op jit(solution)/shard_map/ppermute | solution.py:72
  416.7 47.5 %collective-permute-start.46 = (bf16[512,2048]{1,0:T(8,128)(2,1)S(1)}, bf16[512,2048]{1,0:T(8,128)(2,1)S(1)}, u32[]{:S(2)}, u32[]{:S(2)}) collective-permute-start(bf16[512,2048]{1,0:T(8,128)(2,1)S(1)} %add_convert_fusion.3), channel_id=1, source_target_pairs={{0,2},{1,3},{2,0},{3,1},{4,6},{5,7},{6,4},{7,5},{8,10},{9,11},{10,... | collective-permute-start | bytes 6291464 | tf_op jit(solution)/shard_map/ppermute | solution.py:188
  424.2 40.9 %collective-permute-start.48 = (bf16[1536,256]{1,0:T(8,128)(2,1)S(1)}, bf16[1536,256]{1,0:T(8,128)(2,1)S(1)}, u32[]{:S(2)}, u32[]{:S(2)}) collective-permute-start(bf16[1536,256]{1,0:T(8,128)(2,1)S(1)} %fusion.55), channel_id=1, source_target_pairs={{0,4},{8,0},{16,8},{24,16},{28,24},{20,28},{12,20},{4,12},{1,5},{9... | collective-permute-start | bytes 2359304 | tf_op jit(solution)/shard_map/ppermute | solution.py:72
  427.0 38.1 %collective-permute-start.47 = (bf16[1536,256]{1,0:T(8,128)(2,1)S(1)}, bf16[1536,256]{1,0:T(8,128)(2,1)S(1)}, u32[]{:S(2)}, u32[]{:S(2)}) collective-permute-start(bf16[1536,256]{1,0:T(8,128)(2,1)S(1)} %fusion.54), channel_id=1, source_target_pairs={{0,8},{8,16},{16,24},{24,28},{28,20},{20,12},{12,4},{4,0},{1,9},{9... | collective-permute-start | bytes 2359304 | tf_op jit(solution)/shard_map/ppermute | solution.py:72
  439.5 49.2 %collective-permute-start.53 = (bf16[256,3072]{1,0:T(8,128)(2,1)}, bf16[256,3072]{1,0:T(8,128)(2,1)S(1)}, u32[]{:S(2)}, u32[]{:S(2)}) collective-permute-start(bf16[256,3072]{1,0:T(8,128)(2,1)} %fusion.21), channel_id=1, source_target_pairs={{0,4},{8,0},{16,8},{24,16},{28,24},{20,28},{12,20},{4,12},{1,5},{9... | collective-permute-start | bytes 4718600 | tf_op jit(solution)/shard_map/ppermute | solution.py:72
  444.8 45.5 %collective-permute-start.51 = (bf16[256,3072]{1,0:T(8,128)(2,1)}, bf16[256,3072]{1,0:T(8,128)(2,1)}, u32[]{:S(2)}, u32[]{:S(2)}) collective-permute-start(bf16[256,3072]{1,0:T(8,128)(2,1)} %fusion.20), channel_id=1, source_target_pairs={{0,8},{8,16},{16,24},{24,28},{28,20},{20,12},{12,4},{4,0},{1,9},{9... | collective-permute-start | bytes 4718600 | tf_op jit(solution)/shard_map/ppermute | solution.py:72
  469.9 36.0 %collective-permute-start.55 = (bf16[1536,256]{1,0:T(8,128)(2,1)}, bf16[1536,256]{1,0:T(8,128)(2,1)S(1)}, u32[]{:S(2)}, u32[]{:S(2)}) collective-permute-start(bf16[1536,256]{1,0:T(8,128)(2,1)} %fusion.57), channel_id=1, source_target_pairs={{0,4},{8,0},{16,8},{24,16},{28,24},{20,28},{12,20},{4,12},{1,5},{9... | collective-permute-start | bytes 2359304 | tf_op jit(solution)/shard_map/ppermute | solution.py:72
  472.5 33.9 %collective-permute-start.54 = (bf16[1536,256]{1,0:T(8,128)(2,1)}, bf16[1536,256]{1,0:T(8,128)(2,1)}, u32[]{:S(2)}, u32[]{:S(2)}) collective-permute-start(bf16[1536,256]{1,0:T(8,128)(2,1)} %fusion.56), channel_id=1, source_target_pairs={{0,8},{8,16},{16,24},{24,28},{28,20},{20,12},{12,4},{4,0},{1,9},{9... | collective-permute-start | bytes 2359304 | tf_op jit(solution)/shard_map/ppermute | solution.py:72
  545.8 182.1 %all-reduce.18.cloned.1.call-start = ((), (), s32[]{:S(2)}) async-start(), calls=%async_computation.1 | async-start | bytes 1081344 | tf_op jit(solution)/shard_map/psum | solution.py:876
  546.0 43.5 %collective-permute-start.62 = (bf16[256,3072]{1,0:T(8,128)(2,1)}, bf16[256,3072]{1,0:T(8,128)(2,1)}, u32[]{:S(2)}, u32[]{:S(2)}) collective-permute-start(bf16[256,3072]{1,0:T(8,128)(2,1)} %fusion.23), channel_id=1, source_target_pairs={{0,4},{8,0},{16,8},{24,16},{28,24},{20,28},{12,20},{4,12},{1,5},{9... | collective-permute-start | bytes 4718600 | tf_op jit(solution)/shard_map/ppermute | solution.py:72
  548.7 40.8 %collective-permute-start.61 = (bf16[256,3072]{1,0:T(8,128)(2,1)}, bf16[256,3072]{1,0:T(8,128)(2,1)}, u32[]{:S(2)}, u32[]{:S(2)}) collective-permute-start(bf16[256,3072]{1,0:T(8,128)(2,1)} %fusion.22), channel_id=1, source_target_pairs={{0,8},{8,16},{16,24},{24,28},{28,20},{20,12},{12,4},{4,0},{1,9},{9... | collective-permute-start | bytes 4718600 | tf_op jit(solution)/shard_map/ppermute | solution.py:72
  571.1 43.5 %collective-permute-start.64 = (bf16[1536,256]{1,0:T(8,128)(2,1)}, bf16[1536,256]{1,0:T(8,128)(2,1)}, u32[]{:S(2)}, u32[]{:S(2)}) collective-permute-start(bf16[1536,256]{1,0:T(8,128)(2,1)} %fusion.58), channel_id=1, source_target_pairs={{0,8},{8,16},{16,24},{24,28},{28,20},{20,12},{12,4},{4,0},{1,9},{9... | collective-permute-start | bytes 2359304 | tf_op jit(solution)/shard_map/ppermute | solution.py:72
  594.6 17.9 %collective-permute-start.63 = (bf16[512,2048]{1,0:T(8,128)(2,1)S(1)}, bf16[512,2048]{1,0:T(8,128)(2,1)S(1)}, u32[]{:S(2)}, u32[]{:S(2)}) collective-permute-start(bf16[512,2048]{1,0:T(8,128)(2,1)S(1)} %fusion.46), channel_id=1, source_target_pairs={{0,1},{1,0},{2,3},{3,2},{4,5},{5,4},{6,7},{7,6},{8,9},{9,8},{10,11... | collective-permute-start | bytes 6291464 | tf_op jit(solution)/shard_map/ppermute | solution.py:183
  599.5 37.2 %collective-permute-start.65 = (bf16[256,3072]{1,0:T(8,128)(2,1)S(1)}, bf16[256,3072]{1,0:T(8,128)(2,1)S(1)}, u32[]{:S(2)}, u32[]{:S(2)}) collective-permute-start(bf16[256,3072]{1,0:T(8,128)(2,1)S(1)} %fusion.24), channel_id=1, source_target_pairs={{0,4},{8,0},{16,8},{24,16},{28,24},{20,28},{12,20},{4,12},{1,5},{9... | collective-permute-start | bytes 4718600 | tf_op jit(solution)/shard_map/ppermute | solution.py:72
  606.7 37.4 %collective-permute-start.79 = (bf16[704,256]{1,0:T(8,128)(2,1)S(1)}, bf16[704,256]{1,0:T(8,128)(2,1)S(1)}, u32[]{:S(2)}, u32[]{:S(2)}) collective-permute-start(bf16[704,256]{1,0:T(8,128)(2,1)S(1)} %copy-done.126), channel_id=1, source_target_pairs={{0,4},{8,0},{16,8},{24,16},{28,24},{20,28},{12,20},{4,12},{1,5},{9... | collective-permute-start | bytes 1081352 | tf_op jit(solution)/shard_map/ppermute | solution.py:72
  645.1 49.8 %collective-permute-start.66 = (bf16[512,2048]{1,0:T(8,128)(2,1)}, bf16[512,2048]{1,0:T(8,128)(2,1)}, u32[]{:S(2)}, u32[]{:S(2)}) collective-permute-start(bf16[512,2048]{1,0:T(8,128)(2,1)} %add_convert_fusion.1), channel_id=1, source_target_pairs={{0,2},{1,3},{2,0},{3,1},{4,6},{5,7},{6,4},{7,5},{8,10},{9,11},{10,... | collective-permute-start | bytes 6291464 | tf_op jit(solution)/shard_map/ppermute | solution.py:188
  662.0 27.7 %collective-permute-start.88 = (bf16[704,256]{1,0:T(8,128)(2,1)}, bf16[704,256]{1,0:T(8,128)(2,1)}, u32[]{:S(2)}, u32[]{:S(2)}) collective-permute-start(bf16[704,256]{1,0:T(8,128)(2,1)} %fusion.69), channel_id=1, source_target_pairs={{0,4},{8,0},{16,8},{24,16},{28,24},{20,28},{12,20},{4,12},{1,5},{9... | collective-permute-start | bytes 1081352 | tf_op jit(solution)/shard_map/ppermute | solution.py:72
  662.0 25.4 %collective-permute-start.81 = (bf16[704,256]{1,0:T(8,128)(2,1)}, bf16[704,256]{1,0:T(8,128)(2,1)}, u32[]{:S(2)}, u32[]{:S(2)}) collective-permute-start(bf16[704,256]{1,0:T(8,128)(2,1)} %convolution_convert_fusion.13), channel_id=1, source_target_pairs={{0,4},{8,0},{16,8},{24,16},{28,24},{20,28},{12,20},{4,12},{1,5},{9... | collective-permute-start | bytes 1081352 | tf_op jit(solution)/shard_map/ppermute | solution.py:72
  664.8 26.3 %collective-permute-start.84 = (bf16[704,256]{1,0:T(8,128)(2,1)}, bf16[704,256]{1,0:T(8,128)(2,1)}, u32[]{:S(2)}, u32[]{:S(2)}) collective-permute-start(bf16[704,256]{1,0:T(8,128)(2,1)} %fusion.68), channel_id=1, source_target_pairs={{0,8},{8,16},{16,24},{24,28},{28,20},{20,12},{12,4},{4,0},{1,9},{9... | collective-permute-start | bytes 1081352 | tf_op jit(solution)/shard_map/ppermute | solution.py:72
  689.8 20.3 %collective-permute-start.89 = (bf16[704,256]{1,0:T(8,128)(2,1)S(1)}, bf16[704,256]{1,0:T(8,128)(2,1)}, u32[]{:S(2)}, u32[]{:S(2)}) collective-permute-start(bf16[704,256]{1,0:T(8,128)(2,1)S(1)} %copy-done.128), channel_id=1, source_target_pairs={{0,4},{8,0},{16,8},{24,16},{28,24},{20,28},{12,20},{4,12},{1,5},{9... | collective-permute-start | bytes 1081352 | tf_op jit(solution)/shard_map/ppermute | solution.py:72
  691.1 25.7 %collective-permute-start.85 = (bf16[704,256]{1,0:T(8,128)(2,1)}, bf16[704,256]{1,0:T(8,128)(2,1)}, u32[]{:S(2)}, u32[]{:S(2)}) collective-permute-start(bf16[704,256]{1,0:T(8,128)(2,1)} %convolution_convert_fusion.11), channel_id=1, source_target_pairs={{0,8},{8,16},{16,24},{24,28},{28,20},{20,12},{12,4},{4,0},{1,9},{9... | collective-permute-start | bytes 1081352 | tf_op jit(solution)/shard_map/ppermute | solution.py:72
  719.1 46.3 %collective-permute-start.67 = (bf16[512,2048]{1,0:T(8,128)(2,1)S(1)}, bf16[512,2048]{1,0:T(8,128)(2,1)}, u32[]{:S(2)}, u32[]{:S(2)}) collective-permute-start(bf16[512,2048]{1,0:T(8,128)(2,1)S(1)} %get-tuple-element.403), channel_id=1, source_target_pairs={{0,1},{1,0},{2,3},{3,2},{4,5},{5,4},{6,7},{7,6},{8,9},{9,8},{10,11... | collective-permute-start | bytes 6291464 | tf_op jit(solution)/shard_map/ppermute | solution.py:183
  719.1 31.8 %collective-permute-start.83 = (bf16[704,256]{1,0:T(8,128)(2,1)}, bf16[704,256]{1,0:T(8,128)(2,1)}, u32[]{:S(2)}, u32[]{:S(2)}) collective-permute-start(bf16[704,256]{1,0:T(8,128)(2,1)} %add_convert_fusion.13), channel_id=1, source_target_pairs={{0,4},{8,0},{16,8},{24,16},{28,24},{20,28},{12,20},{4,12},{1,5},{9... | collective-permute-start | bytes 1081352 | tf_op jit(solution)/shard_map/ppermute | solution.py:72
  719.1 21.3 %collective-permute-start.86 = (bf16[704,256]{1,0:T(8,128)(2,1)}, bf16[704,256]{1,0:T(8,128)(2,1)}, u32[]{:S(2)}, u32[]{:S(2)}) collective-permute-start(bf16[704,256]{1,0:T(8,128)(2,1)} %add_convert_fusion.12), channel_id=1, source_target_pairs={{0,8},{8,16},{16,24},{24,28},{28,20},{20,12},{12,4},{4,0},{1,9},{9... | collective-permute-start | bytes 1081352 | tf_op jit(solution)/shard_map/ppermute | solution.py:72
  742.9 19.6 %collective-permute-start.87 = (bf16[704,256]{1,0:T(8,128)(2,1)}, bf16[704,256]{1,0:T(8,128)(2,1)}, u32[]{:S(2)}, u32[]{:S(2)}) collective-permute-start(bf16[704,256]{1,0:T(8,128)(2,1)} %add_convert_fusion.11), channel_id=1, source_target_pairs={{0,8},{8,16},{16,24},{24,28},{28,20},{20,12},{12,4},{4,0},{1,9},{9... | collective-permute-start | bytes 1081352 | tf_op jit(solution)/shard_map/ppermute | solution.py:72
  (169 other events, 2197.3 us)
Sparse Core Ops, SparseCore 0:
  546.0 89.2 all-reduce.15
  639.0 77.0 all-reduce.17

commit v10 on v9

--- a/solution.py
+++ b/solution.py
@@ -858,7 +858,7 @@
     grad_normed1 = tp_sum(
         lambda h: dot(half_of(back, h), w_both),
         chips=hold_output,
-        totals=lambda v: lands(v, 4),
+        totals=lambda v: lands(v, 5),
     )
     mlp_out = late[0]
     ring.drain()

time: 790 us -> 807 us (1.022)
  waiting for transfers between devices: 184 us -> 193 us
    unnamed x333 -> x339, local copies, waits for them, and re-layouts: 65.7 us -> 65.1 us
  transfers between devices with their start and end apart: 95 -> 95, of which waited for: 27 -> 24; matrix products, arithmetic and copies ran while one was open for 39% -> 39% of each run, Pallas kernels for 13% -> 13%
where the time goes in v10:
time: 807 us; the launch traced here: 797 us
  matrix products  198 us (25%)
  waiting for transfers between devices  193 us (24%)
  starting transfers between devices  120 us (15%)
  local copies, waits for them, and re-layouts  111 us (14%)
  Pallas kernels  111 us (14%)
  other arithmetic  46.4 us (6%)
  between operations  16.9 us (2%)
    ppermute x70, waiting for transfers between devices, issue(): flying.append((flow, lax.ppermute(message, 'seq', self.pairs[way])))  136 us
    dot_general x42, matrix products, down(): lax.dot_general(a, b, (((0,), (0,)), ((), ())), preferred_element_type=f32)  109 us
    ppermute x70, starting transfers between devices, issue(): flying.append((flow, lax.ppermute(message, 'seq', self.pairs[way])))  86.3 us
    unnamed x339, local copies, waits for them, and re-layouts  65.1 us
    pallas_call x8, Pallas kernels, by_rows(): pl.pallas_call(body, grid_spec=pltpu.PrefetchScalarGridSpec(num_scalar_pr...  55.8 us
    dot_general x19, matrix products, across(): lax.dot_general(a, b, (((1,), (1,)), ((), ())), preferred_element_type=f32)  47.3 us
    pallas_call x3, Pallas kernels, per_sequence(): pl.pallas_call(kernel, grid=(seqs,), in_specs=[spec(a.shape, kind) for a,...  42.8 us
    dot_general x6, matrix products, dot(): return jnp.dot(a, b, preferred_element_type=f32)  42.4 us
  transfers between devices with their start and end apart: 95, of which 24 were waited for; matrix products, arithmetic and copies ran while one was open for 39% of the time, Pallas kernels for 13%

profile of v10, /device:TPU:0, one launch (start us, length us, event | category | flops | bytes accessed | tf_op | source)
XLA Modules:
  0.0 797.0 jit_solution(10442628570828515006)
XLA Ops:
  29.8 3.4 constant_dynamic-update-slice_fusion.25
  35.5 8.5 %shard_map.255 = (bf16[4,256,2048]{2,1,0:T(8,128)(2,1)S(1)}, bf16[4,256,2048]{2,1,0:T(8,128)(2,1)}) custom-call(s32[4]{0:T(128)S(1)} %and_select_fusion.2.refs_0_, s32[8]{0:T(128)S(1)} %gather_fusion, bf16[4,256,2048]{2,1,0:T(8,128)(2,1)} %refs_2_, bf16[4,256,2048]{2,1,0:T(8,128)(2,1)} %refs_3_), custom_call_target="tpu_custom_call" | custom-call | flops 16777216 | bytes 16777216 | tf_op jit(solution)/shard_map/pallas_call | solution.py:419
  66.3 8.2 %collective-permute-done.7 = bf16[1056,256]{1,0:T(8,128)(2,1)S(1)} collective-permute-done((bf16[1056,256]{1,0:T(8,128)(2,1)}, bf16[1056,256]{1,0:T(8,128)(2,1)S(1)}, u32[]{:S(2)}, u32[]{:S(2)}) %collective-permute-start.7) | collective-permute-done | bytes 540704 | tf_op jit(solution)/shard_map/ppermute | solution.py:72
  77.0 9.6 %collective-permute-done.9 = bf16[1072,256]{1,0:T(8,128)(2,1)S(1)} collective-permute-done((bf16[1072,256]{1,0:T(8,128)(2,1)S(1)}, bf16[1072,256]{1,0:T(8,128)(2,1)S(1)}, u32[]{:S(2)}, u32[]{:S(2)}) %collective-permute-start.9) | collective-permute-done | bytes 548896 | tf_op jit(solution)/shard_map/ppermute | solution.py:72
  89.7 8.2 %collective-permute-done.13 = bf16[1056,256]{1,0:T(8,128)(2,1)S(1)} collective-permute-done((bf16[1056,256]{1,0:T(8,128)(2,1)S(1)}, bf16[1056,256]{1,0:T(8,128)(2,1)S(1)}, u32[]{:S(2)}, u32[]{:S(2)}) %collective-permute-start.13) | collective-permute-done | bytes 540704 | tf_op jit(solution)/shard_map/ppermute | solution.py:72
  113.8 3.4 add_convert_fusion.7
  120.9 3.3 add_convert_fusion.6
  130.3 3.6 collective-permute-start.16
  135.6 13.3 %collective-permute-done.16 = bf16[4,3,704]{2,1,0:T(4,128)(2,1)S(1)} collective-permute-done((bf16[4,3,704]{2,1,0:T(4,128)(2,1)S(1)}, bf16[4,3,704]{2,1,0:T(4,128)(2,1)S(1)}, u32[]{:S(2)}, u32[]{:S(2)}) %collective-permute-start.16) | collective-permute-done | bytes 16928 | tf_op jit(solution)/shard_map/ppermute | solution.py:661
  148.9 3.3 collective-permute-start.22
  155.2 16.0 %shard_map.256 = (f32[4,256,704]{2,1,0:T(8,128)}, f32[4,256,704]{2,1,0:T(8,128)}, f32[4,256,704]{2,1,0:T(8,128)}, f32[4,256,704]{2,1,0:T(8,128)}, f32[4,256,704]...) custom-call(bf16[4,256,704]{2,1,0:T(8,128)(2,1)S(1)} %bitcast.194, ...), custom_call_target="tpu_custom_call" | custom-call | flops 2030043136 | bytes 23812096 | tf_op jit(solution)/shard_map/pallas_call | solution.py:382
  176.9 5.3 collective-permute-start.24
  182.3 7.6 collective-permute-done.24
  189.9 5.3 collective-permute-start.25
  195.3 5.0 collective-permute-start.26
  204.5 6.0 fusion.36
  212.4 3.3 convolution_convert_fusion.4
  227.0 3.4 convolution_convert_fusion.5
  231.4 13.9 %collective-permute-done.30 = bf16[256,1536]{1,0:T(8,128)(2,1)S(1)} collective-permute-done((bf16[256,1536]{1,0:T(8,128)(2,1)S(1)}, bf16[256,1536]{1,0:T(8,128)(2,1)S(1)}, u32[]{:S(2)}, u32[]{:S(2)}) %collective-permute-start.30) | collective-permute-done | bytes 786464 | tf_op jit(solution)/shard_map/ppermute | solution.py:72
  255.1 6.8 collective-permute-done.34
  264.4 5.6 collective-permute-done.38
  272.1 9.2 %collective-permute-done.35 = bf16[1536,256]{1,0:T(8,128)(2,1)S(1)} collective-permute-done((bf16[1536,256]{1,0:T(8,128)(2,1)S(1)}, bf16[1536,256]{1,0:T(8,128)(2,1)S(1)}, u32[]{:S(2)}, u32[]{:S(2)}) %collective-permute-start.35) | collective-permute-done | bytes 786464 | tf_op jit(solution)/shard_map/ppermute | solution.py:72
  284.3 8.2 %collective-permute-done.32 = bf16[512,2048]{1,0:T(8,128)(2,1)S(1)} collective-permute-done((bf16[512,2048]{1,0:T(8,128)(2,1)S(1)}, bf16[512,2048]{1,0:T(8,128)(2,1)S(1)}, u32[]{:S(2)}, u32[]{:S(2)}) %collective-permute-start.32) | collective-permute-done | bytes 2097184 | tf_op jit(solution)/shard_map/ppermute | solution.py:188
  293.5 11.5 %collective-permute-done.40 = bf16[256,1536]{1,0:T(8,128)(2,1)S(1)} collective-permute-done((bf16[256,1536]{1,0:T(8,128)(2,1)S(1)}, bf16[256,1536]{1,0:T(8,128)(2,1)S(1)}, u32[]{:S(2)}, u32[]{:S(2)}) %collective-permute-start.40) | collective-permute-done | bytes 786464 | tf_op jit(solution)/shard_map/ppermute | solution.py:72
  316.1 5.0 shard_map.257
  321.2 5.1 shard_map.258
  328.7 17.5 %convolution_convert_fusion = bf16[1024,3072]{1,0:T(8,128)(2,1)S(1)} fusion(bf16[1024,2048]{1,0:T(8,128)(2,1)} %bitcast.220, bf16[2048,1536]{1,0:T(8,128)(2,1)} %copy-done.109, bf16[2048,1536]{1,0:T(8,128)(2,1)} %copy-done.108), kind=kOutput, calls=%fused_computation.40 | convolution fusion | flops 12913213440 | bytes 23068672 | tf_op jit(solution)/shard_map/dot_general | solution.py:580
  346.2 6.4 fusion.6
  368.8 12.4 %shard_map.259 = bf16[1024,3072]{1,0:T(8,128)(2,1)} custom-call(bf16[1024,2048]{1,0:T(8,128)(2,1)} %bitcast.231, bf16[1536,2048]{1,0:T(8,128)(2,1)} %constant_dynamic-update-slice_fusion.26.w_down, bf16[1024,1536]{1,0:T(8,128)(2,1)S(1)} %get-tuple-element.270.act, bf16[1024,1536]{1,0:T(8,128)(2,1)} %get-tuple-element.271.slope), custom_call_target="tpu_custom_call" | custom-call | flops 6442450944 | bytes 23068672 | tf_op jit(solution)/shard_map/pallas_call | solution.py:740
  381.3 11.8 %fusion.50 = bf16[512,2048]{1,0:T(8,128)(2,1)} fusion(bf16[2048,1536]{1,0:T(8,128)(2,1)} %copy-done.109, bf16[2048,1536]{1,0:T(8,128)(2,1)} %copy-done.108, bf16[1024,3072]{1,0:T(8,128)(2,1)} %shard_map.259), kind=kOutput, calls=%fused_computation.101 | convolution fusion | flops 6468665344 | bytes 17825792 | tf_op jit(solution)/shard_map/dot_general | solution.py:572
  393.2 4.1 convolution_convert_fusion.1
  397.9 4.1 convolution_convert_fusion.2
  403.5 10.8 %fusion.47 = bf16[512,2048]{1,0:T(8,128)(2,1)} fusion(bf16[2048,1536]{1,0:T(8,128)(2,1)} %copy-done.109, bf16[2048,1536]{1,0:T(8,128)(2,1)} %copy-done.108, bf16[1024,3072]{1,0:T(8,128)(2,1)S(1)} %copy-done.26), kind=kOutput, calls=%fused_computation.100 | convolution fusion | flops 6468665344 | bytes 17825792 | tf_op jit(solution)/shard_map/dot_general | solution.py:572
  417.3 4.6 fusion.33
  428.5 6.3 collective-permute-done.52
  434.8 4.7 fusion.21
  440.0 4.7 fusion.20
  446.3 17.9 %collective-permute-done.46 = bf16[512,2048]{1,0:T(8,128)(2,1)S(1)} collective-permute-done((bf16[512,2048]{1,0:T(8,128)(2,1)S(1)}, bf16[512,2048]{1,0:T(8,128)(2,1)S(1)}, u32[]{:S(2)}, u32[]{:S(2)}) %collective-permute-start.46) | collective-permute-done | bytes 2097184 | tf_op jit(solution)/shard_map/ppermute | solution.py:188
  473.9 7.3 shard_map.260
  481.3 7.5 shard_map.261
  490.2 7.8 fusion.86
  498.0 7.9 shard_map.262
  511.8 4.2 fusion.23
  517.7 4.7 fusion.22
  522.4 3.4 fusion.58
  527.2 5.0 collective-permute-done.57
  534.8 11.0 %convolution_convert_fusion.3 = bf16[1024,2048]{1,0:T(8,128)(2,1)} fusion(bf16[1024,1536]{1,0:T(8,128)(2,1)S(1)} %copy-done.64, bf16[1536,2048]{1,0:T(8,128)(2,1)} %constant_dynamic-update-slice_fusion.26.w_down), kind=kOutput, calls=%fused_computation.73 | convolution fusion | flops 6444548096 | bytes 13631488 | tf_op jit(solution)/shard_map/dot_general | solution.py:580
  550.2 19.0 %shard_map.263 = (bf16[2,4,256,704]{3,2,1,0:T(8,128)(2,1)}, bf16[4,256,704]{2,1,0:T(8,128)(2,1)S(1)}, bf16[4,256,704]{2,1,0:T(8,128)(2,1)S(1)}, f32[4,8,704]{2,1...) custom-call(f32[4,256,704]{2,1,0:T(8,128)} %bitcast.241, f32[4,256,704]{2,1,0:T(8,128)} %get-tuple-element.425.slope, ...), custom_call_target="tpu_custom_call" | custom-call | flops 2030043136 | bytes 38514432 | tf_op jit(solution)/shard_map/pallas_call | solution.py:382
  593.1 3.6 fusion.46
  598.3 3.7 fusion.24
  604.4 3.6 fusion.45
  608.0 4.9 collective-permute-done.72
  614.6 31.9 %collective-permute-done.79 = bf16[704,256]{1,0:T(8,128)(2,1)S(1)} collective-permute-done((bf16[704,256]{1,0:T(8,128)(2,1)S(1)}, bf16[704,256]{1,0:T(8,128)(2,1)S(1)}, u32[]{:S(2)}, u32[]{:S(2)}) %collective-permute-start.79) | collective-permute-done | bytes 360480 | tf_op jit(solution)/shard_map/ppermute | solution.py:72
  650.4 5.3 collective-permute-start.73
  655.7 5.3 fusion.19
  669.9 3.5 fusion.53
  673.4 5.6 reshape.426
  681.3 8.5 %shard_map.264 = bf16[4,256,2048]{2,1,0:T(8,128)(2,1)} custom-call(s32[4]{0:T(128)S(1)} %copy-done.25, s32[8]{0:T(128)S(1)} %copy-done.21, f32[4,256,2048]{2,1,0:T(8,128)} %get-tuple-element.243.refs_0_.refs_2_, bf16[4,256,2048]{2,1,0:T(8,128)(2,1)S(1)} %bitcast.196), custom_call_target="tpu_custom_call" | custom-call | flops 16777216 | bytes 16777216 | tf_op jit(solution)/shard_map/pallas_call | solution.py:419
  699.2 4.1 collective-permute-done.88
  708.4 8.1 %collective-permute-done.82 = bf16[704,256]{1,0:T(8,128)(2,1)S(1)} collective-permute-done((bf16[704,256]{1,0:T(8,128)(2,1)S(1)}, bf16[704,256]{1,0:T(8,128)(2,1)S(1)}, u32[]{:S(2)}, u32[]{:S(2)}) %collective-permute-start.82) | collective-permute-done | bytes 360480 | tf_op jit(solution)/shard_map/ppermute | solution.py:72
  722.1 4.0 fusion.18
  731.8 5.1 collective-permute-done.69
  747.8 6.7 shard_map.265.refs_6_
  782.4 7.2 shard_map.266
  (658 shorter events, 303.6 us)
Async XLA Ops:
  7.2 671.8 %all-reduce.16.cloned.1.call-start = ((), (), s32[]{:S(2)}) async-start(), calls=%async_computation | async-start | bytes 8388608 | tf_op jit(solution)/shard_map/psum | solution.py:798
  11.2 22.1 %collective-permute-start = (bf16[1056,256]{1,0:T(8,128)(2,1)}, bf16[1056,256]{1,0:T(8,128)(2,1)S(1)}, u32[]{:S(2)}, u32[]{:S(2)}) collective-permute-start(bf16[1056,256]{1,0:T(8,128)(2,1)} %pad_maximum_fusion.21), channel_id=1, source_target_pairs={{0,8},{8,16},{16,24},{24,28},{28,20},{20,12},{12,4},{4,0},{1,9},{9... | collective-permute-start | bytes 1622024 | tf_op jit(solution)/shard_map/ppermute | solution.py:72
  14.2 19.1 %collective-permute-start.1 = (bf16[1056,256]{1,0:T(8,128)(2,1)}, bf16[1056,256]{1,0:T(8,128)(2,1)}, u32[]{:S(2)}, u32[]{:S(2)}) collective-permute-start(bf16[1056,256]{1,0:T(8,128)(2,1)} %pad_maximum_fusion.21), channel_id=1, source_target_pairs={{0,4},{8,0},{16,8},{24,16},{28,24},{20,28},{12,20},{4,12},{1,5},{9... | collective-permute-start | bytes 1622024 | tf_op jit(solution)/shard_map/ppermute | solution.py:72
  15.1 30.8 %collective-permute-start.2 = (bf16[1072,256]{1,0:T(8,128)(2,1)}, bf16[1072,256]{1,0:T(8,128)(2,1)}, u32[]{:S(2)}, u32[]{:S(2)}) collective-permute-start(bf16[1072,256]{1,0:T(8,128)(2,1)} %pad_maximum_fusion.20), channel_id=1, source_target_pairs={{0,8},{8,16},{16,24},{24,28},{28,20},{20,12},{12,4},{4,0},{1,9},{9... | collective-permute-start | bytes 1646600 | tf_op jit(solution)/shard_map/ppermute | solution.py:72
  17.1 28.8 %collective-permute-start.3 = (bf16[1072,256]{1,0:T(8,128)(2,1)}, bf16[1072,256]{1,0:T(8,128)(2,1)}, u32[]{:S(2)}, u32[]{:S(2)}) collective-permute-start(bf16[1072,256]{1,0:T(8,128)(2,1)} %pad_maximum_fusion.20), channel_id=1, source_target_pairs={{0,4},{8,0},{16,8},{24,16},{28,24},{20,28},{12,20},{4,12},{1,5},{9... | collective-permute-start | bytes 1646600 | tf_op jit(solution)/shard_map/ppermute | solution.py:72
  33.3 23.8 %collective-permute-start.10 = (bf16[1056,256]{1,0:T(8,128)(2,1)}, bf16[1056,256]{1,0:T(8,128)(2,1)S(1)}, u32[]{:S(2)}, u32[]{:S(2)}) collective-permute-start(bf16[1056,256]{1,0:T(8,128)(2,1)} %collective-permute-done.1), channel_id=1, source_target_pairs={{0,4},{8,0},{16,8},{24,16},{28,24},{20,28},{12,20},{4,12},{1,5},{9... | collective-permute-start | bytes 1622024 | tf_op jit(solution)/shard_map/ppermute | solution.py:72
  35.4 23.7 %collective-permute-start.5 = (bf16[1056,256]{1,0:T(8,128)(2,1)S(1)}, bf16[1056,256]{1,0:T(8,128)(2,1)}, u32[]{:S(2)}, u32[]{:S(2)}) collective-permute-start(bf16[1056,256]{1,0:T(8,128)(2,1)S(1)} %collective-permute-done), channel_id=1, source_target_pairs={{0,8},{8,16},{16,24},{24,28},{28,20},{20,12},{12,4},{4,0},{1,9},{9... | collective-permute-start | bytes 1622024 | tf_op jit(solution)/shard_map/ppermute | solution.py:72
  57.2 19.8 %collective-permute-start.11 = (bf16[1056,256]{1,0:T(8,128)(2,1)S(1)}, bf16[1056,256]{1,0:T(8,128)(2,1)S(1)}, u32[]{:S(2)}, u32[]{:S(2)}) collective-permute-start(bf16[1056,256]{1,0:T(8,128)(2,1)S(1)} %collective-permute-done.10), channel_id=1, source_target_pairs={{0,4},{8,0},{16,8},{24,16},{28,24},{20,28},{12,20},{4,12},{1,5},{9... | collective-permute-start | bytes 1622024 | tf_op jit(solution)/shard_map/ppermute | solution.py:72
  62.6 26.0 %collective-permute-start.6 = (bf16[1072,256]{1,0:T(8,128)(2,1)S(1)}, bf16[1072,256]{1,0:T(8,128)(2,1)S(1)}, u32[]{:S(2)}, u32[]{:S(2)}) collective-permute-start(bf16[1072,256]{1,0:T(8,128)(2,1)S(1)} %collective-permute-done.4), channel_id=1, source_target_pairs={{0,8},{8,16},{16,24},{24,28},{28,20},{20,12},{12,4},{4,0},{1,9},{9... | collective-permute-start | bytes 1646600 | tf_op jit(solution)/shard_map/ppermute | solution.py:72
  64.7 21.9 %collective-permute-start.9 = (bf16[1072,256]{1,0:T(8,128)(2,1)S(1)}, bf16[1072,256]{1,0:T(8,128)(2,1)S(1)}, u32[]{:S(2)}, u32[]{:S(2)}) collective-permute-start(bf16[1072,256]{1,0:T(8,128)(2,1)S(1)} %collective-permute-done.8), channel_id=1, source_target_pairs={{0,4},{8,0},{16,8},{24,16},{28,24},{20,28},{12,20},{4,12},{1,5},{9... | collective-permute-start | bytes 1646600 | tf_op jit(solution)/shard_map/ppermute | solution.py:72
  74.5 23.3 %collective-permute-start.13 = (bf16[1056,256]{1,0:T(8,128)(2,1)S(1)}, bf16[1056,256]{1,0:T(8,128)(2,1)S(1)}, u32[]{:S(2)}, u32[]{:S(2)}) collective-permute-start(bf16[1056,256]{1,0:T(8,128)(2,1)S(1)} %collective-permute-done.7), channel_id=1, source_target_pairs={{0,8},{8,16},{16,24},{24,28},{28,20},{20,12},{12,4},{4,0},{1,9},{9... | collective-permute-start | bytes 1622024 | tf_op jit(solution)/shard_map/ppermute | solution.py:72
  86.9 37.3 %collective-permute-start.15 = (bf16[256,1536]{1,0:T(8,128)(2,1)}, bf16[256,1536]{1,0:T(8,128)(2,1)}, u32[]{:S(2)}, u32[]{:S(2)}) collective-permute-start(bf16[256,1536]{1,0:T(8,128)(2,1)} %get-tuple-element.213), channel_id=1, source_target_pairs={{0,4},{8,0},{16,8},{24,16},{28,24},{20,28},{12,20},{4,12},{1,5},{9... | collective-permute-start | bytes 2359304 | tf_op jit(solution)/shard_map/ppermute | solution.py:72
  88.6 35.6 %collective-permute-start.14 = (bf16[256,1536]{1,0:T(8,128)(2,1)}, bf16[256,1536]{1,0:T(8,128)(2,1)}, u32[]{:S(2)}, u32[]{:S(2)}) collective-permute-start(bf16[256,1536]{1,0:T(8,128)(2,1)} %get-tuple-element.213), channel_id=1, source_target_pairs={{0,8},{8,16},{16,24},{24,28},{28,20},{20,12},{12,4},{4,0},{1,9},{9... | collective-permute-start | bytes 2359304 | tf_op jit(solution)/shard_map/ppermute | solution.py:72
  97.8 51.1 %collective-permute-start.17 = (bf16[256,1536]{1,0:T(8,128)(2,1)}, bf16[256,1536]{1,0:T(8,128)(2,1)}, u32[]{:S(2)}, u32[]{:S(2)}) collective-permute-start(bf16[256,1536]{1,0:T(8,128)(2,1)} %get-tuple-element.216), channel_id=1, source_target_pairs={{0,8},{8,16},{16,24},{24,28},{28,20},{20,12},{12,4},{4,0},{1,9},{9... | collective-permute-start | bytes 2359304 | tf_op jit(solution)/shard_map/ppermute | solution.py:72
  109.0 39.9 %collective-permute-start.18 = (bf16[256,1536]{1,0:T(8,128)(2,1)}, bf16[256,1536]{1,0:T(8,128)(2,1)}, u32[]{:S(2)}, u32[]{:S(2)}) collective-permute-start(bf16[256,1536]{1,0:T(8,128)(2,1)} %get-tuple-element.216), channel_id=1, source_target_pairs={{0,4},{8,0},{16,8},{24,16},{28,24},{20,28},{12,20},{4,12},{1,5},{9... | collective-permute-start | bytes 2359304 | tf_op jit(solution)/shard_map/ppermute | solution.py:72
  124.2 47.0 %collective-permute-start.19 = (bf16[256,1536]{1,0:T(8,128)(2,1)}, bf16[256,1536]{1,0:T(8,128)(2,1)}, u32[]{:S(2)}, u32[]{:S(2)}) collective-permute-start(bf16[256,1536]{1,0:T(8,128)(2,1)} %collective-permute-done.14), channel_id=1, source_target_pairs={{0,8},{8,16},{16,24},{24,28},{28,20},{20,12},{12,4},{4,0},{1,9},{9... | collective-permute-start | bytes 2359304 | tf_op jit(solution)/shard_map/ppermute | solution.py:72
  126.0 45.3 %collective-permute-start.20 = (bf16[256,1536]{1,0:T(8,128)(2,1)}, bf16[256,1536]{1,0:T(8,128)(2,1)}, u32[]{:S(2)}, u32[]{:S(2)}) collective-permute-start(bf16[256,1536]{1,0:T(8,128)(2,1)} %collective-permute-done.15), channel_id=1, source_target_pairs={{0,4},{8,0},{16,8},{24,16},{28,24},{20,28},{12,20},{4,12},{1,5},{9... | collective-permute-start | bytes 2359304 | tf_op jit(solution)/shard_map/ppermute | solution.py:72
  130.3 18.6 %collective-permute-start.16 = (bf16[4,3,704]{2,1,0:T(4,128)(2,1)S(1)}, bf16[4,3,704]{2,1,0:T(4,128)(2,1)S(1)}, u32[]{:S(2)}, u32[]{:S(2)}) collective-permute-start(bf16[4,3,704]{2,1,0:T(4,128)(2,1)S(1)} %slice.644), channel_id=1, source_target_pairs={{0,4},{4,8},{8,12},{12,16},{16,20},{20,24},{24,28},{1,5},{5,9},{9,... | collective-permute-start | bytes 50696 | tf_op jit(solution)/shard_map/ppermute | solution.py:661
  148.9 28.0 %collective-permute-start.22 = (bf16[256,1536]{1,0:T(8,128)(2,1)}, bf16[256,1536]{1,0:T(8,128)(2,1)S(1)}, u32[]{:S(2)}, u32[]{:S(2)}) collective-permute-start(bf16[256,1536]{1,0:T(8,128)(2,1)} %collective-permute-done.17), channel_id=1, source_target_pairs={{0,8},{8,16},{16,24},{24,28},{28,20},{20,12},{12,4},{4,0},{1,9},{9... | collective-permute-start | bytes 2359304 | tf_op jit(solution)/shard_map/ppermute | solution.py:72
  152.2 24.7 %collective-permute-start.23 = (bf16[256,1536]{1,0:T(8,128)(2,1)}, bf16[256,1536]{1,0:T(8,128)(2,1)S(1)}, u32[]{:S(2)}, u32[]{:S(2)}) collective-permute-start(bf16[256,1536]{1,0:T(8,128)(2,1)} %collective-permute-done.18), channel_id=1, source_target_pairs={{0,4},{8,0},{16,8},{24,16},{28,24},{20,28},{12,20},{4,12},{1,5},{9... | collective-permute-start | bytes 2359304 | tf_op jit(solution)/shard_map/ppermute | solution.py:72
  174.5 29.2 %collective-permute-start.27 = (bf16[256,1536]{1,0:T(8,128)(2,1)}, bf16[256,1536]{1,0:T(8,128)(2,1)}, u32[]{:S(2)}, u32[]{:S(2)}) collective-permute-start(bf16[256,1536]{1,0:T(8,128)(2,1)} %collective-permute-done.19), channel_id=1, source_target_pairs={{0,8},{8,16},{16,24},{24,28},{28,20},{20,12},{12,4},{4,0},{1,9},{9... | collective-permute-start | bytes 2359304 | tf_op jit(solution)/shard_map/ppermute | solution.py:72
  175.3 28.4 %collective-permute-start.28 = (bf16[256,1536]{1,0:T(8,128)(2,1)}, bf16[256,1536]{1,0:T(8,128)(2,1)S(1)}, u32[]{:S(2)}, u32[]{:S(2)}) collective-permute-start(bf16[256,1536]{1,0:T(8,128)(2,1)} %collective-permute-done.20), channel_id=1, source_target_pairs={{0,4},{8,0},{16,8},{24,16},{28,24},{20,28},{12,20},{4,12},{1,5},{9... | collective-permute-start | bytes 2359304 | tf_op jit(solution)/shard_map/ppermute | solution.py:72
  223.9 21.4 %collective-permute-start.30 = (bf16[256,1536]{1,0:T(8,128)(2,1)S(1)}, bf16[256,1536]{1,0:T(8,128)(2,1)S(1)}, u32[]{:S(2)}, u32[]{:S(2)}) collective-permute-start(bf16[256,1536]{1,0:T(8,128)(2,1)S(1)} %copy-done.100), channel_id=1, source_target_pairs={{0,8},{8,16},{16,24},{24,28},{28,20},{20,12},{12,4},{4,0},{1,9},{9... | collective-permute-start | bytes 2359304 | tf_op jit(solution)/shard_map/ppermute | solution.py:72
  224.8 20.5 %collective-permute-start.31 = (bf16[256,1536]{1,0:T(8,128)(2,1)S(1)}, bf16[256,1536]{1,0:T(8,128)(2,1)S(1)}, u32[]{:S(2)}, u32[]{:S(2)}) collective-permute-start(bf16[256,1536]{1,0:T(8,128)(2,1)S(1)} %copy-done.96), channel_id=1, source_target_pairs={{0,4},{8,0},{16,8},{24,16},{28,24},{20,28},{12,20},{4,12},{1,5},{9... | collective-permute-start | bytes 2359304 | tf_op jit(solution)/shard_map/ppermute | solution.py:72
  230.4 31.6 %collective-permute-start.34 = (bf16[1536,256]{1,0:T(8,128)(2,1)S(1)}, bf16[1536,256]{1,0:T(8,128)(2,1)S(1)}, u32[]{:S(2)}, u32[]{:S(2)}) collective-permute-start(bf16[1536,256]{1,0:T(8,128)(2,1)S(1)} %copy-done.94), channel_id=1, source_target_pairs={{0,8},{8,16},{16,24},{24,28},{28,20},{20,12},{12,4},{4,0},{1,9},{9... | collective-permute-start | bytes 2359304 | tf_op jit(solution)/shard_map/ppermute | solution.py:72
  245.3 47.3 %collective-permute-start.32 = (bf16[512,2048]{1,0:T(8,128)(2,1)S(1)}, bf16[512,2048]{1,0:T(8,128)(2,1)S(1)}, u32[]{:S(2)}, u32[]{:S(2)}) collective-permute-start(bf16[512,2048]{1,0:T(8,128)(2,1)S(1)} %add_convert_fusion.5), channel_id=1, source_target_pairs={{0,2},{1,3},{2,0},{3,1},{4,6},{5,7},{6,4},{7,5},{8,10},{9,11},{10,... | collective-permute-start | bytes 6291464 | tf_op jit(solution)/shard_map/ppermute | solution.py:188
  250.6 19.4 %collective-permute-start.38 = (bf16[1536,256]{1,0:T(8,128)(2,1)S(1)}, bf16[1536,256]{1,0:T(8,128)(2,1)S(1)}, u32[]{:S(2)}, u32[]{:S(2)}) collective-permute-start(bf16[1536,256]{1,0:T(8,128)(2,1)S(1)} %copy-done.94), channel_id=1, source_target_pairs={{0,4},{8,0},{16,8},{24,16},{28,24},{20,28},{12,20},{4,12},{1,5},{9... | collective-permute-start | bytes 2359304 | tf_op jit(solution)/shard_map/ppermute | solution.py:72
  262.0 19.4 %collective-permute-start.35 = (bf16[1536,256]{1,0:T(8,128)(2,1)S(1)}, bf16[1536,256]{1,0:T(8,128)(2,1)S(1)}, u32[]{:S(2)}, u32[]{:S(2)}) collective-permute-start(bf16[1536,256]{1,0:T(8,128)(2,1)S(1)} %collective-permute-done.34), channel_id=1, source_target_pairs={{0,8},{8,16},{16,24},{24,28},{28,20},{20,12},{12,4},{4,0},{1,9},{9... | collective-permute-start | bytes 2359304 | tf_op jit(solution)/shard_map/ppermute | solution.py:72
  270.0 23.6 %collective-permute-start.39 = (bf16[1536,256]{1,0:T(8,128)(2,1)S(1)}, bf16[1536,256]{1,0:T(8,128)(2,1)S(1)}, u32[]{:S(2)}, u32[]{:S(2)}) collective-permute-start(bf16[1536,256]{1,0:T(8,128)(2,1)S(1)} %collective-permute-done.38), channel_id=1, source_target_pairs={{0,4},{8,0},{16,8},{24,16},{28,24},{20,28},{12,20},{4,12},{1,5},{9... | collective-permute-start | bytes 2359304 | tf_op jit(solution)/shard_map/ppermute | solution.py:72
  282.3 22.8 %collective-permute-start.40 = (bf16[256,1536]{1,0:T(8,128)(2,1)S(1)}, bf16[256,1536]{1,0:T(8,128)(2,1)S(1)}, u32[]{:S(2)}, u32[]{:S(2)}) collective-permute-start(bf16[256,1536]{1,0:T(8,128)(2,1)S(1)} %collective-permute-done.31), channel_id=1, source_target_pairs={{0,4},{8,0},{16,8},{24,16},{28,24},{20,28},{12,20},{4,12},{1,5},{9... | collective-permute-start | bytes 2359304 | tf_op jit(solution)/shard_map/ppermute | solution.py:72
  283.8 21.8 %collective-permute-start.36 = (bf16[256,1536]{1,0:T(8,128)(2,1)}, bf16[256,1536]{1,0:T(8,128)(2,1)S(1)}, u32[]{:S(2)}, u32[]{:S(2)}) collective-permute-start(bf16[256,1536]{1,0:T(8,128)(2,1)} %collective-permute-done.27), channel_id=1, source_target_pairs={{0,8},{8,16},{16,24},{24,28},{28,20},{20,12},{12,4},{4,0},{1,9},{9... | collective-permute-start | bytes 2359304 | tf_op jit(solution)/shard_map/ppermute | solution.py:72
  293.4 27.8 %collective-permute-start.33 = (bf16[512,2048]{1,0:T(8,128)(2,1)S(1)}, bf16[512,2048]{1,0:T(8,128)(2,1)S(1)}, u32[]{:S(2)}, u32[]{:S(2)}) collective-permute-start(bf16[512,2048]{1,0:T(8,128)(2,1)S(1)} %add_convert_fusion.4), channel_id=1, source_target_pairs={{0,1},{1,0},{2,3},{3,2},{4,5},{5,4},{6,7},{7,6},{8,9},{9,8},{10,11... | collective-permute-start | bytes 6291464 | tf_op jit(solution)/shard_map/ppermute | solution.py:183
  305.1 21.1 %collective-permute-start.41 = (bf16[1536,256]{1,0:T(8,128)(2,1)S(1)}, bf16[1536,256]{1,0:T(8,128)(2,1)S(1)}, u32[]{:S(2)}, u32[]{:S(2)}) collective-permute-start(bf16[1536,256]{1,0:T(8,128)(2,1)S(1)} %collective-permute-done.39), channel_id=1, source_target_pairs={{0,4},{8,0},{16,8},{24,16},{28,24},{20,28},{12,20},{4,12},{1,5},{9... | collective-permute-start | bytes 2359304 | tf_op jit(solution)/shard_map/ppermute | solution.py:72
  305.6 20.6 %collective-permute-start.37 = (bf16[1536,256]{1,0:T(8,128)(2,1)S(1)}, bf16[1536,256]{1,0:T(8,128)(2,1)}, u32[]{:S(2)}, u32[]{:S(2)}) collective-permute-start(bf16[1536,256]{1,0:T(8,128)(2,1)S(1)} %collective-permute-done.35), channel_id=1, source_target_pairs={{0,8},{8,16},{16,24},{24,28},{28,20},{20,12},{12,4},{4,0},{1,9},{9... | collective-permute-start | bytes 2359304 | tf_op jit(solution)/shard_map/ppermute | solution.py:72
  327.1 28.2 %collective-permute-start.42 = (bf16[1536,256]{1,0:T(8,128)(2,1)}, bf16[1536,256]{1,0:T(8,128)(2,1)}, u32[]{:S(2)}, u32[]{:S(2)}) collective-permute-start(bf16[1536,256]{1,0:T(8,128)(2,1)} %collective-permute-done.37), channel_id=1, source_target_pairs={{0,8},{8,16},{16,24},{24,28},{28,20},{20,12},{12,4},{4,0},{1,9},{9... | collective-permute-start | bytes 2359304 | tf_op jit(solution)/shard_map/ppermute | solution.py:72
  361.4 31.7 %collective-permute-start.44 = (bf16[1536,256]{1,0:T(8,128)(2,1)}, bf16[1536,256]{1,0:T(8,128)(2,1)}, u32[]{:S(2)}, u32[]{:S(2)}) collective-permute-start(bf16[1536,256]{1,0:T(8,128)(2,1)} %convolution_convert_fusion.6), channel_id=1, source_target_pairs={{0,4},{8,0},{16,8},{24,16},{28,24},{20,28},{12,20},{4,12},{1,5},{9... | collective-permute-start | bytes 2359304 | tf_op jit(solution)/shard_map/ppermute | solution.py:72
  362.0 31.1 %collective-permute-start.43 = (bf16[1536,256]{1,0:T(8,128)(2,1)}, bf16[1536,256]{1,0:T(8,128)(2,1)}, u32[]{:S(2)}, u32[]{:S(2)}) collective-permute-start(bf16[1536,256]{1,0:T(8,128)(2,1)} %convolution_convert_fusion.7), channel_id=1, source_target_pairs={{0,8},{8,16},{16,24},{24,28},{28,20},{20,12},{12,4},{4,0},{1,9},{9... | collective-permute-start | bytes 2359304 | tf_op jit(solution)/shard_map/ppermute | solution.py:72
  393.1 21.2 %collective-permute-start.45 = (bf16[512,2048]{1,0:T(8,128)(2,1)}, bf16[512,2048]{1,0:T(8,128)(2,1)S(1)}, u32[]{:S(2)}, u32[]{:S(2)}) collective-permute-start(bf16[512,2048]{1,0:T(8,128)(2,1)} %fusion.50), channel_id=1, source_target_pairs={{0,1},{1,0},{2,3},{3,2},{4,5},{5,4},{6,7},{7,6},{8,9},{9,8},{10,11... | collective-permute-start | bytes 6291464 | tf_op jit(solution)/shard_map/ppermute | solution.py:183
  397.3 37.5 %collective-permute-start.52 = (bf16[256,3072]{1,0:T(8,128)(2,1)}, bf16[256,3072]{1,0:T(8,128)(2,1)}, u32[]{:S(2)}, u32[]{:S(2)}) collective-permute-start(bf16[256,3072]{1,0:T(8,128)(2,1)} %convolution_convert_fusion.1), channel_id=1, source_target_pairs={{0,4},{8,0},{16,8},{24,16},{28,24},{20,28},{12,20},{4,12},{1,5},{9... | collective-permute-start | bytes 4718600 | tf_op jit(solution)/shard_map/ppermute | solution.py:72
  401.9 38.1 %collective-permute-start.50 = (bf16[256,3072]{1,0:T(8,128)(2,1)}, bf16[256,3072]{1,0:T(8,128)(2,1)}, u32[]{:S(2)}, u32[]{:S(2)}) collective-permute-start(bf16[256,3072]{1,0:T(8,128)(2,1)} %convolution_convert_fusion.2), channel_id=1, source_target_pairs={{0,8},{8,16},{16,24},{24,28},{28,20},{20,12},{12,4},{4,0},{1,9},{9... | collective-permute-start | bytes 4718600 | tf_op jit(solution)/shard_map/ppermute | solution.py:72
  416.7 47.5 %collective-permute-start.46 = (bf16[512,2048]{1,0:T(8,128)(2,1)S(1)}, bf16[512,2048]{1,0:T(8,128)(2,1)S(1)}, u32[]{:S(2)}, u32[]{:S(2)}) collective-permute-start(bf16[512,2048]{1,0:T(8,128)(2,1)S(1)} %add_convert_fusion.3), channel_id=1, source_target_pairs={{0,2},{1,3},{2,0},{3,1},{4,6},{5,7},{6,4},{7,5},{8,10},{9,11},{10,... | collective-permute-start | bytes 6291464 | tf_op jit(solution)/shard_map/ppermute | solution.py:188
  424.1 40.9 %collective-permute-start.48 = (bf16[1536,256]{1,0:T(8,128)(2,1)S(1)}, bf16[1536,256]{1,0:T(8,128)(2,1)S(1)}, u32[]{:S(2)}, u32[]{:S(2)}) collective-permute-start(bf16[1536,256]{1,0:T(8,128)(2,1)S(1)} %fusion.55), channel_id=1, source_target_pairs={{0,4},{8,0},{16,8},{24,16},{28,24},{20,28},{12,20},{4,12},{1,5},{9... | collective-permute-start | bytes 2359304 | tf_op jit(solution)/shard_map/ppermute | solution.py:72
  427.0 38.1 %collective-permute-start.47 = (bf16[1536,256]{1,0:T(8,128)(2,1)S(1)}, bf16[1536,256]{1,0:T(8,128)(2,1)S(1)}, u32[]{:S(2)}, u32[]{:S(2)}) collective-permute-start(bf16[1536,256]{1,0:T(8,128)(2,1)S(1)} %fusion.54), channel_id=1, source_target_pairs={{0,8},{8,16},{16,24},{24,28},{28,20},{20,12},{12,4},{4,0},{1,9},{9... | collective-permute-start | bytes 2359304 | tf_op jit(solution)/shard_map/ppermute | solution.py:72
  439.4 49.3 %collective-permute-start.53 = (bf16[256,3072]{1,0:T(8,128)(2,1)}, bf16[256,3072]{1,0:T(8,128)(2,1)S(1)}, u32[]{:S(2)}, u32[]{:S(2)}) collective-permute-start(bf16[256,3072]{1,0:T(8,128)(2,1)} %fusion.21), channel_id=1, source_target_pairs={{0,4},{8,0},{16,8},{24,16},{28,24},{20,28},{12,20},{4,12},{1,5},{9... | collective-permute-start | bytes 4718600 | tf_op jit(solution)/shard_map/ppermute | solution.py:72
  444.7 45.5 %collective-permute-start.51 = (bf16[256,3072]{1,0:T(8,128)(2,1)}, bf16[256,3072]{1,0:T(8,128)(2,1)}, u32[]{:S(2)}, u32[]{:S(2)}) collective-permute-start(bf16[256,3072]{1,0:T(8,128)(2,1)} %fusion.20), channel_id=1, source_target_pairs={{0,8},{8,16},{16,24},{24,28},{28,20},{20,12},{12,4},{4,0},{1,9},{9... | collective-permute-start | bytes 4718600 | tf_op jit(solution)/shard_map/ppermute | solution.py:72
  469.9 36.0 %collective-permute-start.55 = (bf16[1536,256]{1,0:T(8,128)(2,1)}, bf16[1536,256]{1,0:T(8,128)(2,1)S(1)}, u32[]{:S(2)}, u32[]{:S(2)}) collective-permute-start(bf16[1536,256]{1,0:T(8,128)(2,1)} %fusion.57), channel_id=1, source_target_pairs={{0,4},{8,0},{16,8},{24,16},{28,24},{20,28},{12,20},{4,12},{1,5},{9... | collective-permute-start | bytes 2359304 | tf_op jit(solution)/shard_map/ppermute | solution.py:72
  472.5 33.8 %collective-permute-start.54 = (bf16[1536,256]{1,0:T(8,128)(2,1)}, bf16[1536,256]{1,0:T(8,128)(2,1)}, u32[]{:S(2)}, u32[]{:S(2)}) collective-permute-start(bf16[1536,256]{1,0:T(8,128)(2,1)} %fusion.56), channel_id=1, source_target_pairs={{0,8},{8,16},{16,24},{24,28},{28,20},{20,12},{12,4},{4,0},{1,9},{9... | collective-permute-start | bytes 2359304 | tf_op jit(solution)/shard_map/ppermute | solution.py:72
  545.8 210.7 %all-reduce.18.cloned.1.call-start = ((), (), s32[]{:S(2)}) async-start(), calls=%async_computation.1 | async-start | bytes 1081344 | tf_op jit(solution)/shard_map/psum | solution.py:876
  546.0 47.1 %collective-permute-start.62 = (bf16[256,3072]{1,0:T(8,128)(2,1)}, bf16[256,3072]{1,0:T(8,128)(2,1)}, u32[]{:S(2)}, u32[]{:S(2)}) collective-permute-start(bf16[256,3072]{1,0:T(8,128)(2,1)} %fusion.23), channel_id=1, source_target_pairs={{0,4},{8,0},{16,8},{24,16},{28,24},{20,28},{12,20},{4,12},{1,5},{9... | collective-permute-start | bytes 4718600 | tf_op jit(solution)/shard_map/ppermute | solution.py:72
  548.7 44.4 %collective-permute-start.61 = (bf16[256,3072]{1,0:T(8,128)(2,1)}, bf16[256,3072]{1,0:T(8,128)(2,1)}, u32[]{:S(2)}, u32[]{:S(2)}) collective-permute-start(bf16[256,3072]{1,0:T(8,128)(2,1)} %fusion.22), channel_id=1, source_target_pairs={{0,8},{8,16},{16,24},{24,28},{28,20},{20,12},{12,4},{4,0},{1,9},{9... | collective-permute-start | bytes 4718600 | tf_op jit(solution)/shard_map/ppermute | solution.py:72
  571.2 79.2 %collective-permute-start.64 = (bf16[1536,256]{1,0:T(8,128)(2,1)}, bf16[1536,256]{1,0:T(8,128)(2,1)}, u32[]{:S(2)}, u32[]{:S(2)}) collective-permute-start(bf16[1536,256]{1,0:T(8,128)(2,1)} %fusion.58), channel_id=1, source_target_pairs={{0,8},{8,16},{16,24},{24,28},{28,20},{20,12},{12,4},{4,0},{1,9},{9... | collective-permute-start | bytes 2359304 | tf_op jit(solution)/shard_map/ppermute | solution.py:72
  596.8 51.5 %collective-permute-start.63 = (bf16[512,2048]{1,0:T(8,128)(2,1)S(1)}, bf16[512,2048]{1,0:T(8,128)(2,1)S(1)}, u32[]{:S(2)}, u32[]{:S(2)}) collective-permute-start(bf16[512,2048]{1,0:T(8,128)(2,1)S(1)} %fusion.46), channel_id=1, source_target_pairs={{0,1},{1,0},{2,3},{3,2},{4,5},{5,4},{6,7},{7,6},{8,9},{9,8},{10,11... | collective-permute-start | bytes 6291464 | tf_op jit(solution)/shard_map/ppermute | solution.py:183
  602.0 48.4 %collective-permute-start.65 = (bf16[256,3072]{1,0:T(8,128)(2,1)S(1)}, bf16[256,3072]{1,0:T(8,128)(2,1)S(1)}, u32[]{:S(2)}, u32[]{:S(2)}) collective-permute-start(bf16[256,3072]{1,0:T(8,128)(2,1)S(1)} %fusion.24), channel_id=1, source_target_pairs={{0,4},{8,0},{16,8},{24,16},{28,24},{20,28},{12,20},{4,12},{1,5},{9... | collective-permute-start | bytes 4718600 | tf_op jit(solution)/shard_map/ppermute | solution.py:72
  604.1 42.5 %collective-permute-start.79 = (bf16[704,256]{1,0:T(8,128)(2,1)S(1)}, bf16[704,256]{1,0:T(8,128)(2,1)S(1)}, u32[]{:S(2)}, u32[]{:S(2)}) collective-permute-start(bf16[704,256]{1,0:T(8,128)(2,1)S(1)} %copy-done.127), channel_id=1, source_target_pairs={{0,4},{8,0},{16,8},{24,16},{28,24},{20,28},{12,20},{4,12},{1,5},{9... | collective-permute-start | bytes 1081352 | tf_op jit(solution)/shard_map/ppermute | solution.py:72
  661.0 61.1 %collective-permute-start.66 = (bf16[512,2048]{1,0:T(8,128)(2,1)}, bf16[512,2048]{1,0:T(8,128)(2,1)}, u32[]{:S(2)}, u32[]{:S(2)}) collective-permute-start(bf16[512,2048]{1,0:T(8,128)(2,1)} %add_convert_fusion.1), channel_id=1, source_target_pairs={{0,2},{1,3},{2,0},{3,1},{4,6},{5,7},{6,4},{7,5},{8,10},{9,11},{10,... | collective-permute-start | bytes 6291464 | tf_op jit(solution)/shard_map/ppermute | solution.py:188
  666.7 24.9 %collective-permute-start.74 = (bf16[704,256]{1,0:T(8,128)(2,1)}, bf16[704,256]{1,0:T(8,128)(2,1)}, u32[]{:S(2)}, u32[]{:S(2)}) collective-permute-start(bf16[704,256]{1,0:T(8,128)(2,1)} %fusion.65), channel_id=1, source_target_pairs={{0,8},{8,16},{16,24},{24,28},{28,20},{20,12},{12,4},{4,0},{1,9},{9... | collective-permute-start | bytes 1081352 | tf_op jit(solution)/shard_map/ppermute | solution.py:72
  669.2 24.5 %collective-permute-start.81 = (bf16[704,256]{1,0:T(8,128)(2,1)}, bf16[704,256]{1,0:T(8,128)(2,1)}, u32[]{:S(2)}, u32[]{:S(2)}) collective-permute-start(bf16[704,256]{1,0:T(8,128)(2,1)} %convolution_convert_fusion.13), channel_id=1, source_target_pairs={{0,4},{8,0},{16,8},{24,16},{28,24},{20,28},{12,20},{4,12},{1,5},{9... | collective-permute-start | bytes 1081352 | tf_op jit(solution)/shard_map/ppermute | solution.py:72
  695.3 21.2 %collective-permute-start.82 = (bf16[704,256]{1,0:T(8,128)(2,1)S(1)}, bf16[704,256]{1,0:T(8,128)(2,1)S(1)}, u32[]{:S(2)}, u32[]{:S(2)}) collective-permute-start(bf16[704,256]{1,0:T(8,128)(2,1)S(1)} %add_convert_fusion.14), channel_id=1, source_target_pairs={{0,4},{8,0},{16,8},{24,16},{28,24},{20,28},{12,20},{4,12},{1,5},{9... | collective-permute-start | bytes 1081352 | tf_op jit(solution)/shard_map/ppermute | solution.py:72
  697.3 20.6 %collective-permute-start.84 = (bf16[704,256]{1,0:T(8,128)(2,1)S(1)}, bf16[704,256]{1,0:T(8,128)(2,1)S(1)}, u32[]{:S(2)}, u32[]{:S(2)}) collective-permute-start(bf16[704,256]{1,0:T(8,128)(2,1)S(1)} %fusion.68), channel_id=1, source_target_pairs={{0,8},{8,16},{16,24},{24,28},{28,20},{20,12},{12,4},{4,0},{1,9},{9... | collective-permute-start | bytes 1081352 | tf_op jit(solution)/shard_map/ppermute | solution.py:72
  703.3 23.0 %collective-permute-start.89 = (bf16[704,256]{1,0:T(8,128)(2,1)S(1)}, bf16[704,256]{1,0:T(8,128)(2,1)S(1)}, u32[]{:S(2)}, u32[]{:S(2)}) collective-permute-start(bf16[704,256]{1,0:T(8,128)(2,1)S(1)} %copy-done.126), channel_id=1, source_target_pairs={{0,4},{8,0},{16,8},{24,16},{28,24},{20,28},{12,20},{4,12},{1,5},{9... | collective-permute-start | bytes 1081352 | tf_op jit(solution)/shard_map/ppermute | solution.py:72
  706.0 22.9 %collective-permute-start.76 = (bf16[704,256]{1,0:T(8,128)(2,1)}, bf16[704,256]{1,0:T(8,128)(2,1)}, u32[]{:S(2)}, u32[]{:S(2)}) collective-permute-start(bf16[704,256]{1,0:T(8,128)(2,1)} %add_convert_fusion.17), channel_id=1, source_target_pairs={{0,8},{8,16},{16,24},{24,28},{28,20},{20,12},{12,4},{4,0},{1,9},{9... | collective-permute-start | bytes 1081352 | tf_op jit(solution)/shard_map/ppermute | solution.py:72
  717.9 19.2 %collective-permute-start.85 = (bf16[704,256]{1,0:T(8,128)(2,1)S(1)}, bf16[704,256]{1,0:T(8,128)(2,1)}, u32[]{:S(2)}, u32[]{:S(2)}) collective-permute-start(bf16[704,256]{1,0:T(8,128)(2,1)S(1)} %copy-done.125), channel_id=1, source_target_pairs={{0,8},{8,16},{16,24},{24,28},{28,20},{20,12},{12,4},{4,0},{1,9},{9... | collective-permute-start | bytes 1081352 | tf_op jit(solution)/shard_map/ppermute | solution.py:72
  745.6 36.8 %collective-permute-start.67 = (bf16[512,2048]{1,0:T(8,128)(2,1)S(1)}, bf16[512,2048]{1,0:T(8,128)(2,1)}, u32[]{:S(2)}, u32[]{:S(2)}) collective-permute-start(bf16[512,2048]{1,0:T(8,128)(2,1)S(1)} %get-tuple-element.403), channel_id=1, source_target_pairs={{0,1},{1,0},{2,3},{3,2},{4,5},{5,4},{6,7},{7,6},{8,9},{9,8},{10,11... | collective-permute-start | bytes 6291464 | tf_op jit(solution)/shard_map/ppermute | solution.py:183
  745.6 22.1 %collective-permute-start.83 = (bf16[704,256]{1,0:T(8,128)(2,1)S(1)}, bf16[704,256]{1,0:T(8,128)(2,1)}, u32[]{:S(2)}, u32[]{:S(2)}) collective-permute-start(bf16[704,256]{1,0:T(8,128)(2,1)S(1)} %copy-done.129), channel_id=1, source_target_pairs={{0,4},{8,0},{16,8},{24,16},{28,24},{20,28},{12,20},{4,12},{1,5},{9... | collective-permute-start | bytes 1081352 | tf_op jit(solution)/shard_map/ppermute | solution.py:72
  (172 other events, 2219.5 us)
Sparse Core Ops, SparseCore 0:
  546.0 89.2 all-reduce.15
  639.1 76.6 all-reduce.17
